TPU v7x, 32 devices: a whole 2x2x4 slice. The times are simulated.
32 devices in a mesh: members: 2 (over y), lat: 4 (over z), lon: 4 (over x, core).
Axes of the slice: x: 2, y: 2, z: 4, core: 2. Of those that a mesh axis runs over, the one named last changes fastest.
Arguments:
- u_wind: float32 [128, 16, 3584], P(('members', 'lat'), None, 'lon'), parts along dimension 0, may hold values from -6 to 6
- v_wind: float32 [128, 16, 3584], P(('members', 'lat'), None, 'lon'), parts along dimension 0, may hold values from -6 to 6
- theta: float32 [128, 16, 3584], P(('members', 'lat'), None, 'lon'), parts along dimension 0, may hold values from -6 to 6
- geopot: float32 [128, 16, 3584], P(('members', 'lat'), None, 'lon'), parts along dimension 0, may hold values from -6 to 6
- mass: float32 [128, 3584], P(('members', 'lat'), 'lon'), parts along dimension 0, may hold values from 0.5 to 2
- cutoffs: int32 [32], replicated, may hold values from 1 to 447
Outputs:
- u_next: float32 [128, 16, 3584], P(('members', 'lat'), None, 'lon'), parts along dimension 0
- v_next: float32 [128, 16, 3584], P(('members', 'lat'), None, 'lon'), parts along dimension 0
- theta_next: float32 [128, 16, 3584], P(('members', 'lat'), None, 'lon'), parts along dimension 0
- geopot_next: float32 [128, 16, 3584], P(('members', 'lat'), None, 'lon'), parts along dimension 0
There are 2 independent parts, one for each index of `members`. A program takes and returns all parts, laid end to end along the dimension named above; an argument that names none is the same for every part. Nothing has to cross between parts.
All inputs are finite; a program needn't handle non-finite values.
Results may differ from a plain program's by a relative error of at most 0.00005.
Values sent between devices are 32-bit elements; how exact they have to be, the bound alone decides.
No kernel may reach another device: no remote copies, remote signals or barrier semaphores. Data moves between devices by JAX's collectives and lax.ppermute only.
A program may use at most 192 MiB of HBM per device.

v0:
```python
import math

import jax
import jax.numpy as jnp
from jax import lax
from jax.sharding import PartitionSpec as P

STEP = 0.1
SPIN = 0.5
EXACT = lax.Precision.HIGHEST


def padded_2(cells, sides, width, closed):
    for axis, dim in sides:
        count = lax.axis_size(axis)
        ends = count if closed else count - 1
        head = lax.slice_in_dim(cells, 0, width, axis=dim)
        tail = lax.slice_in_dim(cells, cells.shape[dim] - width, cells.shape[dim], axis=dim)
        cells = jnp.concatenate(
            [
                lax.ppermute(tail, axis, [(i, (i + 1) % count) for i in range(ends)]),
                cells,
                lax.ppermute(head, axis, [((i + 1) % count, i) for i in range(ends)]),
            ],
            axis=dim,
        )
    return cells


def window(padded, offset, along, length):
    return lax.slice_in_dim(padded, 3 + offset, 3 + offset + length, axis=along)


def centered(padded, along, length):

    def pick(offset):
        return window(padded, offset, along, length)

    return (45.0 * (pick(1) - pick(-1)) - 9.0 * (pick(2) - pick(-2)) + (pick(3) - pick(-3))) / 60.0


def hyperdiff(padded, along, length):

    def pick(offset):
        return window(padded, offset, along, length)

    return (
        pick(3)
        + pick(-3)
        - 6.0 * (pick(2) + pick(-2))
        + 15.0 * (pick(1) + pick(-1))
        - 20.0 * pick(0)
    ) / 60.0


def tendencies(padded, latitude):
    row_count = padded.shape[0] - 6
    col_count = padded.shape[2] - 6
    levels = (padded.shape[1] - 1) // 4
    across = padded[3 : 3 + row_count]
    upward = padded[:, :, 3 : 3 + col_count]
    grad_x = centered(across, 2, col_count)
    diss_x = hyperdiff(across, 2, col_count)
    grad_y = centered(upward, 0, row_count)
    diss_y = hyperdiff(upward, 0, row_count)
    centre = across[:, :, 3 : 3 + col_count]
    shape_four = (row_count, 4, levels, col_count)
    metric = (1.0 / jnp.cos(latitude))[:, None, None]
    spin_term = (SPIN * jnp.sin(latitude))[:, None, None]
    east = centre[:, 0:levels]
    north = centre[:, levels : 2 * levels]
    potent = centre[:, 2 * levels : 3 * levels]
    column = centre[:, 4 * levels :]
    slope_x = grad_x[:, : 4 * levels].reshape(shape_four)
    smooth_x = diss_x[:, : 4 * levels].reshape(shape_four)
    slope_y = grad_y[:, : 4 * levels].reshape(shape_four)
    smooth_y = diss_y[:, : 4 * levels].reshape(shape_four)
    east_all = east[:, None]
    north_all = north[:, None]
    advect = (
        metric[:, None] * (east_all * slope_x - jnp.abs(east_all) * smooth_x)
        + north_all * slope_y
        - jnp.abs(north_all) * smooth_y
    )
    mass_x = grad_x[:, 4 * levels :] / column
    mass_y = grad_y[:, 4 * levels :] / column
    tend_east = -advect[:, 0] + spin_term * north - metric * (slope_x[:, 3] + potent * mass_x)
    tend_north = -advect[:, 1] - spin_term * east - (slope_y[:, 3] + potent * mass_y)
    return jnp.stack([tend_east, tend_north, -advect[:, 2], -advect[:, 3]], axis=1)


def fourier_table(count, circle, mode_count):
    position = jnp.arange(count, dtype=jnp.int32)
    wave = jnp.arange(mode_count, dtype=jnp.int32)
    phase = position[:, None] * wave[None, :] % circle
    angle = phase.astype(jnp.float32) * (2.0 * math.pi / circle)
    return jnp.concatenate([jnp.cos(angle), jnp.sin(angle)], axis=1)


def keep_modes(coeffs, item_cut, mode_count, circle):
    wave = jnp.arange(2 * mode_count, dtype=jnp.int32) % mode_count
    factor = jnp.where(wave == 0, 1.0 / circle, 2.0 / circle).astype(jnp.float32)
    keep = wave[None, :] <= item_cut[:, None]
    return jnp.where(keep, coeffs * factor[None, :], 0.0)


def spectral_filter(block, row_cut, lon_idx, lon_count):
    row_count, var_count, levels, columns = block.shape
    item_count = row_count * var_count * levels
    flattened = block.reshape(item_count, columns)
    circle = columns * lon_count
    mode_count = circle // 8
    item_cut = jnp.repeat(row_cut, var_count * levels)
    circles = lax.all_to_all(flattened, "lon", split_axis=0, concat_axis=1, tiled=True)
    share_size = item_count // lon_count
    own_cut = lax.dynamic_slice_in_dim(item_cut, lon_idx * share_size, share_size)
    fourier = fourier_table(circle, circle, mode_count)
    coeffs = jnp.dot(circles, fourier, precision=EXACT, preferred_element_type=jnp.float32)
    kept = keep_modes(coeffs, own_cut, mode_count, circle)
    smoothed = jnp.einsum("ic,xc->ix", kept, fourier, precision=EXACT)
    result = lax.all_to_all(smoothed, "lon", split_axis=1, concat_axis=0, tiled=True)
    return result.reshape(block.shape)


def row_cutoffs(cutoffs, owner, row_count, lat_count):
    quarter = lat_count // 4
    first = jnp.where(
        owner < quarter, owner * row_count, owner * row_count - lat_count * row_count // 2
    )
    first = jnp.clip(first, 0, cutoffs.shape[0] - row_count)
    return lax.dynamic_slice_in_dim(cutoffs, first, row_count)


def shards(u_wind, v_wind, theta, geopot, mass, cutoffs):
    row_count, levels, columns = u_wind.shape
    lat_count = lax.axis_size("lat")
    lon_count = lax.axis_size("lon")
    lat_idx = lax.axis_index("lat")
    lon_idx = lax.axis_index("lon")
    nlat_all = row_count * lat_count
    stacked = jnp.concatenate([u_wind, v_wind, theta, geopot, mass[:, None, :]], axis=1)
    wide = padded_2(stacked, (("lon", 2),), 3, True)
    padded = padded_2(wide, (("lat", 0),), 3, False)
    row_global = lat_idx * row_count + jnp.arange(row_count, dtype=jnp.int32)
    latitude = (row_global.astype(jnp.float32) + 0.5) * (math.pi / nlat_all) - math.pi / 2
    tend = tendencies(padded, latitude)
    quarter = lat_count // 4
    polar = (lat_idx < quarter) | (lat_idx >= lat_count - quarter)
    filtered = spectral_filter(
        tend, row_cutoffs(cutoffs, lat_idx, row_count, lat_count), lon_idx, lon_count
    )
    final_tend = jnp.where(polar, filtered, tend)
    updated = stacked[:, : 4 * levels].reshape(row_count, 4, levels, columns) + STEP * final_tend
    return (updated[:, 0], updated[:, 1], updated[:, 2], updated[:, 3])


def solution(mesh):
    return jax.shard_map(
        shards,
        mesh=mesh,
        in_specs=(
            P(("members", "lat"), None, "lon"),
            P(("members", "lat"), None, "lon"),
            P(("members", "lat"), None, "lon"),
            P(("members", "lat"), None, "lon"),
            P(("members", "lat"), "lon"),
            P(),
        ),
        out_specs=(
            P(("members", "lat"), None, "lon"),
            P(("members", "lat"), None, "lon"),
            P(("members", "lat"), None, "lon"),
            P(("members", "lat"), None, "lon"),
        ),
        check_vma=False,
    )
```

profile of v0, /device:TPU:0, one launch (start us, length us, event | category | flops | bytes accessed | tf_op | source)
XLA Modules:
  0.0 261.8 jit_solution(17707277724891463049)
XLA Ops:
  0.6 0.0 copy-start.9
  0.6 0.0 copy-start.13
  0.7 2.7 %fusion.55 = (f32[16,16,896]{2,1,0:T(8,128)}, f32[16,65,896]{2,1,0:T(8,128)}) fusion(f32[16,16,896]{2,1,0:T(8,128)} %param.6), kind=kLoop, calls=%fused_computation.109 | loop fusion | flops 229375 | bytes 2752512 | tf_op jit(solution)/shard_map/abs | solution.py:81
  3.4 0.9 broadcast_in_dim.28
  4.2 2.6 fusion.56
  6.8 0.0 copy-done.9
  6.8 1.0 constant_dynamic-update-slice_fusion.1
  7.8 0.0 copy-done.13
  7.8 1.1 constant_dynamic-update-slice_fusion
  8.9 2.0 dynamic-update-slice.4
  10.9 1.5 fusion.54
  12.3 0.3 copy.21
  12.6 2.4 collective-permute-start
  15.0 0.2 copy.23
  15.2 0.0 collective-permute-start.1
  15.3 1.2 collective-permute-done
  16.5 0.3 copy.22
  16.8 1.7 collective-permute-done.1
  18.5 0.3 copy.24
  18.8 2.0 pad_maximum_fusion.14
  20.8 1.3 collective-permute-start.2
  22.1 4.8 %collective-permute-start.3 = (f32[3,65,902]{2,1,0:T(8,128)S(1)}, f32[3,65,902]{2,1,0:T(8,128)S(1)}, u32[]{:S(2)}, u32[]{:S(2)}) collective-permute-start(f32[3,65,902]{2,1,0:T(8,128)S(1)} %get-tuple-element.19), channel_id=1, source_target_pairs={{0,4},{4,8},{8,12},{1,5},{5,9},{9,13},{2,6},{6,10},{10,14},{3,7},{... | collective-permute-start | bytes 2110688 | tf_op jit(solution)/shard_map/ppermute | solution.py:21
  26.9 22.5 %fusion.15 = (f32[16,65,896]{2,1,0:T(8,128)S(1)}, f32[16,65,896]{2,1,0:T(8,128)}, f32[16,65,896]{2,1,0:T(8,128)}, f32[16,65,896]{2,1,0:T(8,128)}, f32[16,65,896]{2,1,0:T(8,128)}, /*index=5*/f32[16,65,896]{2,1,0:T(8,128)}) fusion(f32[16,65,3]{2,1,0:T(8,128)S(1)} %copy.22, f32[16,65,3]{2,1,0:T(8,128)S(1)} %copy.24, f32[16,65,896]{2,1,0:T(8,128)} %dynamic-update-slice.4), kind=kLoop, calls=%fused_computation.32 | loop fusion | flops 13977600 | bytes 26116480 | tf_op jit(solution)/shard_map/div | solution.py:39
  49.4 2.5 slice.174
  51.9 0.0 collective-permute-done.2
  51.9 0.0 collective-permute-done.3
  51.9 10.3 %pad_maximum_fusion.5 = (f32[19,65,902]{2,1,0:T(8,128)}, f32[19,65,902]{2,1,0:T(8,128)}) fusion(f32[3,65,902]{2,1,0:T(8,128)S(1)} %collective-permute-done.2, f32[16,65,3]{2,1,0:T(8,128)S(1)} %copy.22, f32[16,65,896]{2,1,0:T(8,128)} %dynamic-update-slice.4, f32[16,65,3]{2,1,0:T(8,128)S(1)} %copy.24, f32[3,65,902]{2,1,0:T(8,128)S(1)} %collective-permute-done.3), kind=kLoop, calls=%fused_computation.20 | loop fusion | flops 6683820 | bytes 14071200 | tf_op jit(solution)/shard_map/concatenate | solution.py:19
  62.3 0.0 copy-done.1
  62.3 18.3 %add_multiply_fusion = (f32[16,65,896]{2,1,0:T(8,128)}, f32[16,65,896]{2,1,0:T(8,128)}, f32[16,65,896]{2,1,0:T(8,128)}, f32[16,65,896]{2,1,0:T(8,128)}, f32[16,6...) fusion(f32[19,65,902]{2,1,0:T(8,128)} %get-tuple-element.17, f32[19,65,902]{2,1,0:T(8,128)} %get-tuple-element.16), kind=kLoop, calls=%fused_computation.33 | loop fusion | flops 7454720 | bytes 48455680 | tf_op jit(solution)/shard_map/div | solution.py:39
  80.6 0.0 copy-done.14
  80.6 1.2 slice_divide_fusion.1
  81.8 4.3 %slice.190 = f32[16,64,896]{2,1,0:T(8,128)} slice(f32[16,65,896]{2,1,0:T(8,128)} %get-tuple-element.9), slice={[0:16], [0:64], [0:896]} | slice | bytes 7340032 | tf_op jit(solution)/shard_map/slice | solution.py:76
  86.1 20.7 %fusion.21 = (f32[16,64,896]{2,1,0:T(8,128)}, f32[16,64,896]{2,1,0:T(8,128)}) fusion(f32[16,65,896]{2,1,0:T(8,128)} %dynamic-update-slice.4, f32[16,65,3]{2,1,0:T(8,128)S(1)} %copy.22, f32[16,65,3]{2,1,0:T(8,128)S(1)} %copy.24, f32[16,65,896]{2,1,0:T(8,128)} %get-tuple-element.8, f32[16,65,896]{2,1,0:T(8,128)} %get-tuple-element.7, ...), kind=kLoop, calls=%fused_computation.41 | loop fusion | flops 18350080 | bytes 51462528 | tf_op jit(solution)/shard_map/div | solution.py:47
  106.8 0.0 copy-done.2
  106.8 0.0 copy-done.4
  106.8 7.9 %multiply_subtract_fusion = f32[16,4,16,896]{3,2,1,0:T(8,128)S(1)} fusion(f32[16,4,16,896]{3,2,1,0:T(8,128)} %bitcast.88, f32[16,4,16,896]{3,2,1,0:T(8,128)} %bitcast.85, f32[16,4,16,896]{3,2,1,0:T(8,128)} %bitcast.87, f32[16,4,16,896]{3,2,1,0:T(8,128)} %bitcast.83, f32[16,16,896]{2,1,0:T(8,128)} %get-tuple-element.35, f32[16,16,896]{2,1,0:T(8,128)S(1)} %copy-done.2, ...), kind=kLoop, calls=%fused_computation.60 | loop fusion | flops 7340032 | bytes 22020160 | tf_op jit(solution)/shard_map/sub | solution.py:81
  114.7 0.0 copy-start.10
  114.7 0.1 slice_negate_fusion.1
  114.9 0.0 copy-start.11
  114.9 0.0 copy-start.12
  114.9 1.2 copy-done.10
  116.1 2.1 fusion.41
  118.3 0.0 copy-start.6
  118.3 0.0 copy-start.8
  118.3 0.0 copy-done.11
  118.3 0.9 copy-done.6
  119.2 2.2 pad_maximum_fusion.7
  121.4 4.9 %all-to-all-start = ((f32[4,256,896]{2,1,0:T(8,128)}), f32[4,256,896]{2,1,0:T(8,128)}, u32[]{:S(2)}, u32[]{:S(2)}) async-start(f32[4,256,896]{2,1,0:T(8,128)} %bitcast.90), calls=%async_computation | async-start | bytes 7340032 | tf_op jit(solution)/shard_map/all_to_all | solution.py:114
  126.3 0.1 dynamic_slice.6
  126.4 0.1 broadcast_in_dim.15
  126.5 0.1 reshape.85
  126.6 0.1 dynamic_slice.7
  126.7 31.7 %fusion.6 = (f32[3584,448]{1,0:T(8,128)}, f32[3584,448]{1,0:T(8,128)}) fusion(), kind=kLoop, calls=%fused_computation.9 | loop fusion | flops 14450688 | bytes 12845056 | tf_op jit(solution)/shard_map/sin | solution.py:97
  158.4 10.5 %all-to-all-done = f32[4,256,896]{2,1,0:T(8,128)} async-done(((f32[4,256,896]{2,1,0:T(8,128)}), f32[4,256,896]{2,1,0:T(8,128)}, u32[]{:S(2)}, u32[]{:S(2)}) %all-to-all-start) | async-done | bytes 3670048 | tf_op jit(solution)/shard_map/all_to_all | solution.py:114
  168.9 4.8 %copy.32 = f32[256,4,896]{0,2,1:T(8,128)} copy(f32[256,4,896]{2,0,1:T(8,128)} %bitcast.14) | data formatting | bytes 7340032 | tf_op jit(solution)/shard_map/all_to_all | solution.py:114
  173.7 18.9 %fusion.32 = f32[256,896]{1,0:T(8,128)S(1)} fusion(f32[256,3584]{0,1:T(8,128)} %bitcast.93, f32[3584,448]{1,0:T(8,128)} %get-tuple-element.43, f32[3584,448]{1,0:T(8,128)} %get-tuple-element.44, f32[896]{0:T(1024)S(1)} %compare_select_fusion, s32[896]{0:T(1024)S(1)} %add_select_fusion.1, s32[256]{0:T(256)S(1)} %dynamic_slice.7), kind=kOutput, calls=%fused_computation.63 | convolution fusion | flops 9868902400 | bytes 17440768 | tf_op jit(solution)/shard_map/dot_general | solution.py:118
  192.6 12.7 %fusion = f32[256,3584]{1,0:T(8,128)S(1)} fusion(f32[256,896]{1,0:T(8,128)S(1)} %fusion.32, f32[3584,448]{1,0:T(8,128)S(1)} %bitcast.82, f32[3584,448]{1,0:T(8,128)S(1)} %copy-done), kind=kOutput, calls=%fused_computation.2 | convolution fusion | flops 9868214272 | bytes 17432576 | tf_op jit(solution)/shard_map/ic,xc->ix/dot_general | solution.py:120
  205.4 2.2 copy.43
  207.5 4.9 %all-to-all-start.1 = ((f32[256,4,896]{2,0,1:T(8,128)}), f32[256,4,896]{2,0,1:T(8,128)}, u32[]{:S(2)}, u32[]{:S(2)}) async-start(f32[256,4,896]{2,0,1:T(8,128)} %bitcast.91), calls=%async_computation.1 | async-start | bytes 7340032 | tf_op jit(solution)/shard_map/all_to_all | solution.py:121
  212.4 0.0 copy-start.7
  212.5 3.7 %pad_maximum_fusion.6 = f32[16,64,896]{2,1,0:T(8,128)} fusion(f32[16,16,896]{2,1,0:T(8,128)} %param.9, f32[16,16,896]{2,1,0:T(8,128)} %param.8, f32[16,16,896]{2,1,0:T(8,128)S(1)} %copy-done.3, f32[16,16,896]{2,1,0:T(8,128)S(1)} %copy-done.5), kind=kLoop, calls=%fused_computation.57 | loop fusion | flops 2752512 | bytes 7340032 | tf_op jit(solution)/shard_map/concatenate | solution.py:141
  216.2 38.8 %all-to-all-done.1 = f32[256,4,896]{2,0,1:T(8,128)} async-done(((f32[256,4,896]{2,0,1:T(8,128)}), f32[256,4,896]{2,0,1:T(8,128)}, u32[]{:S(2)}, u32[]{:S(2)}) %all-to-all-start.1) | async-done | bytes 3670048 | tf_op jit(solution)/shard_map/all_to_all | solution.py:121
  255.0 4.7 %multiply_add_fusion = f32[16,4,16,896]{3,2,1,0:T(8,128)S(1)} fusion(f32[16,4,16,896]{3,2,1,0:T(8,128)} %bitcast.92, f32[16,4,16,896]{3,2,1,0:T(8,128)} %bitcast.17, pred[]{:T(512)S(6)} %or.3, f32[16,1,16,896]{3,2,1,0:T(8,128)} %copy-done.12, f32[16,1,16,896]{3,2,1,0:T(8,128)} %copy-done.11, f32[16,1,16,896]{3,2,1,0:T(8,128)} %copy-done.8, ...), kind=kLoop, calls=%fused_computation.59 | loop fusion | flops 5505024 | bytes 14680065 | tf_op jit(solution)/shard_map/add | solution.py:153
  259.7 1.9 slice_bitcast_fusion
  (24 shorter events, 0.1 us)
Async XLA Ops:
  0.6 6.2 %copy-start.9 = (f32[16,16,896]{2,1,0:T(8,128)S(1)}, f32[16,16,896]{2,1,0:T(8,128)}, u32[]{:S(2)}) copy-start(f32[16,16,896]{2,1,0:T(8,128)} %param.8) | copy-start | bytes 2752516
  0.6 7.1 %copy-start.13 = (f32[16,16,896]{2,1,0:T(8,128)S(1)}, f32[16,16,896]{2,1,0:T(8,128)}, u32[]{:S(2)}) copy-start(f32[16,16,896]{2,1,0:T(8,128)} %param.9) | copy-start | bytes 2752516
  12.6 3.9 %collective-permute-start = (f32[16,65,3]{1,0,2:T(8,128)S(1)}, f32[16,65,3]{1,0,2:T(8,128)S(1)}, u32[]{:S(2)}, u32[]{:S(2)}) collective-permute-start(f32[16,65,3]{1,0,2:T(8,128)S(1)} %copy.21), channel_id=1, source_target_pairs={{1,0},{2,1},{3,2},{0,3},{5,4},{6,5},{7,6},{4,7},{9,8},{10,9},{11,1... | collective-permute-start | bytes 37448 | tf_op jit(solution)/shard_map/ppermute | solution.py:23
  15.2 3.3 %collective-permute-start.1 = (f32[16,65,3]{1,0,2:T(8,128)S(1)}, f32[16,65,3]{1,0,2:T(8,128)S(1)}, u32[]{:S(2)}, u32[]{:S(2)}) collective-permute-start(f32[16,65,3]{1,0,2:T(8,128)S(1)} %copy.23), channel_id=1, source_target_pairs={{0,1},{1,2},{2,3},{3,0},{4,5},{5,6},{6,7},{7,4},{8,9},{9,10},{10,1... | collective-permute-start | bytes 37448 | tf_op jit(solution)/shard_map/ppermute | solution.py:21
  20.8 31.2 %collective-permute-start.2 = (f32[3,65,902]{2,1,0:T(8,128)S(1)}, f32[3,65,902]{2,1,0:T(8,128)S(1)}, u32[]{:S(2)}, u32[]{:S(2)}) collective-permute-start(f32[3,65,902]{2,1,0:T(8,128)S(1)} %get-tuple-element.18), channel_id=1, source_target_pairs={{4,0},{8,4},{12,8},{5,1},{9,5},{13,9},{6,2},{10,6},{14,10},{7,3},{... | collective-permute-start | bytes 2110688 | tf_op jit(solution)/shard_map/ppermute | solution.py:23
  22.1 29.9 %collective-permute-start.3 = (f32[3,65,902]{2,1,0:T(8,128)S(1)}, f32[3,65,902]{2,1,0:T(8,128)S(1)}, u32[]{:S(2)}, u32[]{:S(2)}) collective-permute-start(f32[3,65,902]{2,1,0:T(8,128)S(1)} %get-tuple-element.19), channel_id=1, source_target_pairs={{0,4},{4,8},{8,12},{1,5},{5,9},{9,13},{2,6},{6,10},{10,14},{3,7},{... | collective-permute-start | bytes 2110688 | tf_op jit(solution)/shard_map/ppermute | solution.py:21
  49.4 12.9 %copy-start.1 = (f32[16,65,896]{2,1,0:T(8,128)}, f32[16,65,896]{2,1,0:T(8,128)S(1)}, u32[]{:S(2)}) copy-start(f32[16,65,896]{2,1,0:T(8,128)S(1)} %get-tuple-element.4) | copy-start | bytes 11182084
  62.3 18.3 %copy-start.14 = (f32[16,896]{1,0:T(8,128)S(1)}, f32[16,896]{1,0:T(8,128)}, u32[]{:S(2)}) copy-start(f32[16,896]{1,0:T(8,128)} %param.10) | copy-start | bytes 172036
  86.1 20.7 %copy-start.2 = (f32[16,16,896]{2,1,0:T(8,128)S(1)}, f32[16,16,896]{2,1,0:T(8,128)}, u32[]{:S(2)}) copy-start(f32[16,16,896]{2,1,0:T(8,128)} %param.7) | copy-start | bytes 2752516
  86.1 20.7 %copy-start.4 = (f32[16,16,896]{2,1,0:T(8,128)S(1)}, f32[16,16,896]{2,1,0:T(8,128)}, u32[]{:S(2)}) copy-start(f32[16,16,896]{2,1,0:T(8,128)} %param.6) | copy-start | bytes 2752516
  114.7 1.4 copy-start.10
  114.9 3.4 %copy-start.11 = (f32[16,1,16,896]{3,2,1,0:T(8,128)}, f32[16,1,16,896]{3,2,1,0:T(8,128)S(1)}, u32[]{:S(2)}) copy-start(f32[16,1,16,896]{3,2,1,0:T(8,128)S(1)} %get-tuple-element.31) | copy-start | bytes 2752516
  114.9 3.4 %copy-start.12 = (f32[16,1,16,896]{3,2,1,0:T(8,128)}, f32[16,1,16,896]{3,2,1,0:T(8,128)S(1)}, u32[]{:S(2)}) copy-start(f32[16,1,16,896]{3,2,1,0:T(8,128)S(1)} %get-tuple-element.32) | copy-start | bytes 2752516
  118.3 0.9 copy-start.6
  118.3 3.1 %copy-start.8 = (f32[16,1,16,896]{3,2,1,0:T(8,128)}, f32[16,1,16,896]{3,2,1,0:T(8,128)S(1)}, u32[]{:S(2)}) copy-start(f32[16,1,16,896]{3,2,1,0:T(8,128)S(1)} %get-tuple-element.21) | copy-start | bytes 2752516
  121.4 4.9 %copy-start.15 = (s32[32]{0:T(128)S(1)}, s32[32]{0:T(128)}, u32[]{:S(2)}) copy-start(s32[32]{0:T(128)} %param.11) | copy-start | bytes 388
  121.4 47.5 %all-to-all-start = ((f32[4,256,896]{2,1,0:T(8,128)}), f32[4,256,896]{2,1,0:T(8,128)}, u32[]{:S(2)}, u32[]{:S(2)}) async-start(f32[4,256,896]{2,1,0:T(8,128)} %bitcast.90), calls=%async_computation | async-start | bytes 7340032 | tf_op jit(solution)/shard_map/all_to_all | solution.py:114
  168.9 23.7 %slice-start = ((s8[7340032]{0:T(1024)(128)(4,1)}), s8[3145728]{0:T(1024)(128)(4,1)S(1)}, s32[]{:S(2)}) async-start(s8[7340032]{0:T(1024)(128)(4,1)} %bitcast.81), calls=%async_computation.2 | async-start | bytes 6291456
  173.7 18.9 %slice-start.1 = ((s8[7340032]{0:T(1024)(128)(4,1)}), s8[4194304]{0:T(1024)(128)(4,1)S(1)}, s32[]{:S(2)}) async-start(s8[7340032]{0:T(1024)(128)(4,1)} %bitcast.81), calls=%async_computation.3 | async-start | bytes 8388608
  173.7 18.9 %copy-start = (f32[3584,448]{1,0:T(8,128)S(1)}, f32[3584,448]{1,0:T(8,128)}, u32[]{:S(2)}) copy-start(f32[3584,448]{1,0:T(8,128)} %get-tuple-element.44) | copy-start | bytes 19267588
  207.5 4.9 %copy-start.3 = (f32[16,16,896]{2,1,0:T(8,128)S(1)}, f32[16,16,896]{2,1,0:T(8,128)}, u32[]{:S(2)}) copy-start(f32[16,16,896]{2,1,0:T(8,128)} %param.7) | copy-start | bytes 2752516
  207.5 4.9 %copy-start.5 = (f32[16,16,896]{2,1,0:T(8,128)S(1)}, f32[16,16,896]{2,1,0:T(8,128)}, u32[]{:S(2)}) copy-start(f32[16,16,896]{2,1,0:T(8,128)} %param.6) | copy-start | bytes 2752516
  207.5 47.5 %all-to-all-start.1 = ((f32[256,4,896]{2,0,1:T(8,128)}), f32[256,4,896]{2,0,1:T(8,128)}, u32[]{:S(2)}, u32[]{:S(2)}) async-start(f32[256,4,896]{2,0,1:T(8,128)} %bitcast.91), calls=%async_computation.1 | async-start | bytes 7340032 | tf_op jit(solution)/shard_map/all_to_all | solution.py:121
  212.4 42.6 %copy-start.7 = (f32[16,1,16,896]{3,2,1,0:T(8,128)S(1)}, f32[16,1,16,896]{3,2,1,0:T(8,128)}, u32[]{:S(2)}) copy-start(f32[16,1,16,896]{3,2,1,0:T(8,128)} %copy-done.6) | copy-start | bytes 2752516
where the time goes:
time: 265 us; the launch traced here: 262 us
  other arithmetic  133 us (50%)
  waiting for transfers between devices  52.3 us (20%)
  matrix products  31.6 us (12%)
  local copies, waits for them, and re-layouts  25.6 us (10%)
  starting transfers between devices  18.3 us (7%)
    div x2, other arithmetic, centered(): (45.0 * (pick(1) - pick(-1)) - 9.0 * (pick(2) - pick(-2)) + (pick(3) - pi...  40.8 us
    all_to_all x1, waiting for transfers between devices, spectral_filter(): lax.all_to_all(smoothed, 'lon', split_axis=1, concat_axis=0, tiled=True)  38.8 us
    sin x1, other arithmetic, fourier_table(): return jnp.concatenate([jnp.cos(angle), jnp.sin(angle)], axis=1)  31.7 us
    div x1, other arithmetic, hyperdiff(): (pick(3) + pick(-3) - 6.0 * (pick(2) + pick(-2)) + 15.0 * (pick(1) + pick...  20.7 us
    dot_general x1, matrix products, spectral_filter(): jnp.dot(circles, fourier, precision=EXACT, preferred_element_type=jnp.flo...  18.9 us
    dot_general x1, matrix products, spectral_filter(): smoothed = jnp.einsum('ic,xc->ix', kept, fourier, precision=EXACT)  12.7 us
    all_to_all x1, waiting for transfers between devices, spectral_filter(): lax.all_to_all(flattened, 'lon', split_axis=0, concat_axis=1, tiled=True)  10.5 us
    concatenate x1, other arithmetic, padded_2(): jnp.concatenate([lax.ppermute(tail, axis, [(i, (i + 1) % count) for i in...  10.3 us
  transfers between devices with their start and end apart: 6, of which 4 were waited for; matrix products, arithmetic and copies ran while one was open for 23% of the time, Pallas kernels for 0%

commit v1 on v0

v1 whole, which is shorter than its diff:
```python
import functools
import math

import jax
import jax.numpy as jnp
import ml_dtypes
import numpy as np
from jax import lax
from jax.experimental import pallas as pl
from jax.experimental.pallas import tpu as pltpu
from jax.sharding import PartitionSpec as P

STEP = 0.1
SPIN = 0.5
LANES = 128
NEAR = 16
FAR = 8
NODES = 256
F32 = jnp.float32
BF16 = jnp.bfloat16
VMEM_LIMIT = 56 * 1024 * 1024


def pivoted(matrix, count):
    rest = np.array(matrix)
    columns = rest.shape[1]
    tilt = 1.0 + 1e-3 * np.arange(columns) / columns
    picked = []
    tri = np.zeros((count, columns))
    for step in range(count):
        size = (rest * rest).sum(axis=0)
        best = int(np.argmax(size * tilt))
        picked.append(best)
        unit = rest[:, best] / math.sqrt(size[best])
        for _ in range(2):
            part = (unit[:, None] * rest).sum(axis=0)
            rest -= unit[:, None] * part[None, :]
            tri[step] += part
        rest[:, best] = 0.0
    left = tri[:, picked].copy()
    right = tri.copy()
    for step in range(count - 1, -1, -1):
        right[step] /= left[step, step]
        right[:step] -= left[:step, step][:, None] * right[step][None, :]
    right[:, picked] = np.eye(count)
    order = np.argsort(picked)
    return np.asarray(picked)[order], right[order]


def cauchy(target, source, circle):
    gap = target[:, None] - source[None, :]
    angle = np.where(gap == 0, 0.5 * math.pi, gap * math.pi / circle)
    return np.where(gap == 0, 0.0, 1.0 / (circle * np.sin(angle)))


def halves(table):
    table = table.astype(np.float32)
    high = table.astype(ml_dtypes.bfloat16)
    low = (table - high.astype(np.float32)).astype(ml_dtypes.bfloat16)
    return np.stack([high, low])


@functools.lru_cache(maxsize=None)
def filter_tables(sector, circle):
    modes = circle // 8
    place = np.arange(sector)
    wave = np.arange(modes)
    phase = (wave[:, None] * place[None, :]) % circle * (2 * math.pi / circle)
    basis = np.concatenate([np.cos(phase), np.sin(phase[1:])], axis=0)
    nodes, spread = pivoted(basis, NODES)
    own = cauchy(nodes, nodes, circle)
    send = np.zeros((2, 4, NODES, 2 * LANES))
    take = np.zeros((3 * LANES, 4, 2, NODES))
    for name, shift, count in (("east", sector, NEAR), ("west", -sector, NEAR), ("far", 2 * sector, FAR)):
        kernel = cauchy(nodes + shift, nodes, circle)
        pick, weights = pivoted(kernel, count)
        back = kernel[:, pick].T
        for pair in range(2):
            for group in range(4):
                if name == "far":
                    first = LANES + 32 * pair + FAR * group
                    lane = 2 * LANES + 32 * pair + FAR * group
                elif name == "east":
                    first = 64 * pair + NEAR * group
                    lane = 64 * pair + NEAR * group
                else:
                    first = 64 * (1 - pair) + NEAR * group
                    lane = LANES + 64 * (1 - pair) + NEAR * group
                send[pair, group, :, first : first + count] = weights.T
                take[lane : lane + count, 2 * pair + group // 2, group % 2] = back
    return dict(
        nodes=nodes.astype(np.int32),
        spread=halves(spread.T),
        gather=halves(STEP * spread),
        own=halves(own.T),
        send=halves(send),
        take=halves(take.reshape(3 * LANES, 8 * NODES)),
    )


def split(value):
    high = value.astype(BF16)
    return high, (value - high.astype(F32)).astype(BF16)


def dot3(high, low, table_high, table_low):
    def one(a, b):
        return lax.dot_general(a, b, (((1,), (0,)), ((), ())), preferred_element_type=F32)

    return one(high, table_high) + one(low, table_high) + one(high, table_low)


def pack_kernel(*refs):
    fields = refs[:4]
    mass, south, north, west, east, edge, sems = refs[4:]
    rows = mass.shape[0]
    levels = edge.shape[3]
    columns = mass.shape[1]
    copies = []
    for f in range(4):
        copies.append(pltpu.make_async_copy(fields[f].at[:, :, 0:LANES], edge.at[0, f], sems.at[0, f]))
        copies.append(
            pltpu.make_async_copy(
                fields[f].at[:, :, columns - LANES : columns], edge.at[1, f], sems.at[1, f]
            )
        )
    for c in copies:
        c.start()
    strips = []
    for f in range(4):
        for j in range(3):
            into = pl.ds(levels * (3 * f + j), levels)
            strips.append(pltpu.make_async_copy(fields[f].at[j], south.at[into], sems.at[2 + j, f]))
            strips.append(
                pltpu.make_async_copy(fields[f].at[rows - 3 + j], north.at[into], sems.at[5 + j, f])
            )
    for c in strips:
        c.start()
    tail = 12 * levels
    blank = jnp.zeros((5, columns), F32)
    south[tail : tail + 3] = mass[0:3]
    south[tail + 3 : tail + 8] = blank
    north[tail : tail + 3] = mass[rows - 3 : rows]
    north[tail + 3 : tail + 8] = blank
    lane = lax.broadcasted_iota(jnp.int32, (levels, LANES), 1)
    west[2 * levels :] = mass[:, 0:LANES]
    east[2 * levels :] = pltpu.roll(mass[:, columns - LANES : columns], 3, 1)
    for c in copies:
        c.wait()
    for parity in range(2):
        for side, out in ((0, west), (1, east)):
            total = jnp.zeros((levels, LANES), F32)
            for r in range(parity, rows, 2):
                for f in range(4):
                    first = 16 * (r // 2) + 3 * f
                    turn = first if side == 0 else (first + 3) % LANES
                    tile = edge[side, f, r]
                    if turn:
                        tile = pltpu.roll(tile, turn, 1)
                    total = jnp.where((lane >= first) & (lane < first + 3), tile, total)
            out[parity * levels : (parity + 1) * levels] = total
    for c in strips:
        c.wait()


def stencil(center, plus, minus):
    p1, p2, p3 = plus
    m1, m2, m3 = minus
    slope = 45.0 * (p1 - m1) - 9.0 * (p2 - m2) + (p3 - m3)
    smooth = (p3 + m3) - 6.0 * (p2 + m2) + 15.0 * (p1 + m1) - 20.0 * center
    return slope, smooth


def tend_kernel(edge_rows, chained, count, *refs):
    refs = list(refs)

    def some(n):
        taken = refs[:n]
        del refs[:n]
        return taken

    (polar,) = some(1)
    metric, spin = some(2)
    fields = some(4)
    mass, west, east = some(3)
    south, north = some(2) if edge_rows else (None, None)
    cosines, sines, diagonal = some(3)
    spread, own, send = some(3)
    if chained:
        some(4)
    outs = some(4)
    local, to_east, to_west, to_far = some(4)
    ext, tend, mass_ext, mass_x, mass_y, sems = some(6)
    rows, columns = mass.shape
    levels = ext.shape[2]
    items = count * levels

    copies = []
    for f in range(4):
        if edge_rows:
            copies += [
                (fields[f].at[0:6], ext.at[f, 3:9]),
                (fields[f].at[rows - 6 : rows], ext.at[f, 9:15]),
            ]
            for j in range(3):
                rest = pl.ds(levels * (3 * f + j), levels)
                copies += [(south.at[rest], ext.at[f, j]), (north.at[rest], ext.at[f, 15 + j])]
        else:
            copies += [(fields[f], ext.at[f])]
    if edge_rows:
        tail = pl.ds(12 * levels, 8)
        copies += [(south.at[tail], mass_ext.at[0:8]), (north.at[tail], mass_ext.at[24:32])]
    copies = [pltpu.make_async_copy(a, b, sems.at[n]) for n, (a, b) in enumerate(copies)]
    for c in copies:
        c.start()
    mass_ext[8:24] = mass[...]
    if not edge_rows:
        mass_ext[0:8] = jnp.ones((8, columns), F32)
        mass_ext[24:32] = jnp.ones((8, columns), F32)
    for c in copies:
        c.wait()

    def shifted(left, body, right, axis_len):
        wide = jnp.concatenate([left, body, right], axis=1)
        whole = axis_len + 2 * LANES

        def at(k):
            return pltpu.roll(wide, (-k) % whole, 1)[:, LANES : LANES + axis_len]

        return [at(1), at(2), at(3)], [at(-1), at(-2), at(-3)]

    middle = mass[...]
    per_mass = 1.0 / (60.0 * middle)
    plus, minus = shifted(
        pltpu.roll(west[2 * levels :], LANES - 3, 1), middle, east[2 * levels :], columns
    )
    mass_x[...] = stencil(middle, plus, minus)[0] * per_mass
    if edge_rows:
        below = jnp.concatenate([mass_ext[0:3], middle, mass_ext[24:27]], axis=0)
        plus = [below[3 + k : 3 + k + rows] for k in (1, 2, 3)]
        minus = [below[3 - k : 3 - k + rows] for k in (1, 2, 3)]
    else:
        plus = [mass_ext[8 + k : 8 + k + rows] for k in (1, 2, 3)]
        minus = [mass_ext[8 - k : 8 - k + rows] for k in (1, 2, 3)]
    mass_y[...] = stencil(middle, plus, minus)[0] * per_mass

    def one_row(i, carry):
        upper = i // 3 if edge_rows else 0
        row = i + (rows - 6) * upper if edge_rows else i + 3
        at = i + 3 + 6 * upper if edge_rows else i + 3
        metric_row = metric[row]
        spin_row = spin[row]
        along = metric_row * (1.0 / 60.0)
        lead = 16 * (row // 2)
        slope_mass_x = metric_row * mass_x[pl.ds(row, 1), :]
        slope_mass_y = mass_y[pl.ds(row, 1), :]
        for first in range(0, levels, 8):
            lev = slice(first, first + 8)
            halo = pl.ds(pl.multiple_of((row % 2) * levels + first, 8), 8)
            u = ext[0, at, lev]
            v = ext[1, at, lev]
            theta = ext[2, at, lev]
            u_fast = u * along
            u_size = jnp.abs(u_fast)
            v_fast = v * (1.0 / 60.0)
            v_size = jnp.abs(v_fast)
            push_x = push_y = None
            for f in (3, 0, 1, 2):
                q = ext[f, at, lev]
                start = lead + 3 * f
                left = pltpu.roll(west[halo, :], lax.rem(LANES - 3 + LANES - start, LANES), 1)
                right = pltpu.roll(east[halo, :], lax.rem(LANES - start, LANES), 1)
                plus, minus = shifted(left, q, right, columns)
                slope_x, smooth_x = stencil(q, plus, minus)
                slope_y, smooth_y = stencil(
                    q,
                    [ext[f, at + k, lev] for k in (1, 2, 3)],
                    [ext[f, at - k, lev] for k in (1, 2, 3)],
                )
                change = (u_size * smooth_x - u_fast * slope_x) + (v_size * smooth_y - v_fast * slope_y)
                if f == 3:
                    push_x = along * slope_x + theta * slope_mass_x
                    push_y = (1.0 / 60.0) * slope_y + theta * slope_mass_y
                elif f == 0:
                    change = change + (spin_row * v - push_x)
                elif f == 1:
                    change = change - (spin_row * u + push_y)
                tend[f, i, lev] = change
        return carry

    lax.fori_loop(0, count, one_row, 0)

    @pl.when(polar[0] == 0)
    def _():
        def update(i, carry):
            at = i + 3 + 6 * (i // 3) if edge_rows else i + 3
            for f in range(4):
                tend[f, i] = ext[f, at] + STEP * tend[f, i]
            return carry

        lax.fori_loop(0, count, update, 0)
        writes = []
        for f in range(4):
            if edge_rows:
                writes += [
                    (tend.at[f, 0:3], outs[f].at[0:3]),
                    (tend.at[f, 3:6], outs[f].at[rows - 3 : rows]),
                ]
            else:
                writes += [(tend.at[f], outs[f].at[3 : rows - 3])]
        writes = [pltpu.make_async_copy(a, b, sems.at[n]) for n, (a, b) in enumerate(writes)]
        for c in writes:
            c.start()
        for c in writes:
            c.wait()

    @pl.when(polar[0] != 0)
    def _():
        def spread_out(table):
            table = table[...]
            wide = jnp.broadcast_to(table[:, None, :], (count, levels, NODES))
            return wide.reshape(items, NODES)

        c_all, s_all, d_all = spread_out(cosines), spread_out(sines), spread_out(diagonal)
        messages = [None, None]
        for f in range(4):
            high, low = split(tend[f].reshape(items, columns))
            nodal = dot3(high, low, spread[0], spread[1])
            result = d_all * nodal
            for part, factor in ((0, c_all), (1, s_all)):
                high, low = split(factor * nodal)
                moved = dot3(high, low, own[0], own[1])
                result = result + (s_all * moved if part == 0 else -(c_all * moved))
                group = 2 * (f % 2) + part
                sent = dot3(high, low, send[0, f // 2, group], send[1, f // 2, group])
                old = messages[f // 2]
                messages[f // 2] = sent if old is None else old + sent
            local[f] = result
        first, second = messages
        lane = lax.broadcasted_iota(jnp.int32, (items, LANES), 1)
        to_east[...] = jnp.where(lane < 64, first[:, :LANES], second[:, :LANES])
        to_west[...] = jnp.where(lane < 64, second[:, :LANES], first[:, :LANES])
        far = first[:, LANES:] + second[:, LANES:]
        to_far[...] = far[: items // 2] + pltpu.roll(far[items // 2 :], 64, 1)


def finish_kernel(edge_rows, count, *refs):
    polar, signs = refs[:2]
    fields = refs[2:6]
    from_west, from_east, from_far, local, cosines, sines, take, gather = refs[6:14]
    outs = refs[18:22]
    old, new, sems = refs[22:]
    rows = fields[0].shape[0]
    levels, columns = old.shape[2], old.shape[3]
    items = count * levels

    @pl.when(polar[0] != 0)
    def _():
        reads, writes = [], []
        for f in range(4):
            if edge_rows:
                parts = [((0, 3), (0, 3)), ((3, 6), (rows - 3, rows))]
            else:
                parts = [((0, count), (3, rows - 3))]
            for (a, b), (c, d) in parts:
                reads.append((fields[f].at[c:d], old.at[f, a:b]))
                writes.append((new.at[f, a:b], outs[f].at[c:d]))
        reads = [pltpu.make_async_copy(a, b, sems.at[n]) for n, (a, b) in enumerate(reads)]
        writes = [pltpu.make_async_copy(a, b, sems.at[n]) for n, (a, b) in enumerate(writes)]
        for c in reads:
            c.start()

        def spread_out(table):
            table = table[...]
            wide = jnp.broadcast_to(table[:, None, :], (count, levels, NODES))
            return wide.reshape(items, NODES)

        c_all, s_all = spread_out(cosines), spread_out(sines)
        folded = from_far[...] * signs[2]
        come = jnp.concatenate(
            [
                from_west[...] * signs[0],
                from_east[...] * signs[1],
                jnp.concatenate([folded, pltpu.roll(folded, 64, 1)], axis=0),
            ],
            axis=1,
        )
        high, low = split(come)
        for c in reads:
            c.wait()
        for f in range(4):
            span = slice(2 * f * NODES, (2 * f + 2) * NODES)
            both = dot3(high, low, take[0, :, span], take[1, :, span])
            value = local[f] + (s_all * both[:, :NODES] - c_all * both[:, NODES:])
            wide = dot3(*split(value), gather[0], gather[1])
            new[f] = old[f] + wide.reshape(count, levels, columns)
        for c in writes:
            c.start()
        for c in writes:
            c.wait()


def vmem():
    return pl.BlockSpec(memory_space=pltpu.VMEM)


def smem():
    return pl.BlockSpec(memory_space=pltpu.SMEM)


def anywhere():
    return pl.BlockSpec(memory_space=pl.ANY)


def like(*shape):
    return jax.ShapeDtypeStruct(shape, F32)


def params():
    return pltpu.CompilerParams(vmem_limit_bytes=VMEM_LIMIT)


def row_cutoffs(cutoffs, owner, row_count, lat_count):
    quarter = lat_count // 4
    first = jnp.where(
        owner < quarter, owner * row_count, owner * row_count - lat_count * row_count // 2
    )
    first = jnp.clip(first, 0, cutoffs.shape[0] - row_count)
    return lax.dynamic_slice_in_dim(cutoffs, first, row_count)


def pick_rows(table, edge_rows):
    if edge_rows:
        return jnp.concatenate([table[:3], table[-3:]], axis=0)
    return table[3:-3]


def shards(u_wind, v_wind, theta, geopot, mass, cutoffs):
    rows, levels, columns = u_wind.shape
    lat_count = lax.axis_size("lat")
    lon_count = lax.axis_size("lon")
    lat_idx = lax.axis_index("lat")
    lon_idx = lax.axis_index("lon")
    nlat_all = rows * lat_count
    circle = columns * lon_count
    tables = filter_tables(columns, circle)
    fields = (u_wind, v_wind, theta, geopot)

    strip = 12 * levels + 8
    to_south, to_north, to_west, to_east = pl.pallas_call(
        pack_kernel,
        out_shape=[like(strip, columns)] * 2 + [like(2 * levels + rows, LANES)] * 2,
        in_specs=[anywhere()] * 4 + [vmem()],
        out_specs=[vmem()] * 4,
        scratch_shapes=[
            pltpu.VMEM((2, 4, rows, levels, LANES), F32),
            pltpu.SemaphoreType.DMA((8, 4)),
        ],
        compiler_params=params(),
        name="pack_edges",
    )(*fields, mass)

    def ring(value, step):
        return lax.ppermute(value, "lon", [(i, (i + step) % lon_count) for i in range(lon_count)])

    west = ring(to_east, 1)
    east = ring(to_west, -1)
    south = lax.ppermute(to_north, "lat", [(i, i + 1) for i in range(lat_count - 1)])
    north = lax.ppermute(to_south, "lat", [(i + 1, i) for i in range(lat_count - 1)])

    row_global = lat_idx * rows + jnp.arange(rows, dtype=jnp.int32)
    latitude = (row_global.astype(F32) + 0.5) * (math.pi / nlat_all) - math.pi / 2
    metric = 1.0 / jnp.cos(latitude)
    spin = SPIN * jnp.sin(latitude)
    quarter = lat_count // 4
    polar = ((lat_idx < quarter) | (lat_idx >= lat_count - quarter)).astype(jnp.int32)[None]
    twice = 2 * row_cutoffs(cutoffs, lat_idx, rows, lat_count) + 1
    place = lon_idx * columns + jnp.asarray(tables["nodes"])
    angle = (twice[:, None] * place[None, :] % (2 * circle)).astype(F32) * (math.pi / circle)
    cosines, sines = jnp.cos(angle), jnp.sin(angle)
    diagonal = jnp.broadcast_to((twice.astype(F32) / circle)[:, None], (rows, NODES))

    def tendencies(edge_rows, old):
        count = 6 if edge_rows else rows - 6
        items = count * levels
        deep = 18 if edge_rows else rows
        halos = [south, north] if edge_rows else []
        args = (
            [polar, metric, spin, *fields, mass, west, east, *halos]
            + [pick_rows(t, edge_rows) for t in (cosines, sines, diagonal)]
            + [jnp.asarray(tables[k]) for k in ("spread", "own", "send")]
        )
        specs = (
            [smem()] * 3
            + [anywhere()] * 4
            + [vmem()] * 3
            + [anywhere()] * len(halos)
            + [vmem()] * 6
        )
        aliases = {len(args) + f: f for f in range(4)} if old else {}
        return pl.pallas_call(
            functools.partial(tend_kernel, edge_rows, bool(old), count),
            out_shape=[like(rows, levels, columns)] * 4
            + [like(4, items, NODES)]
            + [like(items, LANES)] * 2
            + [like(items // 2, LANES)],
            in_specs=specs + [anywhere()] * len(old),
            out_specs=[anywhere()] * 4 + [vmem()] * 4,
            scratch_shapes=[
                pltpu.VMEM((4, deep, levels, columns), F32),
                pltpu.VMEM((4, count, levels, columns), F32),
                pltpu.VMEM((rows + 16, columns), F32),
                pltpu.VMEM((rows, columns), F32),
                pltpu.VMEM((rows, columns), F32),
                pltpu.SemaphoreType.DMA((40,)),
            ],
            input_output_aliases=aliases,
            compiler_params=params(),
            cost_estimate=pl.CostEstimate(
                flops=items * 4 * columns * 2000, bytes_accessed=8 * items * columns * 4, transcendentals=0
            ),
            name="tend_edge" if edge_rows else "tend_inner",
        )(*args, *old)

    def exchange(east_part, west_part, far_part):
        return ring(east_part, 1), ring(west_part, -1), ring(far_part, 2)

    signs = jnp.stack(
        [
            jnp.where(lon_idx == 0, -1.0, 1.0),
            jnp.where(lon_idx == lon_count - 1, -1.0, 1.0),
            jnp.where(lon_idx < 2, -1.0, 1.0),
        ]
    ).astype(F32)

    def finish(edge_rows, received, local, old):
        count = 6 if edge_rows else rows - 6
        args = [polar, signs, *fields, *received, local]
        args += [pick_rows(t, edge_rows) for t in (cosines, sines)]
        args += [jnp.asarray(tables[k]) for k in ("take", "gather")]
        return pl.pallas_call(
            functools.partial(finish_kernel, edge_rows, count),
            out_shape=[like(rows, levels, columns)] * 4,
            in_specs=[smem()] * 2 + [anywhere()] * 4 + [vmem()] * 8 + [anywhere()] * 4,
            out_specs=[anywhere()] * 4,
            scratch_shapes=[
                pltpu.VMEM((4, count, levels, columns), F32),
                pltpu.VMEM((4, count, levels, columns), F32),
                pltpu.SemaphoreType.DMA((8,)),
            ],
            input_output_aliases={len(args) + f: f for f in range(4)},
            compiler_params=params(),
            name="finish_edge" if edge_rows else "finish_inner",
        )(*args, *old)

    *outs, local_inner, a, b, c = tendencies(False, [])
    received_inner = exchange(a, b, c)
    *outs, local_edge, a, b, c = tendencies(True, outs)
    received_edge = exchange(a, b, c)
    outs = finish(False, received_inner, local_inner, outs)
    outs = finish(True, received_edge, local_edge, outs)
    return tuple(outs)


def solution(mesh):
    return jax.shard_map(
        shards,
        mesh=mesh,
        in_specs=(
            P(("members", "lat"), None, "lon"),
            P(("members", "lat"), None, "lon"),
            P(("members", "lat"), None, "lon"),
            P(("members", "lat"), None, "lon"),
            P(("members", "lat"), "lon"),
            P(),
        ),
        out_specs=(
            P(("members", "lat"), None, "lon"),
            P(("members", "lat"), None, "lon"),
            P(("members", "lat"), None, "lon"),
            P(("members", "lat"), None, "lon"),
        ),
        check_vma=False,
    )
```

time: 265 us -> 71.7 us (0.27); the launches traced: 262 us -> 71.3 us
  other arithmetic: 133 us -> 2.64 us
  waiting for transfers between devices: 52.3 us -> 0.03 us
  Pallas kernels: 0 us -> 49.7 us
  matrix products: 31.6 us -> 0 us
  local copies, waits for them, and re-layouts: 25.6 us -> 4.41 us
  starting transfers between devices: 18.3 us -> 13.7 us
    div x4 -> x1, other arithmetic: 62.8 us -> 0.08 us  [shards(): twice.astype(F32) / circle]
    pallas_call x0 -> x5, Pallas kernels: none -> 49.7 us  [the longest x2 30.5 us: tendencies(): pl.pallas_call(functools.partial(tend_kernel, edge_rows, bool(old), count...]
    all_to_all x2 -> x0, waiting for transfers between devices: 49.4 us -> none  [the longest x1 38.8 us: spectral_filter(): lax.all_to_all(smoothed, 'lon', split_axis=1, concat_axis=0, tiled=True)]
    dot_general x2 -> x0, matrix products: 31.6 us -> none  [the longest x1 18.9 us: spectral_filter(): jnp.dot(circles, fourier, precision=EXACT, preferred_element_type=jnp.flo...]
    sin x1, other arithmetic: 31.7 us -> 0.16 us  [shards(): cosines, sines = (jnp.cos(angle), jnp.sin(angle))]
    concatenate x2 -> x3, other arithmetic: 14 us -> 1.27 us  [pick_rows(): return jnp.concatenate([table[:3], table[-3:]], axis=0)]
    all_to_all x2 -> x0, starting transfers between devices: 9.76 us -> none  [the longest x1 4.89 us: spectral_filter(): lax.all_to_all(smoothed, 'lon', split_axis=1, concat_axis=0, tiled=True)]
    sub x1 -> x0, other arithmetic: 7.91 us -> none  [tendencies(): metric[:, None] * (east_all * slope_x - jnp.abs(east_all) * smooth_x)]
  transfers between devices with their start and end apart: 6 -> 10, of which waited for: 4 -> 0; matrix products, arithmetic and copies ran while one was open for 23% -> 8% of each run, Pallas kernels for 0% -> 54%
where the time goes in v1:
time: 71.7 us; the launch traced here: 71.3 us
  Pallas kernels  49.7 us (69%)
  starting transfers between devices  13.7 us (19%)
  local copies, waits for them, and re-layouts  4.41 us (6%)
  other arithmetic  2.64 us (4%)
  between operations  0.86 us (1%)
    pallas_call x2, Pallas kernels, tendencies(): pl.pallas_call(functools.partial(tend_kernel, edge_rows, bool(old), count...  30.5 us
    pallas_call x2, Pallas kernels, finish(): pl.pallas_call(functools.partial(finish_kernel, edge_rows, count), out_sh...  15.3 us
    ppermute x8, starting transfers between devices, ring(): lax.ppermute(value, 'lon', [(i, (i + step) % lon_count) for i in range(lo...  8.14 us
    ppermute x1, starting transfers between devices, shards(): lax.ppermute(to_north, 'lat', [(i, i + 1) for i in range(lat_count - 1)])  4.26 us
    pallas_call x1, Pallas kernels, shards(): pl.pallas_call(pack_kernel, out_shape=[like(strip, columns)] * 2 + [like(...  3.89 us
    unnamed x24, local copies, waits for them, and re-layouts  1.57 us
  transfers between devices with their start and end apart: 10, of which 0 were waited for; matrix products, arithmetic and copies ran while one was open for 8% of the time, Pallas kernels for 54%

profile of v1, /device:TPU:0, one launch (start us, length us, event | category | flops | bytes accessed | tf_op | source)
XLA Modules:
  0.0 71.3 jit_solution(4595423615212729492)
XLA Ops:
  0.6 0.0 copy-start.10
  0.6 0.0 copy-start.11
  0.7 3.9 %pack_edges.1 = (f32[200,896]{1,0:T(8,128)}, f32[200,896]{1,0:T(8,128)}, f32[48,128]{1,0:T(8,128)}, f32[48,128]{1,0:T(8,128)}) custom-call(f32[16,16,896]{2,1,0:T(8,128)} %refs_2_.5, f32[16,16,896]{2,1,0:T(8,128)} %refs_3_.9, f32[16,16,896]{2,1,0:T(8,128)} %refs_4_.9, f32[16,16,896]{2,1,0:T(8,128)} %refs_5_.7, f32[16,896]{1,0:T(8,128)} %refs_7_.3), custom_call_target="tpu_custom_call" | custom-call | tf_op jit(solution)/shard_map/pack_edges/pallas_call | solution.py:450
  4.5 0.5 collective-permute-start
  5.1 2.0 %collective-permute-start.1 = (f32[48,128]{1,0:T(8,128)}, f32[48,128]{1,0:T(8,128)S(1)}, u32[]{:S(2)}, u32[]{:S(2)}) collective-permute-start(f32[48,128]{1,0:T(8,128)} %get-tuple-element.29), channel_id=1, source_target_pairs={{0,3},{1,0},{2,1},{3,2},{4,7},{5,4},{6,5},{7,6},{8,11},{9,8},{10,9... | collective-permute-start | bytes 73736 | tf_op jit(solution)/shard_map/ppermute | solution.py:464
  7.0 4.3 %collective-permute-start.2 = (f32[200,896]{1,0:T(8,128)}, f32[200,896]{1,0:T(8,128)S(1)}, u32[]{:S(2)}, u32[]{:S(2)}) collective-permute-start(f32[200,896]{1,0:T(8,128)} %get-tuple-element.30), channel_id=1, source_target_pairs={{0,4},{4,8},{8,12},{1,5},{5,9},{9,13},{2,6},{6,10},{10,14},{3,7},{... | collective-permute-start | bytes 2150408 | tf_op jit(solution)/shard_map/ppermute | solution.py:468
  11.3 1.3 %collective-permute-start.3 = (f32[200,896]{1,0:T(8,128)}, f32[200,896]{1,0:T(8,128)S(1)}, u32[]{:S(2)}, u32[]{:S(2)}) collective-permute-start(f32[200,896]{1,0:T(8,128)} %get-tuple-element.31), channel_id=1, source_target_pairs={{4,0},{8,4},{12,8},{5,1},{9,5},{13,9},{6,2},{10,6},{14,10},{7,3},{... | collective-permute-start | bytes 2150408 | tf_op jit(solution)/shard_map/ppermute | solution.py:469
  12.6 0.0 copy-done.10
  12.7 0.0 copy-done.11
  12.7 0.1 convert_multiply_fusion
  12.7 0.2 fusion.4
  12.9 0.5 sine_multiply_fusion
  13.5 0.6 pad_maximum_fusion.1.refs_13_.refs_11_
  14.1 0.6 pad_maximum_fusion.refs_12_.refs_10_
  14.7 0.1 fusion.9
  14.7 0.1 pad_maximum_fusion.2
  14.8 0.1 slice.45
  14.9 0.6 slice.51.refs_11_
  15.5 0.6 slice.50.refs_10_
  16.1 0.0 collective-permute-done.refs_8_
  16.1 0.0 copy-start.2
  16.1 0.0 collective-permute-done.1.refs_9_
  16.1 0.0 copy-start.3
  16.1 0.7 broadcast_in_dim.21.refs_12_
  16.8 0.0 copy-done.2
  16.8 0.0 copy-done.3
  16.8 17.1 %tend_inner.1 = (f32[16,16,896]{2,1,0:T(8,128)}, f32[16,16,896]{2,1,0:T(8,128)}, f32[16,16,896]{2,1,0:T(8,128)}, f32[16,16,896]{2,1,0:T(8,128)}, f32[4,160,256]{...) custom-call(s32[1]{0:T(128)} %bitcast.refs_0_, f32[16]{0:T(128)} %get-tuple-element.63.refs_1_, ...), custom_call_target="tpu_custom_call" | custom-call | flops 1146880000 | bytes 4587520 | tf_op jit(solution)/shard_map/tend_inner/pallas_call | solution.py:501
  33.9 1.6 %collective-permute-start.9 = (f32[80,128]{1,0:T(8,128)}, f32[80,128]{1,0:T(8,128)S(1)}, u32[]{:S(2)}, u32[]{:S(2)}) collective-permute-start(f32[80,128]{1,0:T(8,128)} %get-tuple-element.42), channel_id=1, source_target_pairs={{0,2},{1,3},{2,0},{3,1},{4,6},{5,7},{6,4},{7,5},{8,10},{9,11},{10,... | collective-permute-start | bytes 122888 | tf_op jit(solution)/shard_map/ppermute | solution.py:464
  35.5 0.0 collective-permute-start.7
  35.5 1.7 %collective-permute-start.8 = (f32[160,128]{1,0:T(8,128)}, f32[160,128]{1,0:T(8,128)S(1)}, u32[]{:S(2)}, u32[]{:S(2)}) collective-permute-start(f32[160,128]{1,0:T(8,128)} %get-tuple-element.41), channel_id=1, source_target_pairs={{0,3},{1,0},{2,1},{3,2},{4,7},{5,4},{6,5},{7,6},{8,11},{9,8},{10,9... | collective-permute-start | bytes 245768 | tf_op jit(solution)/shard_map/ppermute | solution.py:464
  37.2 0.0 collective-permute-done.2.refs_10_
  37.2 0.0 copy-start
  37.2 0.0 collective-permute-done.3.refs_11_
  37.2 0.0 copy-start.1
  37.3 0.8 %broadcast.40.refs_14_ = f32[6,256]{1,0:T(8,128)} broadcast(f32[6]{0:T(128)S(1)} %pad_maximum_fusion.2), dimensions={0} | broadcast | bytes 6168 | tf_op jit(solution)/shard_map/concatenate | solution.py:434
  38.1 0.1 copy-done
  38.1 0.2 copy-done.1
  38.4 13.4 %tend_edge.1 = (f32[16,16,896]{2,1,0:T(8,128)}, f32[16,16,896]{2,1,0:T(8,128)}, f32[16,16,896]{2,1,0:T(8,128)}, f32[16,16,896]{2,1,0:T(8,128)}, f32[4,96,256]{2,...) custom-call(s32[1]{0:T(128)} %bitcast.refs_0_, ...), custom_call_target="tpu_custom_call", output_to_operand_aliasing={{0}: (18, {}), {1}: (19, {}), {2}: (20, {}), {3}: (21, {})} | custom-call | flops 688128000 | bytes 2752512 | tf_op jit(solution)/shard_map/tend_edge/pallas_call | solution.py:501
  51.7 0.6 collective-permute-start.6
  52.3 0.0 collective-permute-start.4
  52.3 0.0 collective-permute-done.9.refs_8_
  52.3 0.0 copy-start.8
  52.3 1.7 %collective-permute-start.5 = (f32[96,128]{1,0:T(8,128)}, f32[96,128]{1,0:T(8,128)S(1)}, u32[]{:S(2)}, u32[]{:S(2)}) collective-permute-start(f32[96,128]{1,0:T(8,128)} %get-tuple-element.37), channel_id=1, source_target_pairs={{0,3},{1,0},{2,1},{3,2},{4,7},{5,4},{6,5},{7,6},{8,11},{9,8},{10,9... | collective-permute-start | bytes 147464 | tf_op jit(solution)/shard_map/ppermute | solution.py:464
  54.1 0.6 pad_maximum_fusion.3.refs_1_
  54.7 0.0 collective-permute-done.7.refs_6_
  54.7 0.0 copy-start.4
  54.7 0.0 collective-permute-done.8.refs_7_
  54.7 0.0 copy-start.5
  54.7 0.0 copy-done.8
  54.7 0.6 copy-done.4
  55.3 0.0 copy-done.5
  55.3 8.1 %finish_inner.1 = (f32[16,16,896]{2,1,0:T(8,128)}, f32[16,16,896]{2,1,0:T(8,128)}, f32[16,16,896]{2,1,0:T(8,128)}, f32[16,16,896]{2,1,0:T(8,128)}) custom-call(s32[1]{0:T(128)} %bitcast.refs_0_, f32[3]{0:T(128)} %pad_maximum_fusion.3.refs_1_, f32[16,16,896]{2,1,0:T(8,128)} %refs_2_.5, ...), custom_call_target="tpu_custom_call", output_to_operand_aliasing={{0}: (14, {}), {1}: (15, {}), {2}: (16, {}), {3}: (17, {})} | custom-call | tf_op jit(solution)/shard_map/finish_inner/pallas_call | solution.py:541
  63.5 0.0 collective-permute-done.6.refs_8_
  63.5 0.0 copy-start.9
  63.5 0.0 collective-permute-done.4.refs_6_
  63.5 0.0 copy-start.6
  63.5 0.0 collective-permute-done.5.refs_7_
  63.5 0.0 copy-start.7
  63.5 0.6 copy-done.9
  64.1 0.0 copy-done.6
  64.1 0.0 copy-done.7
  64.1 7.2 %finish_edge.1 = (f32[16,16,896]{2,1,0:T(8,128)}, f32[16,16,896]{2,1,0:T(8,128)}, f32[16,16,896]{2,1,0:T(8,128)}, f32[16,16,896]{2,1,0:T(8,128)}) custom-call(s32[1]{0:T(128)} %bitcast.refs_0_, f32[3]{0:T(128)} %pad_maximum_fusion.3.refs_1_, f32[16,16,896]{2,1,0:T(8,128)} %refs_2_.5, ...), custom_call_target="tpu_custom_call", output_to_operand_aliasing={{0}: (14, {}), {1}: (15, {}), {2}: (16, {}), {3}: (17, {})} | custom-call | tf_op jit(solution)/shard_map/finish_edge/pallas_call | solution.py:541
  (2 shorter events, 0.0 us)
Async XLA Ops:
  0.6 12.0 %copy-start.10 = (s32[256]{0:T(256)S(1)}, s32[256]{0:T(256)}, u32[]{:S(2)}) copy-start(s32[256]{0:T(256)} %constant.65.clone) | copy-start | bytes 3076
  0.6 12.0 %copy-start.11 = (s32[32]{0:T(128)S(1)}, s32[32]{0:T(128)}, u32[]{:S(2)}) copy-start(s32[32]{0:T(128)} %param.17) | copy-start | bytes 388
  4.5 11.5 %collective-permute-start = (f32[48,128]{1,0:T(8,128)}, f32[48,128]{1,0:T(8,128)S(1)}, u32[]{:S(2)}, u32[]{:S(2)}) collective-permute-start(f32[48,128]{1,0:T(8,128)} %get-tuple-element.28), channel_id=1, source_target_pairs={{0,1},{1,2},{2,3},{3,0},{4,5},{5,6},{6,7},{7,4},{8,9},{9,10},{10,1... | collective-permute-start | bytes 73736 | tf_op jit(solution)/shard_map/ppermute | solution.py:464
  5.1 11.0 %collective-permute-start.1 = (f32[48,128]{1,0:T(8,128)}, f32[48,128]{1,0:T(8,128)S(1)}, u32[]{:S(2)}, u32[]{:S(2)}) collective-permute-start(f32[48,128]{1,0:T(8,128)} %get-tuple-element.29), channel_id=1, source_target_pairs={{0,3},{1,0},{2,1},{3,2},{4,7},{5,4},{6,5},{7,6},{8,11},{9,8},{10,9... | collective-permute-start | bytes 73736 | tf_op jit(solution)/shard_map/ppermute | solution.py:464
  7.0 30.2 %collective-permute-start.2 = (f32[200,896]{1,0:T(8,128)}, f32[200,896]{1,0:T(8,128)S(1)}, u32[]{:S(2)}, u32[]{:S(2)}) collective-permute-start(f32[200,896]{1,0:T(8,128)} %get-tuple-element.30), channel_id=1, source_target_pairs={{0,4},{4,8},{8,12},{1,5},{5,9},{9,13},{2,6},{6,10},{10,14},{3,7},{... | collective-permute-start | bytes 2150408 | tf_op jit(solution)/shard_map/ppermute | solution.py:468
  11.3 25.9 %collective-permute-start.3 = (f32[200,896]{1,0:T(8,128)}, f32[200,896]{1,0:T(8,128)S(1)}, u32[]{:S(2)}, u32[]{:S(2)}) collective-permute-start(f32[200,896]{1,0:T(8,128)} %get-tuple-element.31), channel_id=1, source_target_pairs={{4,0},{8,4},{12,8},{5,1},{9,5},{13,9},{6,2},{10,6},{14,10},{7,3},{... | collective-permute-start | bytes 2150408 | tf_op jit(solution)/shard_map/ppermute | solution.py:469
  16.1 0.7 copy-start.2
  16.1 0.7 copy-start.3
  33.9 18.4 %collective-permute-start.9 = (f32[80,128]{1,0:T(8,128)}, f32[80,128]{1,0:T(8,128)S(1)}, u32[]{:S(2)}, u32[]{:S(2)}) collective-permute-start(f32[80,128]{1,0:T(8,128)} %get-tuple-element.42), channel_id=1, source_target_pairs={{0,2},{1,3},{2,0},{3,1},{4,6},{5,7},{6,4},{7,5},{8,10},{9,11},{10,... | collective-permute-start | bytes 122888 | tf_op jit(solution)/shard_map/ppermute | solution.py:464
  35.5 19.2 %collective-permute-start.7 = (f32[160,128]{1,0:T(8,128)}, f32[160,128]{1,0:T(8,128)S(1)}, u32[]{:S(2)}, u32[]{:S(2)}) collective-permute-start(f32[160,128]{1,0:T(8,128)} %get-tuple-element.40), channel_id=1, source_target_pairs={{0,1},{1,2},{2,3},{3,0},{4,5},{5,6},{6,7},{7,4},{8,9},{9,10},{10,1... | collective-permute-start | bytes 245768 | tf_op jit(solution)/shard_map/ppermute | solution.py:464
  35.5 19.2 %collective-permute-start.8 = (f32[160,128]{1,0:T(8,128)}, f32[160,128]{1,0:T(8,128)S(1)}, u32[]{:S(2)}, u32[]{:S(2)}) collective-permute-start(f32[160,128]{1,0:T(8,128)} %get-tuple-element.41), channel_id=1, source_target_pairs={{0,3},{1,0},{2,1},{3,2},{4,7},{5,4},{6,5},{7,6},{8,11},{9,8},{10,9... | collective-permute-start | bytes 245768 | tf_op jit(solution)/shard_map/ppermute | solution.py:464
  37.2 0.9 %copy-start = (f32[200,896]{1,0:T(8,128)}, f32[200,896]{1,0:T(8,128)S(1)}, u32[]{:S(2)}) copy-start(f32[200,896]{1,0:T(8,128)S(1)} %collective-permute-done.2.refs_10_) | copy-start | bytes 2150404
  37.2 1.1 %copy-start.1 = (f32[200,896]{1,0:T(8,128)}, f32[200,896]{1,0:T(8,128)S(1)}, u32[]{:S(2)}) copy-start(f32[200,896]{1,0:T(8,128)S(1)} %collective-permute-done.3.refs_11_) | copy-start | bytes 2150404
  51.7 11.8 %collective-permute-start.6 = (f32[48,128]{1,0:T(8,128)}, f32[48,128]{1,0:T(8,128)S(1)}, u32[]{:S(2)}, u32[]{:S(2)}) collective-permute-start(f32[48,128]{1,0:T(8,128)} %get-tuple-element.38), channel_id=1, source_target_pairs={{0,2},{1,3},{2,0},{3,1},{4,6},{5,7},{6,4},{7,5},{8,10},{9,11},{10,... | collective-permute-start | bytes 73736 | tf_op jit(solution)/shard_map/ppermute | solution.py:464
  52.3 11.2 %collective-permute-start.4 = (f32[96,128]{1,0:T(8,128)}, f32[96,128]{1,0:T(8,128)S(1)}, u32[]{:S(2)}, u32[]{:S(2)}) collective-permute-start(f32[96,128]{1,0:T(8,128)} %get-tuple-element.36), channel_id=1, source_target_pairs={{0,1},{1,2},{2,3},{3,0},{4,5},{5,6},{6,7},{7,4},{8,9},{9,10},{10,1... | collective-permute-start | bytes 147464 | tf_op jit(solution)/shard_map/ppermute | solution.py:464
  52.3 2.4 %copy-start.8 = (f32[80,128]{1,0:T(8,128)}, f32[80,128]{1,0:T(8,128)S(1)}, u32[]{:S(2)}) copy-start(f32[80,128]{1,0:T(8,128)S(1)} %collective-permute-done.9.refs_8_) | copy-start | bytes 122884
  52.3 11.2 %collective-permute-start.5 = (f32[96,128]{1,0:T(8,128)}, f32[96,128]{1,0:T(8,128)S(1)}, u32[]{:S(2)}, u32[]{:S(2)}) collective-permute-start(f32[96,128]{1,0:T(8,128)} %get-tuple-element.37), channel_id=1, source_target_pairs={{0,3},{1,0},{2,1},{3,2},{4,7},{5,4},{6,5},{7,6},{8,11},{9,8},{10,9... | collective-permute-start | bytes 147464 | tf_op jit(solution)/shard_map/ppermute | solution.py:464
  54.7 0.6 copy-start.4
  54.7 0.7 copy-start.5
  63.5 0.6 copy-start.9
  63.5 0.6 copy-start.6
  63.5 0.6 copy-start.7

commit v2 on v1

v2 whole, which is shorter than its diff:
```python
import functools
import math

import jax
import jax.numpy as jnp
import ml_dtypes
import numpy as np
from jax import lax
from jax.experimental import pallas as pl
from jax.experimental.pallas import tpu as pltpu
from jax.sharding import PartitionSpec as P

STEP = 0.1
SPIN = 0.5
LANES = 128
NEAR = 16
FAR = 8
NODES = 256
F32 = jnp.float32
BF16 = jnp.bfloat16
MESSAGE = 2 * NEAR + FAR
VMEM_LIMIT = 56 * 1024 * 1024


def pivoted(matrix, count):
    rest = np.array(matrix)
    columns = rest.shape[1]
    tilt = 1.0 + 1e-3 * np.arange(columns) / columns
    picked = []
    tri = np.zeros((count, columns))
    for step in range(count):
        size = (rest * rest).sum(axis=0)
        best = int(np.argmax(size * tilt))
        picked.append(best)
        unit = rest[:, best] / math.sqrt(size[best])
        for _ in range(2):
            part = (unit[:, None] * rest).sum(axis=0)
            rest -= unit[:, None] * part[None, :]
            tri[step] += part
        rest[:, best] = 0.0
    left = tri[:, picked].copy()
    right = tri.copy()
    for step in range(count - 1, -1, -1):
        right[step] /= left[step, step]
        right[:step] -= left[:step, step][:, None] * right[step][None, :]
    right[:, picked] = np.eye(count)
    order = np.argsort(picked)
    return np.asarray(picked)[order], right[order]


def cauchy(target, source, circle):
    gap = target[:, None] - source[None, :]
    angle = np.where(gap == 0, 0.5 * math.pi, gap * math.pi / circle)
    return np.where(gap == 0, 0.0, 1.0 / (circle * np.sin(angle)))


def stacked_halves(table):
    table = table.astype(np.float32)
    high = table.astype(ml_dtypes.bfloat16)
    low = (table - high.astype(np.float32)).astype(ml_dtypes.bfloat16)
    return np.concatenate([high, high, low], axis=0)


def band_table():
    band = np.zeros((2 * LANES, 2 * LANES))
    slope = {-3: -1, -2: 9, -1: -45, 1: 45, 2: -9, 3: 1}
    smooth = {-3: 1, -2: -6, -1: 15, 0: -20, 1: 15, 2: -6, 3: 1}
    for j in range(LANES):
        for k, value in slope.items():
            band[j + 3 + k, j] = value
        for k, value in smooth.items():
            band[j + 3 + k, LANES + j] = value
    return np.concatenate([band, band], axis=0).astype(ml_dtypes.bfloat16)


@functools.lru_cache(maxsize=None)
def filter_tables(sector, circle):
    modes = circle // 8
    place = np.arange(sector)
    wave = np.arange(modes)
    phase = (wave[:, None] * place[None, :]) % circle * (2 * math.pi / circle)
    basis = np.concatenate([np.cos(phase), np.sin(phase[1:])], axis=0)
    nodes, spread = pivoted(basis, NODES)
    own = cauchy(nodes, nodes, circle)
    send = np.zeros((NODES, LANES))
    take = np.zeros((MESSAGE, NODES))
    at = 0
    for shift, count in ((sector, NEAR), (-sector, NEAR), (2 * sector, FAR)):
        kernel = cauchy(nodes + shift, nodes, circle)
        pick, weights = pivoted(kernel, count)
        send[:, at : at + count] = weights.T
        take[at : at + count] = kernel[:, pick].T
        at += count
    take = stacked_halves(take)
    take = np.concatenate([take, np.zeros((LANES - 3 * MESSAGE, NODES), take.dtype)], axis=0)
    return dict(
        nodes=nodes.astype(np.float32)[None],
        band=band_table(),
        spread=stacked_halves(spread.T),
        own=stacked_halves(own.T),
        send=stacked_halves(send),
        take=take,
        gather=stacked_halves(STEP * spread),
    )


def split(value):
    high = value.astype(BF16)
    low = (value - high.astype(F32)).astype(BF16)
    return jnp.concatenate([high, low, high], axis=1)


def dot(a, b):
    return lax.dot_general(a, b, (((1,), (0,)), ((), ())), preferred_element_type=F32)


def start_all(pairs, sems, first=0):
    copies = [pltpu.make_async_copy(a, b, sems.at[first + n]) for n, (a, b) in enumerate(pairs)]
    for c in copies:
        c.start()
    return copies


def wait_all(copies):
    for c in copies:
        c.wait()


def is_polar():
    owner = lax.axis_index("lat")
    quarter = lax.axis_size("lat") // 4
    return (owner < quarter) | (owner >= lax.axis_size("lat") - quarter)


def pack_kernel(cutoffs, *refs):
    fields = refs[:4]
    mass, nodes, south, north, west, east, waves, edge, own_mass, tails, sems = refs[4:]
    rows, columns = mass.shape
    levels = edge.shape[3]
    tail = 12 * levels
    first = start_all(
        [(mass, own_mass)]
        + [(q.at[:, :, 0:LANES], edge.at[0, f]) for f, q in enumerate(fields)]
        + [(q.at[:, :, columns - LANES : columns], edge.at[1, f]) for f, q in enumerate(fields)],
        sems,
    )
    strips = []
    for f, q in enumerate(fields):
        for j in range(3):
            into = pl.ds(levels * (3 * f + j), levels)
            strips += [(q.at[j], south.at[into]), (q.at[rows - 3 + j], north.at[into])]
    strips = start_all(strips, sems, 9)

    lat_count = lax.axis_size("lat")
    lon_count = lax.axis_size("lon")
    owner = lax.axis_index("lat")
    circle = columns * lon_count
    start = jnp.where(owner < lat_count // 4, owner * rows, owner * rows - lat_count * rows // 2)
    start = jnp.clip(start, 0, lat_count * rows // 2 - rows)
    line = lax.broadcasted_iota(jnp.int32, (rows, NODES), 0)
    twice = jnp.zeros((rows, NODES), F32)
    for r in range(rows):
        twice = jnp.where(line == r, (2 * cutoffs[start + r] + 1).astype(F32), twice)
    place = nodes[...] + (lax.axis_index("lon") * columns).astype(F32)
    turns = twice * place
    angle = (turns - 2.0 * circle * jnp.floor(turns * (0.5 / circle))) * (math.pi / circle)
    waves[0] = jnp.cos(angle)
    waves[1] = jnp.sin(angle)
    waves[2] = twice * (1.0 / circle)

    wait_all(first)
    tails[...] = jnp.zeros_like(tails)
    tails[0, 0:3] = own_mass[0:3]
    tails[1, 0:3] = own_mass[rows - 3 : rows]
    into = pl.ds(tail, 8)
    ends = start_all([(tails.at[0], south.at[into]), (tails.at[1], north.at[into])], sems, 33)
    lane = lax.broadcasted_iota(jnp.int32, (levels, LANES), 1)
    west[2 * levels :] = own_mass[:, 0:LANES]
    east[2 * levels :] = pltpu.roll(own_mass[:, columns - LANES : columns], 3, 1)
    for parity in range(2):
        for side, out in ((0, west), (1, east)):
            total = jnp.zeros((levels, LANES), F32)
            for r in range(parity, rows, 2):
                for f in range(4):
                    lead = 16 * (r // 2) + 3 * f
                    turn = lead if side == 0 else (lead + 3) % LANES
                    tile = edge[side, f, r]
                    if turn:
                        tile = pltpu.roll(tile, turn, 1)
                    total = jnp.where((lane >= lead) & (lane < lead + 3), tile, total)
            out[parity * levels : (parity + 1) * levels] = total
    wait_all(strips + ends)


def stencil(center, plus, minus):
    p1, p2, p3 = plus
    m1, m2, m3 = minus
    slope = 45.0 * (p1 - m1) - 9.0 * (p2 - m2) + (p3 - m3)
    smooth = (p3 + m3) - 6.0 * (p2 + m2) + 15.0 * (p1 + m1) - 20.0 * center
    return slope, smooth


def mass_slopes(mass, west, east, mass_ext, mass_x, mass_y, levels, edge_rows):
    rows, columns = mass.shape
    middle = mass[...]
    per_mass = 1.0 / (60.0 * middle)
    wide = jnp.concatenate(
        [pltpu.roll(west[2 * levels :], LANES - 3, 1), middle, east[2 * levels :]], axis=1
    )
    whole = columns + 2 * LANES

    def at(k):
        return pltpu.roll(wide, (-k) % whole, 1)[:, LANES : LANES + columns]

    def store(out, value):
        out[...] = jnp.broadcast_to(value[:, None, :], out.shape)

    store(mass_x, stencil(middle, [at(1), at(2), at(3)], [at(-1), at(-2), at(-3)])[0] * per_mass)
    if edge_rows:
        tall = jnp.concatenate([mass_ext[0:3], middle, mass_ext[8:11]], axis=0)
    else:
        blank = jnp.zeros((3, columns), F32)
        tall = jnp.concatenate([blank, middle, blank], axis=0)
    plus = [tall[3 + k : 3 + k + rows] for k in (1, 2, 3)]
    minus = [tall[3 - k : 3 - k + rows] for k in (1, 2, 3)]
    store(mass_y, stencil(middle, plus, minus)[0] * per_mass)


def spread_rows(table, count, levels):
    wide = jnp.broadcast_to(table[:, None, :], (count, levels, table.shape[1]))
    return wide.reshape(count * levels, table.shape[1])


def own_waves(waves, part, edge_rows):
    table = waves[part]
    rows = table.shape[0]
    if edge_rows:
        return jnp.concatenate([table[:3], table[rows - 3 :]], axis=0)
    return table[3 : rows - 3]


def tend_kernel(edge_rows, count, metric, spin, *refs):
    refs = list(refs)

    def some(n):
        taken = refs[:n]
        del refs[:n]
        return taken

    fields = some(4)
    mass_in, west_in, east_in, waves_in = some(4)
    south, north = some(2) if edge_rows else (None, None)
    band_in, spread_in, own_in, send_in = some(4)
    if edge_rows:
        some(4)
    outs = some(4)
    local, to_east, to_west, to_far = some(4)
    ext, high, low, cross, new, kept_high, kept_low = some(7)
    mass, mass_ext, mass_x, mass_y, west, east, waves = some(7)
    band, spread, own, send, sems = some(5)
    rows, columns = mass.shape
    levels = ext.shape[2]
    items = count * levels
    tiles = columns // LANES

    pairs = [(west_in, west), (east_in, east), (mass_in, mass), (band_in, band)]
    for f in range(4):
        if edge_rows:
            pairs += [
                (fields[f].at[0:6], ext.at[f, 3:9]),
                (fields[f].at[rows - 6 : rows], ext.at[f, 9:15]),
            ]
            for j in range(3):
                part = pl.ds(levels * (3 * f + j), levels)
                pairs += [(south.at[part], ext.at[f, j]), (north.at[part], ext.at[f, 15 + j])]
        else:
            pairs += [(fields[f], ext.at[f])]
    if edge_rows:
        part = pl.ds(12 * levels, 8)
        pairs += [(south.at[part], mass_ext.at[0:8]), (north.at[part], mass_ext.at[8:16])]
    first = start_all(pairs, sems)
    later = start_all(
        [(waves_in, waves), (spread_in, spread), (own_in, own), (send_in, send)], sems, len(pairs)
    )
    wait_all(first)

    mass_slopes(mass, west, east, mass_ext, mass_x, mass_y, levels, edge_rows)
    lane = lax.broadcasted_iota(jnp.int32, (levels, LANES), 1)

    def where(i):
        if edge_rows:
            return i + (rows - 6) * (i // 3), i + 3 + 6 * (i // 3)
        return i + 3, i + 3

    def cut(i, carry):
        row, at = where(i)
        halo = pl.ds(pl.multiple_of((row % 2) * levels, levels), levels)
        for f in range(4):
            lead = 16 * (row // 2) + 3 * f
            before = pltpu.roll(west[halo, :], lax.rem(LANES - lead, LANES), 1)
            for t in range(tiles + 1):
                if t < tiles:
                    tile = pltpu.roll(ext[f, at, :, t * LANES : (t + 1) * LANES], 3, 1)
                else:
                    tile = pltpu.roll(east[halo, :], lax.rem(LANES + 3 - lead, LANES), 1)
                whole = jnp.where(lane < 3, before, tile)
                top = whole.astype(BF16)
                high[f, i, :, t * LANES : (t + 1) * LANES] = top
                low[f, i, :, t * LANES : (t + 1) * LANES] = (whole - top.astype(F32)).astype(BF16)
                before = tile
        return carry

    lax.fori_loop(0, count, cut, 0)

    for t in range(tiles):
        span = slice(t * LANES, (t + 2) * LANES)
        both = jnp.concatenate(
            [high[:, :, :, span].reshape(4 * items, 2 * LANES), low[:, :, :, span].reshape(4 * items, 2 * LANES)],
            axis=1,
        )
        cross[t] = dot(both, band[...]).reshape(4, count, levels, 2 * LANES)

    start_row = lax.axis_index("lat") * rows

    def whole(lines):
        return jnp.concatenate([lines] * (levels // 8), axis=0)

    def tendency(i, t):
        row, at = where(i)
        span = slice(t * LANES, (t + 1) * LANES)
        metric_row = metric[start_row + row]
        spin_row = spin[start_row + row]
        along = metric_row * (1.0 / 60.0)
        u = ext[0, at, :, span]
        v = ext[1, at, :, span]
        theta = ext[2, at, :, span]
        u_fast = u * along
        u_size = jnp.abs(u_fast)
        v_fast = v * (1.0 / 60.0)
        v_size = jnp.abs(v_fast)
        result = [None] * 4
        for f in (3, 0, 1, 2):
            slope_x = cross[t, f, i, :, :LANES]
            smooth_x = cross[t, f, i, :, LANES:]
            slope_y, smooth_y = stencil(
                ext[f, at, :, span],
                [ext[f, at + k, :, span] for k in (1, 2, 3)],
                [ext[f, at - k, :, span] for k in (1, 2, 3)],
            )
            change = (u_size * smooth_x - u_fast * slope_x) + (v_size * smooth_y - v_fast * slope_y)
            if f == 3:
                push_x = along * slope_x + theta * (metric_row * whole(mass_x[row, :, span]))
                push_y = (1.0 / 60.0) * slope_y + theta * whole(mass_y[row, :, span])
            elif f == 0:
                change = change + (spin_row * v - push_x)
            elif f == 1:
                change = change - (spin_row * u + push_y)
            result[f] = change
        return result, at, span

    @pl.when(jnp.logical_not(is_polar()))
    def _():
        def step(i, carry):
            for t in range(tiles):
                change, at, span = tendency(i, t)
                for f in range(4):
                    new[f, i, :, span] = ext[f, at, :, span] + STEP * change[f]
            return carry

        lax.fori_loop(0, count, step, 0)
        pairs = []
        for f in range(4):
            if edge_rows:
                pairs += [
                    (new.at[f, 0:3], outs[f].at[0:3]),
                    (new.at[f, 3:6], outs[f].at[rows - 3 : rows]),
                ]
            else:
                pairs += [(new.at[f], outs[f].at[3 : rows - 3])]
        writes = start_all(pairs, sems)
        wait_all(later)
        wait_all(writes)

    @pl.when(is_polar())
    def _():
        def step(i, carry):
            for t in range(tiles):
                change, _, span = tendency(i, t)
                for f in range(4):
                    top = change[f].astype(BF16)
                    kept_high[f, i, :, span] = top
                    kept_low[f, i, :, span] = (change[f] - top.astype(F32)).astype(BF16)
            return carry

        lax.fori_loop(0, count, step, 0)
        wait_all(later)
        c_all, s_all, d_all = [
            spread_rows(own_waves(waves, part, edge_rows), count, levels) for part in range(3)
        ]
        top = kept_high[...].reshape(4 * items, columns)
        rest = kept_low[...].reshape(4 * items, columns)
        nodal = dot(jnp.concatenate([top, rest, top], axis=1), spread[...])
        turned = []
        for f in range(4):
            part = nodal[f * items : (f + 1) * items]
            turned += [c_all * part, s_all * part]
        turned = split(jnp.concatenate(turned, axis=0))
        moved = dot(turned, own[...])
        sent = dot(turned, send[...])
        for f in range(4):
            at = 2 * f * items
            local[f] = (
                s_all * moved[at : at + items]
                - c_all * moved[at + items : at + 2 * items]
                + d_all * nodal[f * items : (f + 1) * items]
            )
        wide = lax.broadcasted_iota(jnp.int32, (items, LANES), 1)
        for out, first, size in ((to_east, 0, NEAR), (to_west, NEAR, NEAR), (to_far, 2 * NEAR, FAR)):
            total = jnp.zeros((items, LANES), F32)
            for g in range(8):
                part = sent[g * items : (g + 1) * items]
                turn = (size * g - first) % LANES
                if turn:
                    part = pltpu.roll(part, turn, 1)
                total = jnp.where((wide >= size * g) & (wide < size * (g + 1)), part, total)
            if size == NEAR:
                out[...] = total
            else:
                total = total.reshape(count, 2, levels // 2, LANES)
                upper = pltpu.roll(total[:, 1].reshape(items // 2, LANES), 64, 1)
                out[...] = total[:, 0].reshape(items // 2, LANES) + upper


def finish_kernel(edge_rows, count, *refs):
    fields = refs[:4]
    from_west_in, from_east_in, from_far_in, local_in, waves_in, take_in, gather_in = refs[4:11]
    outs = refs[15:19]
    old, new, from_west, from_east, from_far, local, waves, take, gather, sems = refs[19:]
    rows = fields[0].shape[0]
    levels, columns = old.shape[2], old.shape[3]
    items = count * levels

    @pl.when(is_polar())
    def _():
        first = start_all(
            [
                (from_west_in, from_west),
                (from_east_in, from_east),
                (from_far_in, from_far),
                (waves_in, waves),
                (take_in, take),
                (local_in, local),
            ],
            sems,
        )
        reads, pairs = [(gather_in, gather)], []
        for f in range(4):
            if edge_rows:
                parts = [((0, 3), (0, 3)), ((3, 6), (rows - 3, rows))]
            else:
                parts = [((0, count), (3, rows - 3))]
            for (a, b), (c, d) in parts:
                reads.append((fields[f].at[c:d], old.at[f, a:b]))
                pairs.append((new.at[f, a:b], outs[f].at[c:d]))
        reads = start_all(reads, sems, 6)
        wait_all(first)

        place = lax.axis_index("lon")
        last = lax.axis_size("lon") - 1
        near_west = from_west[...] * jnp.where(place == 0, -1.0, 1.0)
        near_east = from_east[...] * jnp.where(place == last, -1.0, 1.0)
        far = from_far[...] * jnp.where(place < 2, -1.0, 1.0)
        far = far.reshape(count, 1, levels // 2, LANES)
        upper = pltpu.roll(far.reshape(items // 2, LANES), 64, 1).reshape(count, 1, levels // 2, LANES)
        far = jnp.concatenate([far, upper], axis=1).reshape(items, LANES)
        wide = lax.broadcasted_iota(jnp.int32, (items, LANES), 1)

        def turn(value, by):
            by = by % LANES
            return pltpu.roll(value, by, 1) if by else value

        come = []
        for g in range(8):
            part = jnp.where(wide < NEAR, turn(near_west, -NEAR * g), turn(near_east, NEAR - NEAR * g))
            part = jnp.where(wide < 2 * NEAR, part, turn(far, 2 * NEAR - FAR * g))
            part = jnp.where(wide < MESSAGE, part, 0.0)
            top = part.astype(BF16).astype(F32)
            come.append((top + turn(part - top, MESSAGE) + turn(top, 2 * MESSAGE)).astype(BF16))
        moved = dot(jnp.concatenate(come, axis=0), take[...])
        c_all, s_all = [
            spread_rows(own_waves(waves, part, edge_rows), count, levels) for part in range(2)
        ]
        value = []
        for f in range(4):
            at = 2 * f * items
            value.append(
                local[f] + (s_all * moved[at : at + items] - c_all * moved[at + items : at + 2 * items])
            )
        value = split(jnp.concatenate(value, axis=0))
        wait_all(reads)
        change = dot(value, gather[...])
        new[...] = old[...] + change.reshape(4, count, levels, columns)
        wait_all(start_all(pairs, sems))


def vmem():
    return pl.BlockSpec(memory_space=pltpu.VMEM)


def smem():
    return pl.BlockSpec(memory_space=pltpu.SMEM)


def anywhere():
    return pl.BlockSpec(memory_space=pl.ANY)


def like(*shape):
    return jax.ShapeDtypeStruct(shape, F32)


def held(value):
    return pltpu.VMEM(value.shape, value.dtype)


def params():
    return pltpu.CompilerParams(vmem_limit_bytes=VMEM_LIMIT)


def row_factors(count):
    latitude = (np.arange(count).astype(np.float32) + np.float32(0.5)) * np.float32(math.pi / count)
    latitude = latitude - np.float32(math.pi / 2)
    metric = np.float32(1.0) / np.cos(latitude)
    return metric.astype(np.float32), (np.float32(SPIN) * np.sin(latitude)).astype(np.float32)


def shards(u_wind, v_wind, theta, geopot, mass, cutoffs):
    rows, levels, columns = u_wind.shape
    lat_count = lax.axis_size("lat")
    lon_count = lax.axis_size("lon")
    tables = {k: jnp.asarray(v) for k, v in filter_tables(columns, columns * lon_count).items()}
    metric, spin = [jnp.asarray(t) for t in row_factors(rows * lat_count)]
    fields = (u_wind, v_wind, theta, geopot)

    strip = 12 * levels + 8
    edge_lines = 2 * levels + rows
    to_south, to_north, to_west, to_east, waves = pl.pallas_call(
        pack_kernel,
        out_shape=[like(strip, columns)] * 2 + [like(edge_lines, LANES)] * 2 + [like(3, rows, NODES)],
        in_specs=[smem()] + [anywhere()] * 5 + [vmem()],
        out_specs=[anywhere()] * 2 + [vmem()] * 3,
        scratch_shapes=[
            pltpu.VMEM((2, 4, rows, levels, LANES), F32),
            pltpu.VMEM((rows, columns), F32),
            pltpu.VMEM((2, 8, columns), F32),
            pltpu.SemaphoreType.DMA((35,)),
        ],
        compiler_params=params(),
        name="pack_edges",
    )(cutoffs, *fields, mass, tables["nodes"])

    def ring(value, step):
        return lax.ppermute(value, "lon", [(i, (i + step) % lon_count) for i in range(lon_count)])

    west = ring(to_east, 1)
    east = ring(to_west, -1)
    south = lax.ppermute(to_north, "lat", [(i, i + 1) for i in range(lat_count - 1)])
    north = lax.ppermute(to_south, "lat", [(i + 1, i) for i in range(lat_count - 1)])

    def tendencies(edge_rows, old):
        count = 6 if edge_rows else rows - 6
        items = count * levels
        deep = 18 if edge_rows else rows
        halos = [south, north] if edge_rows else []
        weights = [tables[k] for k in ("band", "spread", "own", "send")]
        args = [metric, spin, *fields, mass, west, east, waves, *halos, *weights]
        return pl.pallas_call(
            functools.partial(tend_kernel, edge_rows, count),
            out_shape=[like(rows, levels, columns)] * 4
            + [like(4, items, NODES)]
            + [like(items, LANES)] * 2
            + [like(items // 2, LANES)],
            in_specs=[smem()] * 2 + [anywhere()] * (len(args) - 2 + len(old)),
            out_specs=[anywhere()] * 4 + [vmem()] * 4,
            scratch_shapes=[
                pltpu.VMEM((4, deep, levels, columns), F32),
                pltpu.VMEM((4, count, levels, columns + LANES), BF16),
                pltpu.VMEM((4, count, levels, columns + LANES), BF16),
                pltpu.VMEM((columns // LANES, 4, count, levels, 2 * LANES), F32),
                pltpu.VMEM((4, count, levels, columns), F32),
                pltpu.VMEM((4, count, levels, columns), BF16),
                pltpu.VMEM((4, count, levels, columns), BF16),
                pltpu.VMEM((rows, columns), F32),
                pltpu.VMEM((16, columns), F32),
                pltpu.VMEM((rows, 8, columns), F32),
                pltpu.VMEM((rows, 8, columns), F32),
                pltpu.VMEM((edge_lines, LANES), F32),
                pltpu.VMEM((edge_lines, LANES), F32),
                pltpu.VMEM((3, rows, NODES), F32),
                *[held(w) for w in weights],
                pltpu.SemaphoreType.DMA((48,)),
            ],
            input_output_aliases={len(args) + f: f for f in range(4)} if old else {},
            compiler_params=params(),
            cost_estimate=pl.CostEstimate(
                flops=items * 4 * columns * 2000, bytes_accessed=8 * items * columns * 4, transcendentals=0
            ),
            name="tend_edge" if edge_rows else "tend_inner",
        )(*args, *old)

    def exchange(east_part, west_part, far_part):
        return ring(east_part, 1), ring(west_part, -1), ring(far_part, 2)

    def finish(edge_rows, received, local, old):
        count = 6 if edge_rows else rows - 6
        items = count * levels
        weights = [tables[k] for k in ("take", "gather")]
        args = [*fields, *received, local, waves, *weights]
        return pl.pallas_call(
            functools.partial(finish_kernel, edge_rows, count),
            out_shape=[like(rows, levels, columns)] * 4,
            in_specs=[anywhere()] * (len(args) + 4),
            out_specs=[anywhere()] * 4,
            scratch_shapes=[
                pltpu.VMEM((4, count, levels, columns), F32),
                pltpu.VMEM((4, count, levels, columns), F32),
                pltpu.VMEM((items, LANES), F32),
                pltpu.VMEM((items, LANES), F32),
                pltpu.VMEM((items // 2, LANES), F32),
                pltpu.VMEM((4, items, NODES), F32),
                pltpu.VMEM((3, rows, NODES), F32),
                *[held(w) for w in weights],
                pltpu.SemaphoreType.DMA((16,)),
            ],
            input_output_aliases={len(args) + f: f for f in range(4)},
            compiler_params=params(),
            name="finish_edge" if edge_rows else "finish_inner",
        )(*args, *old)

    *outs, local_inner, a, b, c = tendencies(False, [])
    received_inner = exchange(a, b, c)
    *outs, local_edge, a, b, c = tendencies(True, outs)
    received_edge = exchange(a, b, c)
    outs = finish(False, received_inner, local_inner, outs)
    outs = finish(True, received_edge, local_edge, outs)
    return tuple(outs)


def solution(mesh):
    return jax.shard_map(
        shards,
        mesh=mesh,
        in_specs=(
            P(("members", "lat"), None, "lon"),
            P(("members", "lat"), None, "lon"),
            P(("members", "lat"), None, "lon"),
            P(("members", "lat"), None, "lon"),
            P(("members", "lat"), "lon"),
            P(),
        ),
        out_specs=(
            P(("members", "lat"), None, "lon"),
            P(("members", "lat"), None, "lon"),
            P(("members", "lat"), None, "lon"),
            P(("members", "lat"), None, "lon"),
        ),
        check_vma=False,
    )
```

time: 71.7 us -> 97.5 us (1.36)
  Pallas kernels: 49.7 us -> 78.1 us
  other arithmetic: 2.64 us -> 0 us
  waiting for transfers between devices: 0.03 us -> 1.75 us
  local copies, waits for them, and re-layouts: 4.41 us -> 2.96 us
    pallas_call x1, Pallas kernels: 3.89 us -> 44.4 us  [shards(): pl.pallas_call(pack_kernel, out_shape=[like(strip, columns)] * 2 + [like(...]
    pallas_call x2, Pallas kernels: 30.5 us -> 24.4 us  [tendencies(): pl.pallas_call(functools.partial(tend_kernel, edge_rows, count), out_shap...]
    pallas_call x2, Pallas kernels: 15.3 us -> 9.33 us  [finish(): pl.pallas_call(functools.partial(finish_kernel, edge_rows, count), out_sh...]
    ppermute x8, waiting for transfers between devices: 0.02 us -> 1.74 us  [ring(): lax.ppermute(value, 'lon', [(i, (i + step) % lon_count) for i in range(lo...]
    unnamed x24 -> x20, local copies, waits for them, and re-layouts: 1.57 us -> 2.96 us
    slice x5 -> x0, local copies, waits for them, and re-layouts: 1.35 us -> none  [the longest x3 1.27 us: pick_rows(): return table[3:-3]]
    concatenate x3 -> x0, other arithmetic: 1.27 us -> none  [pick_rows(): return jnp.concatenate([table[:3], table[-3:]], axis=0)]
  transfers between devices with their start and end apart: 10 -> 10, of which waited for: 0 -> 1; matrix products, arithmetic and copies ran while one was open for 8% -> 0% of each run, Pallas kernels for 54% -> 30%
where the time goes in v2:
time: 97.5 us; the launch traced here: 97.3 us
  Pallas kernels  78.1 us (80%)
  starting transfers between devices  13.7 us (14%)
  local copies, waits for them, and re-layouts  2.96 us (3%)
  waiting for transfers between devices  1.75 us (2%)
    pallas_call x1, Pallas kernels, shards(): pl.pallas_call(pack_kernel, out_shape=[like(strip, columns)] * 2 + [like(...  44.4 us
    pallas_call x2, Pallas kernels, tendencies(): pl.pallas_call(functools.partial(tend_kernel, edge_rows, count), out_shap...  24.4 us
    pallas_call x2, Pallas kernels, finish(): pl.pallas_call(functools.partial(finish_kernel, edge_rows, count), out_sh...  9.33 us
    ppermute x8, starting transfers between devices, ring(): lax.ppermute(value, 'lon', [(i, (i + step) % lon_count) for i in range(lo...  7.42 us
    ppermute x1, starting transfers between devices, shards(): lax.ppermute(to_north, 'lat', [(i, i + 1) for i in range(lat_count - 1)])  4.97 us
    unnamed x20, local copies, waits for them, and re-layouts  2.96 us
  transfers between devices with their start and end apart: 10, of which 1 were waited for; matrix products, arithmetic and copies ran while one was open for 0% of the time, Pallas kernels for 30%

profile of v2, /device:TPU:0, one launch (start us, length us, event | category | flops | bytes accessed | tf_op | source)
XLA Modules:
  0.0 97.3 jit_solution(1706530475427691681)
XLA Ops:
  0.6 44.4 %pack_edges.1 = (f32[200,896]{1,0:T(8,128)}, f32[200,896]{1,0:T(8,128)}, f32[48,128]{1,0:T(8,128)}, f32[48,128]{1,0:T(8,128)}, f32[3,16,256]{2,1,0:T(8,128)}) custom-call(s32[32]{0:T(128)} %cutoffs.1, f32[16,16,896]{2,1,0:T(8,128)} %refs_0_.9, f32[16,16,896]{2,1,0:T(8,128)} %refs_1_.9, f32[16,16,896]{2,1,0:T(8,128)} %refs_2_.9, f32[16,16,896]{2,1,0:T(8,128)} %refs_3_.9, ...), custom_call_target="tpu_custom_call" | custom-call | tf_op jit(solution)/shard_map/pack_edges/pallas_call | solution.py:547
  45.1 5.0 %collective-permute-start.2 = (f32[200,896]{1,0:T(8,128)}, f32[200,896]{1,0:T(8,128)S(1)}, u32[]{:S(2)}, u32[]{:S(2)}) collective-permute-start(f32[200,896]{1,0:T(8,128)} %get-tuple-element.32), channel_id=1, source_target_pairs={{0,4},{4,8},{8,12},{1,5},{5,9},{9,13},{2,6},{6,10},{10,14},{3,7},{... | collective-permute-start | bytes 2150408 | tf_op jit(solution)/shard_map/ppermute | solution.py:567
  50.1 1.3 %collective-permute-start.3 = (f32[200,896]{1,0:T(8,128)}, f32[200,896]{1,0:T(8,128)S(1)}, u32[]{:S(2)}, u32[]{:S(2)}) collective-permute-start(f32[200,896]{1,0:T(8,128)} %get-tuple-element.33), channel_id=1, source_target_pairs={{4,0},{8,4},{12,8},{5,1},{9,5},{13,9},{6,2},{10,6},{14,10},{7,3},{... | collective-permute-start | bytes 2150408 | tf_op jit(solution)/shard_map/ppermute | solution.py:568
  51.4 0.1 collective-permute-start
  51.4 1.7 %collective-permute-start.1 = (f32[48,128]{1,0:T(8,128)}, f32[48,128]{1,0:T(8,128)S(1)}, u32[]{:S(2)}, u32[]{:S(2)}) collective-permute-start(f32[48,128]{1,0:T(8,128)} %get-tuple-element.30), channel_id=1, source_target_pairs={{0,3},{1,0},{2,1},{3,2},{4,7},{5,4},{6,5},{7,6},{8,11},{9,8},{10,9... | collective-permute-start | bytes 73736 | tf_op jit(solution)/shard_map/ppermute | solution.py:563
  53.2 1.7 %collective-permute-done.refs_5_ = f32[48,128]{1,0:T(8,128)S(1)} collective-permute-done((f32[48,128]{1,0:T(8,128)}, f32[48,128]{1,0:T(8,128)S(1)}, u32[]{:S(2)}, u32[]{:S(2)}) %collective-permute-start) | collective-permute-done | bytes 24608 | tf_op jit(solution)/shard_map/ppermute | solution.py:563
  54.9 0.0 copy-start.2
  54.9 0.0 collective-permute-done.1.refs_6_
  54.9 0.0 copy-start.3
  54.9 0.6 copy-done.2
  55.5 0.0 copy-done.3
  55.5 13.9 %tend_inner.1 = (f32[16,16,896]{2,1,0:T(8,128)}, f32[16,16,896]{2,1,0:T(8,128)}, f32[16,16,896]{2,1,0:T(8,128)}, f32[16,16,896]{2,1,0:T(8,128)}, f32[4,160,256]{...) custom-call(f32[64]{0:T(128)} %constant.25.clone.metric, f32[64]{0:T(128)} %constant.26.clone.spin, ...), custom_call_target="tpu_custom_call" | custom-call | flops 1146880000 | bytes 4587520 | tf_op jit(solution)/shard_map/tend_inner/pallas_call | solution.py:577
  69.5 1.6 %collective-permute-start.9 = (f32[80,128]{1,0:T(8,128)}, f32[80,128]{1,0:T(8,128)S(1)}, u32[]{:S(2)}, u32[]{:S(2)}) collective-permute-start(f32[80,128]{1,0:T(8,128)} %get-tuple-element.44), channel_id=1, source_target_pairs={{0,2},{1,3},{2,0},{3,1},{4,6},{5,7},{6,4},{7,5},{8,10},{9,11},{10,... | collective-permute-start | bytes 122888 | tf_op jit(solution)/shard_map/ppermute | solution.py:563
  71.0 0.5 collective-permute-start.7
  71.5 1.3 %collective-permute-start.8 = (f32[160,128]{1,0:T(8,128)}, f32[160,128]{1,0:T(8,128)S(1)}, u32[]{:S(2)}, u32[]{:S(2)}) collective-permute-start(f32[160,128]{1,0:T(8,128)} %get-tuple-element.43), channel_id=1, source_target_pairs={{0,3},{1,0},{2,1},{3,2},{4,7},{5,4},{6,5},{7,6},{8,11},{9,8},{10,9... | collective-permute-start | bytes 245768 | tf_op jit(solution)/shard_map/ppermute | solution.py:563
  72.8 0.0 collective-permute-done.2.refs_8_
  72.8 0.0 copy-start
  72.8 0.0 collective-permute-done.3.refs_9_
  72.8 0.0 copy-start.1
  72.8 0.9 copy-done
  73.7 0.2 copy-done.1
  73.9 10.4 %tend_edge.1 = (f32[16,16,896]{2,1,0:T(8,128)}, f32[16,16,896]{2,1,0:T(8,128)}, f32[16,16,896]{2,1,0:T(8,128)}, f32[16,16,896]{2,1,0:T(8,128)}, f32[4,96,256]{2,...) custom-call(f32[64]{0:T(128)} %constant.25.clone.metric, ...), custom_call_target="tpu_custom_call", output_to_operand_aliasing={{0}: (16, {}), {1}: (17, {}), {2}: (18, {}), {3}: (19, {})} | custom-call | flops 688128000 | bytes 2752512 | tf_op jit(solution)/shard_map/tend_edge/pallas_call | solution.py:577
  84.3 0.1 collective-permute-start.4
  84.4 1.7 %collective-permute-start.5 = (f32[96,128]{1,0:T(8,128)}, f32[96,128]{1,0:T(8,128)S(1)}, u32[]{:S(2)}, u32[]{:S(2)}) collective-permute-start(f32[96,128]{1,0:T(8,128)} %get-tuple-element.39), channel_id=1, source_target_pairs={{0,3},{1,0},{2,1},{3,2},{4,7},{5,4},{6,5},{7,6},{8,11},{9,8},{10,9... | collective-permute-start | bytes 147464 | tf_op jit(solution)/shard_map/ppermute | solution.py:563
  86.1 0.0 collective-permute-done.9.refs_6_
  86.1 0.0 copy-start.8
  86.1 0.5 collective-permute-start.6
  86.6 0.0 collective-permute-done.7.refs_4_
  86.7 0.0 copy-start.4
  86.7 0.0 collective-permute-done.8.refs_5_
  86.7 0.0 copy-start.5
  86.7 0.1 copy-done.8
  86.8 0.5 copy-done.4
  87.3 0.0 copy-done.5
  87.3 5.3 %finish_inner.1 = (f32[16,16,896]{2,1,0:T(8,128)}, f32[16,16,896]{2,1,0:T(8,128)}, f32[16,16,896]{2,1,0:T(8,128)}, f32[16,16,896]{2,1,0:T(8,128)}) custom-call(f32[16,16,896]{2,1,0:T(8,128)} %refs_0_.9, f32[16,16,896]{2,1,0:T(8,128)} %refs_1_.9, f32[16,16,896]{2,1,0:T(8,128)} %refs_2_.9, ...), custom_call_target="tpu_custom_call", output_to_operand_aliasing={{0}: (11, {}), {1}: (12, {}), {2}: (13, {}), {3}: (14, {})} | custom-call | tf_op jit(solution)/shard_map/finish_inner/pallas_call | solution.py:619
  92.6 0.0 collective-permute-done.6.refs_6_
  92.6 0.0 copy-start.9
  92.6 0.0 collective-permute-done.4.refs_4_
  92.7 0.0 copy-start.6
  92.7 0.0 collective-permute-done.5.refs_5_
  92.7 0.0 copy-start.7
  92.7 0.5 copy-done.9
  93.2 0.0 copy-done.6
  93.3 0.0 copy-done.7
  93.3 4.0 %finish_edge.1 = (f32[16,16,896]{2,1,0:T(8,128)}, f32[16,16,896]{2,1,0:T(8,128)}, f32[16,16,896]{2,1,0:T(8,128)}, f32[16,16,896]{2,1,0:T(8,128)}) custom-call(f32[16,16,896]{2,1,0:T(8,128)} %refs_0_.9, f32[16,16,896]{2,1,0:T(8,128)} %refs_1_.9, f32[16,16,896]{2,1,0:T(8,128)} %refs_2_.9, ...), custom_call_target="tpu_custom_call", output_to_operand_aliasing={{0}: (11, {}), {1}: (12, {}), {2}: (13, {}), {3}: (14, {})} | custom-call | tf_op jit(solution)/shard_map/finish_edge/pallas_call | solution.py:619
Async XLA Ops:
  45.1 27.7 %collective-permute-start.2 = (f32[200,896]{1,0:T(8,128)}, f32[200,896]{1,0:T(8,128)S(1)}, u32[]{:S(2)}, u32[]{:S(2)}) collective-permute-start(f32[200,896]{1,0:T(8,128)} %get-tuple-element.32), channel_id=1, source_target_pairs={{0,4},{4,8},{8,12},{1,5},{5,9},{9,13},{2,6},{6,10},{10,14},{3,7},{... | collective-permute-start | bytes 2150408 | tf_op jit(solution)/shard_map/ppermute | solution.py:567
  50.1 22.7 %collective-permute-start.3 = (f32[200,896]{1,0:T(8,128)}, f32[200,896]{1,0:T(8,128)S(1)}, u32[]{:S(2)}, u32[]{:S(2)}) collective-permute-start(f32[200,896]{1,0:T(8,128)} %get-tuple-element.33), channel_id=1, source_target_pairs={{4,0},{8,4},{12,8},{5,1},{9,5},{13,9},{6,2},{10,6},{14,10},{7,3},{... | collective-permute-start | bytes 2150408 | tf_op jit(solution)/shard_map/ppermute | solution.py:568
  51.4 3.5 %collective-permute-start = (f32[48,128]{1,0:T(8,128)}, f32[48,128]{1,0:T(8,128)S(1)}, u32[]{:S(2)}, u32[]{:S(2)}) collective-permute-start(f32[48,128]{1,0:T(8,128)} %get-tuple-element.29), channel_id=1, source_target_pairs={{0,1},{1,2},{2,3},{3,0},{4,5},{5,6},{6,7},{7,4},{8,9},{9,10},{10,1... | collective-permute-start | bytes 73736 | tf_op jit(solution)/shard_map/ppermute | solution.py:563
  51.4 3.5 %collective-permute-start.1 = (f32[48,128]{1,0:T(8,128)}, f32[48,128]{1,0:T(8,128)S(1)}, u32[]{:S(2)}, u32[]{:S(2)}) collective-permute-start(f32[48,128]{1,0:T(8,128)} %get-tuple-element.30), channel_id=1, source_target_pairs={{0,3},{1,0},{2,1},{3,2},{4,7},{5,4},{6,5},{7,6},{8,11},{9,8},{10,9... | collective-permute-start | bytes 73736 | tf_op jit(solution)/shard_map/ppermute | solution.py:563
  54.9 0.6 copy-start.2
  54.9 0.6 copy-start.3
  69.5 16.7 %collective-permute-start.9 = (f32[80,128]{1,0:T(8,128)}, f32[80,128]{1,0:T(8,128)S(1)}, u32[]{:S(2)}, u32[]{:S(2)}) collective-permute-start(f32[80,128]{1,0:T(8,128)} %get-tuple-element.44), channel_id=1, source_target_pairs={{0,2},{1,3},{2,0},{3,1},{4,6},{5,7},{6,4},{7,5},{8,10},{9,11},{10,... | collective-permute-start | bytes 122888 | tf_op jit(solution)/shard_map/ppermute | solution.py:563
  71.0 15.6 %collective-permute-start.7 = (f32[160,128]{1,0:T(8,128)}, f32[160,128]{1,0:T(8,128)S(1)}, u32[]{:S(2)}, u32[]{:S(2)}) collective-permute-start(f32[160,128]{1,0:T(8,128)} %get-tuple-element.42), channel_id=1, source_target_pairs={{0,1},{1,2},{2,3},{3,0},{4,5},{5,6},{6,7},{7,4},{8,9},{9,10},{10,1... | collective-permute-start | bytes 245768 | tf_op jit(solution)/shard_map/ppermute | solution.py:563
  71.5 15.2 %collective-permute-start.8 = (f32[160,128]{1,0:T(8,128)}, f32[160,128]{1,0:T(8,128)S(1)}, u32[]{:S(2)}, u32[]{:S(2)}) collective-permute-start(f32[160,128]{1,0:T(8,128)} %get-tuple-element.43), channel_id=1, source_target_pairs={{0,3},{1,0},{2,1},{3,2},{4,7},{5,4},{6,5},{7,6},{8,11},{9,8},{10,9... | collective-permute-start | bytes 245768 | tf_op jit(solution)/shard_map/ppermute | solution.py:563
  72.8 0.9 copy-start
  72.8 1.1 %copy-start.1 = (f32[200,896]{1,0:T(8,128)}, f32[200,896]{1,0:T(8,128)S(1)}, u32[]{:S(2)}) copy-start(f32[200,896]{1,0:T(8,128)S(1)} %collective-permute-done.3.refs_9_) | copy-start | bytes 2150404
  84.3 8.3 %collective-permute-start.4 = (f32[96,128]{1,0:T(8,128)}, f32[96,128]{1,0:T(8,128)S(1)}, u32[]{:S(2)}, u32[]{:S(2)}) collective-permute-start(f32[96,128]{1,0:T(8,128)} %get-tuple-element.38), channel_id=1, source_target_pairs={{0,1},{1,2},{2,3},{3,0},{4,5},{5,6},{6,7},{7,4},{8,9},{9,10},{10,1... | collective-permute-start | bytes 147464 | tf_op jit(solution)/shard_map/ppermute | solution.py:563
  84.4 8.3 %collective-permute-start.5 = (f32[96,128]{1,0:T(8,128)}, f32[96,128]{1,0:T(8,128)S(1)}, u32[]{:S(2)}, u32[]{:S(2)}) collective-permute-start(f32[96,128]{1,0:T(8,128)} %get-tuple-element.39), channel_id=1, source_target_pairs={{0,3},{1,0},{2,1},{3,2},{4,7},{5,4},{6,5},{7,6},{8,11},{9,8},{10,9... | collective-permute-start | bytes 147464 | tf_op jit(solution)/shard_map/ppermute | solution.py:563
  86.1 0.6 copy-start.8
  86.1 6.5 %collective-permute-start.6 = (f32[48,128]{1,0:T(8,128)}, f32[48,128]{1,0:T(8,128)S(1)}, u32[]{:S(2)}, u32[]{:S(2)}) collective-permute-start(f32[48,128]{1,0:T(8,128)} %get-tuple-element.40), channel_id=1, source_target_pairs={{0,2},{1,3},{2,0},{3,1},{4,6},{5,7},{6,4},{7,5},{8,10},{9,11},{10,... | collective-permute-start | bytes 73736 | tf_op jit(solution)/shard_map/ppermute | solution.py:563
  86.7 0.6 copy-start.4
  86.7 0.6 copy-start.5
  92.6 0.6 copy-start.9
  92.7 0.6 copy-start.6
  92.7 0.6 copy-start.7

commit v3 on v2

--- a/solution.py
+++ b/solution.py
@@ -19,7 +19,6 @@
 F32 = jnp.float32
 BF16 = jnp.bfloat16
 MESSAGE = 2 * NEAR + FAR
-VMEM_LIMIT = 56 * 1024 * 1024
 
 
 def pivoted(matrix, count):
@@ -132,24 +131,50 @@
     return (owner < quarter) | (owner >= lax.axis_size("lat") - quarter)
 
 
-def pack_kernel(cutoffs, *refs):
+def pack_lon_kernel(*refs):
     fields = refs[:4]
-    mass, nodes, south, north, west, east, waves, edge, own_mass, tails, sems = refs[4:]
+    mass, west, east, edge, own_mass, sems = refs[4:]
     rows, columns = mass.shape
     levels = edge.shape[3]
-    tail = 12 * levels
-    first = start_all(
+    copies = start_all(
         [(mass, own_mass)]
         + [(q.at[:, :, 0:LANES], edge.at[0, f]) for f, q in enumerate(fields)]
         + [(q.at[:, :, columns - LANES : columns], edge.at[1, f]) for f, q in enumerate(fields)],
         sems,
     )
-    strips = []
+    wait_all(copies)
+    lane = lax.broadcasted_iota(jnp.int32, (levels, LANES), 1)
+    west[2 * levels :] = own_mass[:, 0:LANES]
+    east[2 * levels :] = pltpu.roll(own_mass[:, columns - LANES : columns], 3, 1)
+    for parity in range(2):
+        for side, out in ((0, west), (1, east)):
+            total = jnp.zeros((levels, LANES), F32)
+            for r in range(parity, rows, 2):
+                for f in range(4):
+                    lead = 16 * (r // 2) + 3 * f
+                    turn = lead if side == 0 else (lead + 3) % LANES
+                    tile = edge[side, f, r]
+                    if turn:
+                        tile = pltpu.roll(tile, turn, 1)
+                    total = jnp.where((lane >= lead) & (lane < lead + 3), tile, total)
+            out[parity * levels : (parity + 1) * levels] = total
+
+
+def pack_lat_kernel(cutoffs, *refs):
+    fields = refs[:4]
+    mass, nodes, _, south, north, waves, strips, own_mass, sems = refs[4:]
+    rows, columns = mass.shape
+    levels = fields[0].shape[1]
+    tail = 12 * levels
+    pairs, parts = [], []
     for f, q in enumerate(fields):
-        for j in range(3):
-            into = pl.ds(levels * (3 * f + j), levels)
-            strips += [(q.at[j], south.at[into]), (q.at[rows - 3 + j], north.at[into])]
-    strips = start_all(strips, sems, 9)
+        for side, first in ((0, 0), (1, rows - 3)):
+            for j in range(3):
+                part = pl.ds(levels * (3 * f + j), levels)
+                pairs.append((q.at[first + j], strips.at[side, part]))
+                parts.append((strips.at[side, part], (south, north)[side].at[part]))
+    mass_copy = start_all([(mass, own_mass)], sems)
+    reads = start_all(pairs, sems, 1)
 
     lat_count = lax.axis_size("lat")
     lon_count = lax.axis_size("lon")
@@ -168,28 +193,16 @@
     waves[1] = jnp.sin(angle)
     waves[2] = twice * (1.0 / circle)
 
-    wait_all(first)
-    tails[...] = jnp.zeros_like(tails)
-    tails[0, 0:3] = own_mass[0:3]
-    tails[1, 0:3] = own_mass[rows - 3 : rows]
-    into = pl.ds(tail, 8)
-    ends = start_all([(tails.at[0], south.at[into]), (tails.at[1], north.at[into])], sems, 33)
-    lane = lax.broadcasted_iota(jnp.int32, (levels, LANES), 1)
-    west[2 * levels :] = own_mass[:, 0:LANES]
-    east[2 * levels :] = pltpu.roll(own_mass[:, columns - LANES : columns], 3, 1)
-    for parity in range(2):
-        for side, out in ((0, west), (1, east)):
-            total = jnp.zeros((levels, LANES), F32)
-            for r in range(parity, rows, 2):
-                for f in range(4):
-                    lead = 16 * (r // 2) + 3 * f
-                    turn = lead if side == 0 else (lead + 3) % LANES
-                    tile = edge[side, f, r]
-                    if turn:
-                        tile = pltpu.roll(tile, turn, 1)
-                    total = jnp.where((lane >= lead) & (lane < lead + 3), tile, total)
-            out[parity * levels : (parity + 1) * levels] = total
-    wait_all(strips + ends)
+    wait_all(mass_copy)
+    for side, first in ((0, 0), (1, rows - 3)):
+        strips[side, tail : tail + 3] = own_mass[first : first + 3]
+        strips[side, tail + 3 : tail + 8] = jnp.zeros((5, columns), F32)
+    rest = pl.ds(tail, 8)
+    writes = start_all([(strips.at[0, rest], south.at[rest]), (strips.at[1, rest], north.at[rest])], sems, 25)
+    for n, c in enumerate(reads):
+        c.wait()
+        writes += start_all([parts[n]], sems, 27 + n)
+    wait_all(writes)
 
 
 def stencil(center, plus, minus):
@@ -523,8 +536,8 @@
     return pltpu.VMEM(value.shape, value.dtype)
 
 
-def params():
-    return pltpu.CompilerParams(vmem_limit_bytes=VMEM_LIMIT)
+def params(mebibytes):
+    return pltpu.CompilerParams(vmem_limit_bytes=mebibytes * 1024 * 1024)
 
 
 def row_factors(count):
@@ -544,20 +557,32 @@
 
     strip = 12 * levels + 8
     edge_lines = 2 * levels + rows
-    to_south, to_north, to_west, to_east, waves = pl.pallas_call(
-        pack_kernel,
-        out_shape=[like(strip, columns)] * 2 + [like(edge_lines, LANES)] * 2 + [like(3, rows, NODES)],
-        in_specs=[smem()] + [anywhere()] * 5 + [vmem()],
-        out_specs=[anywhere()] * 2 + [vmem()] * 3,
+    to_west, to_east = pl.pallas_call(
+        pack_lon_kernel,
+        out_shape=[like(edge_lines, LANES)] * 2,
+        in_specs=[anywhere()] * 5,
+        out_specs=[vmem()] * 2,
         scratch_shapes=[
             pltpu.VMEM((2, 4, rows, levels, LANES), F32),
             pltpu.VMEM((rows, columns), F32),
-            pltpu.VMEM((2, 8, columns), F32),
-            pltpu.SemaphoreType.DMA((35,)),
+            pltpu.SemaphoreType.DMA((9,)),
         ],
-        compiler_params=params(),
-        name="pack_edges",
-    )(cutoffs, *fields, mass, tables["nodes"])
+        compiler_params=params(8),
+        name="pack_lon",
+    )(*fields, mass)
+    to_south, to_north, waves = pl.pallas_call(
+        pack_lat_kernel,
+        out_shape=[like(strip, columns)] * 2 + [like(3, rows, NODES)],
+        in_specs=[smem()] + [anywhere()] * 5 + [vmem(), anywhere()],
+        out_specs=[anywhere()] * 2 + [vmem()],
+        scratch_shapes=[
+            pltpu.VMEM((2, strip, columns), F32),
+            pltpu.VMEM((rows, columns), F32),
+            pltpu.SemaphoreType.DMA((51,)),
+        ],
+        compiler_params=params(8),
+        name="pack_lat",
+    )(cutoffs, *fields, mass, tables["nodes"], to_west)
 
     def ring(value, step):
         return lax.ppermute(value, "lon", [(i, (i + step) % lon_count) for i in range(lon_count)])
@@ -601,7 +626,7 @@
                 pltpu.SemaphoreType.DMA((48,)),
             ],
             input_output_aliases={len(args) + f: f for f in range(4)} if old else {},
-            compiler_params=params(),
+            compiler_params=params(36),
             cost_estimate=pl.CostEstimate(
                 flops=items * 4 * columns * 2000, bytes_accessed=8 * items * columns * 4, transcendentals=0
             ),
@@ -633,7 +658,7 @@
                 pltpu.SemaphoreType.DMA((16,)),
             ],
             input_output_aliases={len(args) + f: f for f in range(4)},
-            compiler_params=params(),
+            compiler_params=params(24),
             name="finish_edge" if edge_rows else "finish_inner",
         )(*args, *old)
 

time: 97.5 us -> 63.1 us (0.65)
  Pallas kernels: 78.1 us -> 40.8 us
  local copies, waits for them, and re-layouts: 2.96 us -> 5.64 us
    pallas_call x1 -> x2, Pallas kernels: 44.4 us -> 5.47 us  [the longest x1 4.89 us: shards(): pl.pallas_call(pack_lat_kernel, out_shape=[like(strip, columns)] * 2 + [l...]
    unnamed x20 -> x40, local copies, waits for them, and re-layouts: 2.96 us -> 5.64 us
    pallas_call x2, Pallas kernels: 9.33 us -> 11.1 us  [finish(): pl.pallas_call(functools.partial(finish_kernel, edge_rows, count), out_sh...]
  transfers between devices with their start and end apart: 10 -> 10, of which waited for: 1 -> 1; matrix products, arithmetic and copies ran while one was open for 0% -> 0% of each run, Pallas kernels for 30% -> 47%
where the time goes in v3:
time: 63.1 us; the launch traced here: 62.8 us
  Pallas kernels  40.8 us (65%)
  starting transfers between devices  13.7 us (22%)
  local copies, waits for them, and re-layouts  5.64 us (9%)
  waiting for transfers between devices  1.54 us (2%)
  between operations  1.06 us (2%)
    pallas_call x2, Pallas kernels, tendencies(): pl.pallas_call(functools.partial(tend_kernel, edge_rows, count), out_shap...  24.3 us
    pallas_call x2, Pallas kernels, finish(): pl.pallas_call(functools.partial(finish_kernel, edge_rows, count), out_sh...  11.1 us
    ppermute x8, starting transfers between devices, ring(): lax.ppermute(value, 'lon', [(i, (i + step) % lon_count) for i in range(lo...  7.42 us
    unnamed x40, local copies, waits for them, and re-layouts  5.64 us
    ppermute x1, starting transfers between devices, shards(): lax.ppermute(to_north, 'lat', [(i, i + 1) for i in range(lat_count - 1)])  4.97 us
    pallas_call x1, Pallas kernels, shards(): pl.pallas_call(pack_lat_kernel, out_shape=[like(strip, columns)] * 2 + [l...  4.89 us
    ppermute x8, waiting for transfers between devices, ring(): lax.ppermute(value, 'lon', [(i, (i + step) % lon_count) for i in range(lo...  1.54 us
    ppermute x1, starting transfers between devices, shards(): lax.ppermute(to_south, 'lat', [(i + 1, i) for i in range(lat_count - 1)])  1.29 us
  transfers between devices with their start and end apart: 10, of which 1 were waited for; matrix products, arithmetic and copies ran while one was open for 0% of the time, Pallas kernels for 47%

profile of v3, /device:TPU:0, one launch (start us, length us, event | category | flops | bytes accessed | tf_op | source)
XLA Modules:
  0.0 62.8 jit_solution(7181376043952779358)
XLA Ops:
  0.6 0.0 copy-start.18
  0.6 0.0 copy-start
  0.7 1.2 %copy-done = f32[16,16,896]{2,1,0:T(8,128)S(1)} copy-done((f32[16,16,896]{2,1,0:T(8,128)S(1)}, f32[16,16,896]{2,1,0:T(8,128)}, u32[]{:S(2)}) %copy-start) | copy-done | bytes 917528
  1.8 0.0 copy-start.2
  1.8 1.2 %copy-done.2 = f32[16,16,896]{2,1,0:T(8,128)S(1)} copy-done((f32[16,16,896]{2,1,0:T(8,128)S(1)}, f32[16,16,896]{2,1,0:T(8,128)}, u32[]{:S(2)}) %copy-start.2) | copy-done | bytes 917528
  3.0 0.0 copy-start.4
  3.0 1.2 %copy-done.4 = f32[16,16,896]{2,1,0:T(8,128)S(1)} copy-done((f32[16,16,896]{2,1,0:T(8,128)S(1)}, f32[16,16,896]{2,1,0:T(8,128)}, u32[]{:S(2)}) %copy-start.4) | copy-done | bytes 917528
  4.2 0.0 copy-start.6
  4.2 1.2 %copy-done.6 = f32[16,16,896]{2,1,0:T(8,128)S(1)} copy-done((f32[16,16,896]{2,1,0:T(8,128)S(1)}, f32[16,16,896]{2,1,0:T(8,128)}, u32[]{:S(2)}) %copy-start.6) | copy-done | bytes 917528
  5.4 0.0 copy-start.12
  5.4 0.8 %copy-done.12 = f32[16,896]{1,0:T(8,128)S(1)} copy-done((f32[16,896]{1,0:T(8,128)S(1)}, f32[16,896]{1,0:T(8,128)}, u32[]{:S(2)}) %copy-start.12) | copy-done | bytes 57368
  6.2 0.0 copy-start.8
  6.2 0.0 copy-start.10
  6.2 0.0 copy-start.11
  6.2 0.0 copy-start.14
  6.2 0.6 pack_lon.1
  6.8 0.0 copy-done.18
  6.8 0.0 copy-done.19
  6.8 0.0 copy-start.1
  6.8 0.0 copy-start.3
  6.8 0.0 copy-start.5
  6.9 0.0 copy-start.7
  6.9 0.0 copy-start.13
  6.9 0.0 copy-start.16
  6.9 0.0 copy-start.17
  6.9 4.9 %pack_lat.1 = (f32[200,896]{1,0:T(8,128)S(1)}, f32[200,896]{1,0:T(8,128)S(1)}, f32[3,16,256]{2,1,0:T(8,128)S(1)}) custom-call(s32[32]{0:T(128)S(1)} %copy-done.19, f32[16,16,896]{2,1,0:T(8,128)S(1)} %copy-done, f32[16,16,896]{2,1,0:T(8,128)S(1)} %copy-done.2, f32[16,16,896]{2,1,0:T(8,128)S(1)} %copy-done.4, f32[16,16,896]{2,1,0:T(8,128)S(1)} %copy-done.6, ...), custom_call_target="tpu_custom_call" | custom-call | tf_op jit(solution)/shard_map/pack_lat/pallas_call | solution.py:573
  11.8 5.0 %collective-permute-start.2 = (f32[200,896]{1,0:T(8,128)S(1)}, f32[200,896]{1,0:T(8,128)S(1)}, u32[]{:S(2)}, u32[]{:S(2)}) collective-permute-start(f32[200,896]{1,0:T(8,128)S(1)} %get-tuple-element.32), channel_id=1, source_target_pairs={{0,4},{4,8},{8,12},{1,5},{5,9},{9,13},{2,6},{6,10},{10,14},{3,7},{... | collective-permute-start | bytes 2150408 | tf_op jit(solution)/shard_map/ppermute | solution.py:592
  16.8 1.3 %collective-permute-start.3 = (f32[200,896]{1,0:T(8,128)S(1)}, f32[200,896]{1,0:T(8,128)S(1)}, u32[]{:S(2)}, u32[]{:S(2)}) collective-permute-start(f32[200,896]{1,0:T(8,128)S(1)} %get-tuple-element.33), channel_id=1, source_target_pairs={{4,0},{8,4},{12,8},{5,1},{9,5},{13,9},{6,2},{10,6},{14,10},{7,3},{... | collective-permute-start | bytes 2150408 | tf_op jit(solution)/shard_map/ppermute | solution.py:593
  18.1 0.1 collective-permute-start
  18.2 1.7 %collective-permute-start.1 = (f32[48,128]{1,0:T(8,128)S(1)}, f32[48,128]{1,0:T(8,128)S(1)}, u32[]{:S(2)}, u32[]{:S(2)}) collective-permute-start(f32[48,128]{1,0:T(8,128)S(1)} %get-tuple-element.30.refs_6_), channel_id=1, source_target_pairs={{0,3},{1,0},{2,1},{3,2},{4,7},{5,4},{6,5},{7,6},{8,11},{9,8},{10,9... | collective-permute-start | bytes 73736 | tf_op jit(solution)/shard_map/ppermute | solution.py:588
  19.9 1.5 %collective-permute-done.refs_5_ = f32[48,128]{1,0:T(8,128)S(1)} collective-permute-done((f32[48,128]{1,0:T(8,128)S(1)}, f32[48,128]{1,0:T(8,128)S(1)}, u32[]{:S(2)}, u32[]{:S(2)}) %collective-permute-start) | collective-permute-done | bytes 24608 | tf_op jit(solution)/shard_map/ppermute | solution.py:588
  21.4 0.0 collective-permute-done.1.refs_6_
  21.4 0.0 copy-done.8
  21.4 0.0 copy-done.10
  21.4 0.0 copy-done.11
  21.4 0.0 copy-done.14
  21.4 0.0 copy-done.1
  21.4 0.0 copy-done.3
  21.4 0.0 copy-done.5
  21.5 0.0 copy-done.7
  21.5 0.0 copy-done.13
  21.5 0.0 copy-done.16
  21.5 0.0 copy-done.17
  21.5 12.6 %tend_inner.1 = (f32[16,16,896]{2,1,0:T(8,128)}, f32[16,16,896]{2,1,0:T(8,128)}, f32[16,16,896]{2,1,0:T(8,128)}, f32[16,16,896]{2,1,0:T(8,128)}, f32[4,160,256]{...) custom-call(f32[64]{0:T(128)S(1)} %copy-done.17, f32[64]{0:T(128)S(1)} %copy-done.16, ...), custom_call_target="tpu_custom_call" | custom-call | flops 1146880000 | bytes 4587520 | tf_op jit(solution)/shard_map/tend_inner/pallas_call | solution.py:602
  34.1 1.6 %collective-permute-start.9 = (f32[80,128]{1,0:T(8,128)S(1)}, f32[80,128]{1,0:T(8,128)S(1)}, u32[]{:S(2)}, u32[]{:S(2)}) collective-permute-start(f32[80,128]{1,0:T(8,128)S(1)} %get-tuple-element.44), channel_id=1, source_target_pairs={{0,2},{1,3},{2,0},{3,1},{4,6},{5,7},{6,4},{7,5},{8,10},{9,11},{10,... | collective-permute-start | bytes 122888 | tf_op jit(solution)/shard_map/ppermute | solution.py:588
  35.7 0.5 collective-permute-start.7
  36.1 1.3 %collective-permute-start.8 = (f32[160,128]{1,0:T(8,128)S(1)}, f32[160,128]{1,0:T(8,128)S(1)}, u32[]{:S(2)}, u32[]{:S(2)}) collective-permute-start(f32[160,128]{1,0:T(8,128)S(1)} %get-tuple-element.43), channel_id=1, source_target_pairs={{0,3},{1,0},{2,1},{3,2},{4,7},{5,4},{6,5},{7,6},{8,11},{9,8},{10,9... | collective-permute-start | bytes 245768 | tf_op jit(solution)/shard_map/ppermute | solution.py:588
  37.5 0.0 collective-permute-done.2.refs_8_
  37.5 0.0 collective-permute-done.3.refs_9_
  37.5 0.0 copy-start.15
  37.5 11.7 %tend_edge.1 = (f32[16,16,896]{2,1,0:T(8,128)}, f32[16,16,896]{2,1,0:T(8,128)}, f32[16,16,896]{2,1,0:T(8,128)}, f32[16,16,896]{2,1,0:T(8,128)}, f32[4,96,256]{2,...) custom-call(f32[64]{0:T(128)S(1)} %copy-done.17, ...), custom_call_target="tpu_custom_call", output_to_operand_aliasing={{0}: (16, {}), {1}: (17, {}), {2}: (18, {}), {3}: (19, {})} | custom-call | flops 688128000 | bytes 2752512 | tf_op jit(solution)/shard_map/tend_edge/pallas_call | solution.py:602
  49.2 0.1 collective-permute-start.4
  49.2 1.7 %collective-permute-start.5 = (f32[96,128]{1,0:T(8,128)S(1)}, f32[96,128]{1,0:T(8,128)S(1)}, u32[]{:S(2)}, u32[]{:S(2)}) collective-permute-start(f32[96,128]{1,0:T(8,128)S(1)} %get-tuple-element.39), channel_id=1, source_target_pairs={{0,3},{1,0},{2,1},{3,2},{4,7},{5,4},{6,5},{7,6},{8,11},{9,8},{10,9... | collective-permute-start | bytes 147464 | tf_op jit(solution)/shard_map/ppermute | solution.py:588
  51.0 0.0 collective-permute-done.9.refs_6_
  51.0 0.5 collective-permute-start.6
  51.5 0.0 collective-permute-done.7.refs_4_
  51.5 0.0 collective-permute-done.8.refs_5_
  51.5 0.0 copy-done.9
  51.5 0.0 copy-done.15
  51.5 5.5 %finish_inner.1 = (f32[16,16,896]{2,1,0:T(8,128)}, f32[16,16,896]{2,1,0:T(8,128)}, f32[16,16,896]{2,1,0:T(8,128)}, f32[16,16,896]{2,1,0:T(8,128)}) custom-call(f32[16,16,896]{2,1,0:T(8,128)S(1)} %copy-done.1, f32[16,16,896]{2,1,0:T(8,128)S(1)} %copy-done.3, ...), custom_call_target="tpu_custom_call", output_to_operand_aliasing={{0}: (11, {}), {1}: (12, {}), {2}: (13, {}), {3}: (14, {})} | custom-call | tf_op jit(solution)/shard_map/finish_inner/pallas_call | solution.py:644
  57.0 0.0 collective-permute-done.6.refs_6_
  57.0 0.0 collective-permute-done.4.refs_4_
  57.0 0.0 collective-permute-done.5.refs_5_
  57.0 5.6 %finish_edge.1 = (f32[16,16,896]{2,1,0:T(8,128)}, f32[16,16,896]{2,1,0:T(8,128)}, f32[16,16,896]{2,1,0:T(8,128)}, f32[16,16,896]{2,1,0:T(8,128)}) custom-call(f32[16,16,896]{2,1,0:T(8,128)S(1)} %copy-done.1, f32[16,16,896]{2,1,0:T(8,128)S(1)} %copy-done.3, ...), custom_call_target="tpu_custom_call", output_to_operand_aliasing={{0}: (11, {}), {1}: (12, {}), {2}: (13, {}), {3}: (14, {})} | custom-call | tf_op jit(solution)/shard_map/finish_edge/pallas_call | solution.py:644
  (2 shorter events, 0.0 us)
Async XLA Ops:
  0.6 6.2 %copy-start.18 = (f32[1,256]{1,0:T(1,128)S(1)}, f32[1,256]{1,0:T(1,128)}, u32[]{:S(2)}) copy-start(f32[1,256]{1,0:T(1,128)} %constant.18.clone.refs_5_) | copy-start | bytes 3076
  0.6 1.2 %copy-start = (f32[16,16,896]{2,1,0:T(8,128)S(1)}, f32[16,16,896]{2,1,0:T(8,128)}, u32[]{:S(2)}) copy-start(f32[16,16,896]{2,1,0:T(8,128)} %refs_0_.11) | copy-start | bytes 2752516
  1.8 1.2 %copy-start.2 = (f32[16,16,896]{2,1,0:T(8,128)S(1)}, f32[16,16,896]{2,1,0:T(8,128)}, u32[]{:S(2)}) copy-start(f32[16,16,896]{2,1,0:T(8,128)} %refs_1_.11) | copy-start | bytes 2752516
  3.0 1.2 %copy-start.4 = (f32[16,16,896]{2,1,0:T(8,128)S(1)}, f32[16,16,896]{2,1,0:T(8,128)}, u32[]{:S(2)}) copy-start(f32[16,16,896]{2,1,0:T(8,128)} %refs_2_.11) | copy-start | bytes 2752516
  4.2 1.2 %copy-start.6 = (f32[16,16,896]{2,1,0:T(8,128)S(1)}, f32[16,16,896]{2,1,0:T(8,128)}, u32[]{:S(2)}) copy-start(f32[16,16,896]{2,1,0:T(8,128)} %refs_3_.11) | copy-start | bytes 2752516
  5.4 0.8 %copy-start.12 = (f32[16,896]{1,0:T(8,128)S(1)}, f32[16,896]{1,0:T(8,128)}, u32[]{:S(2)}) copy-start(f32[16,896]{1,0:T(8,128)} %refs_4_.7) | copy-start | bytes 172036
  6.2 0.7 %copy-start.19 = (s32[32]{0:T(128)S(1)}, s32[32]{0:T(128)}, u32[]{:S(2)}) copy-start(s32[32]{0:T(128)} %cutoffs.1) | copy-start | bytes 388
  6.2 15.2 %copy-start.8 = (bf16[2688,256]{1,0:T(8,128)(2,1)S(1)}, bf16[2688,256]{1,0:T(8,128)(2,1)}, u32[]{:S(2)}) copy-start(bf16[2688,256]{1,0:T(8,128)(2,1)} %constant.20.clone.refs_9_.refs_11_) | copy-start | bytes 4128772
  6.2 15.2 %copy-start.10 = (bf16[768,256]{1,0:T(8,128)(2,1)S(1)}, bf16[768,256]{1,0:T(8,128)(2,1)}, u32[]{:S(2)}) copy-start(bf16[768,256]{1,0:T(8,128)(2,1)} %constant.21.clone.refs_10_.refs_12_) | copy-start | bytes 1179652
  6.2 15.2 %copy-start.11 = (bf16[512,256]{1,0:T(8,128)(2,1)S(1)}, bf16[512,256]{1,0:T(8,128)(2,1)}, u32[]{:S(2)}) copy-start(bf16[512,256]{1,0:T(8,128)(2,1)} %constant.19.clone.refs_8_.refs_10_) | copy-start | bytes 786436
  6.2 15.2 %copy-start.14 = (bf16[768,128]{1,0:T(8,128)(2,1)S(1)}, bf16[768,128]{1,0:T(8,128)(2,1)}, u32[]{:S(2)}) copy-start(bf16[768,128]{1,0:T(8,128)(2,1)} %constant.22.clone.refs_11_.refs_13_) | copy-start | bytes 589828
  6.8 14.6 %copy-start.1 = (f32[16,16,896]{2,1,0:T(8,128)S(1)}, f32[16,16,896]{2,1,0:T(8,128)}, u32[]{:S(2)}) copy-start(f32[16,16,896]{2,1,0:T(8,128)} %refs_0_.11) | copy-start | bytes 2752516
  6.8 14.6 %copy-start.3 = (f32[16,16,896]{2,1,0:T(8,128)S(1)}, f32[16,16,896]{2,1,0:T(8,128)}, u32[]{:S(2)}) copy-start(f32[16,16,896]{2,1,0:T(8,128)} %refs_1_.11) | copy-start | bytes 2752516
  6.8 14.6 %copy-start.5 = (f32[16,16,896]{2,1,0:T(8,128)S(1)}, f32[16,16,896]{2,1,0:T(8,128)}, u32[]{:S(2)}) copy-start(f32[16,16,896]{2,1,0:T(8,128)} %refs_2_.11) | copy-start | bytes 2752516
  6.9 14.6 %copy-start.7 = (f32[16,16,896]{2,1,0:T(8,128)S(1)}, f32[16,16,896]{2,1,0:T(8,128)}, u32[]{:S(2)}) copy-start(f32[16,16,896]{2,1,0:T(8,128)} %refs_3_.11) | copy-start | bytes 2752516
  6.9 14.6 %copy-start.13 = (f32[16,896]{1,0:T(8,128)S(1)}, f32[16,896]{1,0:T(8,128)}, u32[]{:S(2)}) copy-start(f32[16,896]{1,0:T(8,128)} %refs_4_.7) | copy-start | bytes 172036
  6.9 14.6 %copy-start.16 = (f32[64]{0:T(128)S(1)}, f32[64]{0:T(128)}, u32[]{:S(2)}) copy-start(f32[64]{0:T(128)} %constant.26.clone.spin) | copy-start | bytes 772
  6.9 14.6 %copy-start.17 = (f32[64]{0:T(128)S(1)}, f32[64]{0:T(128)}, u32[]{:S(2)}) copy-start(f32[64]{0:T(128)} %constant.25.clone.metric) | copy-start | bytes 772
  11.8 25.6 %collective-permute-start.2 = (f32[200,896]{1,0:T(8,128)S(1)}, f32[200,896]{1,0:T(8,128)S(1)}, u32[]{:S(2)}, u32[]{:S(2)}) collective-permute-start(f32[200,896]{1,0:T(8,128)S(1)} %get-tuple-element.32), channel_id=1, source_target_pairs={{0,4},{4,8},{8,12},{1,5},{5,9},{9,13},{2,6},{6,10},{10,14},{3,7},{... | collective-permute-start | bytes 2150408 | tf_op jit(solution)/shard_map/ppermute | solution.py:592
  16.8 20.7 %collective-permute-start.3 = (f32[200,896]{1,0:T(8,128)S(1)}, f32[200,896]{1,0:T(8,128)S(1)}, u32[]{:S(2)}, u32[]{:S(2)}) collective-permute-start(f32[200,896]{1,0:T(8,128)S(1)} %get-tuple-element.33), channel_id=1, source_target_pairs={{4,0},{8,4},{12,8},{5,1},{9,5},{13,9},{6,2},{10,6},{14,10},{7,3},{... | collective-permute-start | bytes 2150408 | tf_op jit(solution)/shard_map/ppermute | solution.py:593
  18.1 3.3 %collective-permute-start = (f32[48,128]{1,0:T(8,128)S(1)}, f32[48,128]{1,0:T(8,128)S(1)}, u32[]{:S(2)}, u32[]{:S(2)}) collective-permute-start(f32[48,128]{1,0:T(8,128)S(1)} %get-tuple-element.29), channel_id=1, source_target_pairs={{0,1},{1,2},{2,3},{3,0},{4,5},{5,6},{6,7},{7,4},{8,9},{9,10},{10,1... | collective-permute-start | bytes 73736 | tf_op jit(solution)/shard_map/ppermute | solution.py:588
  18.2 3.3 %collective-permute-start.1 = (f32[48,128]{1,0:T(8,128)S(1)}, f32[48,128]{1,0:T(8,128)S(1)}, u32[]{:S(2)}, u32[]{:S(2)}) collective-permute-start(f32[48,128]{1,0:T(8,128)S(1)} %get-tuple-element.30.refs_6_), channel_id=1, source_target_pairs={{0,3},{1,0},{2,1},{3,2},{4,7},{5,4},{6,5},{7,6},{8,11},{9,8},{10,9... | collective-permute-start | bytes 73736 | tf_op jit(solution)/shard_map/ppermute | solution.py:588
  34.1 16.9 %collective-permute-start.9 = (f32[80,128]{1,0:T(8,128)S(1)}, f32[80,128]{1,0:T(8,128)S(1)}, u32[]{:S(2)}, u32[]{:S(2)}) collective-permute-start(f32[80,128]{1,0:T(8,128)S(1)} %get-tuple-element.44), channel_id=1, source_target_pairs={{0,2},{1,3},{2,0},{3,1},{4,6},{5,7},{6,4},{7,5},{8,10},{9,11},{10,... | collective-permute-start | bytes 122888 | tf_op jit(solution)/shard_map/ppermute | solution.py:588
  35.7 15.8 %collective-permute-start.7 = (f32[160,128]{1,0:T(8,128)S(1)}, f32[160,128]{1,0:T(8,128)S(1)}, u32[]{:S(2)}, u32[]{:S(2)}) collective-permute-start(f32[160,128]{1,0:T(8,128)S(1)} %get-tuple-element.42), channel_id=1, source_target_pairs={{0,1},{1,2},{2,3},{3,0},{4,5},{5,6},{6,7},{7,4},{8,9},{9,10},{10,1... | collective-permute-start | bytes 245768 | tf_op jit(solution)/shard_map/ppermute | solution.py:588
  36.1 15.3 %collective-permute-start.8 = (f32[160,128]{1,0:T(8,128)S(1)}, f32[160,128]{1,0:T(8,128)S(1)}, u32[]{:S(2)}, u32[]{:S(2)}) collective-permute-start(f32[160,128]{1,0:T(8,128)S(1)} %get-tuple-element.43), channel_id=1, source_target_pairs={{0,3},{1,0},{2,1},{3,2},{4,7},{5,4},{6,5},{7,6},{8,11},{9,8},{10,9... | collective-permute-start | bytes 245768 | tf_op jit(solution)/shard_map/ppermute | solution.py:588
  37.5 14.0 %copy-start.9 = (bf16[768,896]{1,0:T(8,128)(2,1)S(1)}, bf16[768,896]{1,0:T(8,128)(2,1)}, u32[]{:S(2)}) copy-start(bf16[768,896]{1,0:T(8,128)(2,1)} %constant.24.clone.refs_10_) | copy-start | bytes 4128772
  37.5 14.0 %copy-start.15 = (bf16[128,256]{1,0:T(8,128)(2,1)S(1)}, bf16[128,256]{1,0:T(8,128)(2,1)}, u32[]{:S(2)}) copy-start(bf16[128,256]{1,0:T(8,128)(2,1)} %constant.23.clone.refs_9_) | copy-start | bytes 196612
  49.2 7.8 %collective-permute-start.4 = (f32[96,128]{1,0:T(8,128)S(1)}, f32[96,128]{1,0:T(8,128)S(1)}, u32[]{:S(2)}, u32[]{:S(2)}) collective-permute-start(f32[96,128]{1,0:T(8,128)S(1)} %get-tuple-element.38), channel_id=1, source_target_pairs={{0,1},{1,2},{2,3},{3,0},{4,5},{5,6},{6,7},{7,4},{8,9},{9,10},{10,1... | collective-permute-start | bytes 147464 | tf_op jit(solution)/shard_map/ppermute | solution.py:588
  49.2 7.8 %collective-permute-start.5 = (f32[96,128]{1,0:T(8,128)S(1)}, f32[96,128]{1,0:T(8,128)S(1)}, u32[]{:S(2)}, u32[]{:S(2)}) collective-permute-start(f32[96,128]{1,0:T(8,128)S(1)} %get-tuple-element.39), channel_id=1, source_target_pairs={{0,3},{1,0},{2,1},{3,2},{4,7},{5,4},{6,5},{7,6},{8,11},{9,8},{10,9... | collective-permute-start | bytes 147464 | tf_op jit(solution)/shard_map/ppermute | solution.py:588
  51.0 6.0 %collective-permute-start.6 = (f32[48,128]{1,0:T(8,128)S(1)}, f32[48,128]{1,0:T(8,128)S(1)}, u32[]{:S(2)}, u32[]{:S(2)}) collective-permute-start(f32[48,128]{1,0:T(8,128)S(1)} %get-tuple-element.40), channel_id=1, source_target_pairs={{0,2},{1,3},{2,0},{3,1},{4,6},{5,7},{6,4},{7,5},{8,10},{9,11},{10,... | collective-permute-start | bytes 73736 | tf_op jit(solution)/shard_map/ppermute | solution.py:588

commit v4 on v2

--- a/solution.py
+++ b/solution.py
@@ -19,7 +19,6 @@
 F32 = jnp.float32
 BF16 = jnp.bfloat16
 MESSAGE = 2 * NEAR + FAR
-VMEM_LIMIT = 56 * 1024 * 1024
 
 
 def pivoted(matrix, count):
@@ -132,24 +131,17 @@
     return (owner < quarter) | (owner >= lax.axis_size("lat") - quarter)
 
 
-def pack_kernel(cutoffs, *refs):
+def pack_lon_kernel(cutoffs, *refs):
     fields = refs[:4]
-    mass, nodes, south, north, west, east, waves, edge, own_mass, tails, sems = refs[4:]
+    mass, nodes, _, west, east, waves, edge, own_mass, sems = refs[4:]
     rows, columns = mass.shape
     levels = edge.shape[3]
-    tail = 12 * levels
-    first = start_all(
+    copies = start_all(
         [(mass, own_mass)]
         + [(q.at[:, :, 0:LANES], edge.at[0, f]) for f, q in enumerate(fields)]
         + [(q.at[:, :, columns - LANES : columns], edge.at[1, f]) for f, q in enumerate(fields)],
         sems,
     )
-    strips = []
-    for f, q in enumerate(fields):
-        for j in range(3):
-            into = pl.ds(levels * (3 * f + j), levels)
-            strips += [(q.at[j], south.at[into]), (q.at[rows - 3 + j], north.at[into])]
-    strips = start_all(strips, sems, 9)
 
     lat_count = lax.axis_size("lat")
     lon_count = lax.axis_size("lon")
@@ -168,12 +160,7 @@
     waves[1] = jnp.sin(angle)
     waves[2] = twice * (1.0 / circle)
 
-    wait_all(first)
-    tails[...] = jnp.zeros_like(tails)
-    tails[0, 0:3] = own_mass[0:3]
-    tails[1, 0:3] = own_mass[rows - 3 : rows]
-    into = pl.ds(tail, 8)
-    ends = start_all([(tails.at[0], south.at[into]), (tails.at[1], north.at[into])], sems, 33)
+    wait_all(copies)
     lane = lax.broadcasted_iota(jnp.int32, (levels, LANES), 1)
     west[2 * levels :] = own_mass[:, 0:LANES]
     east[2 * levels :] = pltpu.roll(own_mass[:, columns - LANES : columns], 3, 1)
@@ -189,7 +176,26 @@
                         tile = pltpu.roll(tile, turn, 1)
                     total = jnp.where((lane >= lead) & (lane < lead + 3), tile, total)
             out[parity * levels : (parity + 1) * levels] = total
-    wait_all(strips + ends)
+
+
+def pack_lat_kernel(*refs):
+    fields = refs[:4]
+    mass, south, north, own_mass, sems = refs[4:]
+    rows, columns = mass.shape
+    levels = fields[0].shape[1]
+    tail = 12 * levels
+    mass_copy = start_all([(mass, own_mass)], sems)
+    pairs = []
+    for f, q in enumerate(fields):
+        for strip, first in ((south, 0), (north, rows - 3)):
+            for j in range(3):
+                pairs.append((q.at[first + j], strip.at[pl.ds(levels * (3 * f + j), levels)]))
+    copies = start_all(pairs, sems, 1)
+    wait_all(mass_copy)
+    for strip, first in ((south, 0), (north, rows - 3)):
+        strip[tail : tail + 3] = own_mass[first : first + 3]
+        strip[tail + 3 : tail + 8] = jnp.zeros((5, columns), F32)
+    wait_all(copies)
 
 
 def stencil(center, plus, minus):
@@ -200,7 +206,7 @@
     return slope, smooth
 
 
-def mass_slopes(mass, west, east, mass_ext, mass_x, mass_y, levels, edge_rows):
+def mass_slopes(mass, west, east, south, north, mass_x, mass_y, levels):
     rows, columns = mass.shape
     middle = mass[...]
     per_mass = 1.0 / (60.0 * middle)
@@ -216,11 +222,7 @@
         out[...] = jnp.broadcast_to(value[:, None, :], out.shape)
 
     store(mass_x, stencil(middle, [at(1), at(2), at(3)], [at(-1), at(-2), at(-3)])[0] * per_mass)
-    if edge_rows:
-        tall = jnp.concatenate([mass_ext[0:3], middle, mass_ext[8:11]], axis=0)
-    else:
-        blank = jnp.zeros((3, columns), F32)
-        tall = jnp.concatenate([blank, middle, blank], axis=0)
+    tall = jnp.concatenate([south, middle, north], axis=0)
     plus = [tall[3 + k : 3 + k + rows] for k in (1, 2, 3)]
     minus = [tall[3 - k : 3 - k + rows] for k in (1, 2, 3)]
     store(mass_y, stencil(middle, plus, minus)[0] * per_mass)
@@ -248,59 +250,36 @@
         return taken
 
     fields = some(4)
-    mass_in, west_in, east_in, waves_in = some(4)
+    mass, west, east, waves = some(4)
     south, north = some(2) if edge_rows else (None, None)
-    band_in, spread_in, own_in, send_in = some(4)
+    band, spread, own, send = some(4)
     if edge_rows:
         some(4)
     outs = some(4)
     local, to_east, to_west, to_far = some(4)
-    ext, high, low, cross, new, kept_high, kept_low = some(7)
-    mass, mass_ext, mass_x, mass_y, west, east, waves = some(7)
-    band, spread, own, send, sems = some(5)
+    high, low, cross, new, kept_high, kept_low, mass_x, mass_y, sems = some(9)
     rows, columns = mass.shape
-    levels = ext.shape[2]
+    levels = fields[0].shape[1]
     items = count * levels
     tiles = columns // LANES
 
-    pairs = [(west_in, west), (east_in, east), (mass_in, mass), (band_in, band)]
-    for f in range(4):
-        if edge_rows:
-            pairs += [
-                (fields[f].at[0:6], ext.at[f, 3:9]),
-                (fields[f].at[rows - 6 : rows], ext.at[f, 9:15]),
-            ]
-            for j in range(3):
-                part = pl.ds(levels * (3 * f + j), levels)
-                pairs += [(south.at[part], ext.at[f, j]), (north.at[part], ext.at[f, 15 + j])]
-        else:
-            pairs += [(fields[f], ext.at[f])]
+    tail = 12 * levels
     if edge_rows:
-        part = pl.ds(12 * levels, 8)
-        pairs += [(south.at[part], mass_ext.at[0:8]), (north.at[part], mass_ext.at[8:16])]
-    first = start_all(pairs, sems)
-    later = start_all(
-        [(waves_in, waves), (spread_in, spread), (own_in, own), (send_in, send)], sems, len(pairs)
-    )
-    wait_all(first)
-
-    mass_slopes(mass, west, east, mass_ext, mass_x, mass_y, levels, edge_rows)
+        mass_slopes(mass, west, east, south[tail : tail + 3], north[tail : tail + 3], mass_x, mass_y, levels)
+    else:
+        blank = jnp.zeros((3, columns), F32)
+        mass_slopes(mass, west, east, blank, blank, mass_x, mass_y, levels)
     lane = lax.broadcasted_iota(jnp.int32, (levels, LANES), 1)
 
-    def where(i):
-        if edge_rows:
-            return i + (rows - 6) * (i // 3), i + 3 + 6 * (i // 3)
-        return i + 3, i + 3
-
     def cut(i, carry):
-        row, at = where(i)
+        row = i + (rows - 6) * (i // 3) if edge_rows else i + 3
         halo = pl.ds(pl.multiple_of((row % 2) * levels, levels), levels)
         for f in range(4):
             lead = 16 * (row // 2) + 3 * f
             before = pltpu.roll(west[halo, :], lax.rem(LANES - lead, LANES), 1)
             for t in range(tiles + 1):
                 if t < tiles:
-                    tile = pltpu.roll(ext[f, at, :, t * LANES : (t + 1) * LANES], 3, 1)
+                    tile = pltpu.roll(fields[f][row, :, t * LANES : (t + 1) * LANES], 3, 1)
                 else:
                     tile = pltpu.roll(east[halo, :], lax.rem(LANES + 3 - lead, LANES), 1)
                 whole = jnp.where(lane < 3, before, tile)
@@ -325,49 +304,75 @@
     def whole(lines):
         return jnp.concatenate([lines] * (levels // 8), axis=0)
 
-    def tendency(i, t):
-        row, at = where(i)
+    def tendency(t, first, first_row, size, row_of, emit):
         span = slice(t * LANES, (t + 1) * LANES)
-        metric_row = metric[start_row + row]
-        spin_row = spin[start_row + row]
-        along = metric_row * (1.0 / 60.0)
-        u = ext[0, at, :, span]
-        v = ext[1, at, :, span]
-        theta = ext[2, at, :, span]
-        u_fast = u * along
-        u_size = jnp.abs(u_fast)
-        v_fast = v * (1.0 / 60.0)
-        v_size = jnp.abs(v_fast)
-        result = [None] * 4
+        metrics = [metric[start_row + first_row + j] for j in range(size)]
+        spins = [spin[start_row + first_row + j] for j in range(size)]
+        centers = [[row_of(f, j, span) for j in range(size)] for f in range(3)]
+        fast, fast_size, up, up_size = [], [], [], []
+        for j in range(size):
+            fast.append(centers[0][j] * (metrics[j] * (1.0 / 60.0)))
+            fast_size.append(jnp.abs(fast[j]))
+            up.append(centers[1][j] * (1.0 / 60.0))
+            up_size.append(jnp.abs(up[j]))
+        push_x, push_y = [None] * size, [None] * size
         for f in (3, 0, 1, 2):
-            slope_x = cross[t, f, i, :, :LANES]
-            smooth_x = cross[t, f, i, :, LANES:]
-            slope_y, smooth_y = stencil(
-                ext[f, at, :, span],
-                [ext[f, at + k, :, span] for k in (1, 2, 3)],
-                [ext[f, at - k, :, span] for k in (1, 2, 3)],
-            )
-            change = (u_size * smooth_x - u_fast * slope_x) + (v_size * smooth_y - v_fast * slope_y)
-            if f == 3:
-                push_x = along * slope_x + theta * (metric_row * whole(mass_x[row, :, span]))
-                push_y = (1.0 / 60.0) * slope_y + theta * whole(mass_y[row, :, span])
-            elif f == 0:
-                change = change + (spin_row * v - push_x)
-            elif f == 1:
-                change = change - (spin_row * u + push_y)
-            result[f] = change
-        return result, at, span
+            column = [row_of(f, j, span) for j in range(-3, size + 3)]
+            for j in range(size):
+                q = column[j + 3]
+                slope_x = cross[t, f, first + j, :, :LANES]
+                smooth_x = cross[t, f, first + j, :, LANES:]
+                slope_y, smooth_y = stencil(q, column[j + 4 : j + 7], column[j + 2 :: -1][:3])
+                change = (fast_size[j] * smooth_x - fast[j] * slope_x) + (
+                    up_size[j] * smooth_y - up[j] * slope_y
+                )
+                if f == 3:
+                    theta = centers[2][j]
+                    over_x = whole(mass_x[first_row + j, :, span])
+                    over_y = whole(mass_y[first_row + j, :, span])
+                    push_x[j] = metrics[j] * ((1.0 / 60.0) * slope_x + theta * over_x)
+                    push_y[j] = (1.0 / 60.0) * slope_y + theta * over_y
+                elif f == 0:
+                    change = change + (spins[j] * centers[1][j] - push_x[j])
+                elif f == 1:
+                    change = change - (spins[j] * centers[0][j] + push_y[j])
+                emit(f, first + j, span, q, change)
+
+    def all_rows(emit):
+        if edge_rows:
+            for side in range(2):
+                first_row = (rows - 3) * side
+
+                def row_of(f, j, span):
+                    row = first_row + j
+                    if row < 0:
+                        return south[levels * (3 * f + row + 3) : levels * (3 * f + row + 4), span]
+                    if row >= rows:
+                        return north[levels * (3 * f + row - rows) : levels * (3 * f + row - rows + 1), span]
+                    return fields[f][row, :, span]
+
+                for t in range(tiles):
+                    tendency(t, 3 * side, first_row, 3, row_of, emit)
+        else:
+
+            def step(n, carry):
+                first_row = 3 + 2 * n
+
+                def row_of(f, j, span):
+                    return fields[f][first_row + j, :, span]
+
+                for t in range(tiles):
+                    tendency(t, 2 * n, first_row, 2, row_of, emit)
+                return carry
+
+            lax.fori_loop(0, count // 2, step, 0)
 
     @pl.when(jnp.logical_not(is_polar()))
     def _():
-        def step(i, carry):
-            for t in range(tiles):
-                change, at, span = tendency(i, t)
-                for f in range(4):
-                    new[f, i, :, span] = ext[f, at, :, span] + STEP * change[f]
-            return carry
-
-        lax.fori_loop(0, count, step, 0)
+        def emit(f, i, span, q, change):
+            new[f, i, :, span] = q + STEP * change
+
+        all_rows(emit)
         pairs = []
         for f in range(4):
             if edge_rows:
@@ -377,23 +382,16 @@
                 ]
             else:
                 pairs += [(new.at[f], outs[f].at[3 : rows - 3])]
-        writes = start_all(pairs, sems)
-        wait_all(later)
-        wait_all(writes)
+        wait_all(start_all(pairs, sems))
 
     @pl.when(is_polar())
     def _():
-        def step(i, carry):
-            for t in range(tiles):
-                change, _, span = tendency(i, t)
-                for f in range(4):
-                    top = change[f].astype(BF16)
-                    kept_high[f, i, :, span] = top
-                    kept_low[f, i, :, span] = (change[f] - top.astype(F32)).astype(BF16)
-            return carry
-
-        lax.fori_loop(0, count, step, 0)
-        wait_all(later)
+        def emit(f, i, span, q, change):
+            top = change.astype(BF16)
+            kept_high[f, i, :, span] = top
+            kept_low[f, i, :, span] = (change - top.astype(F32)).astype(BF16)
+
+        all_rows(emit)
         c_all, s_all, d_all = [
             spread_rows(own_waves(waves, part, edge_rows), count, levels) for part in range(3)
         ]
@@ -433,38 +431,15 @@
 
 def finish_kernel(edge_rows, count, *refs):
     fields = refs[:4]
-    from_west_in, from_east_in, from_far_in, local_in, waves_in, take_in, gather_in = refs[4:11]
+    from_west, from_east, from_far, local, waves, take, gather = refs[4:11]
     outs = refs[15:19]
-    old, new, from_west, from_east, from_far, local, waves, take, gather, sems = refs[19:]
+    new, sems = refs[19:]
     rows = fields[0].shape[0]
-    levels, columns = old.shape[2], old.shape[3]
+    levels, columns = new.shape[2], new.shape[3]
     items = count * levels
 
     @pl.when(is_polar())
     def _():
-        first = start_all(
-            [
-                (from_west_in, from_west),
-                (from_east_in, from_east),
-                (from_far_in, from_far),
-                (waves_in, waves),
-                (take_in, take),
-                (local_in, local),
-            ],
-            sems,
-        )
-        reads, pairs = [(gather_in, gather)], []
-        for f in range(4):
-            if edge_rows:
-                parts = [((0, 3), (0, 3)), ((3, 6), (rows - 3, rows))]
-            else:
-                parts = [((0, count), (3, rows - 3))]
-            for (a, b), (c, d) in parts:
-                reads.append((fields[f].at[c:d], old.at[f, a:b]))
-                pairs.append((new.at[f, a:b], outs[f].at[c:d]))
-        reads = start_all(reads, sems, 6)
-        wait_all(first)
-
         place = lax.axis_index("lon")
         last = lax.axis_size("lon") - 1
         near_west = from_west[...] * jnp.where(place == 0, -1.0, 1.0)
@@ -490,17 +465,30 @@
         c_all, s_all = [
             spread_rows(own_waves(waves, part, edge_rows), count, levels) for part in range(2)
         ]
-        value = []
-        for f in range(4):
-            at = 2 * f * items
-            value.append(
-                local[f] + (s_all * moved[at : at + items] - c_all * moved[at + items : at + 2 * items])
-            )
-        value = split(jnp.concatenate(value, axis=0))
-        wait_all(reads)
-        change = dot(value, gather[...])
-        new[...] = old[...] + change.reshape(4, count, levels, columns)
-        wait_all(start_all(pairs, sems))
+        writes = []
+        for half in range(2):
+            value = []
+            for f in (2 * half, 2 * half + 1):
+                at = 2 * f * items
+                value.append(
+                    local[f] + (s_all * moved[at : at + items] - c_all * moved[at + items : at + 2 * items])
+                )
+            change = dot(split(jnp.concatenate(value, axis=0)), gather[...])
+            change = change.reshape(2, count, levels, columns)
+            pairs = []
+            for f in (2 * half, 2 * half + 1):
+                if edge_rows:
+                    new[f, 0:3] = fields[f][0:3] + change[f % 2, 0:3]
+                    new[f, 3:6] = fields[f][rows - 3 : rows] + change[f % 2, 3:6]
+                    pairs += [
+                        (new.at[f, 0:3], outs[f].at[0:3]),
+                        (new.at[f, 3:6], outs[f].at[rows - 3 : rows]),
+                    ]
+                else:
+                    new[f] = fields[f][3 : rows - 3] + change[f % 2]
+                    pairs += [(new.at[f], outs[f].at[3 : rows - 3])]
+            writes += start_all(pairs, sems, 4 * half)
+        wait_all(writes)
 
 
 def vmem():
@@ -519,12 +507,8 @@
     return jax.ShapeDtypeStruct(shape, F32)
 
 
-def held(value):
-    return pltpu.VMEM(value.shape, value.dtype)
-
-
-def params():
-    return pltpu.CompilerParams(vmem_limit_bytes=VMEM_LIMIT)
+def params(mebibytes):
+    return pltpu.CompilerParams(vmem_limit_bytes=mebibytes * 1024 * 1024)
 
 
 def row_factors(count):
@@ -544,20 +528,29 @@
 
     strip = 12 * levels + 8
     edge_lines = 2 * levels + rows
-    to_south, to_north, to_west, to_east, waves = pl.pallas_call(
-        pack_kernel,
-        out_shape=[like(strip, columns)] * 2 + [like(edge_lines, LANES)] * 2 + [like(3, rows, NODES)],
-        in_specs=[smem()] + [anywhere()] * 5 + [vmem()],
-        out_specs=[anywhere()] * 2 + [vmem()] * 3,
+    far_fields = [pltpu.with_memory_space_constraint(q, pltpu.HBM) for q in (*fields, mass)]
+    to_south, to_north = pl.pallas_call(
+        pack_lat_kernel,
+        out_shape=[like(strip, columns)] * 2,
+        in_specs=[anywhere()] * 5,
+        out_specs=[vmem()] * 2,
+        scratch_shapes=[pltpu.VMEM((rows, columns), F32), pltpu.SemaphoreType.DMA((25,))],
+        compiler_params=params(8),
+        name="pack_lat",
+    )(*far_fields)
+    to_west, to_east, waves = pl.pallas_call(
+        pack_lon_kernel,
+        out_shape=[like(edge_lines, LANES)] * 2 + [like(3, rows, NODES)],
+        in_specs=[smem()] + [anywhere()] * 5 + [vmem(), anywhere()],
+        out_specs=[vmem()] * 3,
         scratch_shapes=[
             pltpu.VMEM((2, 4, rows, levels, LANES), F32),
             pltpu.VMEM((rows, columns), F32),
-            pltpu.VMEM((2, 8, columns), F32),
-            pltpu.SemaphoreType.DMA((35,)),
+            pltpu.SemaphoreType.DMA((9,)),
         ],
-        compiler_params=params(),
-        name="pack_edges",
-    )(cutoffs, *fields, mass, tables["nodes"])
+        compiler_params=params(8),
+        name="pack_lon",
+    )(cutoffs, *far_fields, tables["nodes"], to_south)
 
     def ring(value, step):
         return lax.ppermute(value, "lon", [(i, (i + step) % lon_count) for i in range(lon_count)])
@@ -570,7 +563,6 @@
     def tendencies(edge_rows, old):
         count = 6 if edge_rows else rows - 6
         items = count * levels
-        deep = 18 if edge_rows else rows
         halos = [south, north] if edge_rows else []
         weights = [tables[k] for k in ("band", "spread", "own", "send")]
         args = [metric, spin, *fields, mass, west, east, waves, *halos, *weights]
@@ -580,28 +572,21 @@
             + [like(4, items, NODES)]
             + [like(items, LANES)] * 2
             + [like(items // 2, LANES)],
-            in_specs=[smem()] * 2 + [anywhere()] * (len(args) - 2 + len(old)),
+            in_specs=[smem()] * 2 + [vmem()] * (len(args) - 2) + [anywhere()] * len(old),
             out_specs=[anywhere()] * 4 + [vmem()] * 4,
             scratch_shapes=[
-                pltpu.VMEM((4, deep, levels, columns), F32),
                 pltpu.VMEM((4, count, levels, columns + LANES), BF16),
                 pltpu.VMEM((4, count, levels, columns + LANES), BF16),
                 pltpu.VMEM((columns // LANES, 4, count, levels, 2 * LANES), F32),
                 pltpu.VMEM((4, count, levels, columns), F32),
                 pltpu.VMEM((4, count, levels, columns), BF16),
                 pltpu.VMEM((4, count, levels, columns), BF16),
-                pltpu.VMEM((rows, columns), F32),
-                pltpu.VMEM((16, columns), F32),
                 pltpu.VMEM((rows, 8, columns), F32),
                 pltpu.VMEM((rows, 8, columns), F32),
-                pltpu.VMEM((edge_lines, LANES), F32),
-                pltpu.VMEM((edge_lines, LANES), F32),
-                pltpu.VMEM((3, rows, NODES), F32),
-                *[held(w) for w in weights],
-                pltpu.SemaphoreType.DMA((48,)),
+                pltpu.SemaphoreType.DMA((8,)),
             ],
             input_output_aliases={len(args) + f: f for f in range(4)} if old else {},
-            compiler_params=params(),
+            compiler_params=params(36),
             cost_estimate=pl.CostEstimate(
                 flops=items * 4 * columns * 2000, bytes_accessed=8 * items * columns * 4, transcendentals=0
             ),
@@ -619,21 +604,14 @@
         return pl.pallas_call(
             functools.partial(finish_kernel, edge_rows, count),
             out_shape=[like(rows, levels, columns)] * 4,
-            in_specs=[anywhere()] * (len(args) + 4),
+            in_specs=[vmem()] * len(args) + [anywhere()] * 4,
             out_specs=[anywhere()] * 4,
             scratch_shapes=[
                 pltpu.VMEM((4, count, levels, columns), F32),
-                pltpu.VMEM((4, count, levels, columns), F32),
-                pltpu.VMEM((items, LANES), F32),
-                pltpu.VMEM((items, LANES), F32),
-                pltpu.VMEM((items // 2, LANES), F32),
-                pltpu.VMEM((4, items, NODES), F32),
-                pltpu.VMEM((3, rows, NODES), F32),
-                *[held(w) for w in weights],
-                pltpu.SemaphoreType.DMA((16,)),
+                pltpu.SemaphoreType.DMA((8,)),
             ],
             input_output_aliases={len(args) + f: f for f in range(4)},
-            compiler_params=params(),
+            compiler_params=params(24),
             name="finish_edge" if edge_rows else "finish_inner",
         )(*args, *old)
 

time: 97.5 us -> 43.1 us (0.44)
  Pallas kernels: 78.1 us -> 26 us
  local copies, waits for them, and re-layouts: 2.96 us -> 0.09 us
    pallas_call x1 -> x2, Pallas kernels: 44.4 us -> 3.95 us  [the longest x1 2.28 us: shards(): pl.pallas_call(pack_lon_kernel, out_shape=[like(edge_lines, LANES)] * 2 +...]
    pallas_call x2, Pallas kernels: 24.4 us -> 16.8 us  [tendencies(): pl.pallas_call(functools.partial(tend_kernel, edge_rows, count), out_shap...]
    pallas_call x2, Pallas kernels: 9.33 us -> 5.24 us  [finish(): pl.pallas_call(functools.partial(finish_kernel, edge_rows, count), out_sh...]
    unnamed x20 -> x30, local copies, waits for them, and re-layouts: 2.96 us -> 0.09 us
  transfers between devices with their start and end apart: 10 -> 10, of which waited for: 1 -> 2; matrix products, arithmetic and copies ran while one was open for 0% -> 0% of each run, Pallas kernels for 30% -> 52%
where the time goes in v4:
time: 43.1 us; the launch traced here: 42.9 us
  Pallas kernels  26 us (60%)
  starting transfers between devices  14 us (32%)
  waiting for transfers between devices  1.77 us (4%)
  between operations  1.07 us (2%)
    pallas_call x2, Pallas kernels, tendencies(): pl.pallas_call(functools.partial(tend_kernel, edge_rows, count), out_shap...  16.8 us
    ppermute x8, starting transfers between devices, ring(): lax.ppermute(value, 'lon', [(i, (i + step) % lon_count) for i in range(lo...  7.45 us
    pallas_call x2, Pallas kernels, finish(): pl.pallas_call(functools.partial(finish_kernel, edge_rows, count), out_sh...  5.24 us
    ppermute x1, starting transfers between devices, shards(): lax.ppermute(to_north, 'lat', [(i, i + 1) for i in range(lat_count - 1)])  4.97 us
    pallas_call x1, Pallas kernels, shards(): pl.pallas_call(pack_lon_kernel, out_shape=[like(edge_lines, LANES)] * 2 +...  2.28 us
    ppermute x8, waiting for transfers between devices, ring(): lax.ppermute(value, 'lon', [(i, (i + step) % lon_count) for i in range(lo...  1.76 us
    pallas_call x1, Pallas kernels, shards(): pl.pallas_call(pack_lat_kernel, out_shape=[like(strip, columns)] * 2, in_...  1.67 us
    ppermute x1, starting transfers between devices, shards(): lax.ppermute(to_south, 'lat', [(i + 1, i) for i in range(lat_count - 1)])  1.56 us
  transfers between devices with their start and end apart: 10, of which 2 were waited for; matrix products, arithmetic and copies ran while one was open for 0% of the time, Pallas kernels for 52%

profile of v4, /device:TPU:0, one launch (start us, length us, event | category | flops | bytes accessed | tf_op | source)
XLA Modules:
  0.0 42.9 jit_solution(4622801481941281580)
XLA Ops:
  0.6 0.0 copy-start.13
  0.6 0.0 copy-start.14
  0.7 0.0 copy-start.4
  0.7 0.0 copy-start.9
  0.7 1.7 %pack_lat.1 = (f32[200,896]{1,0:T(8,128)S(1)}, f32[200,896]{1,0:T(8,128)S(1)}) custom-call(f32[16,16,896]{2,1,0:T(8,128)} %refs_0_.11, f32[16,16,896]{2,1,0:T(8,128)} %refs_1_.11, f32[16,16,896]{2,1,0:T(8,128)} %refs_2_.11, f32[16,16,896]{2,1,0:T(8,128)} %refs_3_.11, f32[16,896]{1,0:T(8,128)} %refs_4_.7), custom_call_target="tpu_custom_call" | custom-call | tf_op jit(solution)/shard_map/pack_lat/pallas_call | solution.py:532
  2.4 5.0 %collective-permute-start.2 = (f32[200,896]{1,0:T(8,128)S(1)}, f32[200,896]{1,0:T(8,128)S(1)}, u32[]{:S(2)}, u32[]{:S(2)}) collective-permute-start(f32[200,896]{1,0:T(8,128)S(1)} %get-tuple-element.33), channel_id=1, source_target_pairs={{0,4},{4,8},{8,12},{1,5},{5,9},{9,13},{2,6},{6,10},{10,14},{3,7},{... | collective-permute-start | bytes 2150408 | tf_op jit(solution)/shard_map/ppermute | solution.py:560
  7.3 0.0 copy-start
  7.4 0.0 copy-start.1
  7.4 0.0 copy-start.2
  7.4 0.0 copy-start.3
  7.4 0.0 copy-start.6
  7.4 0.0 copy-start.7
  7.4 0.0 copy-start.8
  7.4 0.0 copy-start.11
  7.4 0.0 copy-start.12
  7.4 1.6 %collective-permute-start.3 = (f32[200,896]{1,0:T(8,128)S(1)}, f32[200,896]{1,0:T(8,128)S(1)}, u32[]{:S(2)}, u32[]{:S(2)}) collective-permute-start(f32[200,896]{1,0:T(8,128)S(1)} %get-tuple-element.29.refs_6_), channel_id=1, source_target_pairs={{4,0},{8,4},{12,8},{5,1},{9,5},{13,9},{6,2},{10,6},{14,10},{7,3},{... | collective-permute-start | bytes 2150408 | tf_op jit(solution)/shard_map/ppermute | solution.py:561
  9.0 0.0 copy-done.13
  9.0 0.0 copy-done.14
  9.0 2.3 %pack_lon.1 = (f32[48,128]{1,0:T(8,128)S(1)}, f32[48,128]{1,0:T(8,128)S(1)}, f32[3,16,256]{2,1,0:T(8,128)S(1)}) custom-call(s32[32]{0:T(128)S(1)} %copy-done.14, f32[16,16,896]{2,1,0:T(8,128)} %refs_0_.11, f32[16,16,896]{2,1,0:T(8,128)} %refs_1_.11, f32[16,16,896]{2,1,0:T(8,128)} %refs_2_.11, f32[16,16,896]{2,1,0:T(8,128)} %refs_3_.11, f32[16,896]{1,0:T(8,128)} %refs_4_.7, ...), custom_call_target="tpu_custom_call" | custom-call | tf_op jit(solution)/shard_map/pack_lon/pallas_call | solution.py:541
  11.3 0.1 collective-permute-start
  11.4 1.7 %collective-permute-start.1 = (f32[48,128]{1,0:T(8,128)S(1)}, f32[48,128]{1,0:T(8,128)S(1)}, u32[]{:S(2)}, u32[]{:S(2)}) collective-permute-start(f32[48,128]{1,0:T(8,128)S(1)} %get-tuple-element.31), channel_id=1, source_target_pairs={{0,3},{1,0},{2,1},{3,2},{4,7},{5,4},{6,5},{7,6},{8,11},{9,8},{10,9... | collective-permute-start | bytes 73736 | tf_op jit(solution)/shard_map/ppermute | solution.py:556
  13.1 1.5 %collective-permute-done.refs_5_ = f32[48,128]{1,0:T(8,128)S(1)} collective-permute-done((f32[48,128]{1,0:T(8,128)S(1)}, f32[48,128]{1,0:T(8,128)S(1)}, u32[]{:S(2)}, u32[]{:S(2)}) %collective-permute-start) | collective-permute-done | bytes 24608 | tf_op jit(solution)/shard_map/ppermute | solution.py:556
  14.6 0.0 collective-permute-done.1.refs_6_
  14.6 0.0 copy-done.4
  14.6 0.0 copy-done.9
  14.6 0.0 copy-done
  14.6 0.0 copy-done.1
  14.7 0.0 copy-done.2
  14.7 0.0 copy-done.3
  14.7 0.0 copy-done.6
  14.7 0.0 copy-done.7
  14.7 0.0 copy-done.8
  14.7 0.0 copy-done.11
  14.7 0.0 copy-done.12
  14.7 10.4 %tend_inner.1 = (f32[16,16,896]{2,1,0:T(8,128)}, f32[16,16,896]{2,1,0:T(8,128)}, f32[16,16,896]{2,1,0:T(8,128)}, f32[16,16,896]{2,1,0:T(8,128)}, f32[4,160,256]{...) custom-call(f32[64]{0:T(128)S(1)} %copy-done.12, f32[64]{0:T(128)S(1)} %copy-done.11, ...), custom_call_target="tpu_custom_call" | custom-call | flops 1146880000 | bytes 4587520 | tf_op jit(solution)/shard_map/tend_inner/pallas_call | solution.py:569
  25.1 1.6 %collective-permute-start.9 = (f32[80,128]{1,0:T(8,128)S(1)}, f32[80,128]{1,0:T(8,128)S(1)}, u32[]{:S(2)}, u32[]{:S(2)}) collective-permute-start(f32[80,128]{1,0:T(8,128)S(1)} %get-tuple-element.44), channel_id=1, source_target_pairs={{0,2},{1,3},{2,0},{3,1},{4,6},{5,7},{6,4},{7,5},{8,10},{9,11},{10,... | collective-permute-start | bytes 122888 | tf_op jit(solution)/shard_map/ppermute | solution.py:556
  26.6 0.7 %collective-permute-start.7 = (f32[160,128]{1,0:T(8,128)S(1)}, f32[160,128]{1,0:T(8,128)S(1)}, u32[]{:S(2)}, u32[]{:S(2)}) collective-permute-start(f32[160,128]{1,0:T(8,128)S(1)} %get-tuple-element.42), channel_id=1, source_target_pairs={{0,1},{1,2},{2,3},{3,0},{4,5},{5,6},{6,7},{7,4},{8,9},{9,10},{10,1... | collective-permute-start | bytes 245768 | tf_op jit(solution)/shard_map/ppermute | solution.py:556
  27.3 1.1 %collective-permute-start.8 = (f32[160,128]{1,0:T(8,128)S(1)}, f32[160,128]{1,0:T(8,128)S(1)}, u32[]{:S(2)}, u32[]{:S(2)}) collective-permute-start(f32[160,128]{1,0:T(8,128)S(1)} %get-tuple-element.43), channel_id=1, source_target_pairs={{0,3},{1,0},{2,1},{3,2},{4,7},{5,4},{6,5},{7,6},{8,11},{9,8},{10,9... | collective-permute-start | bytes 245768 | tf_op jit(solution)/shard_map/ppermute | solution.py:556
  28.4 0.0 collective-permute-done.2.refs_8_
  28.4 0.0 collective-permute-done.3.refs_9_
  28.4 0.0 copy-start.5
  28.4 0.0 copy-start.10
  28.5 6.4 %tend_edge.1 = (f32[16,16,896]{2,1,0:T(8,128)}, f32[16,16,896]{2,1,0:T(8,128)}, f32[16,16,896]{2,1,0:T(8,128)}, f32[16,16,896]{2,1,0:T(8,128)}, f32[4,96,256]{2,...) custom-call(f32[64]{0:T(128)S(1)} %copy-done.12, ...), custom_call_target="tpu_custom_call", output_to_operand_aliasing={{0}: (16, {}), {1}: (17, {}), {2}: (18, {}), {3}: (19, {})} | custom-call | flops 688128000 | bytes 2752512 | tf_op jit(solution)/shard_map/tend_edge/pallas_call | solution.py:569
  34.9 0.1 collective-permute-start.4
  35.0 1.7 %collective-permute-start.5 = (f32[96,128]{1,0:T(8,128)S(1)}, f32[96,128]{1,0:T(8,128)S(1)}, u32[]{:S(2)}, u32[]{:S(2)}) collective-permute-start(f32[96,128]{1,0:T(8,128)S(1)} %get-tuple-element.39), channel_id=1, source_target_pairs={{0,3},{1,0},{2,1},{3,2},{4,7},{5,4},{6,5},{7,6},{8,11},{9,8},{10,9... | collective-permute-start | bytes 147464 | tf_op jit(solution)/shard_map/ppermute | solution.py:556
  36.7 0.0 collective-permute-done.9.refs_6_
  36.7 0.5 %collective-permute-start.6 = (f32[48,128]{1,0:T(8,128)S(1)}, f32[48,128]{1,0:T(8,128)S(1)}, u32[]{:S(2)}, u32[]{:S(2)}) collective-permute-start(f32[48,128]{1,0:T(8,128)S(1)} %get-tuple-element.40), channel_id=1, source_target_pairs={{0,2},{1,3},{2,0},{3,1},{4,6},{5,7},{6,4},{7,5},{8,10},{9,11},{10,... | collective-permute-start | bytes 73736 | tf_op jit(solution)/shard_map/ppermute | solution.py:556
  37.2 0.0 collective-permute-done.7.refs_4_
  37.2 0.0 collective-permute-done.8.refs_5_
  37.2 0.0 copy-done.5
  37.3 0.0 copy-done.10
  37.3 3.0 %finish_inner.1 = (f32[16,16,896]{2,1,0:T(8,128)}, f32[16,16,896]{2,1,0:T(8,128)}, f32[16,16,896]{2,1,0:T(8,128)}, f32[16,16,896]{2,1,0:T(8,128)}) custom-call(f32[16,16,896]{2,1,0:T(8,128)S(1)} %copy-done, f32[16,16,896]{2,1,0:T(8,128)S(1)} %copy-done.1, ...), custom_call_target="tpu_custom_call", output_to_operand_aliasing={{0}: (11, {}), {1}: (12, {}), {2}: (13, {}), {3}: (14, {})} | custom-call | tf_op jit(solution)/shard_map/finish_inner/pallas_call | solution.py:604
  40.3 0.2 collective-permute-done.6.refs_6_
  40.5 0.0 collective-permute-done.4.refs_4_
  40.5 0.0 collective-permute-done.5.refs_5_
  40.5 2.2 %finish_edge.1 = (f32[16,16,896]{2,1,0:T(8,128)}, f32[16,16,896]{2,1,0:T(8,128)}, f32[16,16,896]{2,1,0:T(8,128)}, f32[16,16,896]{2,1,0:T(8,128)}) custom-call(f32[16,16,896]{2,1,0:T(8,128)S(1)} %copy-done, f32[16,16,896]{2,1,0:T(8,128)S(1)} %copy-done.1, ...), custom_call_target="tpu_custom_call", output_to_operand_aliasing={{0}: (11, {}), {1}: (12, {}), {2}: (13, {}), {3}: (14, {})} | custom-call | tf_op jit(solution)/shard_map/finish_edge/pallas_call | solution.py:604
Async XLA Ops:
  0.6 8.4 %copy-start.13 = (f32[1,256]{1,0:T(1,128)S(1)}, f32[1,256]{1,0:T(1,128)}, u32[]{:S(2)}) copy-start(f32[1,256]{1,0:T(1,128)} %constant.18.clone.refs_5_) | copy-start | bytes 3076
  0.6 8.4 %copy-start.14 = (s32[32]{0:T(128)S(1)}, s32[32]{0:T(128)}, u32[]{:S(2)}) copy-start(s32[32]{0:T(128)} %cutoffs.1) | copy-start | bytes 388
  0.7 14.0 %copy-start.4 = (bf16[2688,256]{1,0:T(8,128)(2,1)S(1)}, bf16[2688,256]{1,0:T(8,128)(2,1)}, u32[]{:S(2)}) copy-start(bf16[2688,256]{1,0:T(8,128)(2,1)} %constant.20.clone.refs_9_.refs_11_) | copy-start | bytes 4128772
  0.7 14.0 %copy-start.9 = (bf16[768,128]{1,0:T(8,128)(2,1)S(1)}, bf16[768,128]{1,0:T(8,128)(2,1)}, u32[]{:S(2)}) copy-start(bf16[768,128]{1,0:T(8,128)(2,1)} %constant.22.clone.refs_11_.refs_13_) | copy-start | bytes 589828
  2.4 26.1 %collective-permute-start.2 = (f32[200,896]{1,0:T(8,128)S(1)}, f32[200,896]{1,0:T(8,128)S(1)}, u32[]{:S(2)}, u32[]{:S(2)}) collective-permute-start(f32[200,896]{1,0:T(8,128)S(1)} %get-tuple-element.33), channel_id=1, source_target_pairs={{0,4},{4,8},{8,12},{1,5},{5,9},{9,13},{2,6},{6,10},{10,14},{3,7},{... | collective-permute-start | bytes 2150408 | tf_op jit(solution)/shard_map/ppermute | solution.py:560
  7.3 7.3 %copy-start = (f32[16,16,896]{2,1,0:T(8,128)S(1)}, f32[16,16,896]{2,1,0:T(8,128)}, u32[]{:S(2)}) copy-start(f32[16,16,896]{2,1,0:T(8,128)} %refs_0_.11) | copy-start | bytes 2752516
  7.4 7.3 %copy-start.1 = (f32[16,16,896]{2,1,0:T(8,128)S(1)}, f32[16,16,896]{2,1,0:T(8,128)}, u32[]{:S(2)}) copy-start(f32[16,16,896]{2,1,0:T(8,128)} %refs_1_.11) | copy-start | bytes 2752516
  7.4 7.3 %copy-start.2 = (f32[16,16,896]{2,1,0:T(8,128)S(1)}, f32[16,16,896]{2,1,0:T(8,128)}, u32[]{:S(2)}) copy-start(f32[16,16,896]{2,1,0:T(8,128)} %refs_2_.11) | copy-start | bytes 2752516
  7.4 7.3 %copy-start.3 = (f32[16,16,896]{2,1,0:T(8,128)S(1)}, f32[16,16,896]{2,1,0:T(8,128)}, u32[]{:S(2)}) copy-start(f32[16,16,896]{2,1,0:T(8,128)} %refs_3_.11) | copy-start | bytes 2752516
  7.4 7.3 %copy-start.6 = (bf16[768,256]{1,0:T(8,128)(2,1)S(1)}, bf16[768,256]{1,0:T(8,128)(2,1)}, u32[]{:S(2)}) copy-start(bf16[768,256]{1,0:T(8,128)(2,1)} %constant.21.clone.refs_10_.refs_12_) | copy-start | bytes 1179652
  7.4 7.3 %copy-start.7 = (bf16[512,256]{1,0:T(8,128)(2,1)S(1)}, bf16[512,256]{1,0:T(8,128)(2,1)}, u32[]{:S(2)}) copy-start(bf16[512,256]{1,0:T(8,128)(2,1)} %constant.19.clone.refs_8_.refs_10_) | copy-start | bytes 786436
  7.4 7.3 %copy-start.8 = (f32[16,896]{1,0:T(8,128)S(1)}, f32[16,896]{1,0:T(8,128)}, u32[]{:S(2)}) copy-start(f32[16,896]{1,0:T(8,128)} %refs_4_.7) | copy-start | bytes 172036
  7.4 7.3 %copy-start.11 = (f32[64]{0:T(128)S(1)}, f32[64]{0:T(128)}, u32[]{:S(2)}) copy-start(f32[64]{0:T(128)} %constant.26.clone.spin) | copy-start | bytes 772
  7.4 7.3 %copy-start.12 = (f32[64]{0:T(128)S(1)}, f32[64]{0:T(128)}, u32[]{:S(2)}) copy-start(f32[64]{0:T(128)} %constant.25.clone.metric) | copy-start | bytes 772
  7.4 21.0 %collective-permute-start.3 = (f32[200,896]{1,0:T(8,128)S(1)}, f32[200,896]{1,0:T(8,128)S(1)}, u32[]{:S(2)}, u32[]{:S(2)}) collective-permute-start(f32[200,896]{1,0:T(8,128)S(1)} %get-tuple-element.29.refs_6_), channel_id=1, source_target_pairs={{4,0},{8,4},{12,8},{5,1},{9,5},{13,9},{6,2},{10,6},{14,10},{7,3},{... | collective-permute-start | bytes 2150408 | tf_op jit(solution)/shard_map/ppermute | solution.py:561
  11.3 3.3 %collective-permute-start = (f32[48,128]{1,0:T(8,128)S(1)}, f32[48,128]{1,0:T(8,128)S(1)}, u32[]{:S(2)}, u32[]{:S(2)}) collective-permute-start(f32[48,128]{1,0:T(8,128)S(1)} %get-tuple-element.30), channel_id=1, source_target_pairs={{0,1},{1,2},{2,3},{3,0},{4,5},{5,6},{6,7},{7,4},{8,9},{9,10},{10,1... | collective-permute-start | bytes 73736 | tf_op jit(solution)/shard_map/ppermute | solution.py:556
  11.4 3.3 %collective-permute-start.1 = (f32[48,128]{1,0:T(8,128)S(1)}, f32[48,128]{1,0:T(8,128)S(1)}, u32[]{:S(2)}, u32[]{:S(2)}) collective-permute-start(f32[48,128]{1,0:T(8,128)S(1)} %get-tuple-element.31), channel_id=1, source_target_pairs={{0,3},{1,0},{2,1},{3,2},{4,7},{5,4},{6,5},{7,6},{8,11},{9,8},{10,9... | collective-permute-start | bytes 73736 | tf_op jit(solution)/shard_map/ppermute | solution.py:556
  25.1 11.6 %collective-permute-start.9 = (f32[80,128]{1,0:T(8,128)S(1)}, f32[80,128]{1,0:T(8,128)S(1)}, u32[]{:S(2)}, u32[]{:S(2)}) collective-permute-start(f32[80,128]{1,0:T(8,128)S(1)} %get-tuple-element.44), channel_id=1, source_target_pairs={{0,2},{1,3},{2,0},{3,1},{4,6},{5,7},{6,4},{7,5},{8,10},{9,11},{10,... | collective-permute-start | bytes 122888 | tf_op jit(solution)/shard_map/ppermute | solution.py:556
  26.6 10.6 %collective-permute-start.7 = (f32[160,128]{1,0:T(8,128)S(1)}, f32[160,128]{1,0:T(8,128)S(1)}, u32[]{:S(2)}, u32[]{:S(2)}) collective-permute-start(f32[160,128]{1,0:T(8,128)S(1)} %get-tuple-element.42), channel_id=1, source_target_pairs={{0,1},{1,2},{2,3},{3,0},{4,5},{5,6},{6,7},{7,4},{8,9},{9,10},{10,1... | collective-permute-start | bytes 245768 | tf_op jit(solution)/shard_map/ppermute | solution.py:556
  27.3 9.9 %collective-permute-start.8 = (f32[160,128]{1,0:T(8,128)S(1)}, f32[160,128]{1,0:T(8,128)S(1)}, u32[]{:S(2)}, u32[]{:S(2)}) collective-permute-start(f32[160,128]{1,0:T(8,128)S(1)} %get-tuple-element.43), channel_id=1, source_target_pairs={{0,3},{1,0},{2,1},{3,2},{4,7},{5,4},{6,5},{7,6},{8,11},{9,8},{10,9... | collective-permute-start | bytes 245768 | tf_op jit(solution)/shard_map/ppermute | solution.py:556
  28.4 8.8 %copy-start.5 = (bf16[768,896]{1,0:T(8,128)(2,1)S(1)}, bf16[768,896]{1,0:T(8,128)(2,1)}, u32[]{:S(2)}) copy-start(bf16[768,896]{1,0:T(8,128)(2,1)} %constant.24.clone.refs_10_) | copy-start | bytes 4128772
  28.4 8.8 %copy-start.10 = (bf16[128,256]{1,0:T(8,128)(2,1)S(1)}, bf16[128,256]{1,0:T(8,128)(2,1)}, u32[]{:S(2)}) copy-start(bf16[128,256]{1,0:T(8,128)(2,1)} %constant.23.clone.refs_9_) | copy-start | bytes 196612
  34.9 5.6 %collective-permute-start.4 = (f32[96,128]{1,0:T(8,128)S(1)}, f32[96,128]{1,0:T(8,128)S(1)}, u32[]{:S(2)}, u32[]{:S(2)}) collective-permute-start(f32[96,128]{1,0:T(8,128)S(1)} %get-tuple-element.38), channel_id=1, source_target_pairs={{0,1},{1,2},{2,3},{3,0},{4,5},{5,6},{6,7},{7,4},{8,9},{9,10},{10,1... | collective-permute-start | bytes 147464 | tf_op jit(solution)/shard_map/ppermute | solution.py:556
  35.0 5.6 %collective-permute-start.5 = (f32[96,128]{1,0:T(8,128)S(1)}, f32[96,128]{1,0:T(8,128)S(1)}, u32[]{:S(2)}, u32[]{:S(2)}) collective-permute-start(f32[96,128]{1,0:T(8,128)S(1)} %get-tuple-element.39), channel_id=1, source_target_pairs={{0,3},{1,0},{2,1},{3,2},{4,7},{5,4},{6,5},{7,6},{8,11},{9,8},{10,9... | collective-permute-start | bytes 147464 | tf_op jit(solution)/shard_map/ppermute | solution.py:556
  36.7 3.8 %collective-permute-start.6 = (f32[48,128]{1,0:T(8,128)S(1)}, f32[48,128]{1,0:T(8,128)S(1)}, u32[]{:S(2)}, u32[]{:S(2)}) collective-permute-start(f32[48,128]{1,0:T(8,128)S(1)} %get-tuple-element.40), channel_id=1, source_target_pairs={{0,2},{1,3},{2,0},{3,1},{4,6},{5,7},{6,4},{7,5},{8,10},{9,11},{10,... | collective-permute-start | bytes 73736 | tf_op jit(solution)/shard_map/ppermute | solution.py:556

commit v5 on v4

--- a/solution.py
+++ b/solution.py
@@ -131,17 +131,34 @@
     return (owner < quarter) | (owner >= lax.axis_size("lat") - quarter)
 
 
-def pack_lon_kernel(cutoffs, *refs):
+def edge_row(entry, rows):
+    north = (lax.axis_index("lat") % 2 == 0) == (entry < 3)
+    return jnp.where(north, rows - 1 - entry % 3, entry % 3)
+
+
+def by_parity(even, odd):
+    return jnp.where(lax.axis_index("lat") % 2 == 0, even, odd)
+
+
+def pack_kernel(cutoffs, *refs):
     fields = refs[:4]
-    mass, nodes, _, west, east, waves, edge, own_mass, sems = refs[4:]
+    mass, nodes, strip_a, strip_b, west, east, waves, edge, own_mass, sems = refs[4:]
     rows, columns = mass.shape
     levels = edge.shape[3]
-    copies = start_all(
+    tail = 12 * levels
+    small = start_all(
         [(mass, own_mass)]
         + [(q.at[:, :, 0:LANES], edge.at[0, f]) for f, q in enumerate(fields)]
         + [(q.at[:, :, columns - LANES : columns], edge.at[1, f]) for f, q in enumerate(fields)],
         sems,
     )
+    pairs = []
+    for entry in range(6):
+        strip = strip_a if entry < 3 else strip_b
+        row = edge_row(entry, rows)
+        for f, q in enumerate(fields):
+            pairs.append((q.at[row], strip.at[pl.ds(levels * (3 * f + entry % 3), levels)]))
+    large = start_all(pairs, sems, 9)
 
     lat_count = lax.axis_size("lat")
     lon_count = lax.axis_size("lon")
@@ -156,11 +173,15 @@
     place = nodes[...] + (lax.axis_index("lon") * columns).astype(F32)
     turns = twice * place
     angle = (turns - 2.0 * circle * jnp.floor(turns * (0.5 / circle))) * (math.pi / circle)
-    waves[0] = jnp.cos(angle)
-    waves[1] = jnp.sin(angle)
-    waves[2] = twice * (1.0 / circle)
-
-    wait_all(copies)
+    for part, table in enumerate((jnp.cos(angle), jnp.sin(angle), twice * (1.0 / circle))):
+        waves[part] = jnp.broadcast_to(table[:, None, :], (rows, 8, NODES))
+
+    wait_all(small)
+    north = jnp.concatenate([own_mass[rows - 1 - m : rows - m] for m in range(3)], axis=0)
+    south = own_mass[0:3]
+    for strip, lines in ((strip_a, by_parity(north, south)), (strip_b, by_parity(south, north))):
+        strip[tail : tail + 3] = lines
+        strip[tail + 3 : tail + 8] = jnp.zeros((5, columns), F32)
     lane = lax.broadcasted_iota(jnp.int32, (levels, LANES), 1)
     west[2 * levels :] = own_mass[:, 0:LANES]
     east[2 * levels :] = pltpu.roll(own_mass[:, columns - LANES : columns], 3, 1)
@@ -176,26 +197,7 @@
                         tile = pltpu.roll(tile, turn, 1)
                     total = jnp.where((lane >= lead) & (lane < lead + 3), tile, total)
             out[parity * levels : (parity + 1) * levels] = total
-
-
-def pack_lat_kernel(*refs):
-    fields = refs[:4]
-    mass, south, north, own_mass, sems = refs[4:]
-    rows, columns = mass.shape
-    levels = fields[0].shape[1]
-    tail = 12 * levels
-    mass_copy = start_all([(mass, own_mass)], sems)
-    pairs = []
-    for f, q in enumerate(fields):
-        for strip, first in ((south, 0), (north, rows - 3)):
-            for j in range(3):
-                pairs.append((q.at[first + j], strip.at[pl.ds(levels * (3 * f + j), levels)]))
-    copies = start_all(pairs, sems, 1)
-    wait_all(mass_copy)
-    for strip, first in ((south, 0), (north, rows - 3)):
-        strip[tail : tail + 3] = own_mass[first : first + 3]
-        strip[tail + 3 : tail + 8] = jnp.zeros((5, columns), F32)
-    wait_all(copies)
+    wait_all(large)
 
 
 def stencil(center, plus, minus):
@@ -228,17 +230,13 @@
     store(mass_y, stencil(middle, plus, minus)[0] * per_mass)
 
 
-def spread_rows(table, count, levels):
-    wide = jnp.broadcast_to(table[:, None, :], (count, levels, table.shape[1]))
-    return wide.reshape(count * levels, table.shape[1])
-
-
-def own_waves(waves, part, edge_rows):
-    table = waves[part]
-    rows = table.shape[0]
+def spread_waves(waves, part, edge_rows, levels):
+    rows = waves.shape[1]
     if edge_rows:
-        return jnp.concatenate([table[:3], table[rows - 3 :]], axis=0)
-    return table[3 : rows - 3]
+        numbers = [edge_row(entry, rows) for entry in range(6)]
+    else:
+        numbers = range(3, rows - 3)
+    return jnp.concatenate([waves[part, n] for n in numbers for _ in range(levels // 8)], axis=0)
 
 
 def tend_kernel(edge_rows, count, metric, spin, *refs):
@@ -251,7 +249,7 @@
 
     fields = some(4)
     mass, west, east, waves = some(4)
-    south, north = some(2) if edge_rows else (None, None)
+    strips = some(2) if edge_rows else None
     band, spread, own, send = some(4)
     if edge_rows:
         some(4)
@@ -263,16 +261,19 @@
     items = count * levels
     tiles = columns // LANES
 
-    tail = 12 * levels
     if edge_rows:
-        mass_slopes(mass, west, east, south[tail : tail + 3], north[tail : tail + 3], mass_x, mass_y, levels)
+        tail = 12 * levels
+        lines = [strip[tail : tail + 3] for strip in strips]
+        upper = by_parity(lines[0], lines[1])
+        lower = by_parity(lines[1], lines[0])
+        lower = jnp.concatenate([lower[2:3], lower[1:2], lower[0:1]], axis=0)
     else:
-        blank = jnp.zeros((3, columns), F32)
-        mass_slopes(mass, west, east, blank, blank, mass_x, mass_y, levels)
+        lower = upper = jnp.zeros((3, columns), F32)
+    mass_slopes(mass, west, east, lower, upper, mass_x, mass_y, levels)
     lane = lax.broadcasted_iota(jnp.int32, (levels, LANES), 1)
 
     def cut(i, carry):
-        row = i + (rows - 6) * (i // 3) if edge_rows else i + 3
+        row = edge_row(i, rows) if edge_rows else i + 3
         halo = pl.ds(pl.multiple_of((row % 2) * levels, levels), levels)
         for f in range(4):
             lead = 16 * (row // 2) + 3 * f
@@ -304,16 +305,18 @@
     def whole(lines):
         return jnp.concatenate([lines] * (levels // 8), axis=0)
 
-    def tendency(t, first, first_row, size, row_of, emit):
+    def tendency(t, first, numbers, row_of, emit, inward=1.0):
+        size = len(numbers)
         span = slice(t * LANES, (t + 1) * LANES)
-        metrics = [metric[start_row + first_row + j] for j in range(size)]
-        spins = [spin[start_row + first_row + j] for j in range(size)]
+        metrics = [metric[start_row + n] for n in numbers]
+        spins = [spin[start_row + n] for n in numbers]
         centers = [[row_of(f, j, span) for j in range(size)] for f in range(3)]
+        per_row = inward * (1.0 / 60.0)
         fast, fast_size, up, up_size = [], [], [], []
         for j in range(size):
             fast.append(centers[0][j] * (metrics[j] * (1.0 / 60.0)))
             fast_size.append(jnp.abs(fast[j]))
-            up.append(centers[1][j] * (1.0 / 60.0))
+            up.append(centers[1][j] * per_row)
             up_size.append(jnp.abs(up[j]))
         push_x, push_y = [None] * size, [None] * size
         for f in (3, 0, 1, 2):
@@ -328,10 +331,10 @@
                 )
                 if f == 3:
                     theta = centers[2][j]
-                    over_x = whole(mass_x[first_row + j, :, span])
-                    over_y = whole(mass_y[first_row + j, :, span])
+                    over_x = whole(mass_x[numbers[j], :, span])
+                    over_y = whole(mass_y[numbers[j], :, span])
                     push_x[j] = metrics[j] * ((1.0 / 60.0) * slope_x + theta * over_x)
-                    push_y[j] = (1.0 / 60.0) * slope_y + theta * over_y
+                    push_y[j] = per_row * slope_y + theta * over_y
                 elif f == 0:
                     change = change + (spins[j] * centers[1][j] - push_x[j])
                 elif f == 1:
@@ -341,18 +344,18 @@
     def all_rows(emit):
         if edge_rows:
             for side in range(2):
-                first_row = (rows - 3) * side
+                edge = edge_row(3 * side, rows)
+                step = jnp.where(edge == 0, 1, -1)
 
                 def row_of(f, j, span):
-                    row = first_row + j
-                    if row < 0:
-                        return south[levels * (3 * f + row + 3) : levels * (3 * f + row + 4), span]
-                    if row >= rows:
-                        return north[levels * (3 * f + row - rows) : levels * (3 * f + row - rows + 1), span]
-                    return fields[f][row, :, span]
-
+                    if j < 0:
+                        first = levels * (3 * f - j - 1)
+                        return strips[side][first : first + levels, span]
+                    return fields[f][edge + step * j, :, span]
+
+                numbers = [edge + step * j for j in range(3)]
                 for t in range(tiles):
-                    tendency(t, 3 * side, first_row, 3, row_of, emit)
+                    tendency(t, 3 * side, numbers, row_of, emit, step.astype(F32))
         else:
 
             def step(n, carry):
@@ -362,10 +365,15 @@
                     return fields[f][first_row + j, :, span]
 
                 for t in range(tiles):
-                    tendency(t, 2 * n, first_row, 2, row_of, emit)
+                    tendency(t, 2 * n, [first_row, first_row + 1], row_of, emit)
                 return carry
 
             lax.fori_loop(0, count // 2, step, 0)
+
+    def write_out(f):
+        if edge_rows:
+            return [(new.at[f, n], outs[f].at[edge_row(n, rows)]) for n in range(6)]
+        return [(new.at[f], outs[f].at[3 : rows - 3])]
 
     @pl.when(jnp.logical_not(is_polar()))
     def _():
@@ -373,15 +381,7 @@
             new[f, i, :, span] = q + STEP * change
 
         all_rows(emit)
-        pairs = []
-        for f in range(4):
-            if edge_rows:
-                pairs += [
-                    (new.at[f, 0:3], outs[f].at[0:3]),
-                    (new.at[f, 3:6], outs[f].at[rows - 3 : rows]),
-                ]
-            else:
-                pairs += [(new.at[f], outs[f].at[3 : rows - 3])]
+        pairs = [pair for f in range(4) for pair in write_out(f)]
         wait_all(start_all(pairs, sems))
 
     @pl.when(is_polar())
@@ -393,7 +393,7 @@
 
         all_rows(emit)
         c_all, s_all, d_all = [
-            spread_rows(own_waves(waves, part, edge_rows), count, levels) for part in range(3)
+            spread_waves(waves, part, edge_rows, levels) for part in range(3)
         ]
         top = kept_high[...].reshape(4 * items, columns)
         rest = kept_low[...].reshape(4 * items, columns)
@@ -462,9 +462,7 @@
             top = part.astype(BF16).astype(F32)
             come.append((top + turn(part - top, MESSAGE) + turn(top, 2 * MESSAGE)).astype(BF16))
         moved = dot(jnp.concatenate(come, axis=0), take[...])
-        c_all, s_all = [
-            spread_rows(own_waves(waves, part, edge_rows), count, levels) for part in range(2)
-        ]
+        c_all, s_all = [spread_waves(waves, part, edge_rows, levels) for part in range(2)]
         writes = []
         for half in range(2):
             value = []
@@ -478,16 +476,14 @@
             pairs = []
             for f in (2 * half, 2 * half + 1):
                 if edge_rows:
-                    new[f, 0:3] = fields[f][0:3] + change[f % 2, 0:3]
-                    new[f, 3:6] = fields[f][rows - 3 : rows] + change[f % 2, 3:6]
-                    pairs += [
-                        (new.at[f, 0:3], outs[f].at[0:3]),
-                        (new.at[f, 3:6], outs[f].at[rows - 3 : rows]),
-                    ]
+                    for n in range(6):
+                        row = edge_row(n, rows)
+                        new[f, n] = fields[f][row] + change[f % 2, n]
+                        pairs.append((new.at[f, n], outs[f].at[row]))
                 else:
                     new[f] = fields[f][3 : rows - 3] + change[f % 2]
-                    pairs += [(new.at[f], outs[f].at[3 : rows - 3])]
-            writes += start_all(pairs, sems, 4 * half)
+                    pairs.append((new.at[f], outs[f].at[3 : rows - 3]))
+            writes += start_all(pairs, sems, 12 * half)
         wait_all(writes)
 
 
@@ -529,41 +525,33 @@
     strip = 12 * levels + 8
     edge_lines = 2 * levels + rows
     far_fields = [pltpu.with_memory_space_constraint(q, pltpu.HBM) for q in (*fields, mass)]
-    to_south, to_north = pl.pallas_call(
-        pack_lat_kernel,
-        out_shape=[like(strip, columns)] * 2,
-        in_specs=[anywhere()] * 5,
-        out_specs=[vmem()] * 2,
-        scratch_shapes=[pltpu.VMEM((rows, columns), F32), pltpu.SemaphoreType.DMA((25,))],
-        compiler_params=params(8),
-        name="pack_lat",
-    )(*far_fields)
-    to_west, to_east, waves = pl.pallas_call(
-        pack_lon_kernel,
-        out_shape=[like(edge_lines, LANES)] * 2 + [like(3, rows, NODES)],
-        in_specs=[smem()] + [anywhere()] * 5 + [vmem(), anywhere()],
-        out_specs=[vmem()] * 3,
+    to_a, to_b, to_west, to_east, waves = pl.pallas_call(
+        pack_kernel,
+        out_shape=[like(strip, columns)] * 2 + [like(edge_lines, LANES)] * 2 + [like(3, rows, 8, NODES)],
+        in_specs=[smem()] + [anywhere()] * 5 + [vmem()],
+        out_specs=[vmem()] * 5,
         scratch_shapes=[
             pltpu.VMEM((2, 4, rows, levels, LANES), F32),
             pltpu.VMEM((rows, columns), F32),
-            pltpu.SemaphoreType.DMA((9,)),
+            pltpu.SemaphoreType.DMA((33,)),
         ],
         compiler_params=params(8),
-        name="pack_lon",
-    )(cutoffs, *far_fields, tables["nodes"], to_south)
+        name="pack_edges",
+    )(cutoffs, *far_fields, tables["nodes"])
 
     def ring(value, step):
         return lax.ppermute(value, "lon", [(i, (i + step) % lon_count) for i in range(lon_count)])
 
     west = ring(to_east, 1)
     east = ring(to_west, -1)
-    south = lax.ppermute(to_north, "lat", [(i, i + 1) for i in range(lat_count - 1)])
-    north = lax.ppermute(to_south, "lat", [(i + 1, i) for i in range(lat_count - 1)])
+    odd_up = [(i, i + 1) for i in range(1, lat_count - 1, 2)]
+    strip_a = lax.ppermute(to_a, "lat", [(i, i ^ 1) for i in range(lat_count)])
+    strip_b = lax.ppermute(to_b, "lat", odd_up + [(j, i) for i, j in odd_up])
 
     def tendencies(edge_rows, old):
         count = 6 if edge_rows else rows - 6
         items = count * levels
-        halos = [south, north] if edge_rows else []
+        halos = [strip_a, strip_b] if edge_rows else []
         weights = [tables[k] for k in ("band", "spread", "own", "send")]
         args = [metric, spin, *fields, mass, west, east, waves, *halos, *weights]
         return pl.pallas_call(
@@ -583,12 +571,12 @@
                 pltpu.VMEM((4, count, levels, columns), BF16),
                 pltpu.VMEM((rows, 8, columns), F32),
                 pltpu.VMEM((rows, 8, columns), F32),
-                pltpu.SemaphoreType.DMA((8,)),
+                pltpu.SemaphoreType.DMA((24,)),
             ],
             input_output_aliases={len(args) + f: f for f in range(4)} if old else {},
             compiler_params=params(36),
             cost_estimate=pl.CostEstimate(
-                flops=items * 4 * columns * 2000, bytes_accessed=8 * items * columns * 4, transcendentals=0
+                flops=items * 4 * columns * 20000, bytes_accessed=8 * items * columns * 4, transcendentals=0
             ),
             name="tend_edge" if edge_rows else "tend_inner",
         )(*args, *old)
@@ -608,7 +596,7 @@
             out_specs=[anywhere()] * 4,
             scratch_shapes=[
                 pltpu.VMEM((4, count, levels, columns), F32),
-                pltpu.SemaphoreType.DMA((8,)),
+                pltpu.SemaphoreType.DMA((24,)),
             ],
             input_output_aliases={len(args) + f: f for f in range(4)},
             compiler_params=params(24),

time: 43.1 us -> 43.8 us (1.016)
  local copies, waits for them, and re-layouts: 0.09 us -> 6 us
  starting transfers between devices: 14 us -> 11.1 us
  waiting for transfers between devices: 1.77 us -> 0.13 us
  Pallas kernels: 26 us -> 25.2 us
    unnamed x30 -> x34, local copies, waits for them, and re-layouts: 0.09 us -> 6 us
    ppermute x2, starting transfers between devices: 6.53 us -> 3.02 us  [the longest x1 2.33 us: shards(): strip_a = lax.ppermute(to_a, 'lat', [(i, i ^ 1) for i in range(lat_count)])]
    ppermute x8, waiting for transfers between devices: 1.76 us -> 0.12 us  [ring(): lax.ppermute(value, 'lon', [(i, (i + step) % lon_count) for i in range(lo...]
    pallas_call x2 -> x1, Pallas kernels: 3.95 us -> 2.54 us  [shards(): pl.pallas_call(pack_kernel, out_shape=[like(strip, columns)] * 2 + [like(...]
    ppermute x8, starting transfers between devices: 7.45 us -> 8.12 us  [ring(): lax.ppermute(value, 'lon', [(i, (i + step) % lon_count) for i in range(lo...]
  transfers between devices with their start and end apart: 10 -> 10, of which waited for: 2 -> 1; matrix products, arithmetic and copies ran while one was open for 0% -> 0% of each run, Pallas kernels for 52% -> 47%
where the time goes in v5:
time: 43.8 us; the launch traced here: 43.5 us
  Pallas kernels  25.2 us (58%)
  starting transfers between devices  11.1 us (25%)
  local copies, waits for them, and re-layouts  6 us (14%)
  between operations  1.04 us (2%)
    pallas_call x2, Pallas kernels, tendencies(): pl.pallas_call(functools.partial(tend_kernel, edge_rows, count), out_shap...  17.2 us
    ppermute x8, starting transfers between devices, ring(): lax.ppermute(value, 'lon', [(i, (i + step) % lon_count) for i in range(lo...  8.12 us
    unnamed x34, local copies, waits for them, and re-layouts  6 us
    pallas_call x2, Pallas kernels, finish(): pl.pallas_call(functools.partial(finish_kernel, edge_rows, count), out_sh...  5.53 us
    pallas_call x1, Pallas kernels, shards(): pl.pallas_call(pack_kernel, out_shape=[like(strip, columns)] * 2 + [like(...  2.54 us
    ppermute x1, starting transfers between devices, shards(): strip_a = lax.ppermute(to_a, 'lat', [(i, i ^ 1) for i in range(lat_count)])  2.33 us
  transfers between devices with their start and end apart: 10, of which 1 were waited for; matrix products, arithmetic and copies ran while one was open for 0% of the time, Pallas kernels for 47%

profile of v5, /device:TPU:0, one launch (start us, length us, event | category | flops | bytes accessed | tf_op | source)
XLA Modules:
  0.0 43.5 jit_solution(10565962202574013832)
XLA Ops:
  0.6 0.0 copy-start.15
  0.6 0.0 copy-start.16
  0.7 0.0 copy-start.3
  0.7 0.0 copy-start.2
  0.7 0.0 copy-start.1
  0.7 0.0 copy-start
  0.7 0.0 copy-start.6
  0.7 0.0 copy-start.7
  0.7 0.8 %copy-done.7 = f32[1,256]{1,0:T(1,128)S(1)} copy-done((f32[1,256]{1,0:T(1,128)S(1)}, f32[1,256]{1,0:T(1,128)}, u32[]{:S(2)}) %copy-start.7) | copy-done | bytes 1048
  1.5 0.0 copy-start.8
  1.5 0.9 %copy-done.8 = s32[32]{0:T(128)S(1)} copy-done((s32[32]{0:T(128)S(1)}, s32[32]{0:T(128)}, u32[]{:S(2)}) %copy-start.8) | copy-done | bytes 152
  2.5 2.5 %pack_edges.1 = (f32[200,896]{1,0:T(8,128)S(1)}, f32[200,896]{1,0:T(8,128)S(1)}, f32[48,128]{1,0:T(8,128)S(1)}, f32[48,128]{1,0:T(8,128)S(1)}, f32[3,16,8,256]{3,2,1,0:T(8,128)S(1)}) custom-call(s32[32]{0:T(128)S(1)} %copy-done.8, f32[16,16,896]{2,1,0:T(8,128)} %refs_0_.9, f32[16,16,896]{2,1,0:T(8,128)} %refs_1_.9, f32[16,16,896]{2,1,0:T(8,128)} %refs_2_.9, ...), custom_call_target="tpu_custom_call" | custom-call | tf_op jit(solution)/shard_map/pack_edges/pallas_call | solution.py:528
  5.0 0.5 %collective-permute-start = (f32[48,128]{1,0:T(8,128)S(1)}, f32[48,128]{1,0:T(8,128)S(1)}, u32[]{:S(2)}, u32[]{:S(2)}) collective-permute-start(f32[48,128]{1,0:T(8,128)S(1)} %get-tuple-element.29), channel_id=1, source_target_pairs={{0,1},{1,2},{2,3},{3,0},{4,5},{5,6},{6,7},{7,4},{8,9},{9,10},{10,1... | collective-permute-start | bytes 73736 | tf_op jit(solution)/shard_map/ppermute | solution.py:543
  5.5 2.0 %collective-permute-start.1 = (f32[48,128]{1,0:T(8,128)S(1)}, f32[48,128]{1,0:T(8,128)S(1)}, u32[]{:S(2)}, u32[]{:S(2)}) collective-permute-start(f32[48,128]{1,0:T(8,128)S(1)} %get-tuple-element.30), channel_id=1, source_target_pairs={{0,3},{1,0},{2,1},{3,2},{4,7},{5,4},{6,5},{7,6},{8,11},{9,8},{10,9... | collective-permute-start | bytes 73736 | tf_op jit(solution)/shard_map/ppermute | solution.py:543
  7.5 2.3 %collective-permute-start.2 = (f32[200,896]{1,0:T(8,128)S(1)}, f32[200,896]{1,0:T(8,128)S(1)}, u32[]{:S(2)}, u32[]{:S(2)}) collective-permute-start(f32[200,896]{1,0:T(8,128)S(1)} %get-tuple-element.32), channel_id=1, source_target_pairs={{0,4},{4,0},{8,12},{12,8},{1,5},{5,1},{9,13},{13,9},{2,6},{6,2},{1... | collective-permute-start | bytes 2150408 | tf_op jit(solution)/shard_map/ppermute | solution.py:548
  9.8 0.7 %collective-permute-start.3 = (f32[200,896]{1,0:T(8,128)S(1)}, f32[200,896]{1,0:T(8,128)S(1)}, u32[]{:S(2)}, u32[]{:S(2)}) collective-permute-start(f32[200,896]{1,0:T(8,128)S(1)} %get-tuple-element.33), channel_id=1, source_target_pairs={{4,8},{8,4},{5,9},{9,5},{6,10},{10,6},{7,11},{11,7},{20,24},{24,20... | collective-permute-start | bytes 2150408 | tf_op jit(solution)/shard_map/ppermute | solution.py:549
  10.5 0.0 collective-permute-done.refs_5_
  10.5 0.0 collective-permute-done.1.refs_6_
  10.6 0.0 copy-done.15
  10.6 0.0 copy-done.16
  10.6 0.0 copy-done.3
  10.6 0.0 copy-done.2
  10.6 0.0 copy-done.1
  10.6 0.0 copy-done
  10.6 0.0 copy-done.6
  10.6 0.0 copy-start.9
  10.6 1.3 %copy-done.9 = bf16[2688,256]{1,0:T(8,128)(2,1)S(1)} copy-done((bf16[2688,256]{1,0:T(8,128)(2,1)S(1)}, bf16[2688,256]{1,0:T(8,128)(2,1)}, u32[]{:S(2)}) %copy-start.9) | copy-done | bytes 1376280
  12.0 0.0 copy-start.10
  12.0 1.0 %copy-done.10 = bf16[768,256]{1,0:T(8,128)(2,1)S(1)} copy-done((bf16[768,256]{1,0:T(8,128)(2,1)S(1)}, bf16[768,256]{1,0:T(8,128)(2,1)}, u32[]{:S(2)}) %copy-start.10) | copy-done | bytes 393240
  13.0 0.0 copy-start.11
  13.0 0.9 %copy-done.11 = bf16[512,256]{1,0:T(8,128)(2,1)S(1)} copy-done((bf16[512,256]{1,0:T(8,128)(2,1)S(1)}, bf16[512,256]{1,0:T(8,128)(2,1)}, u32[]{:S(2)}) %copy-start.11) | copy-done | bytes 262168
  13.9 0.0 copy-start.13
  13.9 0.9 %copy-done.13 = bf16[768,128]{1,0:T(8,128)(2,1)S(1)} copy-done((bf16[768,128]{1,0:T(8,128)(2,1)S(1)}, bf16[768,128]{1,0:T(8,128)(2,1)}, u32[]{:S(2)}) %copy-start.13) | copy-done | bytes 196632
  14.8 0.0 copy-start.12
  14.8 0.0 copy-start.14
  14.8 10.5 %tend_inner.1 = (f32[16,16,896]{2,1,0:T(8,128)}, f32[16,16,896]{2,1,0:T(8,128)}, f32[16,16,896]{2,1,0:T(8,128)}, f32[16,16,896]{2,1,0:T(8,128)}, f32[4,160,256]{...) custom-call(f32[64]{0:T(128)S(1)} %copy-done.16, f32[64]{0:T(128)S(1)} %copy-done.15, ...), custom_call_target="tpu_custom_call" | custom-call | flops 11468800000 | bytes 4587520 | tf_op jit(solution)/shard_map/tend_inner/pallas_call | solution.py:557
  25.3 1.6 %collective-permute-start.9 = (f32[80,128]{1,0:T(8,128)S(1)}, f32[80,128]{1,0:T(8,128)S(1)}, u32[]{:S(2)}, u32[]{:S(2)}) collective-permute-start(f32[80,128]{1,0:T(8,128)S(1)} %get-tuple-element.44), channel_id=1, source_target_pairs={{0,2},{1,3},{2,0},{3,1},{4,6},{5,7},{6,4},{7,5},{8,10},{9,11},{10,... | collective-permute-start | bytes 122888 | tf_op jit(solution)/shard_map/ppermute | solution.py:543
  26.9 0.0 collective-permute-start.7
  26.9 1.7 %collective-permute-start.8 = (f32[160,128]{1,0:T(8,128)S(1)}, f32[160,128]{1,0:T(8,128)S(1)}, u32[]{:S(2)}, u32[]{:S(2)}) collective-permute-start(f32[160,128]{1,0:T(8,128)S(1)} %get-tuple-element.43), channel_id=1, source_target_pairs={{0,3},{1,0},{2,1},{3,2},{4,7},{5,4},{6,5},{7,6},{8,11},{9,8},{10,9... | collective-permute-start | bytes 245768 | tf_op jit(solution)/shard_map/ppermute | solution.py:543
  28.6 0.0 collective-permute-done.2.refs_8_
  28.6 0.0 collective-permute-done.3.refs_9_
  28.6 0.0 copy-done.12
  28.6 0.0 copy-done.14
  28.7 0.0 copy-start.4
  28.7 0.0 copy-start.5
  28.7 6.7 %tend_edge.1 = (f32[16,16,896]{2,1,0:T(8,128)}, f32[16,16,896]{2,1,0:T(8,128)}, f32[16,16,896]{2,1,0:T(8,128)}, f32[16,16,896]{2,1,0:T(8,128)}, f32[4,96,256]{2,...) custom-call(f32[64]{0:T(128)S(1)} %copy-done.16, ...), custom_call_target="tpu_custom_call", output_to_operand_aliasing={{0}: (16, {}), {1}: (17, {}), {2}: (18, {}), {3}: (19, {})} | custom-call | flops 6881280000 | bytes 2752512 | tf_op jit(solution)/shard_map/tend_edge/pallas_call | solution.py:557
  35.4 0.1 collective-permute-start.4
  35.4 1.7 %collective-permute-start.5 = (f32[96,128]{1,0:T(8,128)S(1)}, f32[96,128]{1,0:T(8,128)S(1)}, u32[]{:S(2)}, u32[]{:S(2)}) collective-permute-start(f32[96,128]{1,0:T(8,128)S(1)} %get-tuple-element.39), channel_id=1, source_target_pairs={{0,3},{1,0},{2,1},{3,2},{4,7},{5,4},{6,5},{7,6},{8,11},{9,8},{10,9... | collective-permute-start | bytes 147464 | tf_op jit(solution)/shard_map/ppermute | solution.py:543
  37.2 0.0 collective-permute-done.9.refs_6_
  37.2 0.5 %collective-permute-start.6 = (f32[48,128]{1,0:T(8,128)S(1)}, f32[48,128]{1,0:T(8,128)S(1)}, u32[]{:S(2)}, u32[]{:S(2)}) collective-permute-start(f32[48,128]{1,0:T(8,128)S(1)} %get-tuple-element.40), channel_id=1, source_target_pairs={{0,2},{1,3},{2,0},{3,1},{4,6},{5,7},{6,4},{7,5},{8,10},{9,11},{10,... | collective-permute-start | bytes 73736 | tf_op jit(solution)/shard_map/ppermute | solution.py:543
  37.7 0.0 collective-permute-done.7.refs_4_
  37.7 0.0 collective-permute-done.8.refs_5_
  37.7 0.0 copy-done.4
  37.7 0.0 copy-done.5
  37.7 3.2 %finish_inner.1 = (f32[16,16,896]{2,1,0:T(8,128)}, f32[16,16,896]{2,1,0:T(8,128)}, f32[16,16,896]{2,1,0:T(8,128)}, f32[16,16,896]{2,1,0:T(8,128)}) custom-call(f32[16,16,896]{2,1,0:T(8,128)S(1)} %copy-done, f32[16,16,896]{2,1,0:T(8,128)S(1)} %copy-done.1, ...), custom_call_target="tpu_custom_call", output_to_operand_aliasing={{0}: (11, {}), {1}: (12, {}), {2}: (13, {}), {3}: (14, {})} | custom-call | tf_op jit(solution)/shard_map/finish_inner/pallas_call | solution.py:592
  40.9 0.1 collective-permute-done.6.refs_6_
  41.0 0.0 collective-permute-done.4.refs_4_
  41.0 0.0 collective-permute-done.5.refs_5_
  41.0 2.4 %finish_edge.1 = (f32[16,16,896]{2,1,0:T(8,128)}, f32[16,16,896]{2,1,0:T(8,128)}, f32[16,16,896]{2,1,0:T(8,128)}, f32[16,16,896]{2,1,0:T(8,128)}) custom-call(f32[16,16,896]{2,1,0:T(8,128)S(1)} %copy-done, f32[16,16,896]{2,1,0:T(8,128)S(1)} %copy-done.1, ...), custom_call_target="tpu_custom_call", output_to_operand_aliasing={{0}: (11, {}), {1}: (12, {}), {2}: (13, {}), {3}: (14, {})} | custom-call | tf_op jit(solution)/shard_map/finish_edge/pallas_call | solution.py:592
Async XLA Ops:
  0.6 9.9 %copy-start.15 = (f32[64]{0:T(128)S(1)}, f32[64]{0:T(128)}, u32[]{:S(2)}) copy-start(f32[64]{0:T(128)} %constant.26.clone.spin) | copy-start | bytes 772
  0.6 9.9 %copy-start.16 = (f32[64]{0:T(128)S(1)}, f32[64]{0:T(128)}, u32[]{:S(2)}) copy-start(f32[64]{0:T(128)} %constant.25.clone.metric) | copy-start | bytes 772
  0.7 9.9 %copy-start.3 = (f32[16,16,896]{2,1,0:T(8,128)S(1)}, f32[16,16,896]{2,1,0:T(8,128)}, u32[]{:S(2)}) copy-start(f32[16,16,896]{2,1,0:T(8,128)} %refs_3_.9) | copy-start | bytes 2752516
  0.7 9.9 %copy-start.2 = (f32[16,16,896]{2,1,0:T(8,128)S(1)}, f32[16,16,896]{2,1,0:T(8,128)}, u32[]{:S(2)}) copy-start(f32[16,16,896]{2,1,0:T(8,128)} %refs_2_.9) | copy-start | bytes 2752516
  0.7 9.9 %copy-start.1 = (f32[16,16,896]{2,1,0:T(8,128)S(1)}, f32[16,16,896]{2,1,0:T(8,128)}, u32[]{:S(2)}) copy-start(f32[16,16,896]{2,1,0:T(8,128)} %refs_1_.9) | copy-start | bytes 2752516
  0.7 9.9 %copy-start = (f32[16,16,896]{2,1,0:T(8,128)S(1)}, f32[16,16,896]{2,1,0:T(8,128)}, u32[]{:S(2)}) copy-start(f32[16,16,896]{2,1,0:T(8,128)} %refs_0_.9) | copy-start | bytes 2752516
  0.7 9.9 %copy-start.6 = (f32[16,896]{1,0:T(8,128)S(1)}, f32[16,896]{1,0:T(8,128)}, u32[]{:S(2)}) copy-start(f32[16,896]{1,0:T(8,128)} %refs_4_.5) | copy-start | bytes 172036
  0.7 0.8 %copy-start.7 = (f32[1,256]{1,0:T(1,128)S(1)}, f32[1,256]{1,0:T(1,128)}, u32[]{:S(2)}) copy-start(f32[1,256]{1,0:T(1,128)} %constant.18.clone.refs_5_) | copy-start | bytes 3076
  1.5 0.9 %copy-start.8 = (s32[32]{0:T(128)S(1)}, s32[32]{0:T(128)}, u32[]{:S(2)}) copy-start(s32[32]{0:T(128)} %cutoffs.1) | copy-start | bytes 388
  5.0 5.5 %collective-permute-start = (f32[48,128]{1,0:T(8,128)S(1)}, f32[48,128]{1,0:T(8,128)S(1)}, u32[]{:S(2)}, u32[]{:S(2)}) collective-permute-start(f32[48,128]{1,0:T(8,128)S(1)} %get-tuple-element.29), channel_id=1, source_target_pairs={{0,1},{1,2},{2,3},{3,0},{4,5},{5,6},{6,7},{7,4},{8,9},{9,10},{10,1... | collective-permute-start | bytes 73736 | tf_op jit(solution)/shard_map/ppermute | solution.py:543
  5.5 5.0 %collective-permute-start.1 = (f32[48,128]{1,0:T(8,128)S(1)}, f32[48,128]{1,0:T(8,128)S(1)}, u32[]{:S(2)}, u32[]{:S(2)}) collective-permute-start(f32[48,128]{1,0:T(8,128)S(1)} %get-tuple-element.30), channel_id=1, source_target_pairs={{0,3},{1,0},{2,1},{3,2},{4,7},{5,4},{6,5},{7,6},{8,11},{9,8},{10,9... | collective-permute-start | bytes 73736 | tf_op jit(solution)/shard_map/ppermute | solution.py:543
  7.5 21.1 %collective-permute-start.2 = (f32[200,896]{1,0:T(8,128)S(1)}, f32[200,896]{1,0:T(8,128)S(1)}, u32[]{:S(2)}, u32[]{:S(2)}) collective-permute-start(f32[200,896]{1,0:T(8,128)S(1)} %get-tuple-element.32), channel_id=1, source_target_pairs={{0,4},{4,0},{8,12},{12,8},{1,5},{5,1},{9,13},{13,9},{2,6},{6,2},{1... | collective-permute-start | bytes 2150408 | tf_op jit(solution)/shard_map/ppermute | solution.py:548
  9.8 18.8 %collective-permute-start.3 = (f32[200,896]{1,0:T(8,128)S(1)}, f32[200,896]{1,0:T(8,128)S(1)}, u32[]{:S(2)}, u32[]{:S(2)}) collective-permute-start(f32[200,896]{1,0:T(8,128)S(1)} %get-tuple-element.33), channel_id=1, source_target_pairs={{4,8},{8,4},{5,9},{9,5},{6,10},{10,6},{7,11},{11,7},{20,24},{24,20... | collective-permute-start | bytes 2150408 | tf_op jit(solution)/shard_map/ppermute | solution.py:549
  10.6 1.3 %copy-start.9 = (bf16[2688,256]{1,0:T(8,128)(2,1)S(1)}, bf16[2688,256]{1,0:T(8,128)(2,1)}, u32[]{:S(2)}) copy-start(bf16[2688,256]{1,0:T(8,128)(2,1)} %constant.20.clone.refs_9_.refs_11_) | copy-start | bytes 4128772
  12.0 1.0 %copy-start.10 = (bf16[768,256]{1,0:T(8,128)(2,1)S(1)}, bf16[768,256]{1,0:T(8,128)(2,1)}, u32[]{:S(2)}) copy-start(bf16[768,256]{1,0:T(8,128)(2,1)} %constant.21.clone.refs_10_.refs_12_) | copy-start | bytes 1179652
  13.0 0.9 %copy-start.11 = (bf16[512,256]{1,0:T(8,128)(2,1)S(1)}, bf16[512,256]{1,0:T(8,128)(2,1)}, u32[]{:S(2)}) copy-start(bf16[512,256]{1,0:T(8,128)(2,1)} %constant.19.clone.refs_8_.refs_10_) | copy-start | bytes 786436
  13.9 0.9 %copy-start.13 = (bf16[768,128]{1,0:T(8,128)(2,1)S(1)}, bf16[768,128]{1,0:T(8,128)(2,1)}, u32[]{:S(2)}) copy-start(bf16[768,128]{1,0:T(8,128)(2,1)} %constant.22.clone.refs_11_.refs_13_) | copy-start | bytes 589828
  14.8 13.8 %copy-start.12 = (bf16[512,256]{1,0:T(8,128)(2,1)S(1)}, bf16[512,256]{1,0:T(8,128)(2,1)}, u32[]{:S(2)}) copy-start(bf16[512,256]{1,0:T(8,128)(2,1)} %constant.19.clone.refs_8_.refs_10_) | copy-start | bytes 786436
  14.8 13.8 %copy-start.14 = (bf16[768,128]{1,0:T(8,128)(2,1)S(1)}, bf16[768,128]{1,0:T(8,128)(2,1)}, u32[]{:S(2)}) copy-start(bf16[768,128]{1,0:T(8,128)(2,1)} %constant.22.clone.refs_11_.refs_13_) | copy-start | bytes 589828
  25.3 11.8 %collective-permute-start.9 = (f32[80,128]{1,0:T(8,128)S(1)}, f32[80,128]{1,0:T(8,128)S(1)}, u32[]{:S(2)}, u32[]{:S(2)}) collective-permute-start(f32[80,128]{1,0:T(8,128)S(1)} %get-tuple-element.44), channel_id=1, source_target_pairs={{0,2},{1,3},{2,0},{3,1},{4,6},{5,7},{6,4},{7,5},{8,10},{9,11},{10,... | collective-permute-start | bytes 122888 | tf_op jit(solution)/shard_map/ppermute | solution.py:543
  26.9 10.8 %collective-permute-start.7 = (f32[160,128]{1,0:T(8,128)S(1)}, f32[160,128]{1,0:T(8,128)S(1)}, u32[]{:S(2)}, u32[]{:S(2)}) collective-permute-start(f32[160,128]{1,0:T(8,128)S(1)} %get-tuple-element.42), channel_id=1, source_target_pairs={{0,1},{1,2},{2,3},{3,0},{4,5},{5,6},{6,7},{7,4},{8,9},{9,10},{10,1... | collective-permute-start | bytes 245768 | tf_op jit(solution)/shard_map/ppermute | solution.py:543
  26.9 10.8 %collective-permute-start.8 = (f32[160,128]{1,0:T(8,128)S(1)}, f32[160,128]{1,0:T(8,128)S(1)}, u32[]{:S(2)}, u32[]{:S(2)}) collective-permute-start(f32[160,128]{1,0:T(8,128)S(1)} %get-tuple-element.43), channel_id=1, source_target_pairs={{0,3},{1,0},{2,1},{3,2},{4,7},{5,4},{6,5},{7,6},{8,11},{9,8},{10,9... | collective-permute-start | bytes 245768 | tf_op jit(solution)/shard_map/ppermute | solution.py:543
  28.7 9.0 %copy-start.4 = (bf16[768,896]{1,0:T(8,128)(2,1)S(1)}, bf16[768,896]{1,0:T(8,128)(2,1)}, u32[]{:S(2)}) copy-start(bf16[768,896]{1,0:T(8,128)(2,1)} %constant.24.clone.refs_10_) | copy-start | bytes 4128772
  28.7 9.0 %copy-start.5 = (bf16[128,256]{1,0:T(8,128)(2,1)S(1)}, bf16[128,256]{1,0:T(8,128)(2,1)}, u32[]{:S(2)}) copy-start(bf16[128,256]{1,0:T(8,128)(2,1)} %constant.23.clone.refs_9_) | copy-start | bytes 196612
  35.4 5.6 %collective-permute-start.4 = (f32[96,128]{1,0:T(8,128)S(1)}, f32[96,128]{1,0:T(8,128)S(1)}, u32[]{:S(2)}, u32[]{:S(2)}) collective-permute-start(f32[96,128]{1,0:T(8,128)S(1)} %get-tuple-element.38), channel_id=1, source_target_pairs={{0,1},{1,2},{2,3},{3,0},{4,5},{5,6},{6,7},{7,4},{8,9},{9,10},{10,1... | collective-permute-start | bytes 147464 | tf_op jit(solution)/shard_map/ppermute | solution.py:543
  35.4 5.6 %collective-permute-start.5 = (f32[96,128]{1,0:T(8,128)S(1)}, f32[96,128]{1,0:T(8,128)S(1)}, u32[]{:S(2)}, u32[]{:S(2)}) collective-permute-start(f32[96,128]{1,0:T(8,128)S(1)} %get-tuple-element.39), channel_id=1, source_target_pairs={{0,3},{1,0},{2,1},{3,2},{4,7},{5,4},{6,5},{7,6},{8,11},{9,8},{10,9... | collective-permute-start | bytes 147464 | tf_op jit(solution)/shard_map/ppermute | solution.py:543
  37.2 3.8 %collective-permute-start.6 = (f32[48,128]{1,0:T(8,128)S(1)}, f32[48,128]{1,0:T(8,128)S(1)}, u32[]{:S(2)}, u32[]{:S(2)}) collective-permute-start(f32[48,128]{1,0:T(8,128)S(1)} %get-tuple-element.40), channel_id=1, source_target_pairs={{0,2},{1,3},{2,0},{3,1},{4,6},{5,7},{6,4},{7,5},{8,10},{9,11},{10,... | collective-permute-start | bytes 73736 | tf_op jit(solution)/shard_map/ppermute | solution.py:543

commit v6 on v5

--- a/solution.py
+++ b/solution.py
@@ -140,12 +140,14 @@
     return jnp.where(lax.axis_index("lat") % 2 == 0, even, odd)
 
 
-def pack_kernel(cutoffs, *refs):
+def pack_kernel(*refs):
     fields = refs[:4]
-    mass, nodes, strip_a, strip_b, west, east, waves, edge, own_mass, sems = refs[4:]
+    mass, cutoffs_in, nodes_in, strip_a, strip_b, west, east, waves = refs[4:12]
+    edge, own_mass, cutoffs, nodes, sems = refs[12:]
     rows, columns = mass.shape
     levels = edge.shape[3]
     tail = 12 * levels
+    first = start_all([(cutoffs_in, cutoffs), (nodes_in, nodes)], sems, 33)
     small = start_all(
         [(mass, own_mass)]
         + [(q.at[:, :, 0:LANES], edge.at[0, f]) for f, q in enumerate(fields)]
@@ -160,6 +162,7 @@
             pairs.append((q.at[row], strip.at[pl.ds(levels * (3 * f + entry % 3), levels)]))
     large = start_all(pairs, sems, 9)
 
+    wait_all(first)
     lat_count = lax.axis_size("lat")
     lon_count = lax.axis_size("lon")
     owner = lax.axis_index("lat")
@@ -250,17 +253,19 @@
     fields = some(4)
     mass, west, east, waves = some(4)
     strips = some(2) if edge_rows else None
-    band, spread, own, send = some(4)
+    tables_in = some(4)
     if edge_rows:
         some(4)
     outs = some(4)
     local, to_east, to_west, to_far = some(4)
-    high, low, cross, new, kept_high, kept_low, mass_x, mass_y, sems = some(9)
+    high, low, cross, new, kept_high, kept_low, mass_x, mass_y, *tables, sems = some(13)
+    band, spread, own, send = tables
     rows, columns = mass.shape
     levels = fields[0].shape[1]
     items = count * levels
     tiles = columns // LANES
 
+    fetched = start_all(zip(tables_in, tables), sems, 24)
     if edge_rows:
         tail = 12 * levels
         lines = [strip[tail : tail + 3] for strip in strips]
@@ -292,6 +297,7 @@
 
     lax.fori_loop(0, count, cut, 0)
 
+    wait_all(fetched[:1])
     for t in range(tiles):
         span = slice(t * LANES, (t + 2) * LANES)
         both = jnp.concatenate(
@@ -383,6 +389,7 @@
         all_rows(emit)
         pairs = [pair for f in range(4) for pair in write_out(f)]
         wait_all(start_all(pairs, sems))
+        wait_all(fetched[1:])
 
     @pl.when(is_polar())
     def _():
@@ -392,6 +399,7 @@
             kept_low[f, i, :, span] = (change - top.astype(F32)).astype(BF16)
 
         all_rows(emit)
+        wait_all(fetched[1:])
         c_all, s_all, d_all = [
             spread_waves(waves, part, edge_rows, levels) for part in range(3)
         ]
@@ -431,15 +439,17 @@
 
 def finish_kernel(edge_rows, count, *refs):
     fields = refs[:4]
-    from_west, from_east, from_far, local, waves, take, gather = refs[4:11]
+    from_west, from_east, from_far, local, waves, take_in, gather_in = refs[4:11]
     outs = refs[15:19]
-    new, sems = refs[19:]
+    new, take, gather, sems = refs[19:]
     rows = fields[0].shape[0]
     levels, columns = new.shape[2], new.shape[3]
     items = count * levels
 
     @pl.when(is_polar())
     def _():
+        fetched = start_all([(take_in, take), (gather_in, gather)], sems, 24)
+
         place = lax.axis_index("lon")
         last = lax.axis_size("lon") - 1
         near_west = from_west[...] * jnp.where(place == 0, -1.0, 1.0)
@@ -461,8 +471,10 @@
             part = jnp.where(wide < MESSAGE, part, 0.0)
             top = part.astype(BF16).astype(F32)
             come.append((top + turn(part - top, MESSAGE) + turn(top, 2 * MESSAGE)).astype(BF16))
+        wait_all(fetched[:1])
         moved = dot(jnp.concatenate(come, axis=0), take[...])
         c_all, s_all = [spread_waves(waves, part, edge_rows, levels) for part in range(2)]
+        wait_all(fetched[1:])
         writes = []
         for half in range(2):
             value = []
@@ -503,6 +515,10 @@
     return jax.ShapeDtypeStruct(shape, F32)
 
 
+def in_hbm(value):
+    return pltpu.with_memory_space_constraint(value, pltpu.HBM)
+
+
 def params(mebibytes):
     return pltpu.CompilerParams(vmem_limit_bytes=mebibytes * 1024 * 1024)
 
@@ -518,26 +534,29 @@
     rows, levels, columns = u_wind.shape
     lat_count = lax.axis_size("lat")
     lon_count = lax.axis_size("lon")
-    tables = {k: jnp.asarray(v) for k, v in filter_tables(columns, columns * lon_count).items()}
+    tables = filter_tables(columns, columns * lon_count)
+    tables = {k: in_hbm(jnp.asarray(v)) for k, v in tables.items()}
     metric, spin = [jnp.asarray(t) for t in row_factors(rows * lat_count)]
     fields = (u_wind, v_wind, theta, geopot)
 
     strip = 12 * levels + 8
     edge_lines = 2 * levels + rows
-    far_fields = [pltpu.with_memory_space_constraint(q, pltpu.HBM) for q in (*fields, mass)]
+    far_fields = [in_hbm(q) for q in (*fields, mass)]
     to_a, to_b, to_west, to_east, waves = pl.pallas_call(
         pack_kernel,
         out_shape=[like(strip, columns)] * 2 + [like(edge_lines, LANES)] * 2 + [like(3, rows, 8, NODES)],
-        in_specs=[smem()] + [anywhere()] * 5 + [vmem()],
+        in_specs=[anywhere()] * 7,
         out_specs=[vmem()] * 5,
         scratch_shapes=[
             pltpu.VMEM((2, 4, rows, levels, LANES), F32),
             pltpu.VMEM((rows, columns), F32),
-            pltpu.SemaphoreType.DMA((33,)),
+            pltpu.SMEM(cutoffs.shape, jnp.int32),
+            pltpu.VMEM((1, NODES), F32),
+            pltpu.SemaphoreType.DMA((35,)),
         ],
         compiler_params=params(8),
         name="pack_edges",
-    )(cutoffs, *far_fields, tables["nodes"])
+    )(*far_fields, in_hbm(cutoffs), tables["nodes"])
 
     def ring(value, step):
         return lax.ppermute(value, "lon", [(i, (i + step) % lon_count) for i in range(lon_count)])
@@ -560,7 +579,7 @@
             + [like(4, items, NODES)]
             + [like(items, LANES)] * 2
             + [like(items // 2, LANES)],
-            in_specs=[smem()] * 2 + [vmem()] * (len(args) - 2) + [anywhere()] * len(old),
+            in_specs=[smem()] * 2 + [vmem()] * (len(args) - 6) + [anywhere()] * (4 + len(old)),
             out_specs=[anywhere()] * 4 + [vmem()] * 4,
             scratch_shapes=[
                 pltpu.VMEM((4, count, levels, columns + LANES), BF16),
@@ -571,7 +590,8 @@
                 pltpu.VMEM((4, count, levels, columns), BF16),
                 pltpu.VMEM((rows, 8, columns), F32),
                 pltpu.VMEM((rows, 8, columns), F32),
-                pltpu.SemaphoreType.DMA((24,)),
+                *[pltpu.VMEM(w.shape, w.dtype) for w in weights],
+                pltpu.SemaphoreType.DMA((28,)),
             ],
             input_output_aliases={len(args) + f: f for f in range(4)} if old else {},
             compiler_params=params(36),
@@ -592,11 +612,12 @@
         return pl.pallas_call(
             functools.partial(finish_kernel, edge_rows, count),
             out_shape=[like(rows, levels, columns)] * 4,
-            in_specs=[vmem()] * len(args) + [anywhere()] * 4,
+            in_specs=[vmem()] * (len(args) - 2) + [anywhere()] * 6,
             out_specs=[anywhere()] * 4,
             scratch_shapes=[
                 pltpu.VMEM((4, count, levels, columns), F32),
-                pltpu.SemaphoreType.DMA((24,)),
+                *[pltpu.VMEM(w.shape, w.dtype) for w in weights],
+                pltpu.SemaphoreType.DMA((26,)),
             ],
             input_output_aliases={len(args) + f: f for f in range(4)},
             compiler_params=params(24),

time: 43.8 us -> 42.8 us (0.977)
  local copies, waits for them, and re-layouts: 6 us -> 0.03 us
  Pallas kernels: 25.2 us -> 28.9 us
  waiting for transfers between devices: 0.13 us -> 1.61 us
    unnamed x34 -> x14, local copies, waits for them, and re-layouts: 6 us -> 0.03 us
    pallas_call x2, Pallas kernels: 5.53 us -> 9 us  [finish(): pl.pallas_call(functools.partial(finish_kernel, edge_rows, count), out_sh...]
    ppermute x1, waiting for transfers between devices: 0.01 us -> 1.59 us  [shards(): strip_a = lax.ppermute(to_a, 'lat', [(i, i ^ 1) for i in range(lat_count)])]
    pallas_call x2, Pallas kernels: 17.2 us -> 17.7 us  [tendencies(): pl.pallas_call(functools.partial(tend_kernel, edge_rows, count), out_shap...]
  transfers between devices with their start and end apart: 10 -> 10, of which waited for: 1 -> 1; matrix products, arithmetic and copies ran while one was open for 0% -> 0% of each run, Pallas kernels for 47% -> 53%
where the time goes in v6:
time: 42.8 us; the launch traced here: 42.6 us
  Pallas kernels  28.9 us (68%)
  starting transfers between devices  11.1 us (26%)
  waiting for transfers between devices  1.61 us (4%)
  between operations  1 us (2%)
    pallas_call x2, Pallas kernels, tendencies(): pl.pallas_call(functools.partial(tend_kernel, edge_rows, count), out_shap...  17.7 us
    pallas_call x2, Pallas kernels, finish(): pl.pallas_call(functools.partial(finish_kernel, edge_rows, count), out_sh...  9 us
    ppermute x8, starting transfers between devices, ring(): lax.ppermute(value, 'lon', [(i, (i + step) % lon_count) for i in range(lo...  8.04 us
    ppermute x1, starting transfers between devices, shards(): strip_a = lax.ppermute(to_a, 'lat', [(i, i ^ 1) for i in range(lat_count)])  2.33 us
    pallas_call x1, Pallas kernels, shards(): pl.pallas_call(pack_kernel, out_shape=[like(strip, columns)] * 2 + [like(...  2.18 us
    ppermute x1, waiting for transfers between devices, shards(): strip_a = lax.ppermute(to_a, 'lat', [(i, i ^ 1) for i in range(lat_count)])  1.59 us
  transfers between devices with their start and end apart: 10, of which 1 were waited for; matrix products, arithmetic and copies ran while one was open for 0% of the time, Pallas kernels for 53%

profile of v6, /device:TPU:0, one launch (start us, length us, event | category | flops | bytes accessed | tf_op | source)
XLA Modules:
  0.0 42.6 jit_solution(12676187516541322328)
XLA Ops:
  0.6 0.0 copy-start.5
  0.6 0.0 copy-start.6
  0.7 0.0 copy-start.3
  0.7 0.0 copy-start.2
  0.7 0.0 copy-start.1
  0.7 0.0 copy-start
  0.7 0.0 copy-start.4
  0.7 2.2 %pack_edges.1 = (f32[200,896]{1,0:T(8,128)S(1)}, f32[200,896]{1,0:T(8,128)S(1)}, f32[48,128]{1,0:T(8,128)S(1)}, f32[48,128]{1,0:T(8,128)S(1)}, f32[3,16,8,256]{3,2,1,0:T(8,128)S(1)}) custom-call(f32[16,16,896]{2,1,0:T(8,128)} %refs_0_.9, f32[16,16,896]{2,1,0:T(8,128)} %refs_1_.9, f32[16,16,896]{2,1,0:T(8,128)} %refs_2_.9, f32[16,16,896]{2,1,0:T(8,128)} %refs_3_.9, ...), custom_call_target="tpu_custom_call" | custom-call | tf_op jit(solution)/shard_map/pack_edges/pallas_call | solution.py:545
  2.9 0.5 %collective-permute-start = (f32[48,128]{1,0:T(8,128)S(1)}, f32[48,128]{1,0:T(8,128)S(1)}, u32[]{:S(2)}, u32[]{:S(2)}) collective-permute-start(f32[48,128]{1,0:T(8,128)S(1)} %get-tuple-element.29), channel_id=1, source_target_pairs={{0,1},{1,2},{2,3},{3,0},{4,5},{5,6},{6,7},{7,4},{8,9},{9,10},{10,1... | collective-permute-start | bytes 73736 | tf_op jit(solution)/shard_map/ppermute | solution.py:562
  3.4 2.0 %collective-permute-start.1 = (f32[48,128]{1,0:T(8,128)S(1)}, f32[48,128]{1,0:T(8,128)S(1)}, u32[]{:S(2)}, u32[]{:S(2)}) collective-permute-start(f32[48,128]{1,0:T(8,128)S(1)} %get-tuple-element.30), channel_id=1, source_target_pairs={{0,3},{1,0},{2,1},{3,2},{4,7},{5,4},{6,5},{7,6},{8,11},{9,8},{10,9... | collective-permute-start | bytes 73736 | tf_op jit(solution)/shard_map/ppermute | solution.py:562
  5.4 2.3 %collective-permute-start.2 = (f32[200,896]{1,0:T(8,128)S(1)}, f32[200,896]{1,0:T(8,128)S(1)}, u32[]{:S(2)}, u32[]{:S(2)}) collective-permute-start(f32[200,896]{1,0:T(8,128)S(1)} %get-tuple-element.32), channel_id=1, source_target_pairs={{0,4},{4,0},{8,12},{12,8},{1,5},{5,1},{9,13},{13,9},{2,6},{6,2},{1... | collective-permute-start | bytes 2150408 | tf_op jit(solution)/shard_map/ppermute | solution.py:567
  7.7 0.7 %collective-permute-start.3 = (f32[200,896]{1,0:T(8,128)S(1)}, f32[200,896]{1,0:T(8,128)S(1)}, u32[]{:S(2)}, u32[]{:S(2)}) collective-permute-start(f32[200,896]{1,0:T(8,128)S(1)} %get-tuple-element.33), channel_id=1, source_target_pairs={{4,8},{8,4},{5,9},{9,5},{6,10},{10,6},{7,11},{11,7},{20,24},{24,20... | collective-permute-start | bytes 2150408 | tf_op jit(solution)/shard_map/ppermute | solution.py:568
  8.4 0.0 collective-permute-done.refs_5_
  8.4 0.0 collective-permute-done.1.refs_6_
  8.4 0.0 copy-done.5
  8.5 0.0 copy-done.6
  8.5 0.0 copy-done.3
  8.5 0.0 copy-done.2
  8.5 0.0 copy-done.1
  8.5 0.0 copy-done
  8.5 0.0 copy-done.4
  8.5 10.5 %tend_inner.1 = (f32[16,16,896]{2,1,0:T(8,128)}, f32[16,16,896]{2,1,0:T(8,128)}, f32[16,16,896]{2,1,0:T(8,128)}, f32[16,16,896]{2,1,0:T(8,128)}, f32[4,160,256]{...) custom-call(f32[64]{0:T(128)S(1)} %copy-done.6, f32[64]{0:T(128)S(1)} %copy-done.5, ...), custom_call_target="tpu_custom_call" | custom-call | flops 11468800000 | bytes 4587520 | tf_op jit(solution)/shard_map/tend_inner/pallas_call | solution.py:576
  19.1 1.6 %collective-permute-start.9 = (f32[80,128]{1,0:T(8,128)S(1)}, f32[80,128]{1,0:T(8,128)S(1)}, u32[]{:S(2)}, u32[]{:S(2)}) collective-permute-start(f32[80,128]{1,0:T(8,128)S(1)} %get-tuple-element.44), channel_id=1, source_target_pairs={{0,2},{1,3},{2,0},{3,1},{4,6},{5,7},{6,4},{7,5},{8,10},{9,11},{10,... | collective-permute-start | bytes 122888 | tf_op jit(solution)/shard_map/ppermute | solution.py:562
  20.6 0.0 collective-permute-start.7
  20.6 1.7 %collective-permute-start.8 = (f32[160,128]{1,0:T(8,128)S(1)}, f32[160,128]{1,0:T(8,128)S(1)}, u32[]{:S(2)}, u32[]{:S(2)}) collective-permute-start(f32[160,128]{1,0:T(8,128)S(1)} %get-tuple-element.43), channel_id=1, source_target_pairs={{0,3},{1,0},{2,1},{3,2},{4,7},{5,4},{6,5},{7,6},{8,11},{9,8},{10,9... | collective-permute-start | bytes 245768 | tf_op jit(solution)/shard_map/ppermute | solution.py:562
  22.4 1.6 %collective-permute-done.2.refs_8_ = f32[200,896]{1,0:T(8,128)S(1)} collective-permute-done((f32[200,896]{1,0:T(8,128)S(1)}, f32[200,896]{1,0:T(8,128)S(1)}, u32[]{:S(2)}, u32[]{:S(2)}) %collective-permute-start.2) | collective-permute-done | bytes 716832 | tf_op jit(solution)/shard_map/ppermute | solution.py:567
  24.0 0.0 collective-permute-done.3.refs_9_
  24.0 7.1 %tend_edge.1 = (f32[16,16,896]{2,1,0:T(8,128)}, f32[16,16,896]{2,1,0:T(8,128)}, f32[16,16,896]{2,1,0:T(8,128)}, f32[16,16,896]{2,1,0:T(8,128)}, f32[4,96,256]{2,...) custom-call(f32[64]{0:T(128)S(1)} %copy-done.6, ...), custom_call_target="tpu_custom_call", output_to_operand_aliasing={{0}: (16, {}), {1}: (17, {}), {2}: (18, {}), {3}: (19, {})} | custom-call | flops 6881280000 | bytes 2752512 | tf_op jit(solution)/shard_map/tend_edge/pallas_call | solution.py:576
  31.1 0.1 collective-permute-start.4
  31.2 1.7 %collective-permute-start.5 = (f32[96,128]{1,0:T(8,128)S(1)}, f32[96,128]{1,0:T(8,128)S(1)}, u32[]{:S(2)}, u32[]{:S(2)}) collective-permute-start(f32[96,128]{1,0:T(8,128)S(1)} %get-tuple-element.39), channel_id=1, source_target_pairs={{0,3},{1,0},{2,1},{3,2},{4,7},{5,4},{6,5},{7,6},{8,11},{9,8},{10,9... | collective-permute-start | bytes 147464 | tf_op jit(solution)/shard_map/ppermute | solution.py:562
  32.9 0.0 collective-permute-done.9.refs_6_
  32.9 0.5 %collective-permute-start.6 = (f32[48,128]{1,0:T(8,128)S(1)}, f32[48,128]{1,0:T(8,128)S(1)}, u32[]{:S(2)}, u32[]{:S(2)}) collective-permute-start(f32[48,128]{1,0:T(8,128)S(1)} %get-tuple-element.40), channel_id=1, source_target_pairs={{0,2},{1,3},{2,0},{3,1},{4,6},{5,7},{6,4},{7,5},{8,10},{9,11},{10,... | collective-permute-start | bytes 73736 | tf_op jit(solution)/shard_map/ppermute | solution.py:562
  33.4 0.0 collective-permute-done.7.refs_4_
  33.4 0.0 collective-permute-done.8.refs_5_
  33.4 5.0 %finish_inner.1 = (f32[16,16,896]{2,1,0:T(8,128)}, f32[16,16,896]{2,1,0:T(8,128)}, f32[16,16,896]{2,1,0:T(8,128)}, f32[16,16,896]{2,1,0:T(8,128)}) custom-call(f32[16,16,896]{2,1,0:T(8,128)S(1)} %copy-done, f32[16,16,896]{2,1,0:T(8,128)S(1)} %copy-done.1, ...), custom_call_target="tpu_custom_call", output_to_operand_aliasing={{0}: (11, {}), {1}: (12, {}), {2}: (13, {}), {3}: (14, {})} | custom-call | tf_op jit(solution)/shard_map/finish_inner/pallas_call | solution.py:612
  38.3 0.0 collective-permute-done.6.refs_6_
  38.3 0.0 collective-permute-done.4.refs_4_
  38.4 0.0 collective-permute-done.5.refs_5_
  38.4 4.0 %finish_edge.1 = (f32[16,16,896]{2,1,0:T(8,128)}, f32[16,16,896]{2,1,0:T(8,128)}, f32[16,16,896]{2,1,0:T(8,128)}, f32[16,16,896]{2,1,0:T(8,128)}) custom-call(f32[16,16,896]{2,1,0:T(8,128)S(1)} %copy-done, f32[16,16,896]{2,1,0:T(8,128)S(1)} %copy-done.1, ...), custom_call_target="tpu_custom_call", output_to_operand_aliasing={{0}: (11, {}), {1}: (12, {}), {2}: (13, {}), {3}: (14, {})} | custom-call | tf_op jit(solution)/shard_map/finish_edge/pallas_call | solution.py:612
Async XLA Ops:
  0.6 7.8 %copy-start.5 = (f32[64]{0:T(128)S(1)}, f32[64]{0:T(128)}, u32[]{:S(2)}) copy-start(f32[64]{0:T(128)} %constant.26.clone.spin) | copy-start | bytes 772
  0.6 7.8 %copy-start.6 = (f32[64]{0:T(128)S(1)}, f32[64]{0:T(128)}, u32[]{:S(2)}) copy-start(f32[64]{0:T(128)} %constant.25.clone.metric) | copy-start | bytes 772
  0.7 7.8 %copy-start.3 = (f32[16,16,896]{2,1,0:T(8,128)S(1)}, f32[16,16,896]{2,1,0:T(8,128)}, u32[]{:S(2)}) copy-start(f32[16,16,896]{2,1,0:T(8,128)} %refs_3_.9) | copy-start | bytes 2752516
  0.7 7.8 %copy-start.2 = (f32[16,16,896]{2,1,0:T(8,128)S(1)}, f32[16,16,896]{2,1,0:T(8,128)}, u32[]{:S(2)}) copy-start(f32[16,16,896]{2,1,0:T(8,128)} %refs_2_.9) | copy-start | bytes 2752516
  0.7 7.8 %copy-start.1 = (f32[16,16,896]{2,1,0:T(8,128)S(1)}, f32[16,16,896]{2,1,0:T(8,128)}, u32[]{:S(2)}) copy-start(f32[16,16,896]{2,1,0:T(8,128)} %refs_1_.9) | copy-start | bytes 2752516
  0.7 7.8 %copy-start = (f32[16,16,896]{2,1,0:T(8,128)S(1)}, f32[16,16,896]{2,1,0:T(8,128)}, u32[]{:S(2)}) copy-start(f32[16,16,896]{2,1,0:T(8,128)} %refs_0_.9) | copy-start | bytes 2752516
  0.7 7.8 %copy-start.4 = (f32[16,896]{1,0:T(8,128)S(1)}, f32[16,896]{1,0:T(8,128)}, u32[]{:S(2)}) copy-start(f32[16,896]{1,0:T(8,128)} %refs_4_.5) | copy-start | bytes 172036
  2.9 5.5 %collective-permute-start = (f32[48,128]{1,0:T(8,128)S(1)}, f32[48,128]{1,0:T(8,128)S(1)}, u32[]{:S(2)}, u32[]{:S(2)}) collective-permute-start(f32[48,128]{1,0:T(8,128)S(1)} %get-tuple-element.29), channel_id=1, source_target_pairs={{0,1},{1,2},{2,3},{3,0},{4,5},{5,6},{6,7},{7,4},{8,9},{9,10},{10,1... | collective-permute-start | bytes 73736 | tf_op jit(solution)/shard_map/ppermute | solution.py:562
  3.4 5.0 %collective-permute-start.1 = (f32[48,128]{1,0:T(8,128)S(1)}, f32[48,128]{1,0:T(8,128)S(1)}, u32[]{:S(2)}, u32[]{:S(2)}) collective-permute-start(f32[48,128]{1,0:T(8,128)S(1)} %get-tuple-element.30), channel_id=1, source_target_pairs={{0,3},{1,0},{2,1},{3,2},{4,7},{5,4},{6,5},{7,6},{8,11},{9,8},{10,9... | collective-permute-start | bytes 73736 | tf_op jit(solution)/shard_map/ppermute | solution.py:562
  5.4 18.6 %collective-permute-start.2 = (f32[200,896]{1,0:T(8,128)S(1)}, f32[200,896]{1,0:T(8,128)S(1)}, u32[]{:S(2)}, u32[]{:S(2)}) collective-permute-start(f32[200,896]{1,0:T(8,128)S(1)} %get-tuple-element.32), channel_id=1, source_target_pairs={{0,4},{4,0},{8,12},{12,8},{1,5},{5,1},{9,13},{13,9},{2,6},{6,2},{1... | collective-permute-start | bytes 2150408 | tf_op jit(solution)/shard_map/ppermute | solution.py:567
  7.7 16.2 %collective-permute-start.3 = (f32[200,896]{1,0:T(8,128)S(1)}, f32[200,896]{1,0:T(8,128)S(1)}, u32[]{:S(2)}, u32[]{:S(2)}) collective-permute-start(f32[200,896]{1,0:T(8,128)S(1)} %get-tuple-element.33), channel_id=1, source_target_pairs={{4,8},{8,4},{5,9},{9,5},{6,10},{10,6},{7,11},{11,7},{20,24},{24,20... | collective-permute-start | bytes 2150408 | tf_op jit(solution)/shard_map/ppermute | solution.py:568
  19.1 13.8 %collective-permute-start.9 = (f32[80,128]{1,0:T(8,128)S(1)}, f32[80,128]{1,0:T(8,128)S(1)}, u32[]{:S(2)}, u32[]{:S(2)}) collective-permute-start(f32[80,128]{1,0:T(8,128)S(1)} %get-tuple-element.44), channel_id=1, source_target_pairs={{0,2},{1,3},{2,0},{3,1},{4,6},{5,7},{6,4},{7,5},{8,10},{9,11},{10,... | collective-permute-start | bytes 122888 | tf_op jit(solution)/shard_map/ppermute | solution.py:562
  20.6 12.7 %collective-permute-start.7 = (f32[160,128]{1,0:T(8,128)S(1)}, f32[160,128]{1,0:T(8,128)S(1)}, u32[]{:S(2)}, u32[]{:S(2)}) collective-permute-start(f32[160,128]{1,0:T(8,128)S(1)} %get-tuple-element.42), channel_id=1, source_target_pairs={{0,1},{1,2},{2,3},{3,0},{4,5},{5,6},{6,7},{7,4},{8,9},{9,10},{10,1... | collective-permute-start | bytes 245768 | tf_op jit(solution)/shard_map/ppermute | solution.py:562
  20.6 12.7 %collective-permute-start.8 = (f32[160,128]{1,0:T(8,128)S(1)}, f32[160,128]{1,0:T(8,128)S(1)}, u32[]{:S(2)}, u32[]{:S(2)}) collective-permute-start(f32[160,128]{1,0:T(8,128)S(1)} %get-tuple-element.43), channel_id=1, source_target_pairs={{0,3},{1,0},{2,1},{3,2},{4,7},{5,4},{6,5},{7,6},{8,11},{9,8},{10,9... | collective-permute-start | bytes 245768 | tf_op jit(solution)/shard_map/ppermute | solution.py:562
  31.1 7.2 %collective-permute-start.4 = (f32[96,128]{1,0:T(8,128)S(1)}, f32[96,128]{1,0:T(8,128)S(1)}, u32[]{:S(2)}, u32[]{:S(2)}) collective-permute-start(f32[96,128]{1,0:T(8,128)S(1)} %get-tuple-element.38), channel_id=1, source_target_pairs={{0,1},{1,2},{2,3},{3,0},{4,5},{5,6},{6,7},{7,4},{8,9},{9,10},{10,1... | collective-permute-start | bytes 147464 | tf_op jit(solution)/shard_map/ppermute | solution.py:562
  31.2 7.2 %collective-permute-start.5 = (f32[96,128]{1,0:T(8,128)S(1)}, f32[96,128]{1,0:T(8,128)S(1)}, u32[]{:S(2)}, u32[]{:S(2)}) collective-permute-start(f32[96,128]{1,0:T(8,128)S(1)} %get-tuple-element.39), channel_id=1, source_target_pairs={{0,3},{1,0},{2,1},{3,2},{4,7},{5,4},{6,5},{7,6},{8,11},{9,8},{10,9... | collective-permute-start | bytes 147464 | tf_op jit(solution)/shard_map/ppermute | solution.py:562
  32.9 5.4 %collective-permute-start.6 = (f32[48,128]{1,0:T(8,128)S(1)}, f32[48,128]{1,0:T(8,128)S(1)}, u32[]{:S(2)}, u32[]{:S(2)}) collective-permute-start(f32[48,128]{1,0:T(8,128)S(1)} %get-tuple-element.40), channel_id=1, source_target_pairs={{0,2},{1,3},{2,0},{3,1},{4,6},{5,7},{6,4},{7,5},{8,10},{9,11},{10,... | collective-permute-start | bytes 73736 | tf_op jit(solution)/shard_map/ppermute | solution.py:562

commit v7 on v6

--- a/solution.py
+++ b/solution.py
@@ -136,6 +136,14 @@
     return jnp.where(north, rows - 1 - entry % 3, entry % 3)
 
 
+def entry_row(inner, entry, rows):
+    if not inner:
+        return edge_row(entry, rows)
+    if isinstance(entry, int):
+        return entry + 3 if entry < rows - 6 else edge_row(entry - (rows - 6) + 3, rows)
+    return jnp.where(entry < rows - 6, entry + 3, edge_row(entry - (rows - 6) + 3, rows))
+
+
 def by_parity(even, odd):
     return jnp.where(lax.axis_index("lat") % 2 == 0, even, odd)
 
@@ -233,16 +241,14 @@
     store(mass_y, stencil(middle, plus, minus)[0] * per_mass)
 
 
-def spread_waves(waves, part, edge_rows, levels):
+def spread_waves(waves, part, inner, kept, levels):
     rows = waves.shape[1]
-    if edge_rows:
-        numbers = [edge_row(entry, rows) for entry in range(6)]
-    else:
-        numbers = range(3, rows - 3)
+    numbers = [entry_row(inner, entry, rows) for entry in range(kept)]
     return jnp.concatenate([waves[part, n] for n in numbers for _ in range(levels // 8)], axis=0)
 
 
-def tend_kernel(edge_rows, count, metric, spin, *refs):
+def tend_kernel(inner, count, kept, metric, spin, *refs):
+    edge_rows = not inner
     refs = list(refs)
 
     def some(n):
@@ -258,14 +264,16 @@
         some(4)
     outs = some(4)
     local, to_east, to_west, to_far = some(4)
-    high, low, cross, new, kept_high, kept_low, mass_x, mass_y, *tables, sems = some(13)
+    high, low, cross, new, kept_high, kept_low, mass_x, mass_y, sems = some(9)
+    tables = refs if inner else tables_in
     band, spread, own, send = tables
     rows, columns = mass.shape
     levels = fields[0].shape[1]
     items = count * levels
+    kept_items = kept * levels
     tiles = columns // LANES
 
-    fetched = start_all(zip(tables_in, tables), sems, 24)
+    fetched = start_all(zip(tables_in, tables), sems, 24) if inner else []
     if edge_rows:
         tail = 12 * levels
         lines = [strip[tail : tail + 3] for strip in strips]
@@ -278,7 +286,7 @@
     lane = lax.broadcasted_iota(jnp.int32, (levels, LANES), 1)
 
     def cut(i, carry):
-        row = edge_row(i, rows) if edge_rows else i + 3
+        row = entry_row(inner, i, rows)
         halo = pl.ds(pl.multiple_of((row % 2) * levels, levels), levels)
         for f in range(4):
             lead = 16 * (row // 2) + 3 * f
@@ -347,46 +355,50 @@
                     change = change - (spins[j] * centers[0][j] + push_y[j])
                 emit(f, first + j, span, q, change)
 
-    def all_rows(emit):
-        if edge_rows:
-            for side in range(2):
-                edge = edge_row(3 * side, rows)
-                step = jnp.where(edge == 0, 1, -1)
-
-                def row_of(f, j, span):
-                    if j < 0:
-                        first = levels * (3 * f - j - 1)
-                        return strips[side][first : first + levels, span]
-                    return fields[f][edge + step * j, :, span]
-
-                numbers = [edge + step * j for j in range(3)]
-                for t in range(tiles):
-                    tendency(t, 3 * side, numbers, row_of, emit, step.astype(F32))
-        else:
-
-            def step(n, carry):
-                first_row = 3 + 2 * n
-
-                def row_of(f, j, span):
-                    return fields[f][first_row + j, :, span]
-
-                for t in range(tiles):
-                    tendency(t, 2 * n, [first_row, first_row + 1], row_of, emit)
-                return carry
-
-            lax.fori_loop(0, count // 2, step, 0)
+    def edge_side(side, first, emit):
+        edge = edge_row(3 * side, rows)
+        step = jnp.where(edge == 0, 1, -1)
+
+        def row_of(f, j, span):
+            if j >= 0:
+                return fields[f][edge + step * j, :, span]
+            if inner:
+                return jnp.zeros((levels, LANES), F32)
+            start = levels * (3 * f - j - 1)
+            return strips[side][start : start + levels, span]
+
+        numbers = [edge + step * j for j in range(3)]
+        for t in range(tiles):
+            tendency(t, first, numbers, row_of, emit, step.astype(F32))
+
+    def inner_rows(emit):
+        def step(n, carry):
+            first_row = 3 + 2 * n
+
+            def row_of(f, j, span):
+                return fields[f][first_row + j, :, span]
+
+            for t in range(tiles):
+                tendency(t, 2 * n, [first_row, first_row + 1], row_of, emit)
+            return carry
+
+        lax.fori_loop(0, (rows - 6) // 2, step, 0)
 
     def write_out(f):
         if edge_rows:
             return [(new.at[f, n], outs[f].at[edge_row(n, rows)]) for n in range(6)]
-        return [(new.at[f], outs[f].at[3 : rows - 3])]
+        return [(new.at[f, 0 : rows - 6], outs[f].at[3 : rows - 3])]
 
     @pl.when(jnp.logical_not(is_polar()))
     def _():
         def emit(f, i, span, q, change):
             new[f, i, :, span] = q + STEP * change
 
-        all_rows(emit)
+        if inner:
+            inner_rows(emit)
+        else:
+            edge_side(0, 0, emit)
+            edge_side(1, 3, emit)
         pairs = [pair for f in range(4) for pair in write_out(f)]
         wait_all(start_all(pairs, sems))
         wait_all(fetched[1:])
@@ -398,33 +410,40 @@
             kept_high[f, i, :, span] = top
             kept_low[f, i, :, span] = (change - top.astype(F32)).astype(BF16)
 
-        all_rows(emit)
+        if inner:
+            inner_rows(emit)
+            if kept > rows - 6:
+                edge_side(1, rows - 6, emit)
+        else:
+            edge_side(0, 0, emit)
+            if kept > 3:
+                edge_side(1, 3, emit)
         wait_all(fetched[1:])
         c_all, s_all, d_all = [
-            spread_waves(waves, part, edge_rows, levels) for part in range(3)
+            spread_waves(waves, part, inner, kept, levels) for part in range(3)
         ]
-        top = kept_high[...].reshape(4 * items, columns)
-        rest = kept_low[...].reshape(4 * items, columns)
+        top = kept_high[...].reshape(4 * kept_items, columns)
+        rest = kept_low[...].reshape(4 * kept_items, columns)
         nodal = dot(jnp.concatenate([top, rest, top], axis=1), spread[...])
         turned = []
         for f in range(4):
-            part = nodal[f * items : (f + 1) * items]
+            part = nodal[f * kept_items : (f + 1) * kept_items]
             turned += [c_all * part, s_all * part]
         turned = split(jnp.concatenate(turned, axis=0))
         moved = dot(turned, own[...])
         sent = dot(turned, send[...])
         for f in range(4):
-            at = 2 * f * items
+            at = 2 * f * kept_items
             local[f] = (
-                s_all * moved[at : at + items]
-                - c_all * moved[at + items : at + 2 * items]
-                + d_all * nodal[f * items : (f + 1) * items]
+                s_all * moved[at : at + kept_items]
+                - c_all * moved[at + kept_items : at + 2 * kept_items]
+                + d_all * nodal[f * kept_items : (f + 1) * kept_items]
             )
-        wide = lax.broadcasted_iota(jnp.int32, (items, LANES), 1)
+        wide = lax.broadcasted_iota(jnp.int32, (kept_items, LANES), 1)
         for out, first, size in ((to_east, 0, NEAR), (to_west, NEAR, NEAR), (to_far, 2 * NEAR, FAR)):
-            total = jnp.zeros((items, LANES), F32)
+            total = jnp.zeros((kept_items, LANES), F32)
             for g in range(8):
-                part = sent[g * items : (g + 1) * items]
+                part = sent[g * kept_items : (g + 1) * kept_items]
                 turn = (size * g - first) % LANES
                 if turn:
                     part = pltpu.roll(part, turn, 1)
@@ -432,24 +451,22 @@
             if size == NEAR:
                 out[...] = total
             else:
-                total = total.reshape(count, 2, levels // 2, LANES)
-                upper = pltpu.roll(total[:, 1].reshape(items // 2, LANES), 64, 1)
-                out[...] = total[:, 0].reshape(items // 2, LANES) + upper
-
-
-def finish_kernel(edge_rows, count, *refs):
+                total = total.reshape(kept, 2, levels // 2, LANES)
+                upper = pltpu.roll(total[:, 1].reshape(kept_items // 2, LANES), 64, 1)
+                out[...] = total[:, 0].reshape(kept_items // 2, LANES) + upper
+
+
+def finish_kernel(inner, count, *refs):
     fields = refs[:4]
-    from_west, from_east, from_far, local, waves, take_in, gather_in = refs[4:11]
+    from_west, from_east, from_far, local, waves, take, gather = refs[4:11]
     outs = refs[15:19]
-    new, take, gather, sems = refs[19:]
+    new, sems = refs[19:]
     rows = fields[0].shape[0]
     levels, columns = new.shape[2], new.shape[3]
     items = count * levels
 
     @pl.when(is_polar())
     def _():
-        fetched = start_all([(take_in, take), (gather_in, gather)], sems, 24)
-
         place = lax.axis_index("lon")
         last = lax.axis_size("lon") - 1
         near_west = from_west[...] * jnp.where(place == 0, -1.0, 1.0)
@@ -471,10 +488,8 @@
             part = jnp.where(wide < MESSAGE, part, 0.0)
             top = part.astype(BF16).astype(F32)
             come.append((top + turn(part - top, MESSAGE) + turn(top, 2 * MESSAGE)).astype(BF16))
-        wait_all(fetched[:1])
         moved = dot(jnp.concatenate(come, axis=0), take[...])
-        c_all, s_all = [spread_waves(waves, part, edge_rows, levels) for part in range(2)]
-        wait_all(fetched[1:])
+        c_all, s_all = [spread_waves(waves, part, inner, count, levels) for part in range(2)]
         writes = []
         for half in range(2):
             value = []
@@ -487,14 +502,13 @@
             change = change.reshape(2, count, levels, columns)
             pairs = []
             for f in (2 * half, 2 * half + 1):
-                if edge_rows:
-                    for n in range(6):
-                        row = edge_row(n, rows)
-                        new[f, n] = fields[f][row] + change[f % 2, n]
-                        pairs.append((new.at[f, n], outs[f].at[row]))
-                else:
-                    new[f] = fields[f][3 : rows - 3] + change[f % 2]
-                    pairs.append((new.at[f], outs[f].at[3 : rows - 3]))
+                for n in range(count):
+                    new[f, n] = fields[f][entry_row(inner, n, rows)] + change[f % 2, n]
+                off_edge = rows - 6 if inner else 0
+                if inner:
+                    pairs.append((new.at[f, 0:off_edge], outs[f].at[3 : rows - 3]))
+                for n in range(off_edge, count):
+                    pairs.append((new.at[f, n], outs[f].at[entry_row(inner, n, rows)]))
             writes += start_all(pairs, sems, 12 * half)
         wait_all(writes)
 
@@ -535,7 +549,7 @@
     lat_count = lax.axis_size("lat")
     lon_count = lax.axis_size("lon")
     tables = filter_tables(columns, columns * lon_count)
-    tables = {k: in_hbm(jnp.asarray(v)) for k, v in tables.items()}
+    tables = {k: jnp.asarray(v) for k, v in tables.items()}
     metric, spin = [jnp.asarray(t) for t in row_factors(rows * lat_count)]
     fields = (u_wind, v_wind, theta, geopot)
 
@@ -556,7 +570,7 @@
         ],
         compiler_params=params(8),
         name="pack_edges",
-    )(*far_fields, in_hbm(cutoffs), tables["nodes"])
+    )(*far_fields, in_hbm(cutoffs), in_hbm(tables["nodes"]))
 
     def ring(value, step):
         return lax.ppermute(value, "lon", [(i, (i + step) % lon_count) for i in range(lon_count)])
@@ -567,69 +581,76 @@
     strip_a = lax.ppermute(to_a, "lat", [(i, i ^ 1) for i in range(lat_count)])
     strip_b = lax.ppermute(to_b, "lat", odd_up + [(j, i) for i, j in odd_up])
 
-    def tendencies(edge_rows, old):
-        count = 6 if edge_rows else rows - 6
-        items = count * levels
-        halos = [strip_a, strip_b] if edge_rows else []
+    at_poles = lat_count == 4
+    inner_count = rows - 3 if at_poles else rows - 6
+    edge_kept = 3 if at_poles else 6
+
+    def tendencies(inner, old):
+        count, kept = (inner_count, inner_count) if inner else (6, edge_kept)
+        kept_items = kept * levels
+        halos = [] if inner else [strip_a, strip_b]
         weights = [tables[k] for k in ("band", "spread", "own", "send")]
+        if inner:
+            weights = [in_hbm(w) for w in weights]
         args = [metric, spin, *fields, mass, west, east, waves, *halos, *weights]
         return pl.pallas_call(
-            functools.partial(tend_kernel, edge_rows, count),
+            functools.partial(tend_kernel, inner, count, kept),
             out_shape=[like(rows, levels, columns)] * 4
-            + [like(4, items, NODES)]
-            + [like(items, LANES)] * 2
-            + [like(items // 2, LANES)],
-            in_specs=[smem()] * 2 + [vmem()] * (len(args) - 6) + [anywhere()] * (4 + len(old)),
+            + [like(4, kept_items, NODES)]
+            + [like(kept_items, LANES)] * 2
+            + [like(kept_items // 2, LANES)],
+            in_specs=[smem()] * 2
+            + [vmem()] * (len(args) - 6)
+            + [anywhere() if inner else vmem()] * 4
+            + [anywhere()] * len(old),
             out_specs=[anywhere()] * 4 + [vmem()] * 4,
             scratch_shapes=[
                 pltpu.VMEM((4, count, levels, columns + LANES), BF16),
                 pltpu.VMEM((4, count, levels, columns + LANES), BF16),
                 pltpu.VMEM((columns // LANES, 4, count, levels, 2 * LANES), F32),
                 pltpu.VMEM((4, count, levels, columns), F32),
-                pltpu.VMEM((4, count, levels, columns), BF16),
-                pltpu.VMEM((4, count, levels, columns), BF16),
+                pltpu.VMEM((4, kept, levels, columns), BF16),
+                pltpu.VMEM((4, kept, levels, columns), BF16),
                 pltpu.VMEM((rows, 8, columns), F32),
                 pltpu.VMEM((rows, 8, columns), F32),
-                *[pltpu.VMEM(w.shape, w.dtype) for w in weights],
                 pltpu.SemaphoreType.DMA((28,)),
+                *[pltpu.VMEM(w.shape, w.dtype) for w in weights if inner],
             ],
             input_output_aliases={len(args) + f: f for f in range(4)} if old else {},
-            compiler_params=params(36),
+            compiler_params=params(40),
             cost_estimate=pl.CostEstimate(
-                flops=items * 4 * columns * 20000, bytes_accessed=8 * items * columns * 4, transcendentals=0
+                flops=count * levels * 4 * columns * 20000, bytes_accessed=2**22, transcendentals=0
             ),
-            name="tend_edge" if edge_rows else "tend_inner",
+            name="tend_inner" if inner else "tend_edge",
         )(*args, *old)
 
     def exchange(east_part, west_part, far_part):
         return ring(east_part, 1), ring(west_part, -1), ring(far_part, 2)
 
-    def finish(edge_rows, received, local, old):
-        count = 6 if edge_rows else rows - 6
-        items = count * levels
+    def finish(inner, received, local, old):
+        count = inner_count if inner else edge_kept
         weights = [tables[k] for k in ("take", "gather")]
         args = [*fields, *received, local, waves, *weights]
         return pl.pallas_call(
-            functools.partial(finish_kernel, edge_rows, count),
+            functools.partial(finish_kernel, inner, count),
             out_shape=[like(rows, levels, columns)] * 4,
-            in_specs=[vmem()] * (len(args) - 2) + [anywhere()] * 6,
+            in_specs=[vmem()] * len(args) + [anywhere()] * 4,
             out_specs=[anywhere()] * 4,
             scratch_shapes=[
                 pltpu.VMEM((4, count, levels, columns), F32),
-                *[pltpu.VMEM(w.shape, w.dtype) for w in weights],
-                pltpu.SemaphoreType.DMA((26,)),
+                pltpu.SemaphoreType.DMA((24,)),
             ],
             input_output_aliases={len(args) + f: f for f in range(4)},
             compiler_params=params(24),
-            name="finish_edge" if edge_rows else "finish_inner",
+            name="finish_inner" if inner else "finish_edge",
         )(*args, *old)
 
-    *outs, local_inner, a, b, c = tendencies(False, [])
+    *outs, local_inner, a, b, c = tendencies(True, [])
     received_inner = exchange(a, b, c)
-    *outs, local_edge, a, b, c = tendencies(True, outs)
+    *outs, local_edge, a, b, c = tendencies(False, outs)
     received_edge = exchange(a, b, c)
-    outs = finish(False, received_inner, local_inner, outs)
-    outs = finish(True, received_edge, local_edge, outs)
+    outs = finish(True, received_inner, local_inner, outs)
+    outs = finish(False, received_edge, local_edge, outs)
     return tuple(outs)
 
 

time: 42.8 us -> 38.9 us (0.909)
  Pallas kernels: 28.9 us -> 26.4 us
  waiting for transfers between devices: 1.61 us -> 0.03 us
    pallas_call x4, Pallas kernels: 26.7 us -> 24.2 us  [the longest x2 18.5 us: tendencies(): pl.pallas_call(functools.partial(tend_kernel, inner, count, kept), out_sh...]
    ppermute x1, waiting for transfers between devices: 1.59 us -> 0.01 us  [shards(): strip_a = lax.ppermute(to_a, 'lat', [(i, i ^ 1) for i in range(lat_count)])]
  transfers between devices with their start and end apart: 10 -> 10, of which waited for: 1 -> 0; matrix products, arithmetic and copies ran while one was open for 0% -> 0% of each run, Pallas kernels for 53% -> 58%
where the time goes in v7:
time: 38.9 us; the launch traced here: 38.7 us
  Pallas kernels  26.4 us (68%)
  starting transfers between devices  11.1 us (29%)
  between operations  1.08 us (3%)
    pallas_call x2, Pallas kernels, tendencies(): pl.pallas_call(functools.partial(tend_kernel, inner, count, kept), out_sh...  18.5 us
    ppermute x8, starting transfers between devices, ring(): lax.ppermute(value, 'lon', [(i, (i + step) % lon_count) for i in range(lo...  8.12 us
    pallas_call x2, Pallas kernels, finish(): pl.pallas_call(functools.partial(finish_kernel, inner, count), out_shape=...  5.71 us
    ppermute x1, starting transfers between devices, shards(): strip_a = lax.ppermute(to_a, 'lat', [(i, i ^ 1) for i in range(lat_count)])  2.33 us
    pallas_call x1, Pallas kernels, shards(): pl.pallas_call(pack_kernel, out_shape=[like(strip, columns)] * 2 + [like(...  2.18 us
  transfers between devices with their start and end apart: 10, of which 0 were waited for; matrix products, arithmetic and copies ran while one was open for 0% of the time, Pallas kernels for 58%

profile of v7, /device:TPU:0, one launch (start us, length us, event | category | flops | bytes accessed | tf_op | source)
XLA Modules:
  0.0 38.7 jit_solution(6008700576548817218)
XLA Ops:
  0.6 0.0 copy-start.11
  0.6 0.0 copy-start.12
  0.7 0.0 copy-start.3
  0.7 0.0 copy-start.2
  0.7 0.0 copy-start.1
  0.7 0.0 copy-start
  0.7 0.0 copy-start.6
  0.7 2.2 %pack_edges.1 = (f32[200,896]{1,0:T(8,128)S(1)}, f32[200,896]{1,0:T(8,128)S(1)}, f32[48,128]{1,0:T(8,128)S(1)}, f32[48,128]{1,0:T(8,128)S(1)}, f32[3,16,8,256]{3,2,1,0:T(8,128)S(1)}) custom-call(f32[16,16,896]{2,1,0:T(8,128)} %refs_0_.9, f32[16,16,896]{2,1,0:T(8,128)} %refs_1_.9, f32[16,16,896]{2,1,0:T(8,128)} %refs_2_.9, f32[16,16,896]{2,1,0:T(8,128)} %refs_3_.9, ...), custom_call_target="tpu_custom_call" | custom-call | tf_op jit(solution)/shard_map/pack_edges/pallas_call | solution.py:559
  2.9 0.5 %collective-permute-start = (f32[48,128]{1,0:T(8,128)S(1)}, f32[48,128]{1,0:T(8,128)S(1)}, u32[]{:S(2)}, u32[]{:S(2)}) collective-permute-start(f32[48,128]{1,0:T(8,128)S(1)} %get-tuple-element.29), channel_id=1, source_target_pairs={{0,1},{1,2},{2,3},{3,0},{4,5},{5,6},{6,7},{7,4},{8,9},{9,10},{10,1... | collective-permute-start | bytes 73736 | tf_op jit(solution)/shard_map/ppermute | solution.py:576
  3.4 2.0 %collective-permute-start.1 = (f32[48,128]{1,0:T(8,128)S(1)}, f32[48,128]{1,0:T(8,128)S(1)}, u32[]{:S(2)}, u32[]{:S(2)}) collective-permute-start(f32[48,128]{1,0:T(8,128)S(1)} %get-tuple-element.30), channel_id=1, source_target_pairs={{0,3},{1,0},{2,1},{3,2},{4,7},{5,4},{6,5},{7,6},{8,11},{9,8},{10,9... | collective-permute-start | bytes 73736 | tf_op jit(solution)/shard_map/ppermute | solution.py:576
  5.4 2.3 %collective-permute-start.2 = (f32[200,896]{1,0:T(8,128)S(1)}, f32[200,896]{1,0:T(8,128)S(1)}, u32[]{:S(2)}, u32[]{:S(2)}) collective-permute-start(f32[200,896]{1,0:T(8,128)S(1)} %get-tuple-element.32), channel_id=1, source_target_pairs={{0,4},{4,0},{8,12},{12,8},{1,5},{5,1},{9,13},{13,9},{2,6},{6,2},{1... | collective-permute-start | bytes 2150408 | tf_op jit(solution)/shard_map/ppermute | solution.py:581
  7.7 0.7 %collective-permute-start.3 = (f32[200,896]{1,0:T(8,128)S(1)}, f32[200,896]{1,0:T(8,128)S(1)}, u32[]{:S(2)}, u32[]{:S(2)}) collective-permute-start(f32[200,896]{1,0:T(8,128)S(1)} %get-tuple-element.33), channel_id=1, source_target_pairs={{4,8},{8,4},{5,9},{9,5},{6,10},{10,6},{7,11},{11,7},{20,24},{24,20... | collective-permute-start | bytes 2150408 | tf_op jit(solution)/shard_map/ppermute | solution.py:582
  8.4 0.0 collective-permute-done.refs_5_
  8.4 0.0 collective-permute-done.1.refs_6_
  8.4 0.0 copy-done.11
  8.5 0.0 copy-done.12
  8.5 0.0 copy-done.3
  8.5 0.0 copy-done.2
  8.5 0.0 copy-done.1
  8.5 0.0 copy-done
  8.5 0.0 copy-done.6
  8.5 0.0 copy-start.7
  8.5 0.0 copy-start.8
  8.5 0.0 copy-start.9
  8.6 0.0 copy-start.10
  8.6 13.3 %tend_inner.1 = (f32[16,16,896]{2,1,0:T(8,128)}, f32[16,16,896]{2,1,0:T(8,128)}, f32[16,16,896]{2,1,0:T(8,128)}, f32[16,16,896]{2,1,0:T(8,128)}, f32[4,208,256]{...) custom-call(f32[64]{0:T(128)S(1)} %copy-done.12, f32[64]{0:T(128)S(1)} %copy-done.11, ...), custom_call_target="tpu_custom_call" | custom-call | flops 14909440000 | bytes 4194304 | tf_op jit(solution)/shard_map/tend_inner/pallas_call | solution.py:596
  21.9 1.6 %collective-permute-start.9 = (f32[104,128]{1,0:T(8,128)S(1)}, f32[104,128]{1,0:T(8,128)S(1)}, u32[]{:S(2)}, u32[]{:S(2)}) collective-permute-start(f32[104,128]{1,0:T(8,128)S(1)} %get-tuple-element.44), channel_id=1, source_target_pairs={{0,2},{1,3},{2,0},{3,1},{4,6},{5,7},{6,4},{7,5},{8,10},{9,11},{10,... | collective-permute-start | bytes 159752 | tf_op jit(solution)/shard_map/ppermute | solution.py:576
  23.5 0.0 collective-permute-start.7
  23.5 1.7 %collective-permute-start.8 = (f32[208,128]{1,0:T(8,128)S(1)}, f32[208,128]{1,0:T(8,128)S(1)}, u32[]{:S(2)}, u32[]{:S(2)}) collective-permute-start(f32[208,128]{1,0:T(8,128)S(1)} %get-tuple-element.43), channel_id=1, source_target_pairs={{0,3},{1,0},{2,1},{3,2},{4,7},{5,4},{6,5},{7,6},{8,11},{9,8},{10,9... | collective-permute-start | bytes 319496 | tf_op jit(solution)/shard_map/ppermute | solution.py:576
  25.2 0.0 collective-permute-done.2.refs_8_
  25.2 0.0 collective-permute-done.3.refs_9_
  25.2 0.0 copy-done.7
  25.2 0.0 copy-done.8
  25.2 0.0 copy-done.9
  25.3 0.0 copy-done.10
  25.3 0.0 copy-start.4
  25.3 0.0 copy-start.5
  25.3 5.1 %tend_edge.1 = (f32[16,16,896]{2,1,0:T(8,128)}, f32[16,16,896]{2,1,0:T(8,128)}, f32[16,16,896]{2,1,0:T(8,128)}, f32[16,16,896]{2,1,0:T(8,128)}, f32[4,48,256]{2,...) custom-call(f32[64]{0:T(128)S(1)} %copy-done.12, ...), custom_call_target="tpu_custom_call", output_to_operand_aliasing={{0}: (16, {}), {1}: (17, {}), {2}: (18, {}), {3}: (19, {})} | custom-call | flops 6881280000 | bytes 4194304 | tf_op jit(solution)/shard_map/tend_edge/pallas_call | solution.py:596
  30.4 0.1 collective-permute-start.4
  30.5 1.7 %collective-permute-start.5 = (f32[48,128]{1,0:T(8,128)S(1)}, f32[48,128]{1,0:T(8,128)S(1)}, u32[]{:S(2)}, u32[]{:S(2)}) collective-permute-start(f32[48,128]{1,0:T(8,128)S(1)} %get-tuple-element.39), channel_id=1, source_target_pairs={{0,3},{1,0},{2,1},{3,2},{4,7},{5,4},{6,5},{7,6},{8,11},{9,8},{10,9... | collective-permute-start | bytes 73736 | tf_op jit(solution)/shard_map/ppermute | solution.py:576
  32.2 0.0 collective-permute-done.9.refs_6_
  32.2 0.5 %collective-permute-start.6 = (f32[24,128]{1,0:T(8,128)S(1)}, f32[24,128]{1,0:T(8,128)S(1)}, u32[]{:S(2)}, u32[]{:S(2)}) collective-permute-start(f32[24,128]{1,0:T(8,128)S(1)} %get-tuple-element.40), channel_id=1, source_target_pairs={{0,2},{1,3},{2,0},{3,1},{4,6},{5,7},{6,4},{7,5},{8,10},{9,11},{10,... | collective-permute-start | bytes 36872 | tf_op jit(solution)/shard_map/ppermute | solution.py:576
  32.8 0.0 collective-permute-done.7.refs_4_
  32.8 0.0 collective-permute-done.8.refs_5_
  32.8 0.0 copy-done.4
  32.8 0.0 copy-done.5
  32.8 3.8 %finish_inner.1 = (f32[16,16,896]{2,1,0:T(8,128)}, f32[16,16,896]{2,1,0:T(8,128)}, f32[16,16,896]{2,1,0:T(8,128)}, f32[16,16,896]{2,1,0:T(8,128)}) custom-call(f32[16,16,896]{2,1,0:T(8,128)S(1)} %copy-done, f32[16,16,896]{2,1,0:T(8,128)S(1)} %copy-done.1, ...), custom_call_target="tpu_custom_call", output_to_operand_aliasing={{0}: (11, {}), {1}: (12, {}), {2}: (13, {}), {3}: (14, {})} | custom-call | tf_op jit(solution)/shard_map/finish_inner/pallas_call | solution.py:634
  36.6 0.0 collective-permute-done.6.refs_6_
  36.6 0.0 collective-permute-done.4.refs_4_
  36.6 0.0 collective-permute-done.5.refs_5_
  36.6 1.9 %finish_edge.1 = (f32[16,16,896]{2,1,0:T(8,128)}, f32[16,16,896]{2,1,0:T(8,128)}, f32[16,16,896]{2,1,0:T(8,128)}, f32[16,16,896]{2,1,0:T(8,128)}) custom-call(f32[16,16,896]{2,1,0:T(8,128)S(1)} %copy-done, f32[16,16,896]{2,1,0:T(8,128)S(1)} %copy-done.1, ...), custom_call_target="tpu_custom_call", output_to_operand_aliasing={{0}: (11, {}), {1}: (12, {}), {2}: (13, {}), {3}: (14, {})} | custom-call | tf_op jit(solution)/shard_map/finish_edge/pallas_call | solution.py:634
Async XLA Ops:
  0.6 7.8 %copy-start.11 = (f32[64]{0:T(128)S(1)}, f32[64]{0:T(128)}, u32[]{:S(2)}) copy-start(f32[64]{0:T(128)} %constant.26.clone.spin) | copy-start | bytes 772
  0.6 7.8 %copy-start.12 = (f32[64]{0:T(128)S(1)}, f32[64]{0:T(128)}, u32[]{:S(2)}) copy-start(f32[64]{0:T(128)} %constant.25.clone.metric) | copy-start | bytes 772
  0.7 7.8 %copy-start.3 = (f32[16,16,896]{2,1,0:T(8,128)S(1)}, f32[16,16,896]{2,1,0:T(8,128)}, u32[]{:S(2)}) copy-start(f32[16,16,896]{2,1,0:T(8,128)} %refs_3_.9) | copy-start | bytes 2752516
  0.7 7.8 %copy-start.2 = (f32[16,16,896]{2,1,0:T(8,128)S(1)}, f32[16,16,896]{2,1,0:T(8,128)}, u32[]{:S(2)}) copy-start(f32[16,16,896]{2,1,0:T(8,128)} %refs_2_.9) | copy-start | bytes 2752516
  0.7 7.8 %copy-start.1 = (f32[16,16,896]{2,1,0:T(8,128)S(1)}, f32[16,16,896]{2,1,0:T(8,128)}, u32[]{:S(2)}) copy-start(f32[16,16,896]{2,1,0:T(8,128)} %refs_1_.9) | copy-start | bytes 2752516
  0.7 7.8 %copy-start = (f32[16,16,896]{2,1,0:T(8,128)S(1)}, f32[16,16,896]{2,1,0:T(8,128)}, u32[]{:S(2)}) copy-start(f32[16,16,896]{2,1,0:T(8,128)} %refs_0_.9) | copy-start | bytes 2752516
  0.7 7.8 %copy-start.6 = (f32[16,896]{1,0:T(8,128)S(1)}, f32[16,896]{1,0:T(8,128)}, u32[]{:S(2)}) copy-start(f32[16,896]{1,0:T(8,128)} %refs_4_.5) | copy-start | bytes 172036
  2.9 5.5 %collective-permute-start = (f32[48,128]{1,0:T(8,128)S(1)}, f32[48,128]{1,0:T(8,128)S(1)}, u32[]{:S(2)}, u32[]{:S(2)}) collective-permute-start(f32[48,128]{1,0:T(8,128)S(1)} %get-tuple-element.29), channel_id=1, source_target_pairs={{0,1},{1,2},{2,3},{3,0},{4,5},{5,6},{6,7},{7,4},{8,9},{9,10},{10,1... | collective-permute-start | bytes 73736 | tf_op jit(solution)/shard_map/ppermute | solution.py:576
  3.4 5.0 %collective-permute-start.1 = (f32[48,128]{1,0:T(8,128)S(1)}, f32[48,128]{1,0:T(8,128)S(1)}, u32[]{:S(2)}, u32[]{:S(2)}) collective-permute-start(f32[48,128]{1,0:T(8,128)S(1)} %get-tuple-element.30), channel_id=1, source_target_pairs={{0,3},{1,0},{2,1},{3,2},{4,7},{5,4},{6,5},{7,6},{8,11},{9,8},{10,9... | collective-permute-start | bytes 73736 | tf_op jit(solution)/shard_map/ppermute | solution.py:576
  5.4 19.8 %collective-permute-start.2 = (f32[200,896]{1,0:T(8,128)S(1)}, f32[200,896]{1,0:T(8,128)S(1)}, u32[]{:S(2)}, u32[]{:S(2)}) collective-permute-start(f32[200,896]{1,0:T(8,128)S(1)} %get-tuple-element.32), channel_id=1, source_target_pairs={{0,4},{4,0},{8,12},{12,8},{1,5},{5,1},{9,13},{13,9},{2,6},{6,2},{1... | collective-permute-start | bytes 2150408 | tf_op jit(solution)/shard_map/ppermute | solution.py:581
  7.7 17.5 %collective-permute-start.3 = (f32[200,896]{1,0:T(8,128)S(1)}, f32[200,896]{1,0:T(8,128)S(1)}, u32[]{:S(2)}, u32[]{:S(2)}) collective-permute-start(f32[200,896]{1,0:T(8,128)S(1)} %get-tuple-element.33), channel_id=1, source_target_pairs={{4,8},{8,4},{5,9},{9,5},{6,10},{10,6},{7,11},{11,7},{20,24},{24,20... | collective-permute-start | bytes 2150408 | tf_op jit(solution)/shard_map/ppermute | solution.py:582
  8.5 16.7 %copy-start.7 = (bf16[2688,256]{1,0:T(8,128)(2,1)S(1)}, bf16[2688,256]{1,0:T(8,128)(2,1)}, u32[]{:S(2)}) copy-start(bf16[2688,256]{1,0:T(8,128)(2,1)} %constant.20.clone.refs_9_.refs_11_) | copy-start | bytes 4128772
  8.5 16.7 %copy-start.8 = (bf16[768,256]{1,0:T(8,128)(2,1)S(1)}, bf16[768,256]{1,0:T(8,128)(2,1)}, u32[]{:S(2)}) copy-start(bf16[768,256]{1,0:T(8,128)(2,1)} %constant.21.clone.refs_10_.refs_12_) | copy-start | bytes 1179652
  8.5 16.7 %copy-start.9 = (bf16[512,256]{1,0:T(8,128)(2,1)S(1)}, bf16[512,256]{1,0:T(8,128)(2,1)}, u32[]{:S(2)}) copy-start(bf16[512,256]{1,0:T(8,128)(2,1)} %constant.19.clone.refs_8_.refs_10_) | copy-start | bytes 786436
  8.6 16.7 %copy-start.10 = (bf16[768,128]{1,0:T(8,128)(2,1)S(1)}, bf16[768,128]{1,0:T(8,128)(2,1)}, u32[]{:S(2)}) copy-start(bf16[768,128]{1,0:T(8,128)(2,1)} %constant.22.clone.refs_11_.refs_13_) | copy-start | bytes 589828
  21.9 10.3 %collective-permute-start.9 = (f32[104,128]{1,0:T(8,128)S(1)}, f32[104,128]{1,0:T(8,128)S(1)}, u32[]{:S(2)}, u32[]{:S(2)}) collective-permute-start(f32[104,128]{1,0:T(8,128)S(1)} %get-tuple-element.44), channel_id=1, source_target_pairs={{0,2},{1,3},{2,0},{3,1},{4,6},{5,7},{6,4},{7,5},{8,10},{9,11},{10,... | collective-permute-start | bytes 159752 | tf_op jit(solution)/shard_map/ppermute | solution.py:576
  23.5 9.3 %collective-permute-start.7 = (f32[208,128]{1,0:T(8,128)S(1)}, f32[208,128]{1,0:T(8,128)S(1)}, u32[]{:S(2)}, u32[]{:S(2)}) collective-permute-start(f32[208,128]{1,0:T(8,128)S(1)} %get-tuple-element.42), channel_id=1, source_target_pairs={{0,1},{1,2},{2,3},{3,0},{4,5},{5,6},{6,7},{7,4},{8,9},{9,10},{10,1... | collective-permute-start | bytes 319496 | tf_op jit(solution)/shard_map/ppermute | solution.py:576
  23.5 9.3 %collective-permute-start.8 = (f32[208,128]{1,0:T(8,128)S(1)}, f32[208,128]{1,0:T(8,128)S(1)}, u32[]{:S(2)}, u32[]{:S(2)}) collective-permute-start(f32[208,128]{1,0:T(8,128)S(1)} %get-tuple-element.43), channel_id=1, source_target_pairs={{0,3},{1,0},{2,1},{3,2},{4,7},{5,4},{6,5},{7,6},{8,11},{9,8},{10,9... | collective-permute-start | bytes 319496 | tf_op jit(solution)/shard_map/ppermute | solution.py:576
  25.3 7.5 %copy-start.4 = (bf16[768,896]{1,0:T(8,128)(2,1)S(1)}, bf16[768,896]{1,0:T(8,128)(2,1)}, u32[]{:S(2)}) copy-start(bf16[768,896]{1,0:T(8,128)(2,1)} %constant.24.clone.refs_10_) | copy-start | bytes 4128772
  25.3 7.5 %copy-start.5 = (bf16[128,256]{1,0:T(8,128)(2,1)S(1)}, bf16[128,256]{1,0:T(8,128)(2,1)}, u32[]{:S(2)}) copy-start(bf16[128,256]{1,0:T(8,128)(2,1)} %constant.23.clone.refs_9_) | copy-start | bytes 196612
  30.4 6.2 %collective-permute-start.4 = (f32[48,128]{1,0:T(8,128)S(1)}, f32[48,128]{1,0:T(8,128)S(1)}, u32[]{:S(2)}, u32[]{:S(2)}) collective-permute-start(f32[48,128]{1,0:T(8,128)S(1)} %get-tuple-element.38), channel_id=1, source_target_pairs={{0,1},{1,2},{2,3},{3,0},{4,5},{5,6},{6,7},{7,4},{8,9},{9,10},{10,1... | collective-permute-start | bytes 73736 | tf_op jit(solution)/shard_map/ppermute | solution.py:576
  30.5 6.1 %collective-permute-start.5 = (f32[48,128]{1,0:T(8,128)S(1)}, f32[48,128]{1,0:T(8,128)S(1)}, u32[]{:S(2)}, u32[]{:S(2)}) collective-permute-start(f32[48,128]{1,0:T(8,128)S(1)} %get-tuple-element.39), channel_id=1, source_target_pairs={{0,3},{1,0},{2,1},{3,2},{4,7},{5,4},{6,5},{7,6},{8,11},{9,8},{10,9... | collective-permute-start | bytes 73736 | tf_op jit(solution)/shard_map/ppermute | solution.py:576
  32.2 4.4 %collective-permute-start.6 = (f32[24,128]{1,0:T(8,128)S(1)}, f32[24,128]{1,0:T(8,128)S(1)}, u32[]{:S(2)}, u32[]{:S(2)}) collective-permute-start(f32[24,128]{1,0:T(8,128)S(1)} %get-tuple-element.40), channel_id=1, source_target_pairs={{0,2},{1,3},{2,0},{3,1},{4,6},{5,7},{6,4},{7,5},{8,10},{9,11},{10,... | collective-permute-start | bytes 36872 | tf_op jit(solution)/shard_map/ppermute | solution.py:576

commit v8 on v7

--- a/solution.py
+++ b/solution.py
@@ -263,7 +263,7 @@
     if edge_rows:
         some(4)
     outs = some(4)
-    local, to_east, to_west, to_far = some(4)
+    local, messages = some(2)
     high, low, cross, new, kept_high, kept_low, mass_x, mass_y, sems = some(9)
     tables = refs if inner else tables_in
     band, spread, own, send = tables
@@ -440,7 +440,8 @@
                 + d_all * nodal[f * kept_items : (f + 1) * kept_items]
             )
         wide = lax.broadcasted_iota(jnp.int32, (kept_items, LANES), 1)
-        for out, first, size in ((to_east, 0, NEAR), (to_west, NEAR, NEAR), (to_far, 2 * NEAR, FAR)):
+        place = lax.axis_index("lon")
+        for ahead, first, size in ((1, 0, NEAR), (3, NEAR, NEAR), (2, 2 * NEAR, FAR)):
             total = jnp.zeros((kept_items, LANES), F32)
             for g in range(8):
                 part = sent[g * kept_items : (g + 1) * kept_items]
@@ -448,19 +449,14 @@
                 if turn:
                     part = pltpu.roll(part, turn, 1)
                 total = jnp.where((wide >= size * g) & (wide < size * (g + 1)), part, total)
-            if size == NEAR:
-                out[...] = total
-            else:
-                total = total.reshape(kept, 2, levels // 2, LANES)
-                upper = pltpu.roll(total[:, 1].reshape(kept_items // 2, LANES), 64, 1)
-                out[...] = total[:, 0].reshape(kept_items // 2, LANES) + upper
+            messages[lax.rem(place + ahead, 4)] = total
 
 
 def finish_kernel(inner, count, *refs):
     fields = refs[:4]
-    from_west, from_east, from_far, local, waves, take, gather = refs[4:11]
-    outs = refs[15:19]
-    new, sems = refs[19:]
+    messages, local, waves, take, gather = refs[4:9]
+    outs = refs[13:17]
+    new, sems = refs[17:]
     rows = fields[0].shape[0]
     levels, columns = new.shape[2], new.shape[3]
     items = count * levels
@@ -468,13 +464,9 @@
     @pl.when(is_polar())
     def _():
         place = lax.axis_index("lon")
-        last = lax.axis_size("lon") - 1
-        near_west = from_west[...] * jnp.where(place == 0, -1.0, 1.0)
-        near_east = from_east[...] * jnp.where(place == last, -1.0, 1.0)
-        far = from_far[...] * jnp.where(place < 2, -1.0, 1.0)
-        far = far.reshape(count, 1, levels // 2, LANES)
-        upper = pltpu.roll(far.reshape(items // 2, LANES), 64, 1).reshape(count, 1, levels // 2, LANES)
-        far = jnp.concatenate([far, upper], axis=1).reshape(items, LANES)
+        near_west = messages[lax.rem(place + 3, 4)] * jnp.where(place == 0, -1.0, 1.0)
+        near_east = messages[lax.rem(place + 1, 4)] * jnp.where(place == 3, -1.0, 1.0)
+        far = messages[lax.rem(place + 2, 4)] * jnp.where(place < 2, -1.0, 1.0)
         wide = lax.broadcasted_iota(jnp.int32, (items, LANES), 1)
 
         def turn(value, by):
@@ -597,13 +589,12 @@
             functools.partial(tend_kernel, inner, count, kept),
             out_shape=[like(rows, levels, columns)] * 4
             + [like(4, kept_items, NODES)]
-            + [like(kept_items, LANES)] * 2
-            + [like(kept_items // 2, LANES)],
+            + [like(lon_count, kept_items, LANES)],
             in_specs=[smem()] * 2
             + [vmem()] * (len(args) - 6)
             + [anywhere() if inner else vmem()] * 4
             + [anywhere()] * len(old),
-            out_specs=[anywhere()] * 4 + [vmem()] * 4,
+            out_specs=[anywhere()] * 4 + [vmem()] * 2,
             scratch_shapes=[
                 pltpu.VMEM((4, count, levels, columns + LANES), BF16),
                 pltpu.VMEM((4, count, levels, columns + LANES), BF16),
@@ -624,13 +615,13 @@
             name="tend_inner" if inner else "tend_edge",
         )(*args, *old)
 
-    def exchange(east_part, west_part, far_part):
-        return ring(east_part, 1), ring(west_part, -1), ring(far_part, 2)
+    def exchange(messages):
+        return lax.all_to_all(messages, "lon", split_axis=0, concat_axis=0, tiled=True)
 
     def finish(inner, received, local, old):
         count = inner_count if inner else edge_kept
         weights = [tables[k] for k in ("take", "gather")]
-        args = [*fields, *received, local, waves, *weights]
+        args = [*fields, received, local, waves, *weights]
         return pl.pallas_call(
             functools.partial(finish_kernel, inner, count),
             out_shape=[like(rows, levels, columns)] * 4,
@@ -645,10 +636,10 @@
             name="finish_inner" if inner else "finish_edge",
         )(*args, *old)
 
-    *outs, local_inner, a, b, c = tendencies(True, [])
-    received_inner = exchange(a, b, c)
-    *outs, local_edge, a, b, c = tendencies(False, outs)
-    received_edge = exchange(a, b, c)
+    *outs, local_inner, messages = tendencies(True, [])
+    received_inner = exchange(messages)
+    *outs, local_edge, messages = tendencies(False, outs)
+    received_edge = exchange(messages)
     outs = finish(True, received_inner, local_inner, outs)
     outs = finish(False, received_edge, local_edge, outs)
     return tuple(outs)

time: 38.9 us -> 62.4 us (1.60); the launches traced: 38.7 us -> 61.4 us
  local copies, waits for them, and re-layouts: 0.08 us -> 19.2 us
  starting transfers between devices: 11.1 us -> 13.1 us
  Pallas kernels: 26.4 us -> 28 us
    unnamed x26 -> x60, local copies, waits for them, and re-layouts: 0.08 us -> 19.2 us
    all_to_all x0 -> x2, starting transfers between devices: none -> 6.76 us  [exchange(): lax.all_to_all(messages, 'lon', split_axis=0, concat_axis=0, tiled=True)]
    ppermute x8 -> x2, starting transfers between devices: 8.12 us -> 2.49 us  [ring(): lax.ppermute(value, 'lon', [(i, (i + step) % lon_count) for i in range(lo...]
    pallas_call x1, Pallas kernels: 2.18 us -> 3.3 us  [shards(): pl.pallas_call(pack_kernel, out_shape=[like(strip, columns)] * 2 + [like(...]
    ppermute x1, starting transfers between devices: 0.69 us -> 1.52 us  [shards(): strip_b = lax.ppermute(to_b, 'lat', odd_up + [(j, i) for i, j in odd_up])]
    pallas_call x2, Pallas kernels: 18.5 us -> 19.2 us  [tendencies(): pl.pallas_call(functools.partial(tend_kernel, inner, count, kept), out_sh...]
  transfers between devices with their start and end apart: 10 -> 6, of which waited for: 0 -> 0; matrix products, arithmetic and copies ran while one was open for 0% -> 0% of each run, Pallas kernels for 58% -> 37%
where the time goes in v8:
time: 62.4 us; the launch traced here: 61.4 us
  Pallas kernels  28 us (45%)
  local copies, waits for them, and re-layouts  19.2 us (31%)
  starting transfers between devices  13.1 us (21%)
  between operations  1.09 us (2%)
    pallas_call x2, Pallas kernels, tendencies(): pl.pallas_call(functools.partial(tend_kernel, inner, count, kept), out_sh...  19.2 us
    unnamed x60, local copies, waits for them, and re-layouts  19.2 us
    all_to_all x2, starting transfers between devices, exchange(): lax.all_to_all(messages, 'lon', split_axis=0, concat_axis=0, tiled=True)  6.76 us
    pallas_call x2, Pallas kernels, finish(): pl.pallas_call(functools.partial(finish_kernel, inner, count), out_shape=...  5.52 us
    pallas_call x1, Pallas kernels, shards(): pl.pallas_call(pack_kernel, out_shape=[like(strip, columns)] * 2 + [like(...  3.3 us
    ppermute x2, starting transfers between devices, ring(): lax.ppermute(value, 'lon', [(i, (i + step) % lon_count) for i in range(lo...  2.49 us
    ppermute x1, starting transfers between devices, shards(): strip_a = lax.ppermute(to_a, 'lat', [(i, i ^ 1) for i in range(lat_count)])  2.33 us
    ppermute x1, starting transfers between devices, shards(): strip_b = lax.ppermute(to_b, 'lat', odd_up + [(j, i) for i, j in odd_up])  1.52 us
  transfers between devices with their start and end apart: 6, of which 0 were waited for; matrix products, arithmetic and copies ran while one was open for 0% of the time, Pallas kernels for 37%

profile of v8, /device:TPU:0, one launch (start us, length us, event | category | flops | bytes accessed | tf_op | source)
XLA Modules:
  0.0 61.4 jit_solution(2049373946068604037)
XLA Ops:
  0.6 0.0 copy-start.28
  0.6 0.0 copy-start.29
  0.7 0.0 copy-start.3
  0.7 0.0 copy-start.2
  0.7 0.0 copy-start.1
  0.7 0.0 copy-start
  0.7 0.0 copy-start.18
  0.7 3.3 %pack_edges.1 = (f32[200,896]{1,0:T(8,128)}, f32[200,896]{1,0:T(8,128)}, f32[48,128]{1,0:T(8,128)S(1)}, f32[48,128]{1,0:T(8,128)S(1)}, f32[3,16,8,256]{3,2,1,0:T(8,128)S(1)}) custom-call(f32[16,16,896]{2,1,0:T(8,128)} %refs_0_.9, f32[16,16,896]{2,1,0:T(8,128)} %refs_1_.9, f32[16,16,896]{2,1,0:T(8,128)} %refs_2_.9, f32[16,16,896]{2,1,0:T(8,128)} %refs_3_.9, ...), custom_call_target="tpu_custom_call" | custom-call | tf_op jit(solution)/shard_map/pack_edges/pallas_call | solution.py:551
  4.0 0.0 copy-start.9
  4.0 0.5 collective-permute-start
  4.5 2.0 %collective-permute-start.1 = (f32[48,128]{1,0:T(8,128)S(1)}, f32[48,128]{1,0:T(8,128)S(1)}, u32[]{:S(2)}, u32[]{:S(2)}) collective-permute-start(f32[48,128]{1,0:T(8,128)S(1)} %get-tuple-element.26), channel_id=1, source_target_pairs={{0,3},{1,0},{2,1},{3,2},{4,7},{5,4},{6,5},{7,6},{8,11},{9,8},{10,9... | collective-permute-start | bytes 73736 | tf_op jit(solution)/shard_map/ppermute | solution.py:568
  6.5 2.3 %collective-permute-start.2 = (f32[200,896]{1,0:T(8,128)}, f32[200,896]{1,0:T(8,128)}, u32[]{:S(2)}, u32[]{:S(2)}) collective-permute-start(f32[200,896]{1,0:T(8,128)} %get-tuple-element.28), channel_id=1, source_target_pairs={{0,4},{4,0},{8,12},{12,8},{1,5},{5,1},{9,13},{13,9},{2,6},{6,2},{1... | collective-permute-start | bytes 2150408 | tf_op jit(solution)/shard_map/ppermute | solution.py:573
  8.8 1.5 %collective-permute-start.3 = (f32[200,896]{1,0:T(8,128)}, f32[200,896]{1,0:T(8,128)}, u32[]{:S(2)}, u32[]{:S(2)}) collective-permute-start(f32[200,896]{1,0:T(8,128)} %get-tuple-element.29), channel_id=1, source_target_pairs={{4,8},{8,4},{5,9},{9,5},{6,10},{10,6},{7,11},{11,7},{20,24},{24,20... | collective-permute-start | bytes 2150408 | tf_op jit(solution)/shard_map/ppermute | solution.py:574
  10.4 0.0 collective-permute-done.refs_5_
  10.4 0.0 copy-start.20
  10.4 0.0 collective-permute-done.1.refs_6_
  10.4 0.0 copy-start.22
  10.4 0.0 copy-done.28
  10.4 0.0 copy-done.29
  10.4 0.0 copy-done.3
  10.4 0.0 copy-done.2
  10.4 0.0 copy-done.1
  10.4 0.0 copy-done
  10.4 0.0 copy-done.18
  10.4 13.3 %tend_inner.1 = (f32[16,16,896]{2,1,0:T(8,128)}, f32[16,16,896]{2,1,0:T(8,128)}, f32[16,16,896]{2,1,0:T(8,128)}, f32[16,16,896]{2,1,0:T(8,128)}, f32[4,208,256]{2,1,0:T(8,128)S(1)}, /*index=5*/f32[4,208,128]{2,1,0:T(8,128)S(1)}) custom-call(f32[64]{0:T(128)S(1)} %copy-done.29, f32[64]{0:T(128)S(1)} %copy-done.28, f32[16,16,896]{2,1,0:T(8,128)S(1)} %copy-done, ...), custom_call_target="tpu_custom_call" | custom-call | flops 14909440000 | bytes 4194304 | tf_op jit(solution)/shard_map/tend_inner/pallas_call | solution.py:588
  23.8 0.0 copy-done.9
  23.8 0.0 copy-done.20
  23.8 0.0 copy-done.22
  23.8 0.0 copy-start.13
  23.8 0.9 %copy-done.13 = f32[4,208,256]{2,1,0:T(8,128)} copy-done((f32[4,208,256]{2,1,0:T(8,128)}, f32[4,208,256]{2,1,0:T(8,128)S(1)}, u32[]{:S(2)}) %copy-start.13) | copy-done | bytes 851992
  24.7 0.0 copy-start.15
  24.7 0.8 %copy-done.15 = f32[4,208,128]{2,1,0:T(8,128)} copy-done((f32[4,208,128]{2,1,0:T(8,128)}, f32[4,208,128]{2,1,0:T(8,128)S(1)}, u32[]{:S(2)}) %copy-start.15) | copy-done | bytes 426008
  25.5 3.5 %all-to-all-start.1 = ((f32[4,208,128]{2,1,0:T(8,128)}), f32[4,208,128]{2,1,0:T(8,128)S(1)}, u32[]{:S(2)}, u32[]{:S(2)}) async-start(f32[4,208,128]{2,1,0:T(8,128)} %copy-done.15), calls=%async_computation.1 | async-start | bytes 851968 | tf_op jit(solution)/shard_map/all_to_all | solution.py:619
  29.0 0.0 collective-permute-done.2.refs_8_
  29.0 0.0 collective-permute-done.3.refs_9_
  29.0 0.0 copy-start.4
  29.0 1.2 %copy-done.4 = f32[16,16,896]{2,1,0:T(8,128)S(1)} copy-done((f32[16,16,896]{2,1,0:T(8,128)S(1)}, f32[16,16,896]{2,1,0:T(8,128)}, u32[]{:S(2)}) %copy-start.4) | copy-done | bytes 917528
  30.2 0.0 copy-start.10
  30.2 1.0 %copy-done.10 = f32[3,16,8,256]{3,2,1,0:T(8,128)S(1)} copy-done((f32[3,16,8,256]{3,2,1,0:T(8,128)S(1)}, f32[3,16,8,256]{3,2,1,0:T(8,128)}, u32[]{:S(2)}) %copy-start.10) | copy-done | bytes 393240
  31.2 0.8 %copy-done.19 = f32[16,896]{1,0:T(8,128)S(1)} copy-done((f32[16,896]{1,0:T(8,128)S(1)}, f32[16,896]{1,0:T(8,128)}, u32[]{:S(2)}) %copy-start.19) | copy-done | bytes 57368
  32.0 0.7 %copy-done.21 = f32[48,128]{1,0:T(8,128)S(1)} copy-done((f32[48,128]{1,0:T(8,128)S(1)}, f32[48,128]{1,0:T(8,128)}, u32[]{:S(2)}) %copy-start.21) | copy-done | bytes 24600
  32.7 0.7 %copy-done.23 = f32[48,128]{1,0:T(8,128)S(1)} copy-done((f32[48,128]{1,0:T(8,128)S(1)}, f32[48,128]{1,0:T(8,128)}, u32[]{:S(2)}) %copy-start.23) | copy-done | bytes 24600
  33.5 1.3 %copy-done.24 = bf16[2688,256]{1,0:T(8,128)(2,1)S(1)} copy-done((bf16[2688,256]{1,0:T(8,128)(2,1)S(1)}, bf16[2688,256]{1,0:T(8,128)(2,1)}, u32[]{:S(2)}) %copy-start.24) | copy-done | bytes 1376280
  34.8 1.0 %copy-done.25 = bf16[768,256]{1,0:T(8,128)(2,1)S(1)} copy-done((bf16[768,256]{1,0:T(8,128)(2,1)S(1)}, bf16[768,256]{1,0:T(8,128)(2,1)}, u32[]{:S(2)}) %copy-start.25) | copy-done | bytes 393240
  35.8 0.9 %copy-done.26 = bf16[512,256]{1,0:T(8,128)(2,1)S(1)} copy-done((bf16[512,256]{1,0:T(8,128)(2,1)S(1)}, bf16[512,256]{1,0:T(8,128)(2,1)}, u32[]{:S(2)}) %copy-start.26) | copy-done | bytes 262168
  36.7 0.9 %copy-done.27 = bf16[768,128]{1,0:T(8,128)(2,1)S(1)} copy-done((bf16[768,128]{1,0:T(8,128)(2,1)S(1)}, bf16[768,128]{1,0:T(8,128)(2,1)}, u32[]{:S(2)}) %copy-start.27) | copy-done | bytes 196632
  37.7 5.9 %tend_edge.1 = (f32[16,16,896]{2,1,0:T(8,128)}, f32[16,16,896]{2,1,0:T(8,128)}, f32[16,16,896]{2,1,0:T(8,128)}, f32[16,16,896]{2,1,0:T(8,128)}, f32[4,48,256]{2,1,0:T(8,128)S(1)}, /*index=5*/f32[4,48,128]{2,1,0:T(8,128)S(1)}) custom-call(f32[64]{0:T(128)S(1)} %copy-done.29, ...), custom_call_target="tpu_custom_call", output_to_operand_aliasing={{0}: (16, {}), {1}: (17, {}), {2}: (18, {}), {3}: (19, {})} | custom-call | flops 6881280000 | bytes 4194304 | tf_op jit(solution)/shard_map/tend_edge/pallas_call | solution.py:588
  43.6 0.0 copy-start.17
  43.6 0.0 all-to-all-done.1.refs_4_
  43.6 0.6 %copy-done.17 = f32[4,48,128]{2,1,0:T(8,128)} copy-done((f32[4,48,128]{2,1,0:T(8,128)}, f32[4,48,128]{2,1,0:T(8,128)S(1)}, u32[]{:S(2)}) %copy-start.17) | copy-done | bytes 98328
  44.2 3.3 %all-to-all-start = ((f32[4,48,128]{2,1,0:T(8,128)}), f32[4,48,128]{2,1,0:T(8,128)S(1)}, u32[]{:S(2)}, u32[]{:S(2)}) async-start(f32[4,48,128]{2,1,0:T(8,128)} %copy-done.17), calls=%async_computation | async-start | bytes 196608 | tf_op jit(solution)/shard_map/all_to_all | solution.py:619
  47.5 0.0 copy-done.16
  47.5 0.0 copy-start.5
  47.5 1.2 %copy-done.5 = f32[16,16,896]{2,1,0:T(8,128)S(1)} copy-done((f32[16,16,896]{2,1,0:T(8,128)S(1)}, f32[16,16,896]{2,1,0:T(8,128)}, u32[]{:S(2)}) %copy-start.5) | copy-done | bytes 917528
  48.7 1.3 %copy-done.7 = bf16[768,896]{1,0:T(8,128)(2,1)S(1)} copy-done((bf16[768,896]{1,0:T(8,128)(2,1)S(1)}, bf16[768,896]{1,0:T(8,128)(2,1)}, u32[]{:S(2)}) %copy-start.7) | copy-done | bytes 1376280
  50.1 1.0 %copy-done.11 = f32[3,16,8,256]{3,2,1,0:T(8,128)S(1)} copy-done((f32[3,16,8,256]{3,2,1,0:T(8,128)S(1)}, f32[3,16,8,256]{3,2,1,0:T(8,128)}, u32[]{:S(2)}) %copy-start.11) | copy-done | bytes 393240
  51.1 1.2 %copy-done.14 = f32[4,208,256]{2,1,0:T(8,128)S(1)} copy-done((f32[4,208,256]{2,1,0:T(8,128)S(1)}, f32[4,208,256]{2,1,0:T(8,128)}, u32[]{:S(2)}) %copy-start.14) | copy-done | bytes 851992
  52.2 3.7 %finish_inner.1 = (f32[16,16,896]{2,1,0:T(8,128)}, f32[16,16,896]{2,1,0:T(8,128)}, f32[16,16,896]{2,1,0:T(8,128)}, f32[16,16,896]{2,1,0:T(8,128)}) custom-call(f32[16,16,896]{2,1,0:T(8,128)S(1)} %copy-done, f32[16,16,896]{2,1,0:T(8,128)S(1)} %copy-done.1, ...), custom_call_target="tpu_custom_call", output_to_operand_aliasing={{0}: (9, {}), {1}: (10, {}), {2}: (11, {}), {3}: (12, {})} | custom-call | tf_op jit(solution)/shard_map/finish_inner/pallas_call | solution.py:625
  55.9 0.0 all-to-all-done.refs_4_
  55.9 0.0 copy-start.6
  55.9 1.2 %copy-done.6 = f32[16,16,896]{2,1,0:T(8,128)S(1)} copy-done((f32[16,16,896]{2,1,0:T(8,128)S(1)}, f32[16,16,896]{2,1,0:T(8,128)}, u32[]{:S(2)}) %copy-start.6) | copy-done | bytes 917528
  57.1 1.3 %copy-done.8 = bf16[768,896]{1,0:T(8,128)(2,1)S(1)} copy-done((bf16[768,896]{1,0:T(8,128)(2,1)S(1)}, bf16[768,896]{1,0:T(8,128)(2,1)}, u32[]{:S(2)}) %copy-start.8) | copy-done | bytes 1376280
  58.4 1.0 %copy-done.12 = f32[3,16,8,256]{3,2,1,0:T(8,128)S(1)} copy-done((f32[3,16,8,256]{3,2,1,0:T(8,128)S(1)}, f32[3,16,8,256]{3,2,1,0:T(8,128)}, u32[]{:S(2)}) %copy-start.12) | copy-done | bytes 393240
  59.4 1.8 %finish_edge.1 = (f32[16,16,896]{2,1,0:T(8,128)}, f32[16,16,896]{2,1,0:T(8,128)}, f32[16,16,896]{2,1,0:T(8,128)}, f32[16,16,896]{2,1,0:T(8,128)}) custom-call(f32[16,16,896]{2,1,0:T(8,128)S(1)} %copy-done, f32[16,16,896]{2,1,0:T(8,128)S(1)} %copy-done.1, ...), custom_call_target="tpu_custom_call", output_to_operand_aliasing={{0}: (9, {}), {1}: (10, {}), {2}: (11, {}), {3}: (12, {})} | custom-call | tf_op jit(solution)/shard_map/finish_edge/pallas_call | solution.py:625
  (13 shorter events, 0.0 us)
Async XLA Ops:
  0.6 9.7 %copy-start.28 = (f32[64]{0:T(128)S(1)}, f32[64]{0:T(128)}, u32[]{:S(2)}) copy-start(f32[64]{0:T(128)} %constant.26.clone.spin) | copy-start | bytes 772
  0.6 9.7 %copy-start.29 = (f32[64]{0:T(128)S(1)}, f32[64]{0:T(128)}, u32[]{:S(2)}) copy-start(f32[64]{0:T(128)} %constant.25.clone.metric) | copy-start | bytes 772
  0.7 9.7 %copy-start.3 = (f32[16,16,896]{2,1,0:T(8,128)S(1)}, f32[16,16,896]{2,1,0:T(8,128)}, u32[]{:S(2)}) copy-start(f32[16,16,896]{2,1,0:T(8,128)} %refs_3_.9) | copy-start | bytes 2752516
  0.7 9.7 %copy-start.2 = (f32[16,16,896]{2,1,0:T(8,128)S(1)}, f32[16,16,896]{2,1,0:T(8,128)}, u32[]{:S(2)}) copy-start(f32[16,16,896]{2,1,0:T(8,128)} %refs_2_.9) | copy-start | bytes 2752516
  0.7 9.7 %copy-start.1 = (f32[16,16,896]{2,1,0:T(8,128)S(1)}, f32[16,16,896]{2,1,0:T(8,128)}, u32[]{:S(2)}) copy-start(f32[16,16,896]{2,1,0:T(8,128)} %refs_1_.9) | copy-start | bytes 2752516
  0.7 9.7 %copy-start = (f32[16,16,896]{2,1,0:T(8,128)S(1)}, f32[16,16,896]{2,1,0:T(8,128)}, u32[]{:S(2)}) copy-start(f32[16,16,896]{2,1,0:T(8,128)} %refs_0_.9) | copy-start | bytes 2752516
  0.7 9.7 %copy-start.18 = (f32[16,896]{1,0:T(8,128)S(1)}, f32[16,896]{1,0:T(8,128)}, u32[]{:S(2)}) copy-start(f32[16,896]{1,0:T(8,128)} %refs_4_.5) | copy-start | bytes 172036
  4.0 19.8 %copy-start.9 = (f32[3,16,8,256]{3,2,1,0:T(8,128)}, f32[3,16,8,256]{3,2,1,0:T(8,128)S(1)}, u32[]{:S(2)}) copy-start(f32[3,16,8,256]{3,2,1,0:T(8,128)S(1)} %get-tuple-element.27.refs_7_.refs_6_) | copy-start | bytes 1179652
  4.0 6.3 %collective-permute-start = (f32[48,128]{1,0:T(8,128)S(1)}, f32[48,128]{1,0:T(8,128)S(1)}, u32[]{:S(2)}, u32[]{:S(2)}) collective-permute-start(f32[48,128]{1,0:T(8,128)S(1)} %get-tuple-element.25), channel_id=1, source_target_pairs={{0,1},{1,2},{2,3},{3,0},{4,5},{5,6},{6,7},{7,4},{8,9},{9,10},{10,1... | collective-permute-start | bytes 73736 | tf_op jit(solution)/shard_map/ppermute | solution.py:568
  4.5 5.8 %collective-permute-start.1 = (f32[48,128]{1,0:T(8,128)S(1)}, f32[48,128]{1,0:T(8,128)S(1)}, u32[]{:S(2)}, u32[]{:S(2)}) collective-permute-start(f32[48,128]{1,0:T(8,128)S(1)} %get-tuple-element.26), channel_id=1, source_target_pairs={{0,3},{1,0},{2,1},{3,2},{4,7},{5,4},{6,5},{7,6},{8,11},{9,8},{10,9... | collective-permute-start | bytes 73736 | tf_op jit(solution)/shard_map/ppermute | solution.py:568
  6.5 22.4 %collective-permute-start.2 = (f32[200,896]{1,0:T(8,128)}, f32[200,896]{1,0:T(8,128)}, u32[]{:S(2)}, u32[]{:S(2)}) collective-permute-start(f32[200,896]{1,0:T(8,128)} %get-tuple-element.28), channel_id=1, source_target_pairs={{0,4},{4,0},{8,12},{12,8},{1,5},{5,1},{9,13},{13,9},{2,6},{6,2},{1... | collective-permute-start | bytes 2150408 | tf_op jit(solution)/shard_map/ppermute | solution.py:573
  8.8 20.1 %collective-permute-start.3 = (f32[200,896]{1,0:T(8,128)}, f32[200,896]{1,0:T(8,128)}, u32[]{:S(2)}, u32[]{:S(2)}) collective-permute-start(f32[200,896]{1,0:T(8,128)} %get-tuple-element.29), channel_id=1, source_target_pairs={{4,8},{8,4},{5,9},{9,5},{6,10},{10,6},{7,11},{11,7},{20,24},{24,20... | collective-permute-start | bytes 2150408 | tf_op jit(solution)/shard_map/ppermute | solution.py:574
  10.4 13.4 %copy-start.20 = (f32[48,128]{1,0:T(8,128)}, f32[48,128]{1,0:T(8,128)S(1)}, u32[]{:S(2)}) copy-start(f32[48,128]{1,0:T(8,128)S(1)} %collective-permute-done.refs_5_) | copy-start | bytes 73732
  10.4 13.4 %copy-start.22 = (f32[48,128]{1,0:T(8,128)}, f32[48,128]{1,0:T(8,128)S(1)}, u32[]{:S(2)}) copy-start(f32[48,128]{1,0:T(8,128)S(1)} %collective-permute-done.1.refs_6_) | copy-start | bytes 73732
  23.8 0.9 %copy-start.13 = (f32[4,208,256]{2,1,0:T(8,128)}, f32[4,208,256]{2,1,0:T(8,128)S(1)}, u32[]{:S(2)}) copy-start(f32[4,208,256]{2,1,0:T(8,128)S(1)} %get-tuple-element.37.refs_5_) | copy-start | bytes 2555908
  24.7 0.8 %copy-start.15 = (f32[4,208,128]{2,1,0:T(8,128)}, f32[4,208,128]{2,1,0:T(8,128)S(1)}, u32[]{:S(2)}) copy-start(f32[4,208,128]{2,1,0:T(8,128)S(1)} %get-tuple-element.36) | copy-start | bytes 1277956
  25.5 18.1 %all-to-all-start.1 = ((f32[4,208,128]{2,1,0:T(8,128)}), f32[4,208,128]{2,1,0:T(8,128)S(1)}, u32[]{:S(2)}, u32[]{:S(2)}) async-start(f32[4,208,128]{2,1,0:T(8,128)} %copy-done.15), calls=%async_computation.1 | async-start | bytes 851968 | tf_op jit(solution)/shard_map/all_to_all | solution.py:619
  29.0 1.2 %copy-start.4 = (f32[16,16,896]{2,1,0:T(8,128)S(1)}, f32[16,16,896]{2,1,0:T(8,128)}, u32[]{:S(2)}) copy-start(f32[16,16,896]{2,1,0:T(8,128)} %refs_3_.9) | copy-start | bytes 2752516
  30.2 1.0 %copy-start.10 = (f32[3,16,8,256]{3,2,1,0:T(8,128)S(1)}, f32[3,16,8,256]{3,2,1,0:T(8,128)}, u32[]{:S(2)}) copy-start(f32[3,16,8,256]{3,2,1,0:T(8,128)} %copy-done.9) | copy-start | bytes 1179652
  31.2 0.8 %copy-start.19 = (f32[16,896]{1,0:T(8,128)S(1)}, f32[16,896]{1,0:T(8,128)}, u32[]{:S(2)}) copy-start(f32[16,896]{1,0:T(8,128)} %refs_4_.5) | copy-start | bytes 172036
  32.0 0.7 %copy-start.21 = (f32[48,128]{1,0:T(8,128)S(1)}, f32[48,128]{1,0:T(8,128)}, u32[]{:S(2)}) copy-start(f32[48,128]{1,0:T(8,128)} %copy-done.20) | copy-start | bytes 73732
  32.7 0.7 %copy-start.23 = (f32[48,128]{1,0:T(8,128)S(1)}, f32[48,128]{1,0:T(8,128)}, u32[]{:S(2)}) copy-start(f32[48,128]{1,0:T(8,128)} %copy-done.22) | copy-start | bytes 73732
  33.5 1.3 %copy-start.24 = (bf16[2688,256]{1,0:T(8,128)(2,1)S(1)}, bf16[2688,256]{1,0:T(8,128)(2,1)}, u32[]{:S(2)}) copy-start(bf16[2688,256]{1,0:T(8,128)(2,1)} %constant.20.clone.refs_9_.refs_11_) | copy-start | bytes 4128772
  34.8 1.0 %copy-start.25 = (bf16[768,256]{1,0:T(8,128)(2,1)S(1)}, bf16[768,256]{1,0:T(8,128)(2,1)}, u32[]{:S(2)}) copy-start(bf16[768,256]{1,0:T(8,128)(2,1)} %constant.21.clone.refs_10_.refs_12_) | copy-start | bytes 1179652
  35.8 0.9 %copy-start.26 = (bf16[512,256]{1,0:T(8,128)(2,1)S(1)}, bf16[512,256]{1,0:T(8,128)(2,1)}, u32[]{:S(2)}) copy-start(bf16[512,256]{1,0:T(8,128)(2,1)} %constant.19.clone.refs_8_.refs_10_) | copy-start | bytes 786436
  36.7 0.9 %copy-start.27 = (bf16[768,128]{1,0:T(8,128)(2,1)S(1)}, bf16[768,128]{1,0:T(8,128)(2,1)}, u32[]{:S(2)}) copy-start(bf16[768,128]{1,0:T(8,128)(2,1)} %constant.22.clone.refs_11_.refs_13_) | copy-start | bytes 589828
  37.7 9.9 %copy-start.16 = (bf16[128,256]{1,0:T(8,128)(2,1)S(1)}, bf16[128,256]{1,0:T(8,128)(2,1)}, u32[]{:S(2)}) copy-start(bf16[128,256]{1,0:T(8,128)(2,1)} %constant.23.clone.refs_7_) | copy-start | bytes 196612
  43.6 0.6 %copy-start.17 = (f32[4,48,128]{2,1,0:T(8,128)}, f32[4,48,128]{2,1,0:T(8,128)S(1)}, u32[]{:S(2)}) copy-start(f32[4,48,128]{2,1,0:T(8,128)S(1)} %get-tuple-element.34) | copy-start | bytes 294916
  44.2 11.7 %all-to-all-start = ((f32[4,48,128]{2,1,0:T(8,128)}), f32[4,48,128]{2,1,0:T(8,128)S(1)}, u32[]{:S(2)}, u32[]{:S(2)}) async-start(f32[4,48,128]{2,1,0:T(8,128)} %copy-done.17), calls=%async_computation | async-start | bytes 196608 | tf_op jit(solution)/shard_map/all_to_all | solution.py:619
  47.5 1.2 %copy-start.5 = (f32[16,16,896]{2,1,0:T(8,128)S(1)}, f32[16,16,896]{2,1,0:T(8,128)}, u32[]{:S(2)}) copy-start(f32[16,16,896]{2,1,0:T(8,128)} %refs_3_.9) | copy-start | bytes 2752516
  48.7 1.3 %copy-start.7 = (bf16[768,896]{1,0:T(8,128)(2,1)S(1)}, bf16[768,896]{1,0:T(8,128)(2,1)}, u32[]{:S(2)}) copy-start(bf16[768,896]{1,0:T(8,128)(2,1)} %constant.24.clone.refs_8_) | copy-start | bytes 4128772
  50.1 1.0 %copy-start.11 = (f32[3,16,8,256]{3,2,1,0:T(8,128)S(1)}, f32[3,16,8,256]{3,2,1,0:T(8,128)}, u32[]{:S(2)}) copy-start(f32[3,16,8,256]{3,2,1,0:T(8,128)} %copy-done.9) | copy-start | bytes 1179652
  51.0 1.2 %copy-start.14 = (f32[4,208,256]{2,1,0:T(8,128)S(1)}, f32[4,208,256]{2,1,0:T(8,128)}, u32[]{:S(2)}) copy-start(f32[4,208,256]{2,1,0:T(8,128)} %copy-done.13) | copy-start | bytes 2555908
  55.9 1.2 %copy-start.6 = (f32[16,16,896]{2,1,0:T(8,128)S(1)}, f32[16,16,896]{2,1,0:T(8,128)}, u32[]{:S(2)}) copy-start(f32[16,16,896]{2,1,0:T(8,128)} %refs_3_.9) | copy-start | bytes 2752516
  57.1 1.3 %copy-start.8 = (bf16[768,896]{1,0:T(8,128)(2,1)S(1)}, bf16[768,896]{1,0:T(8,128)(2,1)}, u32[]{:S(2)}) copy-start(bf16[768,896]{1,0:T(8,128)(2,1)} %constant.24.clone.refs_8_) | copy-start | bytes 4128772
  58.4 1.0 %copy-start.12 = (f32[3,16,8,256]{3,2,1,0:T(8,128)S(1)}, f32[3,16,8,256]{3,2,1,0:T(8,128)}, u32[]{:S(2)}) copy-start(f32[3,16,8,256]{3,2,1,0:T(8,128)} %copy-done.9) | copy-start | bytes 1179652

commit v9 on v7

--- a/solution.py
+++ b/solution.py
@@ -61,14 +61,14 @@
 
 
 def band_table():
-    band = np.zeros((2 * LANES, 2 * LANES))
+    band = np.zeros((3 * LANES, 2 * LANES))
     slope = {-3: -1, -2: 9, -1: -45, 1: 45, 2: -9, 3: 1}
     smooth = {-3: 1, -2: -6, -1: 15, 0: -20, 1: 15, 2: -6, 3: 1}
     for j in range(LANES):
         for k, value in slope.items():
-            band[j + 3 + k, j] = value
+            band[LANES + j + k, j] = value
         for k, value in smooth.items():
-            band[j + 3 + k, LANES + j] = value
+            band[LANES + j + k, LANES + j] = value
     return np.concatenate([band, band], axis=0).astype(ml_dtypes.bfloat16)
 
 
@@ -219,10 +219,13 @@
     return slope, smooth
 
 
-def mass_slopes(mass, west, east, south, north, mass_x, mass_y, levels):
-    rows, columns = mass.shape
+def over_levels(value):
+    return jnp.broadcast_to(value[:, None, :], (value.shape[0], 8, value.shape[1]))
+
+
+def mass_slope_x(mass, west, east, levels):
+    columns = mass.shape[1]
     middle = mass[...]
-    per_mass = 1.0 / (60.0 * middle)
     wide = jnp.concatenate(
         [pltpu.roll(west[2 * levels :], LANES - 3, 1), middle, east[2 * levels :]], axis=1
     )
@@ -231,14 +234,16 @@
     def at(k):
         return pltpu.roll(wide, (-k) % whole, 1)[:, LANES : LANES + columns]
 
-    def store(out, value):
-        out[...] = jnp.broadcast_to(value[:, None, :], out.shape)
-
-    store(mass_x, stencil(middle, [at(1), at(2), at(3)], [at(-1), at(-2), at(-3)])[0] * per_mass)
-    tall = jnp.concatenate([south, middle, north], axis=0)
-    plus = [tall[3 + k : 3 + k + rows] for k in (1, 2, 3)]
-    minus = [tall[3 - k : 3 - k + rows] for k in (1, 2, 3)]
-    store(mass_y, stencil(middle, plus, minus)[0] * per_mass)
+    slope = stencil(middle, [at(1), at(2), at(3)], [at(-1), at(-2), at(-3)])[0]
+    return over_levels(slope / (60.0 * middle))
+
+
+def mass_slope_y(tall):
+    size = tall.shape[0] - 6
+    plus = [tall[3 + k : 3 + k + size] for k in (1, 2, 3)]
+    minus = [tall[3 - k : 3 - k + size] for k in (1, 2, 3)]
+    middle = tall[3 : 3 + size]
+    return over_levels(stencil(middle, plus, minus)[0] / (60.0 * middle))
 
 
 def spread_waves(waves, part, inner, kept, levels):
@@ -259,12 +264,14 @@
     fields = some(4)
     mass, west, east, waves = some(4)
     strips = some(2) if edge_rows else None
+    mass_x = some(1)[0] if edge_rows else None
     tables_in = some(4)
     if edge_rows:
         some(4)
     outs = some(4)
     local, to_east, to_west, to_far = some(4)
-    high, low, cross, new, kept_high, kept_low, mass_x, mass_y, sems = some(9)
+    mass_x = some(1)[0] if inner else mass_x
+    high, low, cross, new, kept_high, kept_low, mass_y, sems = some(8)
     tables = refs if inner else tables_in
     band, spread, own, send = tables
     rows, columns = mass.shape
@@ -280,39 +287,44 @@
         upper = by_parity(lines[0], lines[1])
         lower = by_parity(lines[1], lines[0])
         lower = jnp.concatenate([lower[2:3], lower[1:2], lower[0:1]], axis=0)
+        mass_y[0:3] = mass_slope_y(jnp.concatenate([lower, mass[0:6]], axis=0))
+        mass_y[rows - 3 :] = mass_slope_y(jnp.concatenate([mass[rows - 6 :], upper], axis=0))
     else:
-        lower = upper = jnp.zeros((3, columns), F32)
-    mass_slopes(mass, west, east, lower, upper, mass_x, mass_y, levels)
-    lane = lax.broadcasted_iota(jnp.int32, (levels, LANES), 1)
+        blank = jnp.zeros((3, columns), F32)
+        mass_x[...] = mass_slope_x(mass, west, east, levels)
+        mass_y[...] = mass_slope_y(jnp.concatenate([blank, mass[...], blank], axis=0))
 
     def cut(i, carry):
         row = entry_row(inner, i, rows)
         halo = pl.ds(pl.multiple_of((row % 2) * levels, levels), levels)
         for f in range(4):
             lead = 16 * (row // 2) + 3 * f
-            before = pltpu.roll(west[halo, :], lax.rem(LANES - lead, LANES), 1)
-            for t in range(tiles + 1):
-                if t < tiles:
-                    tile = pltpu.roll(fields[f][row, :, t * LANES : (t + 1) * LANES], 3, 1)
+            for t in range(tiles + 2):
+                if t == 0:
+                    tile = pltpu.roll(west[halo, :], lax.rem(2 * LANES - 3 - lead, LANES), 1)
+                elif t <= tiles:
+                    tile = fields[f][row, :, (t - 1) * LANES : t * LANES]
                 else:
-                    tile = pltpu.roll(east[halo, :], lax.rem(LANES + 3 - lead, LANES), 1)
-                whole = jnp.where(lane < 3, before, tile)
-                top = whole.astype(BF16)
+                    tile = pltpu.roll(east[halo, :], lax.rem(LANES - lead, LANES), 1)
+                top = tile.astype(BF16)
                 high[f, i, :, t * LANES : (t + 1) * LANES] = top
-                low[f, i, :, t * LANES : (t + 1) * LANES] = (whole - top.astype(F32)).astype(BF16)
-                before = tile
+                low[f, i, :, t * LANES : (t + 1) * LANES] = (tile - top.astype(F32)).astype(BF16)
         return carry
 
-    lax.fori_loop(0, count, cut, 0)
-
-    wait_all(fetched[:1])
-    for t in range(tiles):
-        span = slice(t * LANES, (t + 2) * LANES)
-        both = jnp.concatenate(
-            [high[:, :, :, span].reshape(4 * items, 2 * LANES), low[:, :, :, span].reshape(4 * items, 2 * LANES)],
-            axis=1,
-        )
-        cross[t] = dot(both, band[...]).reshape(4, count, levels, 2 * LANES)
+    def slopes_x(first, size):
+        lax.fori_loop(first, first + size, cut, 0)
+        wait_all(fetched[:1])
+        for t in range(tiles):
+            span = slice(t * LANES, (t + 3) * LANES)
+            some_rows = slice(first, first + size)
+            both = jnp.concatenate(
+                [
+                    table[:, some_rows, :, span].reshape(4 * size * levels, 3 * LANES)
+                    for table in (high, low)
+                ],
+                axis=1,
+            )
+            cross[t, :, some_rows] = dot(both, band[...]).reshape(4, size, levels, 2 * LANES)
 
     start_row = lax.axis_index("lat") * rows
 
@@ -395,8 +407,10 @@
             new[f, i, :, span] = q + STEP * change
 
         if inner:
+            slopes_x(0, rows - 6)
             inner_rows(emit)
         else:
+            slopes_x(0, 6)
             edge_side(0, 0, emit)
             edge_side(1, 3, emit)
         pairs = [pair for f in range(4) for pair in write_out(f)]
@@ -410,6 +424,7 @@
             kept_high[f, i, :, span] = top
             kept_low[f, i, :, span] = (change - top.astype(F32)).astype(BF16)
 
+        slopes_x(0, kept)
         if inner:
             inner_rows(emit)
             if kept > rows - 6:
@@ -588,30 +603,31 @@
     def tendencies(inner, old):
         count, kept = (inner_count, inner_count) if inner else (6, edge_kept)
         kept_items = kept * levels
-        halos = [] if inner else [strip_a, strip_b]
         weights = [tables[k] for k in ("band", "spread", "own", "send")]
         if inner:
             weights = [in_hbm(w) for w in weights]
+        halos = [] if inner else [strip_a, strip_b, *old[4:]]
+        old = old[:4]
         args = [metric, spin, *fields, mass, west, east, waves, *halos, *weights]
         return pl.pallas_call(
             functools.partial(tend_kernel, inner, count, kept),
             out_shape=[like(rows, levels, columns)] * 4
             + [like(4, kept_items, NODES)]
             + [like(kept_items, LANES)] * 2
-            + [like(kept_items // 2, LANES)],
+            + [like(kept_items // 2, LANES)]
+            + [like(rows, 8, columns)] * inner,
             in_specs=[smem()] * 2
             + [vmem()] * (len(args) - 6)
             + [anywhere() if inner else vmem()] * 4
             + [anywhere()] * len(old),
-            out_specs=[anywhere()] * 4 + [vmem()] * 4,
+            out_specs=[anywhere()] * 4 + [vmem()] * (4 + inner),
             scratch_shapes=[
-                pltpu.VMEM((4, count, levels, columns + LANES), BF16),
-                pltpu.VMEM((4, count, levels, columns + LANES), BF16),
+                pltpu.VMEM((4, count, levels, columns + 2 * LANES), BF16),
+                pltpu.VMEM((4, count, levels, columns + 2 * LANES), BF16),
                 pltpu.VMEM((columns // LANES, 4, count, levels, 2 * LANES), F32),
                 pltpu.VMEM((4, count, levels, columns), F32),
                 pltpu.VMEM((4, kept, levels, columns), BF16),
                 pltpu.VMEM((4, kept, levels, columns), BF16),
-                pltpu.VMEM((rows, 8, columns), F32),
                 pltpu.VMEM((rows, 8, columns), F32),
                 pltpu.SemaphoreType.DMA((28,)),
                 *[pltpu.VMEM(w.shape, w.dtype) for w in weights if inner],
@@ -624,8 +640,18 @@
             name="tend_inner" if inner else "tend_edge",
         )(*args, *old)
 
+    quarter = lat_count // 4
+    polar_bands = [*range(quarter), *range(lat_count - quarter, lat_count)]
+
+    def polar_ring(value, step):
+        pairs = []
+        for band in polar_bands:
+            first = band * lon_count
+            pairs += [(first + i, first + (i + step) % lon_count) for i in range(lon_count)]
+        return lax.ppermute(value, ("lat", "lon"), pairs)
+
     def exchange(east_part, west_part, far_part):
-        return ring(east_part, 1), ring(west_part, -1), ring(far_part, 2)
+        return polar_ring(east_part, 1), polar_ring(west_part, -1), polar_ring(far_part, 2)
 
     def finish(inner, received, local, old):
         count = inner_count if inner else edge_kept
@@ -645,8 +671,9 @@
             name="finish_inner" if inner else "finish_edge",
         )(*args, *old)
 
-    *outs, local_inner, a, b, c = tendencies(True, [])
+    *outs, local_inner, a, b, c, mass_x = tendencies(True, [])
     received_inner = exchange(a, b, c)
+    outs = [*outs, mass_x]
     *outs, local_edge, a, b, c = tendencies(False, outs)
     received_edge = exchange(a, b, c)
     outs = finish(True, received_inner, local_inner, outs)

time: 38.9 us -> 49.1 us (1.26)
  starting transfers between devices: 11.1 us -> 22.5 us
  Pallas kernels: 26.4 us -> 25.1 us
    ppermute x0 -> x6, starting transfers between devices: none -> 17 us  [polar_ring(): return lax.ppermute(value, ('lat', 'lon'), pairs)]
    ppermute x8 -> x2, starting transfers between devices: 8.12 us -> 2.49 us  [ring(): lax.ppermute(value, 'lon', [(i, (i + step) % lon_count) for i in range(lo...]
    pallas_call x2, Pallas kernels: 18.5 us -> 17.2 us  [tendencies(): pl.pallas_call(functools.partial(tend_kernel, inner, count, kept), out_sh...]
  transfers between devices with their start and end apart: 10 -> 10, of which waited for: 0 -> 0; matrix products, arithmetic and copies ran while one was open for 0% -> 0% of each run, Pallas kernels for 58% -> 43%
where the time goes in v9:
time: 49.1 us; the launch traced here: 48.8 us
  Pallas kernels  25.1 us (51%)
  starting transfers between devices  22.5 us (46%)
  between operations  1.17 us (2%)
    pallas_call x2, Pallas kernels, tendencies(): pl.pallas_call(functools.partial(tend_kernel, inner, count, kept), out_sh...  17.2 us
    ppermute x6, starting transfers between devices, polar_ring(): return lax.ppermute(value, ('lat', 'lon'), pairs)  17 us
    pallas_call x2, Pallas kernels, finish(): pl.pallas_call(functools.partial(finish_kernel, inner, count), out_shape=...  5.71 us
    ppermute x2, starting transfers between devices, ring(): lax.ppermute(value, 'lon', [(i, (i + step) % lon_count) for i in range(lo...  2.49 us
    ppermute x1, starting transfers between devices, shards(): strip_a = lax.ppermute(to_a, 'lat', [(i, i ^ 1) for i in range(lat_count)])  2.33 us
    pallas_call x1, Pallas kernels, shards(): pl.pallas_call(pack_kernel, out_shape=[like(strip, columns)] * 2 + [like(...  2.18 us
  transfers between devices with their start and end apart: 10, of which 0 were waited for; matrix products, arithmetic and copies ran while one was open for 0% of the time, Pallas kernels for 43%

profile of v9, /device:TPU:0, one launch (start us, length us, event | category | flops | bytes accessed | tf_op | source)
XLA Modules:
  0.0 48.8 jit_solution(8609109415014168454)
XLA Ops:
  0.6 0.0 copy-start.11
  0.6 0.0 copy-start.12
  0.7 0.0 copy-start.3
  0.7 0.0 copy-start.2
  0.7 0.0 copy-start.1
  0.7 0.0 copy-start
  0.7 0.0 copy-start.6
  0.7 2.2 %pack_edges.1 = (f32[200,896]{1,0:T(8,128)S(1)}, f32[200,896]{1,0:T(8,128)S(1)}, f32[48,128]{1,0:T(8,128)S(1)}, f32[48,128]{1,0:T(8,128)S(1)}, f32[3,16,8,256]{3,2,1,0:T(8,128)S(1)}) custom-call(f32[16,16,896]{2,1,0:T(8,128)} %refs_0_.9, f32[16,16,896]{2,1,0:T(8,128)} %refs_1_.9, f32[16,16,896]{2,1,0:T(8,128)} %refs_2_.9, f32[16,16,896]{2,1,0:T(8,128)} %refs_3_.9, ...), custom_call_target="tpu_custom_call" | custom-call | tf_op jit(solution)/shard_map/pack_edges/pallas_call | solution.py:574
  2.9 0.5 %collective-permute-start = (f32[48,128]{1,0:T(8,128)S(1)}, f32[48,128]{1,0:T(8,128)S(1)}, u32[]{:S(2)}, u32[]{:S(2)}) collective-permute-start(f32[48,128]{1,0:T(8,128)S(1)} %get-tuple-element.30), channel_id=1, source_target_pairs={{0,1},{1,2},{2,3},{3,0},{4,5},{5,6},{6,7},{7,4},{8,9},{9,10},{10,1... | collective-permute-start | bytes 73736 | tf_op jit(solution)/shard_map/ppermute | solution.py:591
  3.4 2.0 %collective-permute-start.1 = (f32[48,128]{1,0:T(8,128)S(1)}, f32[48,128]{1,0:T(8,128)S(1)}, u32[]{:S(2)}, u32[]{:S(2)}) collective-permute-start(f32[48,128]{1,0:T(8,128)S(1)} %get-tuple-element.31), channel_id=1, source_target_pairs={{0,3},{1,0},{2,1},{3,2},{4,7},{5,4},{6,5},{7,6},{8,11},{9,8},{10,9... | collective-permute-start | bytes 73736 | tf_op jit(solution)/shard_map/ppermute | solution.py:591
  5.4 2.3 %collective-permute-start.2 = (f32[200,896]{1,0:T(8,128)S(1)}, f32[200,896]{1,0:T(8,128)S(1)}, u32[]{:S(2)}, u32[]{:S(2)}) collective-permute-start(f32[200,896]{1,0:T(8,128)S(1)} %get-tuple-element.33), channel_id=1, source_target_pairs={{0,4},{4,0},{8,12},{12,8},{1,5},{5,1},{9,13},{13,9},{2,6},{6,2},{1... | collective-permute-start | bytes 2150408 | tf_op jit(solution)/shard_map/ppermute | solution.py:596
  7.7 0.7 %collective-permute-start.3 = (f32[200,896]{1,0:T(8,128)S(1)}, f32[200,896]{1,0:T(8,128)S(1)}, u32[]{:S(2)}, u32[]{:S(2)}) collective-permute-start(f32[200,896]{1,0:T(8,128)S(1)} %get-tuple-element.34), channel_id=1, source_target_pairs={{4,8},{8,4},{5,9},{9,5},{6,10},{10,6},{7,11},{11,7},{20,24},{24,20... | collective-permute-start | bytes 2150408 | tf_op jit(solution)/shard_map/ppermute | solution.py:597
  8.4 0.0 collective-permute-done.refs_5_
  8.4 0.0 collective-permute-done.1.refs_6_
  8.4 0.0 copy-done.11
  8.5 0.0 copy-done.12
  8.5 0.0 copy-done.3
  8.5 0.0 copy-done.2
  8.5 0.0 copy-done.1
  8.5 0.0 copy-done
  8.5 0.0 copy-done.6
  8.5 0.0 copy-start.7
  8.5 0.0 copy-start.8
  8.5 0.0 copy-start.9
  8.6 0.0 copy-start.10
  8.6 13.5 %tend_inner.1 = (f32[16,16,896]{2,1,0:T(8,128)}, f32[16,16,896]{2,1,0:T(8,128)}, f32[16,16,896]{2,1,0:T(8,128)}, f32[16,16,896]{2,1,0:T(8,128)}, f32[4,208,256]{...) custom-call(f32[64]{0:T(128)S(1)} %copy-done.12, ...), custom_call_target="tpu_custom_call" | custom-call | flops 14909440000 | bytes 4194304 | tf_op jit(solution)/shard_map/tend_inner/pallas_call | solution.py:612
  22.0 3.4 %collective-permute-start.9 = (f32[104,128]{1,0:T(8,128)S(1)}, f32[104,128]{1,0:T(8,128)S(1)}, u32[]{:S(2)}, u32[]{:S(2)}) collective-permute-start(f32[104,128]{1,0:T(8,128)S(1)} %get-tuple-element.46), channel_id=1, source_target_pairs={{0,2},{1,3},{2,0},{3,1},{12,14},{13,15},{14,12},{15,13},{16,18},{1... | collective-permute-start | bytes 159752 | tf_op jit(solution)/shard_map/ppermute | solution.py:651
  25.4 1.9 %collective-permute-start.7 = (f32[208,128]{1,0:T(8,128)S(1)}, f32[208,128]{1,0:T(8,128)S(1)}, u32[]{:S(2)}, u32[]{:S(2)}) collective-permute-start(f32[208,128]{1,0:T(8,128)S(1)} %get-tuple-element.44), channel_id=1, source_target_pairs={{0,1},{1,2},{2,3},{3,0},{12,13},{13,14},{14,15},{15,12},{16,17},{1... | collective-permute-start | bytes 319496 | tf_op jit(solution)/shard_map/ppermute | solution.py:651
  27.4 3.6 %collective-permute-start.8 = (f32[208,128]{1,0:T(8,128)S(1)}, f32[208,128]{1,0:T(8,128)S(1)}, u32[]{:S(2)}, u32[]{:S(2)}) collective-permute-start(f32[208,128]{1,0:T(8,128)S(1)} %get-tuple-element.45), channel_id=1, source_target_pairs={{0,3},{1,0},{2,1},{3,2},{12,15},{13,12},{14,13},{15,14},{16,19},{1... | collective-permute-start | bytes 319496 | tf_op jit(solution)/shard_map/ppermute | solution.py:651
  31.0 0.0 collective-permute-done.2.refs_8_
  31.0 0.0 collective-permute-done.3.refs_9_
  31.0 0.0 copy-done.7
  31.1 0.0 copy-done.8
  31.1 0.0 copy-done.9
  31.1 0.0 copy-done.10
  31.1 0.0 copy-start.4
  31.1 0.0 copy-start.5
  31.1 3.7 %tend_edge.1 = (f32[16,16,896]{2,1,0:T(8,128)}, f32[16,16,896]{2,1,0:T(8,128)}, f32[16,16,896]{2,1,0:T(8,128)}, f32[16,16,896]{2,1,0:T(8,128)}, f32[4,48,256]{2,...) custom-call(f32[64]{0:T(128)S(1)} %copy-done.12, ...), custom_call_target="tpu_custom_call", output_to_operand_aliasing={{0}: (17, {}), {1}: (18, {}), {2}: (19, {}), {3}: (20, {})} | custom-call | flops 6881280000 | bytes 4194304 | tf_op jit(solution)/shard_map/tend_edge/pallas_call | solution.py:612
  34.8 1.9 %collective-permute-start.4 = (f32[48,128]{1,0:T(8,128)S(1)}, f32[48,128]{1,0:T(8,128)S(1)}, u32[]{:S(2)}, u32[]{:S(2)}) collective-permute-start(f32[48,128]{1,0:T(8,128)S(1)} %get-tuple-element.40), channel_id=1, source_target_pairs={{0,1},{1,2},{2,3},{3,0},{12,13},{13,14},{14,15},{15,12},{16,17},{1... | collective-permute-start | bytes 73736 | tf_op jit(solution)/shard_map/ppermute | solution.py:651
  36.8 3.6 %collective-permute-start.5 = (f32[48,128]{1,0:T(8,128)S(1)}, f32[48,128]{1,0:T(8,128)S(1)}, u32[]{:S(2)}, u32[]{:S(2)}) collective-permute-start(f32[48,128]{1,0:T(8,128)S(1)} %get-tuple-element.41), channel_id=1, source_target_pairs={{0,3},{1,0},{2,1},{3,2},{12,15},{13,12},{14,13},{15,14},{16,19},{1... | collective-permute-start | bytes 73736 | tf_op jit(solution)/shard_map/ppermute | solution.py:651
  40.4 0.0 collective-permute-done.9.refs_6_
  40.4 2.4 %collective-permute-start.6 = (f32[24,128]{1,0:T(8,128)S(1)}, f32[24,128]{1,0:T(8,128)S(1)}, u32[]{:S(2)}, u32[]{:S(2)}) collective-permute-start(f32[24,128]{1,0:T(8,128)S(1)} %get-tuple-element.42), channel_id=1, source_target_pairs={{0,2},{1,3},{2,0},{3,1},{12,14},{13,15},{14,12},{15,13},{16,18},{1... | collective-permute-start | bytes 36872 | tf_op jit(solution)/shard_map/ppermute | solution.py:651
  42.9 0.0 collective-permute-done.7.refs_4_
  42.9 0.0 collective-permute-done.8.refs_5_
  42.9 0.0 copy-done.4
  42.9 0.0 copy-done.5
  42.9 3.8 %finish_inner.1 = (f32[16,16,896]{2,1,0:T(8,128)}, f32[16,16,896]{2,1,0:T(8,128)}, f32[16,16,896]{2,1,0:T(8,128)}, f32[16,16,896]{2,1,0:T(8,128)}) custom-call(f32[16,16,896]{2,1,0:T(8,128)S(1)} %copy-done, f32[16,16,896]{2,1,0:T(8,128)S(1)} %copy-done.1, ...), custom_call_target="tpu_custom_call", output_to_operand_aliasing={{0}: (11, {}), {1}: (12, {}), {2}: (13, {}), {3}: (14, {})} | custom-call | tf_op jit(solution)/shard_map/finish_inner/pallas_call | solution.py:660
  46.7 0.0 collective-permute-done.6.refs_6_
  46.7 0.0 collective-permute-done.4.refs_4_
  46.7 0.0 collective-permute-done.5.refs_5_
  46.7 1.9 %finish_edge.1 = (f32[16,16,896]{2,1,0:T(8,128)}, f32[16,16,896]{2,1,0:T(8,128)}, f32[16,16,896]{2,1,0:T(8,128)}, f32[16,16,896]{2,1,0:T(8,128)}) custom-call(f32[16,16,896]{2,1,0:T(8,128)S(1)} %copy-done, f32[16,16,896]{2,1,0:T(8,128)S(1)} %copy-done.1, ...), custom_call_target="tpu_custom_call", output_to_operand_aliasing={{0}: (11, {}), {1}: (12, {}), {2}: (13, {}), {3}: (14, {})} | custom-call | tf_op jit(solution)/shard_map/finish_edge/pallas_call | solution.py:660
Async XLA Ops:
  0.6 7.8 %copy-start.11 = (f32[64]{0:T(128)S(1)}, f32[64]{0:T(128)}, u32[]{:S(2)}) copy-start(f32[64]{0:T(128)} %constant.26.clone.spin) | copy-start | bytes 772
  0.6 7.8 %copy-start.12 = (f32[64]{0:T(128)S(1)}, f32[64]{0:T(128)}, u32[]{:S(2)}) copy-start(f32[64]{0:T(128)} %constant.25.clone.metric) | copy-start | bytes 772
  0.7 7.8 %copy-start.3 = (f32[16,16,896]{2,1,0:T(8,128)S(1)}, f32[16,16,896]{2,1,0:T(8,128)}, u32[]{:S(2)}) copy-start(f32[16,16,896]{2,1,0:T(8,128)} %refs_3_.9) | copy-start | bytes 2752516
  0.7 7.8 %copy-start.2 = (f32[16,16,896]{2,1,0:T(8,128)S(1)}, f32[16,16,896]{2,1,0:T(8,128)}, u32[]{:S(2)}) copy-start(f32[16,16,896]{2,1,0:T(8,128)} %refs_2_.9) | copy-start | bytes 2752516
  0.7 7.8 %copy-start.1 = (f32[16,16,896]{2,1,0:T(8,128)S(1)}, f32[16,16,896]{2,1,0:T(8,128)}, u32[]{:S(2)}) copy-start(f32[16,16,896]{2,1,0:T(8,128)} %refs_1_.9) | copy-start | bytes 2752516
  0.7 7.8 %copy-start = (f32[16,16,896]{2,1,0:T(8,128)S(1)}, f32[16,16,896]{2,1,0:T(8,128)}, u32[]{:S(2)}) copy-start(f32[16,16,896]{2,1,0:T(8,128)} %refs_0_.9) | copy-start | bytes 2752516
  0.7 7.8 %copy-start.6 = (f32[16,896]{1,0:T(8,128)S(1)}, f32[16,896]{1,0:T(8,128)}, u32[]{:S(2)}) copy-start(f32[16,896]{1,0:T(8,128)} %refs_4_.5) | copy-start | bytes 172036
  2.9 5.5 %collective-permute-start = (f32[48,128]{1,0:T(8,128)S(1)}, f32[48,128]{1,0:T(8,128)S(1)}, u32[]{:S(2)}, u32[]{:S(2)}) collective-permute-start(f32[48,128]{1,0:T(8,128)S(1)} %get-tuple-element.30), channel_id=1, source_target_pairs={{0,1},{1,2},{2,3},{3,0},{4,5},{5,6},{6,7},{7,4},{8,9},{9,10},{10,1... | collective-permute-start | bytes 73736 | tf_op jit(solution)/shard_map/ppermute | solution.py:591
  3.4 5.0 %collective-permute-start.1 = (f32[48,128]{1,0:T(8,128)S(1)}, f32[48,128]{1,0:T(8,128)S(1)}, u32[]{:S(2)}, u32[]{:S(2)}) collective-permute-start(f32[48,128]{1,0:T(8,128)S(1)} %get-tuple-element.31), channel_id=1, source_target_pairs={{0,3},{1,0},{2,1},{3,2},{4,7},{5,4},{6,5},{7,6},{8,11},{9,8},{10,9... | collective-permute-start | bytes 73736 | tf_op jit(solution)/shard_map/ppermute | solution.py:591
  5.4 25.6 %collective-permute-start.2 = (f32[200,896]{1,0:T(8,128)S(1)}, f32[200,896]{1,0:T(8,128)S(1)}, u32[]{:S(2)}, u32[]{:S(2)}) collective-permute-start(f32[200,896]{1,0:T(8,128)S(1)} %get-tuple-element.33), channel_id=1, source_target_pairs={{0,4},{4,0},{8,12},{12,8},{1,5},{5,1},{9,13},{13,9},{2,6},{6,2},{1... | collective-permute-start | bytes 2150408 | tf_op jit(solution)/shard_map/ppermute | solution.py:596
  7.7 23.3 %collective-permute-start.3 = (f32[200,896]{1,0:T(8,128)S(1)}, f32[200,896]{1,0:T(8,128)S(1)}, u32[]{:S(2)}, u32[]{:S(2)}) collective-permute-start(f32[200,896]{1,0:T(8,128)S(1)} %get-tuple-element.34), channel_id=1, source_target_pairs={{4,8},{8,4},{5,9},{9,5},{6,10},{10,6},{7,11},{11,7},{20,24},{24,20... | collective-permute-start | bytes 2150408 | tf_op jit(solution)/shard_map/ppermute | solution.py:597
  8.5 22.5 %copy-start.7 = (bf16[2688,256]{1,0:T(8,128)(2,1)S(1)}, bf16[2688,256]{1,0:T(8,128)(2,1)}, u32[]{:S(2)}) copy-start(bf16[2688,256]{1,0:T(8,128)(2,1)} %constant.20.clone.refs_9_.refs_12_) | copy-start | bytes 4128772
  8.5 22.5 %copy-start.8 = (bf16[768,256]{1,0:T(8,128)(2,1)S(1)}, bf16[768,256]{1,0:T(8,128)(2,1)}, u32[]{:S(2)}) copy-start(bf16[768,256]{1,0:T(8,128)(2,1)} %constant.21.clone.refs_10_.refs_13_) | copy-start | bytes 1179652
  8.5 22.5 %copy-start.9 = (bf16[768,256]{1,0:T(8,128)(2,1)S(1)}, bf16[768,256]{1,0:T(8,128)(2,1)}, u32[]{:S(2)}) copy-start(bf16[768,256]{1,0:T(8,128)(2,1)} %constant.19.clone.refs_8_.refs_11_) | copy-start | bytes 1179652
  8.6 22.5 %copy-start.10 = (bf16[768,128]{1,0:T(8,128)(2,1)S(1)}, bf16[768,128]{1,0:T(8,128)(2,1)}, u32[]{:S(2)}) copy-start(bf16[768,128]{1,0:T(8,128)(2,1)} %constant.22.clone.refs_11_.refs_14_) | copy-start | bytes 589828
  22.0 18.4 %collective-permute-start.9 = (f32[104,128]{1,0:T(8,128)S(1)}, f32[104,128]{1,0:T(8,128)S(1)}, u32[]{:S(2)}, u32[]{:S(2)}) collective-permute-start(f32[104,128]{1,0:T(8,128)S(1)} %get-tuple-element.46), channel_id=1, source_target_pairs={{0,2},{1,3},{2,0},{3,1},{12,14},{13,15},{14,12},{15,13},{16,18},{1... | collective-permute-start | bytes 159752 | tf_op jit(solution)/shard_map/ppermute | solution.py:651
  25.4 17.4 %collective-permute-start.7 = (f32[208,128]{1,0:T(8,128)S(1)}, f32[208,128]{1,0:T(8,128)S(1)}, u32[]{:S(2)}, u32[]{:S(2)}) collective-permute-start(f32[208,128]{1,0:T(8,128)S(1)} %get-tuple-element.44), channel_id=1, source_target_pairs={{0,1},{1,2},{2,3},{3,0},{12,13},{13,14},{14,15},{15,12},{16,17},{1... | collective-permute-start | bytes 319496 | tf_op jit(solution)/shard_map/ppermute | solution.py:651
  27.4 15.5 %collective-permute-start.8 = (f32[208,128]{1,0:T(8,128)S(1)}, f32[208,128]{1,0:T(8,128)S(1)}, u32[]{:S(2)}, u32[]{:S(2)}) collective-permute-start(f32[208,128]{1,0:T(8,128)S(1)} %get-tuple-element.45), channel_id=1, source_target_pairs={{0,3},{1,0},{2,1},{3,2},{12,15},{13,12},{14,13},{15,14},{16,19},{1... | collective-permute-start | bytes 319496 | tf_op jit(solution)/shard_map/ppermute | solution.py:651
  31.1 11.8 %copy-start.4 = (bf16[768,896]{1,0:T(8,128)(2,1)S(1)}, bf16[768,896]{1,0:T(8,128)(2,1)}, u32[]{:S(2)}) copy-start(bf16[768,896]{1,0:T(8,128)(2,1)} %constant.24.clone.refs_10_) | copy-start | bytes 4128772
  31.1 11.8 %copy-start.5 = (bf16[128,256]{1,0:T(8,128)(2,1)S(1)}, bf16[128,256]{1,0:T(8,128)(2,1)}, u32[]{:S(2)}) copy-start(bf16[128,256]{1,0:T(8,128)(2,1)} %constant.23.clone.refs_9_) | copy-start | bytes 196612
  34.8 11.9 %collective-permute-start.4 = (f32[48,128]{1,0:T(8,128)S(1)}, f32[48,128]{1,0:T(8,128)S(1)}, u32[]{:S(2)}, u32[]{:S(2)}) collective-permute-start(f32[48,128]{1,0:T(8,128)S(1)} %get-tuple-element.40), channel_id=1, source_target_pairs={{0,1},{1,2},{2,3},{3,0},{12,13},{13,14},{14,15},{15,12},{16,17},{1... | collective-permute-start | bytes 73736 | tf_op jit(solution)/shard_map/ppermute | solution.py:651
  36.8 10.0 %collective-permute-start.5 = (f32[48,128]{1,0:T(8,128)S(1)}, f32[48,128]{1,0:T(8,128)S(1)}, u32[]{:S(2)}, u32[]{:S(2)}) collective-permute-start(f32[48,128]{1,0:T(8,128)S(1)} %get-tuple-element.41), channel_id=1, source_target_pairs={{0,3},{1,0},{2,1},{3,2},{12,15},{13,12},{14,13},{15,14},{16,19},{1... | collective-permute-start | bytes 73736 | tf_op jit(solution)/shard_map/ppermute | solution.py:651
  40.4 6.3 %collective-permute-start.6 = (f32[24,128]{1,0:T(8,128)S(1)}, f32[24,128]{1,0:T(8,128)S(1)}, u32[]{:S(2)}, u32[]{:S(2)}) collective-permute-start(f32[24,128]{1,0:T(8,128)S(1)} %get-tuple-element.42), channel_id=1, source_target_pairs={{0,2},{1,3},{2,0},{3,1},{12,14},{13,15},{14,12},{15,13},{16,18},{1... | collective-permute-start | bytes 36872 | tf_op jit(solution)/shard_map/ppermute | solution.py:651

commit v10 on v9

--- a/solution.py
+++ b/solution.py
@@ -61,14 +61,14 @@
 
 
 def band_table():
-    band = np.zeros((3 * LANES, 2 * LANES))
+    band = np.zeros((2 * LANES, 2 * LANES))
     slope = {-3: -1, -2: 9, -1: -45, 1: 45, 2: -9, 3: 1}
     smooth = {-3: 1, -2: -6, -1: 15, 0: -20, 1: 15, 2: -6, 3: 1}
     for j in range(LANES):
         for k, value in slope.items():
-            band[LANES + j + k, j] = value
+            band[j + 3 + k, j] = value
         for k, value in smooth.items():
-            band[LANES + j + k, LANES + j] = value
+            band[j + 3 + k, LANES + j] = value
     return np.concatenate([band, band], axis=0).astype(ml_dtypes.bfloat16)
 
 
@@ -96,8 +96,7 @@
         nodes=nodes.astype(np.float32)[None],
         band=band_table(),
         spread=stacked_halves(spread.T),
-        own=stacked_halves(own.T),
-        send=stacked_halves(send),
+        own=stacked_halves(np.concatenate([own.T, send, np.zeros((NODES, LANES))], axis=1)),
         take=take,
         gather=stacked_halves(STEP * spread),
     )
@@ -265,15 +264,15 @@
     mass, west, east, waves = some(4)
     strips = some(2) if edge_rows else None
     mass_x = some(1)[0] if edge_rows else None
-    tables_in = some(4)
+    tables_in = some(3)
     if edge_rows:
         some(4)
     outs = some(4)
     local, to_east, to_west, to_far = some(4)
     mass_x = some(1)[0] if inner else mass_x
-    high, low, cross, new, kept_high, kept_low, mass_y, sems = some(8)
+    high, low, cross, new, kept_parts, mass_y, sems = some(7)
     tables = refs if inner else tables_in
-    band, spread, own, send = tables
+    band, spread, own = tables
     rows, columns = mass.shape
     levels = fields[0].shape[1]
     items = count * levels
@@ -294,32 +293,35 @@
         mass_x[...] = mass_slope_x(mass, west, east, levels)
         mass_y[...] = mass_slope_y(jnp.concatenate([blank, mass[...], blank], axis=0))
 
+    lane = lax.broadcasted_iota(jnp.int32, (levels, LANES), 1)
+
     def cut(i, carry):
         row = entry_row(inner, i, rows)
         halo = pl.ds(pl.multiple_of((row % 2) * levels, levels), levels)
         for f in range(4):
             lead = 16 * (row // 2) + 3 * f
-            for t in range(tiles + 2):
-                if t == 0:
-                    tile = pltpu.roll(west[halo, :], lax.rem(2 * LANES - 3 - lead, LANES), 1)
-                elif t <= tiles:
-                    tile = fields[f][row, :, (t - 1) * LANES : t * LANES]
+            before = pltpu.roll(west[halo, :], lax.rem(LANES - lead, LANES), 1)
+            for t in range(tiles + 1):
+                if t < tiles:
+                    tile = pltpu.roll(fields[f][row, :, t * LANES : (t + 1) * LANES], 3, 1)
                 else:
-                    tile = pltpu.roll(east[halo, :], lax.rem(LANES - lead, LANES), 1)
-                top = tile.astype(BF16)
+                    tile = pltpu.roll(east[halo, :], lax.rem(LANES + 3 - lead, LANES), 1)
+                whole = jnp.where(lane < 3, before, tile)
+                top = whole.astype(BF16)
                 high[f, i, :, t * LANES : (t + 1) * LANES] = top
-                low[f, i, :, t * LANES : (t + 1) * LANES] = (tile - top.astype(F32)).astype(BF16)
+                low[f, i, :, t * LANES : (t + 1) * LANES] = (whole - top.astype(F32)).astype(BF16)
+                before = tile
         return carry
 
     def slopes_x(first, size):
         lax.fori_loop(first, first + size, cut, 0)
         wait_all(fetched[:1])
         for t in range(tiles):
-            span = slice(t * LANES, (t + 3) * LANES)
+            span = slice(t * LANES, (t + 2) * LANES)
             some_rows = slice(first, first + size)
             both = jnp.concatenate(
                 [
-                    table[:, some_rows, :, span].reshape(4 * size * levels, 3 * LANES)
+                    table[:, some_rows, :, span].reshape(4 * size * levels, 2 * LANES)
                     for table in (high, low)
                 ],
                 axis=1,
@@ -421,8 +423,11 @@
     def _():
         def emit(f, i, span, q, change):
             top = change.astype(BF16)
-            kept_high[f, i, :, span] = top
-            kept_low[f, i, :, span] = (change - top.astype(F32)).astype(BF16)
+            first = span.start
+            kept_parts[f, i, :, first : first + LANES] = top
+            kept_parts[f, i, :, 2 * columns + first : 2 * columns + first + LANES] = top
+            rest = (change - top.astype(F32)).astype(BF16)
+            kept_parts[f, i, :, columns + first : columns + first + LANES] = rest
 
         slopes_x(0, kept)
         if inner:
@@ -437,16 +442,15 @@
         c_all, s_all, d_all = [
             spread_waves(waves, part, inner, kept, levels) for part in range(3)
         ]
-        top = kept_high[...].reshape(4 * kept_items, columns)
-        rest = kept_low[...].reshape(4 * kept_items, columns)
-        nodal = dot(jnp.concatenate([top, rest, top], axis=1), spread[...])
+        nodal = dot(kept_parts[...].reshape(4 * kept_items, 3 * columns), spread[...])
         turned = []
         for f in range(4):
             part = nodal[f * kept_items : (f + 1) * kept_items]
             turned += [c_all * part, s_all * part]
         turned = split(jnp.concatenate(turned, axis=0))
         moved = dot(turned, own[...])
-        sent = dot(turned, send[...])
+        sent = moved[:, NODES : NODES + LANES]
+        moved = moved[:, :NODES]
         for f in range(4):
             at = 2 * f * kept_items
             local[f] = (
@@ -603,7 +607,7 @@
     def tendencies(inner, old):
         count, kept = (inner_count, inner_count) if inner else (6, edge_kept)
         kept_items = kept * levels
-        weights = [tables[k] for k in ("band", "spread", "own", "send")]
+        weights = [tables[k] for k in ("band", "spread", "own")]
         if inner:
             weights = [in_hbm(w) for w in weights]
         halos = [] if inner else [strip_a, strip_b, *old[4:]]
@@ -617,17 +621,16 @@
             + [like(kept_items // 2, LANES)]
             + [like(rows, 8, columns)] * inner,
             in_specs=[smem()] * 2
-            + [vmem()] * (len(args) - 6)
-            + [anywhere() if inner else vmem()] * 4
+            + [vmem()] * (len(args) - 5)
+            + [anywhere() if inner else vmem()] * 3
             + [anywhere()] * len(old),
             out_specs=[anywhere()] * 4 + [vmem()] * (4 + inner),
             scratch_shapes=[
-                pltpu.VMEM((4, count, levels, columns + 2 * LANES), BF16),
-                pltpu.VMEM((4, count, levels, columns + 2 * LANES), BF16),
+                pltpu.VMEM((4, count, levels, columns + LANES), BF16),
+                pltpu.VMEM((4, count, levels, columns + LANES), BF16),
                 pltpu.VMEM((columns // LANES, 4, count, levels, 2 * LANES), F32),
                 pltpu.VMEM((4, count, levels, columns), F32),
-                pltpu.VMEM((4, kept, levels, columns), BF16),
-                pltpu.VMEM((4, kept, levels, columns), BF16),
+                pltpu.VMEM((4, kept, levels, 3 * columns), BF16),
                 pltpu.VMEM((rows, 8, columns), F32),
                 pltpu.SemaphoreType.DMA((28,)),
                 *[pltpu.VMEM(w.shape, w.dtype) for w in weights if inner],
@@ -640,18 +643,8 @@
             name="tend_inner" if inner else "tend_edge",
         )(*args, *old)
 
-    quarter = lat_count // 4
-    polar_bands = [*range(quarter), *range(lat_count - quarter, lat_count)]
-
-    def polar_ring(value, step):
-        pairs = []
-        for band in polar_bands:
-            first = band * lon_count
-            pairs += [(first + i, first + (i + step) % lon_count) for i in range(lon_count)]
-        return lax.ppermute(value, ("lat", "lon"), pairs)
-
     def exchange(east_part, west_part, far_part):
-        return polar_ring(east_part, 1), polar_ring(west_part, -1), polar_ring(far_part, 2)
+        return ring(east_part, 1), ring(west_part, -1), ring(far_part, 2)
 
     def finish(inner, received, local, old):
         count = inner_count if inner else edge_kept

time: 49.1 us -> 37.5 us (0.76)
  starting transfers between devices: 22.5 us -> 11.1 us
    ppermute x6 -> x0, starting transfers between devices: 17 us -> none  [polar_ring(): return lax.ppermute(value, ('lat', 'lon'), pairs)]
    ppermute x2 -> x8, starting transfers between devices: 2.49 us -> 8.11 us  [ring(): lax.ppermute(value, 'lon', [(i, (i + step) % lon_count) for i in range(lo...]
  transfers between devices with their start and end apart: 10 -> 10, of which waited for: 0 -> 0; matrix products, arithmetic and copies ran while one was open for 0% -> 0% of each run, Pallas kernels for 43% -> 56%
where the time goes in v10:
time: 37.5 us; the launch traced here: 37.3 us
  Pallas kernels  25 us (67%)
  starting transfers between devices  11.1 us (30%)
  between operations  1.07 us (3%)
    pallas_call x2, Pallas kernels, tendencies(): pl.pallas_call(functools.partial(tend_kernel, inner, count, kept), out_sh...  17.1 us
    ppermute x8, starting transfers between devices, ring(): lax.ppermute(value, 'lon', [(i, (i + step) % lon_count) for i in range(lo...  8.11 us
    pallas_call x2, Pallas kernels, finish(): pl.pallas_call(functools.partial(finish_kernel, inner, count), out_shape=...  5.71 us
    ppermute x1, starting transfers between devices, shards(): strip_a = lax.ppermute(to_a, 'lat', [(i, i ^ 1) for i in range(lat_count)])  2.33 us
    pallas_call x1, Pallas kernels, shards(): pl.pallas_call(pack_kernel, out_shape=[like(strip, columns)] * 2 + [like(...  2.18 us
  transfers between devices with their start and end apart: 10, of which 0 were waited for; matrix products, arithmetic and copies ran while one was open for 0% of the time, Pallas kernels for 56%

profile of v10, /device:TPU:0, one launch (start us, length us, event | category | flops | bytes accessed | tf_op | source)
XLA Modules:
  0.0 37.3 jit_solution(1214225866706712035)
XLA Ops:
  0.6 0.0 copy-start.10
  0.6 0.0 copy-start.11
  0.7 0.0 copy-start.3
  0.7 0.0 copy-start.2
  0.7 0.0 copy-start.1
  0.7 0.0 copy-start
  0.7 0.0 copy-start.6
  0.7 2.2 %pack_edges.1 = (f32[200,896]{1,0:T(8,128)S(1)}, f32[200,896]{1,0:T(8,128)S(1)}, f32[48,128]{1,0:T(8,128)S(1)}, f32[48,128]{1,0:T(8,128)S(1)}, f32[3,16,8,256]{3,2,1,0:T(8,128)S(1)}) custom-call(f32[16,16,896]{2,1,0:T(8,128)} %refs_0_.9, f32[16,16,896]{2,1,0:T(8,128)} %refs_1_.9, f32[16,16,896]{2,1,0:T(8,128)} %refs_2_.9, f32[16,16,896]{2,1,0:T(8,128)} %refs_3_.9, ...), custom_call_target="tpu_custom_call" | custom-call | tf_op jit(solution)/shard_map/pack_edges/pallas_call | solution.py:578
  2.9 0.5 %collective-permute-start = (f32[48,128]{1,0:T(8,128)S(1)}, f32[48,128]{1,0:T(8,128)S(1)}, u32[]{:S(2)}, u32[]{:S(2)}) collective-permute-start(f32[48,128]{1,0:T(8,128)S(1)} %get-tuple-element.30), channel_id=1, source_target_pairs={{0,1},{1,2},{2,3},{3,0},{4,5},{5,6},{6,7},{7,4},{8,9},{9,10},{10,1... | collective-permute-start | bytes 73736 | tf_op jit(solution)/shard_map/ppermute | solution.py:595
  3.4 2.0 %collective-permute-start.1 = (f32[48,128]{1,0:T(8,128)S(1)}, f32[48,128]{1,0:T(8,128)S(1)}, u32[]{:S(2)}, u32[]{:S(2)}) collective-permute-start(f32[48,128]{1,0:T(8,128)S(1)} %get-tuple-element.31), channel_id=1, source_target_pairs={{0,3},{1,0},{2,1},{3,2},{4,7},{5,4},{6,5},{7,6},{8,11},{9,8},{10,9... | collective-permute-start | bytes 73736 | tf_op jit(solution)/shard_map/ppermute | solution.py:595
  5.4 2.3 %collective-permute-start.2 = (f32[200,896]{1,0:T(8,128)S(1)}, f32[200,896]{1,0:T(8,128)S(1)}, u32[]{:S(2)}, u32[]{:S(2)}) collective-permute-start(f32[200,896]{1,0:T(8,128)S(1)} %get-tuple-element.33), channel_id=1, source_target_pairs={{0,4},{4,0},{8,12},{12,8},{1,5},{5,1},{9,13},{13,9},{2,6},{6,2},{1... | collective-permute-start | bytes 2150408 | tf_op jit(solution)/shard_map/ppermute | solution.py:600
  7.7 0.7 %collective-permute-start.3 = (f32[200,896]{1,0:T(8,128)S(1)}, f32[200,896]{1,0:T(8,128)S(1)}, u32[]{:S(2)}, u32[]{:S(2)}) collective-permute-start(f32[200,896]{1,0:T(8,128)S(1)} %get-tuple-element.34), channel_id=1, source_target_pairs={{4,8},{8,4},{5,9},{9,5},{6,10},{10,6},{7,11},{11,7},{20,24},{24,20... | collective-permute-start | bytes 2150408 | tf_op jit(solution)/shard_map/ppermute | solution.py:601
  8.4 0.0 collective-permute-done.refs_5_
  8.4 0.0 collective-permute-done.1.refs_6_
  8.4 0.0 copy-done.10
  8.5 0.0 copy-done.11
  8.5 0.0 copy-done.3
  8.5 0.0 copy-done.2
  8.5 0.0 copy-done.1
  8.5 0.0 copy-done
  8.5 0.0 copy-done.6
  8.5 0.0 copy-start.7
  8.5 0.0 copy-start.8
  8.5 0.0 copy-start.9
  8.6 13.3 %tend_inner.1 = (f32[16,16,896]{2,1,0:T(8,128)}, f32[16,16,896]{2,1,0:T(8,128)}, f32[16,16,896]{2,1,0:T(8,128)}, f32[16,16,896]{2,1,0:T(8,128)}, f32[4,208,256]{...) custom-call(f32[64]{0:T(128)S(1)} %copy-done.11, ...), custom_call_target="tpu_custom_call" | custom-call | flops 14909440000 | bytes 4194304 | tf_op jit(solution)/shard_map/tend_inner/pallas_call | solution.py:616
  21.8 1.6 %collective-permute-start.9 = (f32[104,128]{1,0:T(8,128)S(1)}, f32[104,128]{1,0:T(8,128)S(1)}, u32[]{:S(2)}, u32[]{:S(2)}) collective-permute-start(f32[104,128]{1,0:T(8,128)S(1)} %get-tuple-element.46), channel_id=1, source_target_pairs={{0,2},{1,3},{2,0},{3,1},{4,6},{5,7},{6,4},{7,5},{8,10},{9,11},{10,... | collective-permute-start | bytes 159752 | tf_op jit(solution)/shard_map/ppermute | solution.py:595
  23.4 0.0 collective-permute-start.7
  23.4 1.7 %collective-permute-start.8 = (f32[208,128]{1,0:T(8,128)S(1)}, f32[208,128]{1,0:T(8,128)S(1)}, u32[]{:S(2)}, u32[]{:S(2)}) collective-permute-start(f32[208,128]{1,0:T(8,128)S(1)} %get-tuple-element.45), channel_id=1, source_target_pairs={{0,3},{1,0},{2,1},{3,2},{4,7},{5,4},{6,5},{7,6},{8,11},{9,8},{10,9... | collective-permute-start | bytes 319496 | tf_op jit(solution)/shard_map/ppermute | solution.py:595
  25.1 0.0 collective-permute-done.2.refs_8_
  25.1 0.0 collective-permute-done.3.refs_9_
  25.1 0.0 copy-done.7
  25.1 0.0 copy-done.8
  25.1 0.0 copy-done.9
  25.2 0.0 copy-start.4
  25.2 0.0 copy-start.5
  25.2 3.8 %tend_edge.1 = (f32[16,16,896]{2,1,0:T(8,128)}, f32[16,16,896]{2,1,0:T(8,128)}, f32[16,16,896]{2,1,0:T(8,128)}, f32[16,16,896]{2,1,0:T(8,128)}, f32[4,48,256]{2,...) custom-call(f32[64]{0:T(128)S(1)} %copy-done.11, ...), custom_call_target="tpu_custom_call", output_to_operand_aliasing={{0}: (16, {}), {1}: (17, {}), {2}: (18, {}), {3}: (19, {})} | custom-call | flops 6881280000 | bytes 4194304 | tf_op jit(solution)/shard_map/tend_edge/pallas_call | solution.py:616
  29.0 0.1 collective-permute-start.4
  29.1 1.7 %collective-permute-start.5 = (f32[48,128]{1,0:T(8,128)S(1)}, f32[48,128]{1,0:T(8,128)S(1)}, u32[]{:S(2)}, u32[]{:S(2)}) collective-permute-start(f32[48,128]{1,0:T(8,128)S(1)} %get-tuple-element.41), channel_id=1, source_target_pairs={{0,3},{1,0},{2,1},{3,2},{4,7},{5,4},{6,5},{7,6},{8,11},{9,8},{10,9... | collective-permute-start | bytes 73736 | tf_op jit(solution)/shard_map/ppermute | solution.py:595
  30.8 0.0 collective-permute-done.9.refs_6_
  30.8 0.5 %collective-permute-start.6 = (f32[24,128]{1,0:T(8,128)S(1)}, f32[24,128]{1,0:T(8,128)S(1)}, u32[]{:S(2)}, u32[]{:S(2)}) collective-permute-start(f32[24,128]{1,0:T(8,128)S(1)} %get-tuple-element.42), channel_id=1, source_target_pairs={{0,2},{1,3},{2,0},{3,1},{4,6},{5,7},{6,4},{7,5},{8,10},{9,11},{10,... | collective-permute-start | bytes 36872 | tf_op jit(solution)/shard_map/ppermute | solution.py:595
  31.4 0.0 collective-permute-done.7.refs_4_
  31.4 0.0 collective-permute-done.8.refs_5_
  31.4 0.0 copy-done.4
  31.4 0.0 copy-done.5
  31.4 3.8 %finish_inner.1 = (f32[16,16,896]{2,1,0:T(8,128)}, f32[16,16,896]{2,1,0:T(8,128)}, f32[16,16,896]{2,1,0:T(8,128)}, f32[16,16,896]{2,1,0:T(8,128)}) custom-call(f32[16,16,896]{2,1,0:T(8,128)S(1)} %copy-done, f32[16,16,896]{2,1,0:T(8,128)S(1)} %copy-done.1, ...), custom_call_target="tpu_custom_call", output_to_operand_aliasing={{0}: (11, {}), {1}: (12, {}), {2}: (13, {}), {3}: (14, {})} | custom-call | tf_op jit(solution)/shard_map/finish_inner/pallas_call | solution.py:653
  35.2 0.0 collective-permute-done.6.refs_6_
  35.2 0.0 collective-permute-done.4.refs_4_
  35.2 0.0 collective-permute-done.5.refs_5_
  35.2 1.9 %finish_edge.1 = (f32[16,16,896]{2,1,0:T(8,128)}, f32[16,16,896]{2,1,0:T(8,128)}, f32[16,16,896]{2,1,0:T(8,128)}, f32[16,16,896]{2,1,0:T(8,128)}) custom-call(f32[16,16,896]{2,1,0:T(8,128)S(1)} %copy-done, f32[16,16,896]{2,1,0:T(8,128)S(1)} %copy-done.1, ...), custom_call_target="tpu_custom_call", output_to_operand_aliasing={{0}: (11, {}), {1}: (12, {}), {2}: (13, {}), {3}: (14, {})} | custom-call | tf_op jit(solution)/shard_map/finish_edge/pallas_call | solution.py:653
Async XLA Ops:
  0.6 7.8 %copy-start.10 = (f32[64]{0:T(128)S(1)}, f32[64]{0:T(128)}, u32[]{:S(2)}) copy-start(f32[64]{0:T(128)} %constant.23.clone.spin) | copy-start | bytes 772
  0.6 7.8 %copy-start.11 = (f32[64]{0:T(128)S(1)}, f32[64]{0:T(128)}, u32[]{:S(2)}) copy-start(f32[64]{0:T(128)} %constant.22.clone.metric) | copy-start | bytes 772
  0.7 7.8 %copy-start.3 = (f32[16,16,896]{2,1,0:T(8,128)S(1)}, f32[16,16,896]{2,1,0:T(8,128)}, u32[]{:S(2)}) copy-start(f32[16,16,896]{2,1,0:T(8,128)} %refs_3_.9) | copy-start | bytes 2752516
  0.7 7.8 %copy-start.2 = (f32[16,16,896]{2,1,0:T(8,128)S(1)}, f32[16,16,896]{2,1,0:T(8,128)}, u32[]{:S(2)}) copy-start(f32[16,16,896]{2,1,0:T(8,128)} %refs_2_.9) | copy-start | bytes 2752516
  0.7 7.8 %copy-start.1 = (f32[16,16,896]{2,1,0:T(8,128)S(1)}, f32[16,16,896]{2,1,0:T(8,128)}, u32[]{:S(2)}) copy-start(f32[16,16,896]{2,1,0:T(8,128)} %refs_1_.9) | copy-start | bytes 2752516
  0.7 7.8 %copy-start = (f32[16,16,896]{2,1,0:T(8,128)S(1)}, f32[16,16,896]{2,1,0:T(8,128)}, u32[]{:S(2)}) copy-start(f32[16,16,896]{2,1,0:T(8,128)} %refs_0_.9) | copy-start | bytes 2752516
  0.7 7.8 %copy-start.6 = (f32[16,896]{1,0:T(8,128)S(1)}, f32[16,896]{1,0:T(8,128)}, u32[]{:S(2)}) copy-start(f32[16,896]{1,0:T(8,128)} %refs_4_.5) | copy-start | bytes 172036
  2.9 5.5 %collective-permute-start = (f32[48,128]{1,0:T(8,128)S(1)}, f32[48,128]{1,0:T(8,128)S(1)}, u32[]{:S(2)}, u32[]{:S(2)}) collective-permute-start(f32[48,128]{1,0:T(8,128)S(1)} %get-tuple-element.30), channel_id=1, source_target_pairs={{0,1},{1,2},{2,3},{3,0},{4,5},{5,6},{6,7},{7,4},{8,9},{9,10},{10,1... | collective-permute-start | bytes 73736 | tf_op jit(solution)/shard_map/ppermute | solution.py:595
  3.4 5.0 %collective-permute-start.1 = (f32[48,128]{1,0:T(8,128)S(1)}, f32[48,128]{1,0:T(8,128)S(1)}, u32[]{:S(2)}, u32[]{:S(2)}) collective-permute-start(f32[48,128]{1,0:T(8,128)S(1)} %get-tuple-element.31), channel_id=1, source_target_pairs={{0,3},{1,0},{2,1},{3,2},{4,7},{5,4},{6,5},{7,6},{8,11},{9,8},{10,9... | collective-permute-start | bytes 73736 | tf_op jit(solution)/shard_map/ppermute | solution.py:595
  5.4 19.7 %collective-permute-start.2 = (f32[200,896]{1,0:T(8,128)S(1)}, f32[200,896]{1,0:T(8,128)S(1)}, u32[]{:S(2)}, u32[]{:S(2)}) collective-permute-start(f32[200,896]{1,0:T(8,128)S(1)} %get-tuple-element.33), channel_id=1, source_target_pairs={{0,4},{4,0},{8,12},{12,8},{1,5},{5,1},{9,13},{13,9},{2,6},{6,2},{1... | collective-permute-start | bytes 2150408 | tf_op jit(solution)/shard_map/ppermute | solution.py:600
  7.7 17.4 %collective-permute-start.3 = (f32[200,896]{1,0:T(8,128)S(1)}, f32[200,896]{1,0:T(8,128)S(1)}, u32[]{:S(2)}, u32[]{:S(2)}) collective-permute-start(f32[200,896]{1,0:T(8,128)S(1)} %get-tuple-element.34), channel_id=1, source_target_pairs={{4,8},{8,4},{5,9},{9,5},{6,10},{10,6},{7,11},{11,7},{20,24},{24,20... | collective-permute-start | bytes 2150408 | tf_op jit(solution)/shard_map/ppermute | solution.py:601
  8.5 16.6 %copy-start.7 = (bf16[2688,256]{1,0:T(8,128)(2,1)S(1)}, bf16[2688,256]{1,0:T(8,128)(2,1)}, u32[]{:S(2)}) copy-start(bf16[2688,256]{1,0:T(8,128)(2,1)} %constant.18.clone.refs_9_.refs_12_) | copy-start | bytes 4128772
  8.5 16.6 %copy-start.8 = (bf16[768,512]{1,0:T(8,128)(2,1)S(1)}, bf16[768,512]{1,0:T(8,128)(2,1)}, u32[]{:S(2)}) copy-start(bf16[768,512]{1,0:T(8,128)(2,1)} %constant.19.clone.refs_10_.refs_13_) | copy-start | bytes 2359300
  8.5 16.6 %copy-start.9 = (bf16[512,256]{1,0:T(8,128)(2,1)S(1)}, bf16[512,256]{1,0:T(8,128)(2,1)}, u32[]{:S(2)}) copy-start(bf16[512,256]{1,0:T(8,128)(2,1)} %constant.17.clone.refs_8_.refs_11_) | copy-start | bytes 786436
  21.8 9.0 %collective-permute-start.9 = (f32[104,128]{1,0:T(8,128)S(1)}, f32[104,128]{1,0:T(8,128)S(1)}, u32[]{:S(2)}, u32[]{:S(2)}) collective-permute-start(f32[104,128]{1,0:T(8,128)S(1)} %get-tuple-element.46), channel_id=1, source_target_pairs={{0,2},{1,3},{2,0},{3,1},{4,6},{5,7},{6,4},{7,5},{8,10},{9,11},{10,... | collective-permute-start | bytes 159752 | tf_op jit(solution)/shard_map/ppermute | solution.py:595
  23.4 8.0 %collective-permute-start.7 = (f32[208,128]{1,0:T(8,128)S(1)}, f32[208,128]{1,0:T(8,128)S(1)}, u32[]{:S(2)}, u32[]{:S(2)}) collective-permute-start(f32[208,128]{1,0:T(8,128)S(1)} %get-tuple-element.44), channel_id=1, source_target_pairs={{0,1},{1,2},{2,3},{3,0},{4,5},{5,6},{6,7},{7,4},{8,9},{9,10},{10,1... | collective-permute-start | bytes 319496 | tf_op jit(solution)/shard_map/ppermute | solution.py:595
  23.4 8.0 %collective-permute-start.8 = (f32[208,128]{1,0:T(8,128)S(1)}, f32[208,128]{1,0:T(8,128)S(1)}, u32[]{:S(2)}, u32[]{:S(2)}) collective-permute-start(f32[208,128]{1,0:T(8,128)S(1)} %get-tuple-element.45), channel_id=1, source_target_pairs={{0,3},{1,0},{2,1},{3,2},{4,7},{5,4},{6,5},{7,6},{8,11},{9,8},{10,9... | collective-permute-start | bytes 319496 | tf_op jit(solution)/shard_map/ppermute | solution.py:595
  25.2 6.2 %copy-start.4 = (bf16[768,896]{1,0:T(8,128)(2,1)S(1)}, bf16[768,896]{1,0:T(8,128)(2,1)}, u32[]{:S(2)}) copy-start(bf16[768,896]{1,0:T(8,128)(2,1)} %constant.21.clone.refs_10_) | copy-start | bytes 4128772
  25.2 6.2 %copy-start.5 = (bf16[128,256]{1,0:T(8,128)(2,1)S(1)}, bf16[128,256]{1,0:T(8,128)(2,1)}, u32[]{:S(2)}) copy-start(bf16[128,256]{1,0:T(8,128)(2,1)} %constant.20.clone.refs_9_) | copy-start | bytes 196612
  29.0 6.2 %collective-permute-start.4 = (f32[48,128]{1,0:T(8,128)S(1)}, f32[48,128]{1,0:T(8,128)S(1)}, u32[]{:S(2)}, u32[]{:S(2)}) collective-permute-start(f32[48,128]{1,0:T(8,128)S(1)} %get-tuple-element.40), channel_id=1, source_target_pairs={{0,1},{1,2},{2,3},{3,0},{4,5},{5,6},{6,7},{7,4},{8,9},{9,10},{10,1... | collective-permute-start | bytes 73736 | tf_op jit(solution)/shard_map/ppermute | solution.py:595
  29.1 6.1 %collective-permute-start.5 = (f32[48,128]{1,0:T(8,128)S(1)}, f32[48,128]{1,0:T(8,128)S(1)}, u32[]{:S(2)}, u32[]{:S(2)}) collective-permute-start(f32[48,128]{1,0:T(8,128)S(1)} %get-tuple-element.41), channel_id=1, source_target_pairs={{0,3},{1,0},{2,1},{3,2},{4,7},{5,4},{6,5},{7,6},{8,11},{9,8},{10,9... | collective-permute-start | bytes 73736 | tf_op jit(solution)/shard_map/ppermute | solution.py:595
  30.8 4.3 %collective-permute-start.6 = (f32[24,128]{1,0:T(8,128)S(1)}, f32[24,128]{1,0:T(8,128)S(1)}, u32[]{:S(2)}, u32[]{:S(2)}) collective-permute-start(f32[24,128]{1,0:T(8,128)S(1)} %get-tuple-element.42), channel_id=1, source_target_pairs={{0,2},{1,3},{2,0},{3,1},{4,6},{5,7},{6,4},{7,5},{8,10},{9,11},{10,... | collective-permute-start | bytes 36872 | tf_op jit(solution)/shard_map/ppermute | solution.py:595

commit v11 on v10

--- a/solution.py
+++ b/solution.py
@@ -95,7 +95,9 @@
     return dict(
         nodes=nodes.astype(np.float32)[None],
         band=band_table(),
-        spread=stacked_halves(spread.T),
+        spread=np.stack(
+            [stacked_halves(spread.T[t : t + LANES]) for t in range(0, sector, LANES)]
+        ),
         own=stacked_halves(np.concatenate([own.T, send, np.zeros((NODES, LANES))], axis=1)),
         take=take,
         gather=stacked_halves(STEP * spread),
@@ -251,6 +253,14 @@
     return jnp.concatenate([waves[part, n] for n in numbers for _ in range(levels // 8)], axis=0)
 
 
+def sizes_of_groups(inner, count):
+    if not inner:
+        return [3] * (count // 3)
+    at_pole = 3 if count % 2 else 0
+    half = (count - at_pole) // 2
+    return [half, half] + [3] * (at_pole // 3)
+
+
 def tend_kernel(inner, count, kept, metric, spin, *refs):
     edge_rows = not inner
     refs = list(refs)
@@ -270,7 +280,9 @@
     outs = some(4)
     local, to_east, to_west, to_far = some(4)
     mass_x = some(1)[0] if inner else mass_x
-    high, low, cross, new, kept_parts, mass_y, sems = some(7)
+    high, low, new, mass_y, sems = some(5)
+    group_sizes = sizes_of_groups(inner, count)
+    crosses, kept_parts, nodals = [some(len(group_sizes)) for _ in range(3)]
     tables = refs if inner else tables_in
     band, spread, own = tables
     rows, columns = mass.shape
@@ -313,29 +325,31 @@
                 before = tile
         return carry
 
-    def slopes_x(first, size):
-        lax.fori_loop(first, first + size, cut, 0)
-        wait_all(fetched[:1])
-        for t in range(tiles):
-            span = slice(t * LANES, (t + 2) * LANES)
-            some_rows = slice(first, first + size)
-            both = jnp.concatenate(
-                [
-                    table[:, some_rows, :, span].reshape(4 * size * levels, 2 * LANES)
-                    for table in (high, low)
-                ],
-                axis=1,
-            )
-            cross[t, :, some_rows] = dot(both, band[...]).reshape(4, size, levels, 2 * LANES)
+    def columns_of(t, width=1):
+        return pl.ds(pl.multiple_of(t * LANES, LANES), width * LANES)
+
+    def slopes_x(g, first, t):
+        size = group_sizes[g]
+        parts = [
+            table[:, first : first + size, :, columns_of(t, 2)].reshape(4 * size * levels, 2 * LANES)
+            for table in (high, low)
+        ]
+        product = dot(jnp.concatenate(parts, axis=1), band[...])
+        crosses[g][t] = product.reshape(4, size, levels, 2 * LANES)
+
+    def to_nodes(g, t):
+        size = group_sizes[g]
+        part = dot(kept_parts[g][t].reshape(4 * size * levels, 3 * LANES), spread[t])
+        nodals[g][...] += part.reshape(4, size * levels, NODES)
 
     start_row = lax.axis_index("lat") * rows
 
     def whole(lines):
         return jnp.concatenate([lines] * (levels // 8), axis=0)
 
-    def tendency(t, first, numbers, row_of, emit, inward=1.0):
+    def tendency(t, g, first, numbers, row_of, emit, inward=1.0):
         size = len(numbers)
-        span = slice(t * LANES, (t + 1) * LANES)
+        span = columns_of(t)
         metrics = [metric[start_row + n] for n in numbers]
         spins = [spin[start_row + n] for n in numbers]
         centers = [[row_of(f, j, span) for j in range(size)] for f in range(3)]
@@ -351,8 +365,8 @@
             column = [row_of(f, j, span) for j in range(-3, size + 3)]
             for j in range(size):
                 q = column[j + 3]
-                slope_x = cross[t, f, first + j, :, :LANES]
-                smooth_x = cross[t, f, first + j, :, LANES:]
+                slope_x = crosses[g][t, f, j, :, :LANES]
+                smooth_x = crosses[g][t, f, j, :, LANES:]
                 slope_y, smooth_y = stencil(q, column[j + 4 : j + 7], column[j + 2 :: -1][:3])
                 change = (fast_size[j] * smooth_x - fast[j] * slope_x) + (
                     up_size[j] * smooth_y - up[j] * slope_y
@@ -367,9 +381,9 @@
                     change = change + (spins[j] * centers[1][j] - push_x[j])
                 elif f == 1:
                     change = change - (spins[j] * centers[0][j] + push_y[j])
-                emit(f, first + j, span, q, change)
-
-    def edge_side(side, first, emit):
+                emit(g, f, j, first + j, t, q, change)
+
+    def edge_group(side):
         edge = edge_row(3 * side, rows)
         step = jnp.where(edge == 0, 1, -1)
 
@@ -381,22 +395,49 @@
             start = levels * (3 * f - j - 1)
             return strips[side][start : start + levels, span]
 
-        numbers = [edge + step * j for j in range(3)]
-        for t in range(tiles):
-            tendency(t, first, numbers, row_of, emit, step.astype(F32))
-
-    def inner_rows(emit):
-        def step(n, carry):
-            first_row = 3 + 2 * n
-
-            def row_of(f, j, span):
-                return fields[f][first_row + j, :, span]
-
-            for t in range(tiles):
-                tendency(t, 2 * n, [first_row, first_row + 1], row_of, emit)
+        return [edge + step * j for j in range(3)], row_of, step.astype(F32)
+
+    def inner_group(g):
+        size = group_sizes[0]
+        first_row = 3 + size * g
+
+        def row_of(f, j, span):
+            return fields[f][first_row + j, :, span]
+
+        return [first_row + j for j in range(size)], row_of, 1.0
+
+    def run(groups, emit, filtered):
+        starts = [sum(group_sizes[:g]) for g in range(len(groups) + 1)]
+        lax.fori_loop(0, starts[-1], cut, 0)
+        wait_all(fetched[:1])
+
+        def prepare(t, carry):
+            slopes_x(0, 0, t)
             return carry
 
-        lax.fori_loop(0, (rows - 6) // 2, step, 0)
+        lax.fori_loop(0, tiles, prepare, 0)
+        if filtered:
+            wait_all(fetched[1:])
+        for g, (numbers, row_of, inward) in enumerate(groups):
+
+            def step(t, carry):
+                if g + 1 < len(groups):
+                    slopes_x(g + 1, starts[g + 1], t)
+                if filtered and g > 0:
+                    to_nodes(g - 1, t)
+                tendency(t, g, starts[g], numbers, row_of, emit, inward)
+                return carry
+
+            if filtered:
+                nodals[g][...] = jnp.zeros(nodals[g].shape, F32)
+            lax.fori_loop(0, tiles, step, 0)
+
+        def complete(t, carry):
+            to_nodes(len(groups) - 1, t)
+            return carry
+
+        if filtered:
+            lax.fori_loop(0, tiles, complete, 0)
 
     def write_out(f):
         if edge_rows:
@@ -405,48 +446,36 @@
 
     @pl.when(jnp.logical_not(is_polar()))
     def _():
-        def emit(f, i, span, q, change):
-            new[f, i, :, span] = q + STEP * change
-
-        if inner:
-            slopes_x(0, rows - 6)
-            inner_rows(emit)
-        else:
-            slopes_x(0, 6)
-            edge_side(0, 0, emit)
-            edge_side(1, 3, emit)
+        def emit(g, f, j, i, t, q, change):
+            new[f, i, :, columns_of(t)] = q + STEP * change
+
+        groups = [inner_group(0), inner_group(1)] if inner else [edge_group(0), edge_group(1)]
+        run(groups, emit, False)
         pairs = [pair for f in range(4) for pair in write_out(f)]
         wait_all(start_all(pairs, sems))
         wait_all(fetched[1:])
 
     @pl.when(is_polar())
     def _():
-        def emit(f, i, span, q, change):
+        def emit(g, f, j, i, t, q, change):
             top = change.astype(BF16)
-            first = span.start
-            kept_parts[f, i, :, first : first + LANES] = top
-            kept_parts[f, i, :, 2 * columns + first : 2 * columns + first + LANES] = top
             rest = (change - top.astype(F32)).astype(BF16)
-            kept_parts[f, i, :, columns + first : columns + first + LANES] = rest
-
-        slopes_x(0, kept)
+            kept_parts[g][t, f, j] = jnp.concatenate([top, rest, top], axis=1)
+
         if inner:
-            inner_rows(emit)
-            if kept > rows - 6:
-                edge_side(1, rows - 6, emit)
+            groups = [inner_group(0), inner_group(1)] + [edge_group(1)] * (kept > rows - 6)
         else:
-            edge_side(0, 0, emit)
-            if kept > 3:
-                edge_side(1, 3, emit)
-        wait_all(fetched[1:])
+            groups = [edge_group(side) for side in range(kept // 3)]
+        run(groups, emit, True)
         c_all, s_all, d_all = [
             spread_waves(waves, part, inner, kept, levels) for part in range(3)
         ]
-        nodal = dot(kept_parts[...].reshape(4 * kept_items, 3 * columns), spread[...])
+        nodal = [
+            jnp.concatenate([nodals[g][f] for g in range(len(groups))], axis=0) for f in range(4)
+        ]
         turned = []
         for f in range(4):
-            part = nodal[f * kept_items : (f + 1) * kept_items]
-            turned += [c_all * part, s_all * part]
+            turned += [c_all * nodal[f], s_all * nodal[f]]
         turned = split(jnp.concatenate(turned, axis=0))
         moved = dot(turned, own[...])
         sent = moved[:, NODES : NODES + LANES]
@@ -456,7 +485,7 @@
             local[f] = (
                 s_all * moved[at : at + kept_items]
                 - c_all * moved[at + kept_items : at + 2 * kept_items]
-                + d_all * nodal[f * kept_items : (f + 1) * kept_items]
+                + d_all * nodal[f]
             )
         wide = lax.broadcasted_iota(jnp.int32, (kept_items, LANES), 1)
         for out, first, size in ((to_east, 0, NEAR), (to_west, NEAR, NEAR), (to_far, 2 * NEAR, FAR)):
@@ -607,6 +636,8 @@
     def tendencies(inner, old):
         count, kept = (inner_count, inner_count) if inner else (6, edge_kept)
         kept_items = kept * levels
+        tiles = columns // LANES
+        group_sizes = sizes_of_groups(inner, count)
         weights = [tables[k] for k in ("band", "spread", "own")]
         if inner:
             weights = [in_hbm(w) for w in weights]
@@ -628,11 +659,12 @@
             scratch_shapes=[
                 pltpu.VMEM((4, count, levels, columns + LANES), BF16),
                 pltpu.VMEM((4, count, levels, columns + LANES), BF16),
-                pltpu.VMEM((columns // LANES, 4, count, levels, 2 * LANES), F32),
                 pltpu.VMEM((4, count, levels, columns), F32),
-                pltpu.VMEM((4, kept, levels, 3 * columns), BF16),
                 pltpu.VMEM((rows, 8, columns), F32),
                 pltpu.SemaphoreType.DMA((28,)),
+                *[pltpu.VMEM((tiles, 4, n, levels, 2 * LANES), F32) for n in group_sizes],
+                *[pltpu.VMEM((tiles, 4, n, levels, 3 * LANES), BF16) for n in group_sizes],
+                *[pltpu.VMEM((4, n * levels, NODES), F32) for n in group_sizes],
                 *[pltpu.VMEM(w.shape, w.dtype) for w in weights if inner],
             ],
             input_output_aliases={len(args) + f: f for f in range(4)} if old else {},

time: 37.5 us -> 42.4 us (1.13)
  Pallas kernels: 25 us -> 30.1 us
    pallas_call x2, Pallas kernels: 17.1 us -> 22.3 us  [tendencies(): pl.pallas_call(functools.partial(tend_kernel, inner, count, kept), out_sh...]
  transfers between devices with their start and end apart: 10 -> 10, of which waited for: 0 -> 0; matrix products, arithmetic and copies ran while one was open for 0% -> 0% of each run, Pallas kernels for 56% -> 62%
where the time goes in v11:
time: 42.4 us; the launch traced here: 42.3 us
  Pallas kernels  30.1 us (71%)
  starting transfers between devices  11.1 us (26%)
  between operations  0.91 us (2%)
    pallas_call x2, Pallas kernels, tendencies(): pl.pallas_call(functools.partial(tend_kernel, inner, count, kept), out_sh...  22.3 us
    ppermute x8, starting transfers between devices, ring(): lax.ppermute(value, 'lon', [(i, (i + step) % lon_count) for i in range(lo...  8.12 us
    pallas_call x2, Pallas kernels, finish(): pl.pallas_call(functools.partial(finish_kernel, inner, count), out_shape=...  5.71 us
    ppermute x1, starting transfers between devices, shards(): strip_a = lax.ppermute(to_a, 'lat', [(i, i ^ 1) for i in range(lat_count)])  2.33 us
    pallas_call x1, Pallas kernels, shards(): pl.pallas_call(pack_kernel, out_shape=[like(strip, columns)] * 2 + [like(...  2.18 us
  transfers between devices with their start and end apart: 10, of which 0 were waited for; matrix products, arithmetic and copies ran while one was open for 0% of the time, Pallas kernels for 62%

profile of v11, /device:TPU:0, one launch (start us, length us, event | category | flops | bytes accessed | tf_op | source)
XLA Modules:
  0.0 42.3 jit_solution(2782182053977088063)
XLA Ops:
  0.6 0.0 copy-start.10
  0.6 0.0 copy-start.11
  0.7 0.0 copy-start.3
  0.7 0.0 copy-start.2
  0.7 0.0 copy-start.1
  0.7 0.0 copy-start
  0.7 0.0 copy-start.6
  0.7 2.2 %pack_edges.1 = (f32[200,896]{1,0:T(8,128)S(1)}, f32[200,896]{1,0:T(8,128)S(1)}, f32[48,128]{1,0:T(8,128)S(1)}, f32[48,128]{1,0:T(8,128)S(1)}, f32[3,16,8,256]{3,2,1,0:T(8,128)S(1)}) custom-call(f32[16,16,896]{2,1,0:T(8,128)} %refs_0_.9, f32[16,16,896]{2,1,0:T(8,128)} %refs_1_.9, f32[16,16,896]{2,1,0:T(8,128)} %refs_2_.9, f32[16,16,896]{2,1,0:T(8,128)} %refs_3_.9, ...), custom_call_target="tpu_custom_call" | custom-call | tf_op jit(solution)/shard_map/pack_edges/pallas_call | solution.py:607
  2.9 0.5 %collective-permute-start = (f32[48,128]{1,0:T(8,128)S(1)}, f32[48,128]{1,0:T(8,128)S(1)}, u32[]{:S(2)}, u32[]{:S(2)}) collective-permute-start(f32[48,128]{1,0:T(8,128)S(1)} %get-tuple-element.30), channel_id=1, source_target_pairs={{0,1},{1,2},{2,3},{3,0},{4,5},{5,6},{6,7},{7,4},{8,9},{9,10},{10,1... | collective-permute-start | bytes 73736 | tf_op jit(solution)/shard_map/ppermute | solution.py:624
  3.4 2.0 %collective-permute-start.1 = (f32[48,128]{1,0:T(8,128)S(1)}, f32[48,128]{1,0:T(8,128)S(1)}, u32[]{:S(2)}, u32[]{:S(2)}) collective-permute-start(f32[48,128]{1,0:T(8,128)S(1)} %get-tuple-element.31), channel_id=1, source_target_pairs={{0,3},{1,0},{2,1},{3,2},{4,7},{5,4},{6,5},{7,6},{8,11},{9,8},{10,9... | collective-permute-start | bytes 73736 | tf_op jit(solution)/shard_map/ppermute | solution.py:624
  5.4 2.3 %collective-permute-start.2 = (f32[200,896]{1,0:T(8,128)S(1)}, f32[200,896]{1,0:T(8,128)S(1)}, u32[]{:S(2)}, u32[]{:S(2)}) collective-permute-start(f32[200,896]{1,0:T(8,128)S(1)} %get-tuple-element.33), channel_id=1, source_target_pairs={{0,4},{4,0},{8,12},{12,8},{1,5},{5,1},{9,13},{13,9},{2,6},{6,2},{1... | collective-permute-start | bytes 2150408 | tf_op jit(solution)/shard_map/ppermute | solution.py:629
  7.7 0.7 %collective-permute-start.3 = (f32[200,896]{1,0:T(8,128)S(1)}, f32[200,896]{1,0:T(8,128)S(1)}, u32[]{:S(2)}, u32[]{:S(2)}) collective-permute-start(f32[200,896]{1,0:T(8,128)S(1)} %get-tuple-element.34), channel_id=1, source_target_pairs={{4,8},{8,4},{5,9},{9,5},{6,10},{10,6},{7,11},{11,7},{20,24},{24,20... | collective-permute-start | bytes 2150408 | tf_op jit(solution)/shard_map/ppermute | solution.py:630
  8.4 0.0 collective-permute-done.refs_5_
  8.4 0.0 collective-permute-done.1.refs_6_
  8.4 0.0 copy-done.10
  8.5 0.0 copy-done.11
  8.5 0.0 copy-done.3
  8.5 0.0 copy-done.2
  8.5 0.0 copy-done.1
  8.5 0.0 copy-done
  8.5 0.0 copy-done.6
  8.5 0.0 copy-start.7
  8.5 0.0 copy-start.8
  8.5 0.0 copy-start.9
  8.6 16.4 %tend_inner.1 = (f32[16,16,896]{2,1,0:T(8,128)}, f32[16,16,896]{2,1,0:T(8,128)}, f32[16,16,896]{2,1,0:T(8,128)}, f32[16,16,896]{2,1,0:T(8,128)}, f32[4,208,256]{...) custom-call(f32[64]{0:T(128)S(1)} %copy-done.11, ...), custom_call_target="tpu_custom_call" | custom-call | flops 14909440000 | bytes 4194304 | tf_op jit(solution)/shard_map/tend_inner/pallas_call | solution.py:647
  25.0 1.6 %collective-permute-start.9 = (f32[104,128]{1,0:T(8,128)S(1)}, f32[104,128]{1,0:T(8,128)S(1)}, u32[]{:S(2)}, u32[]{:S(2)}) collective-permute-start(f32[104,128]{1,0:T(8,128)S(1)} %get-tuple-element.46), channel_id=1, source_target_pairs={{0,2},{1,3},{2,0},{3,1},{4,6},{5,7},{6,4},{7,5},{8,10},{9,11},{10,... | collective-permute-start | bytes 159752 | tf_op jit(solution)/shard_map/ppermute | solution.py:624
  26.6 0.0 collective-permute-start.7
  26.6 1.7 %collective-permute-start.8 = (f32[208,128]{1,0:T(8,128)S(1)}, f32[208,128]{1,0:T(8,128)S(1)}, u32[]{:S(2)}, u32[]{:S(2)}) collective-permute-start(f32[208,128]{1,0:T(8,128)S(1)} %get-tuple-element.45), channel_id=1, source_target_pairs={{0,3},{1,0},{2,1},{3,2},{4,7},{5,4},{6,5},{7,6},{8,11},{9,8},{10,9... | collective-permute-start | bytes 319496 | tf_op jit(solution)/shard_map/ppermute | solution.py:624
  28.3 0.0 collective-permute-done.2.refs_8_
  28.3 0.0 collective-permute-done.3.refs_9_
  28.3 0.0 copy-done.7
  28.3 0.0 copy-done.8
  28.3 0.0 copy-done.9
  28.4 0.0 copy-start.4
  28.4 0.0 copy-start.5
  28.4 5.8 %tend_edge.1 = (f32[16,16,896]{2,1,0:T(8,128)}, f32[16,16,896]{2,1,0:T(8,128)}, f32[16,16,896]{2,1,0:T(8,128)}, f32[16,16,896]{2,1,0:T(8,128)}, f32[4,48,256]{2,...) custom-call(f32[64]{0:T(128)S(1)} %copy-done.11, ...), custom_call_target="tpu_custom_call", output_to_operand_aliasing={{0}: (16, {}), {1}: (17, {}), {2}: (18, {}), {3}: (19, {})} | custom-call | flops 6881280000 | bytes 4194304 | tf_op jit(solution)/shard_map/tend_edge/pallas_call | solution.py:647
  34.2 0.1 collective-permute-start.4
  34.3 1.7 %collective-permute-start.5 = (f32[48,128]{1,0:T(8,128)S(1)}, f32[48,128]{1,0:T(8,128)S(1)}, u32[]{:S(2)}, u32[]{:S(2)}) collective-permute-start(f32[48,128]{1,0:T(8,128)S(1)} %get-tuple-element.41), channel_id=1, source_target_pairs={{0,3},{1,0},{2,1},{3,2},{4,7},{5,4},{6,5},{7,6},{8,11},{9,8},{10,9... | collective-permute-start | bytes 73736 | tf_op jit(solution)/shard_map/ppermute | solution.py:624
  36.0 0.0 collective-permute-done.9.refs_6_
  36.0 0.5 %collective-permute-start.6 = (f32[24,128]{1,0:T(8,128)S(1)}, f32[24,128]{1,0:T(8,128)S(1)}, u32[]{:S(2)}, u32[]{:S(2)}) collective-permute-start(f32[24,128]{1,0:T(8,128)S(1)} %get-tuple-element.42), channel_id=1, source_target_pairs={{0,2},{1,3},{2,0},{3,1},{4,6},{5,7},{6,4},{7,5},{8,10},{9,11},{10,... | collective-permute-start | bytes 36872 | tf_op jit(solution)/shard_map/ppermute | solution.py:624
  36.5 0.0 collective-permute-done.7.refs_4_
  36.5 0.0 collective-permute-done.8.refs_5_
  36.5 0.0 copy-done.4
  36.5 0.0 copy-done.5
  36.5 3.8 %finish_inner.1 = (f32[16,16,896]{2,1,0:T(8,128)}, f32[16,16,896]{2,1,0:T(8,128)}, f32[16,16,896]{2,1,0:T(8,128)}, f32[16,16,896]{2,1,0:T(8,128)}) custom-call(f32[16,16,896]{2,1,0:T(8,128)S(1)} %copy-done, f32[16,16,896]{2,1,0:T(8,128)S(1)} %copy-done.1, ...), custom_call_target="tpu_custom_call", output_to_operand_aliasing={{0}: (11, {}), {1}: (12, {}), {2}: (13, {}), {3}: (14, {})} | custom-call | tf_op jit(solution)/shard_map/finish_inner/pallas_call | solution.py:685
  40.3 0.0 collective-permute-done.6.refs_6_
  40.4 0.0 collective-permute-done.4.refs_4_
  40.4 0.0 collective-permute-done.5.refs_5_
  40.4 1.9 %finish_edge.1 = (f32[16,16,896]{2,1,0:T(8,128)}, f32[16,16,896]{2,1,0:T(8,128)}, f32[16,16,896]{2,1,0:T(8,128)}, f32[16,16,896]{2,1,0:T(8,128)}) custom-call(f32[16,16,896]{2,1,0:T(8,128)S(1)} %copy-done, f32[16,16,896]{2,1,0:T(8,128)S(1)} %copy-done.1, ...), custom_call_target="tpu_custom_call", output_to_operand_aliasing={{0}: (11, {}), {1}: (12, {}), {2}: (13, {}), {3}: (14, {})} | custom-call | tf_op jit(solution)/shard_map/finish_edge/pallas_call | solution.py:685
Async XLA Ops:
  0.6 7.8 %copy-start.10 = (f32[64]{0:T(128)S(1)}, f32[64]{0:T(128)}, u32[]{:S(2)}) copy-start(f32[64]{0:T(128)} %constant.23.clone.spin) | copy-start | bytes 772
  0.6 7.8 %copy-start.11 = (f32[64]{0:T(128)S(1)}, f32[64]{0:T(128)}, u32[]{:S(2)}) copy-start(f32[64]{0:T(128)} %constant.22.clone.metric) | copy-start | bytes 772
  0.7 7.8 %copy-start.3 = (f32[16,16,896]{2,1,0:T(8,128)S(1)}, f32[16,16,896]{2,1,0:T(8,128)}, u32[]{:S(2)}) copy-start(f32[16,16,896]{2,1,0:T(8,128)} %refs_3_.9) | copy-start | bytes 2752516
  0.7 7.8 %copy-start.2 = (f32[16,16,896]{2,1,0:T(8,128)S(1)}, f32[16,16,896]{2,1,0:T(8,128)}, u32[]{:S(2)}) copy-start(f32[16,16,896]{2,1,0:T(8,128)} %refs_2_.9) | copy-start | bytes 2752516
  0.7 7.8 %copy-start.1 = (f32[16,16,896]{2,1,0:T(8,128)S(1)}, f32[16,16,896]{2,1,0:T(8,128)}, u32[]{:S(2)}) copy-start(f32[16,16,896]{2,1,0:T(8,128)} %refs_1_.9) | copy-start | bytes 2752516
  0.7 7.8 %copy-start = (f32[16,16,896]{2,1,0:T(8,128)S(1)}, f32[16,16,896]{2,1,0:T(8,128)}, u32[]{:S(2)}) copy-start(f32[16,16,896]{2,1,0:T(8,128)} %refs_0_.9) | copy-start | bytes 2752516
  0.7 7.8 %copy-start.6 = (f32[16,896]{1,0:T(8,128)S(1)}, f32[16,896]{1,0:T(8,128)}, u32[]{:S(2)}) copy-start(f32[16,896]{1,0:T(8,128)} %refs_4_.5) | copy-start | bytes 172036
  2.9 5.5 %collective-permute-start = (f32[48,128]{1,0:T(8,128)S(1)}, f32[48,128]{1,0:T(8,128)S(1)}, u32[]{:S(2)}, u32[]{:S(2)}) collective-permute-start(f32[48,128]{1,0:T(8,128)S(1)} %get-tuple-element.30), channel_id=1, source_target_pairs={{0,1},{1,2},{2,3},{3,0},{4,5},{5,6},{6,7},{7,4},{8,9},{9,10},{10,1... | collective-permute-start | bytes 73736 | tf_op jit(solution)/shard_map/ppermute | solution.py:624
  3.4 5.0 %collective-permute-start.1 = (f32[48,128]{1,0:T(8,128)S(1)}, f32[48,128]{1,0:T(8,128)S(1)}, u32[]{:S(2)}, u32[]{:S(2)}) collective-permute-start(f32[48,128]{1,0:T(8,128)S(1)} %get-tuple-element.31), channel_id=1, source_target_pairs={{0,3},{1,0},{2,1},{3,2},{4,7},{5,4},{6,5},{7,6},{8,11},{9,8},{10,9... | collective-permute-start | bytes 73736 | tf_op jit(solution)/shard_map/ppermute | solution.py:624
  5.4 22.9 %collective-permute-start.2 = (f32[200,896]{1,0:T(8,128)S(1)}, f32[200,896]{1,0:T(8,128)S(1)}, u32[]{:S(2)}, u32[]{:S(2)}) collective-permute-start(f32[200,896]{1,0:T(8,128)S(1)} %get-tuple-element.33), channel_id=1, source_target_pairs={{0,4},{4,0},{8,12},{12,8},{1,5},{5,1},{9,13},{13,9},{2,6},{6,2},{1... | collective-permute-start | bytes 2150408 | tf_op jit(solution)/shard_map/ppermute | solution.py:629
  7.7 20.6 %collective-permute-start.3 = (f32[200,896]{1,0:T(8,128)S(1)}, f32[200,896]{1,0:T(8,128)S(1)}, u32[]{:S(2)}, u32[]{:S(2)}) collective-permute-start(f32[200,896]{1,0:T(8,128)S(1)} %get-tuple-element.34), channel_id=1, source_target_pairs={{4,8},{8,4},{5,9},{9,5},{6,10},{10,6},{7,11},{11,7},{20,24},{24,20... | collective-permute-start | bytes 2150408 | tf_op jit(solution)/shard_map/ppermute | solution.py:630
  8.5 19.8 %copy-start.7 = (bf16[7,384,256]{2,1,0:T(8,128)(2,1)S(1)}, bf16[7,384,256]{2,1,0:T(8,128)(2,1)}, u32[]{:S(2)}) copy-start(bf16[7,384,256]{2,1,0:T(8,128)(2,1)} %constant.18.clone.refs_9_.refs_12_) | copy-start | bytes 4128772
  8.5 19.8 %copy-start.8 = (bf16[768,512]{1,0:T(8,128)(2,1)S(1)}, bf16[768,512]{1,0:T(8,128)(2,1)}, u32[]{:S(2)}) copy-start(bf16[768,512]{1,0:T(8,128)(2,1)} %constant.19.clone.refs_10_.refs_13_) | copy-start | bytes 2359300
  8.5 19.8 %copy-start.9 = (bf16[512,256]{1,0:T(8,128)(2,1)S(1)}, bf16[512,256]{1,0:T(8,128)(2,1)}, u32[]{:S(2)}) copy-start(bf16[512,256]{1,0:T(8,128)(2,1)} %constant.17.clone.refs_8_.refs_11_) | copy-start | bytes 786436
  25.0 11.0 %collective-permute-start.9 = (f32[104,128]{1,0:T(8,128)S(1)}, f32[104,128]{1,0:T(8,128)S(1)}, u32[]{:S(2)}, u32[]{:S(2)}) collective-permute-start(f32[104,128]{1,0:T(8,128)S(1)} %get-tuple-element.46), channel_id=1, source_target_pairs={{0,2},{1,3},{2,0},{3,1},{4,6},{5,7},{6,4},{7,5},{8,10},{9,11},{10,... | collective-permute-start | bytes 159752 | tf_op jit(solution)/shard_map/ppermute | solution.py:624
  26.6 9.9 %collective-permute-start.7 = (f32[208,128]{1,0:T(8,128)S(1)}, f32[208,128]{1,0:T(8,128)S(1)}, u32[]{:S(2)}, u32[]{:S(2)}) collective-permute-start(f32[208,128]{1,0:T(8,128)S(1)} %get-tuple-element.44), channel_id=1, source_target_pairs={{0,1},{1,2},{2,3},{3,0},{4,5},{5,6},{6,7},{7,4},{8,9},{9,10},{10,1... | collective-permute-start | bytes 319496 | tf_op jit(solution)/shard_map/ppermute | solution.py:624
  26.6 9.9 %collective-permute-start.8 = (f32[208,128]{1,0:T(8,128)S(1)}, f32[208,128]{1,0:T(8,128)S(1)}, u32[]{:S(2)}, u32[]{:S(2)}) collective-permute-start(f32[208,128]{1,0:T(8,128)S(1)} %get-tuple-element.45), channel_id=1, source_target_pairs={{0,3},{1,0},{2,1},{3,2},{4,7},{5,4},{6,5},{7,6},{8,11},{9,8},{10,9... | collective-permute-start | bytes 319496 | tf_op jit(solution)/shard_map/ppermute | solution.py:624
  28.4 8.2 %copy-start.4 = (bf16[768,896]{1,0:T(8,128)(2,1)S(1)}, bf16[768,896]{1,0:T(8,128)(2,1)}, u32[]{:S(2)}) copy-start(bf16[768,896]{1,0:T(8,128)(2,1)} %constant.21.clone.refs_10_) | copy-start | bytes 4128772
  28.4 8.2 %copy-start.5 = (bf16[128,256]{1,0:T(8,128)(2,1)S(1)}, bf16[128,256]{1,0:T(8,128)(2,1)}, u32[]{:S(2)}) copy-start(bf16[128,256]{1,0:T(8,128)(2,1)} %constant.20.clone.refs_9_) | copy-start | bytes 196612
  34.2 6.2 %collective-permute-start.4 = (f32[48,128]{1,0:T(8,128)S(1)}, f32[48,128]{1,0:T(8,128)S(1)}, u32[]{:S(2)}, u32[]{:S(2)}) collective-permute-start(f32[48,128]{1,0:T(8,128)S(1)} %get-tuple-element.40), channel_id=1, source_target_pairs={{0,1},{1,2},{2,3},{3,0},{4,5},{5,6},{6,7},{7,4},{8,9},{9,10},{10,1... | collective-permute-start | bytes 73736 | tf_op jit(solution)/shard_map/ppermute | solution.py:624
  34.3 6.1 %collective-permute-start.5 = (f32[48,128]{1,0:T(8,128)S(1)}, f32[48,128]{1,0:T(8,128)S(1)}, u32[]{:S(2)}, u32[]{:S(2)}) collective-permute-start(f32[48,128]{1,0:T(8,128)S(1)} %get-tuple-element.41), channel_id=1, source_target_pairs={{0,3},{1,0},{2,1},{3,2},{4,7},{5,4},{6,5},{7,6},{8,11},{9,8},{10,9... | collective-permute-start | bytes 73736 | tf_op jit(solution)/shard_map/ppermute | solution.py:624
  36.0 4.3 %collective-permute-start.6 = (f32[24,128]{1,0:T(8,128)S(1)}, f32[24,128]{1,0:T(8,128)S(1)}, u32[]{:S(2)}, u32[]{:S(2)}) collective-permute-start(f32[24,128]{1,0:T(8,128)S(1)} %get-tuple-element.42), channel_id=1, source_target_pairs={{0,2},{1,3},{2,0},{3,1},{4,6},{5,7},{6,4},{7,5},{8,10},{9,11},{10,... | collective-permute-start | bytes 36872 | tf_op jit(solution)/shard_map/ppermute | solution.py:624

commit v12 on v10

--- a/solution.py
+++ b/solution.py
@@ -270,7 +270,8 @@
     outs = some(4)
     local, to_east, to_west, to_far = some(4)
     mass_x = some(1)[0] if inner else mass_x
-    high, low, cross, new, kept_parts, mass_y, sems = some(7)
+    high, low, new, kept_parts, mass_y, sems = some(6)
+    crosses = some(mass.shape[1] // LANES)
     tables = refs if inner else tables_in
     band, spread, own = tables
     rows, columns = mass.shape
@@ -313,20 +314,11 @@
                 before = tile
         return carry
 
-    def slopes_x(first, size):
-        lax.fori_loop(first, first + size, cut, 0)
-        wait_all(fetched[:1])
-        for t in range(tiles):
-            span = slice(t * LANES, (t + 2) * LANES)
-            some_rows = slice(first, first + size)
-            both = jnp.concatenate(
-                [
-                    table[:, some_rows, :, span].reshape(4 * size * levels, 2 * LANES)
-                    for table in (high, low)
-                ],
-                axis=1,
-            )
-            cross[t, :, some_rows] = dot(both, band[...]).reshape(4, size, levels, 2 * LANES)
+    def slopes_x(t, size):
+        span = slice(t * LANES, (t + 2) * LANES)
+        parts = [table[:, 0:size, :, span].reshape(4 * size * levels, 2 * LANES) for table in (high, low)]
+        product = dot(jnp.concatenate(parts, axis=1), band[...])
+        crosses[t][:, 0:size] = product.reshape(4, size, levels, 2 * LANES)
 
     start_row = lax.axis_index("lat") * rows
 
@@ -351,8 +343,8 @@
             column = [row_of(f, j, span) for j in range(-3, size + 3)]
             for j in range(size):
                 q = column[j + 3]
-                slope_x = cross[t, f, first + j, :, :LANES]
-                smooth_x = cross[t, f, first + j, :, LANES:]
+                slope_x = crosses[t][f, first + j, :, :LANES]
+                smooth_x = crosses[t][f, first + j, :, LANES:]
                 slope_y, smooth_y = stencil(q, column[j + 4 : j + 7], column[j + 2 :: -1][:3])
                 change = (fast_size[j] * smooth_x - fast[j] * slope_x) + (
                     up_size[j] * smooth_y - up[j] * slope_y
@@ -369,7 +361,7 @@
                     change = change - (spins[j] * centers[0][j] + push_y[j])
                 emit(f, first + j, span, q, change)
 
-    def edge_side(side, first, emit):
+    def edge_group(side, first):
         edge = edge_row(3 * side, rows)
         step = jnp.where(edge == 0, 1, -1)
 
@@ -381,22 +373,26 @@
             start = levels * (3 * f - j - 1)
             return strips[side][start : start + levels, span]
 
-        numbers = [edge + step * j for j in range(3)]
+        return first, [edge + step * j for j in range(3)], row_of, step.astype(F32)
+
+    def inner_group(first, size):
+        def row_of(f, j, span):
+            return fields[f][3 + first + j, :, span]
+
+        return first, [3 + first + j for j in range(size)], row_of, 1.0
+
+    def run(groups, size, emit):
+        lax.fori_loop(0, size, cut, 0)
+        wait_all(fetched[:1])
+        slopes_x(0, size)
         for t in range(tiles):
-            tendency(t, first, numbers, row_of, emit, step.astype(F32))
-
-    def inner_rows(emit):
-        def step(n, carry):
-            first_row = 3 + 2 * n
-
-            def row_of(f, j, span):
-                return fields[f][first_row + j, :, span]
-
-            for t in range(tiles):
-                tendency(t, 2 * n, [first_row, first_row + 1], row_of, emit)
-            return carry
-
-        lax.fori_loop(0, (rows - 6) // 2, step, 0)
+            if t + 1 < tiles:
+                slopes_x(t + 1, size)
+            for first, numbers, row_of, inward in groups:
+                tendency(t, first, numbers, row_of, emit, inward)
+
+    half = (rows - 6) // 2
+    inner_groups = [inner_group(0, half), inner_group(half, rows - 6 - half)]
 
     def write_out(f):
         if edge_rows:
@@ -409,12 +405,9 @@
             new[f, i, :, span] = q + STEP * change
 
         if inner:
-            slopes_x(0, rows - 6)
-            inner_rows(emit)
+            run(inner_groups, rows - 6, emit)
         else:
-            slopes_x(0, 6)
-            edge_side(0, 0, emit)
-            edge_side(1, 3, emit)
+            run([edge_group(0, 0), edge_group(1, 3)], 6, emit)
         pairs = [pair for f in range(4) for pair in write_out(f)]
         wait_all(start_all(pairs, sems))
         wait_all(fetched[1:])
@@ -429,15 +422,10 @@
             rest = (change - top.astype(F32)).astype(BF16)
             kept_parts[f, i, :, columns + first : columns + first + LANES] = rest
 
-        slopes_x(0, kept)
         if inner:
-            inner_rows(emit)
-            if kept > rows - 6:
-                edge_side(1, rows - 6, emit)
+            run(inner_groups + [edge_group(1, rows - 6)] * (kept > rows - 6), kept, emit)
         else:
-            edge_side(0, 0, emit)
-            if kept > 3:
-                edge_side(1, 3, emit)
+            run([edge_group(side, 3 * side) for side in range(kept // 3)], kept, emit)
         wait_all(fetched[1:])
         c_all, s_all, d_all = [
             spread_waves(waves, part, inner, kept, levels) for part in range(3)
@@ -628,11 +616,11 @@
             scratch_shapes=[
                 pltpu.VMEM((4, count, levels, columns + LANES), BF16),
                 pltpu.VMEM((4, count, levels, columns + LANES), BF16),
-                pltpu.VMEM((columns // LANES, 4, count, levels, 2 * LANES), F32),
                 pltpu.VMEM((4, count, levels, columns), F32),
                 pltpu.VMEM((4, kept, levels, 3 * columns), BF16),
                 pltpu.VMEM((rows, 8, columns), F32),
                 pltpu.SemaphoreType.DMA((28,)),
+                *[pltpu.VMEM((4, count, levels, 2 * LANES), F32)] * (columns // LANES),
                 *[pltpu.VMEM(w.shape, w.dtype) for w in weights if inner],
             ],
             input_output_aliases={len(args) + f: f for f in range(4)} if old else {},

time: 37.5 us -> 36.5 us (0.973)
  Pallas kernels: 25 us -> 23.8 us
    pallas_call x2, Pallas kernels: 17.1 us -> 15.9 us  [tendencies(): pl.pallas_call(functools.partial(tend_kernel, inner, count, kept), out_sh...]
  transfers between devices with their start and end apart: 10 -> 10, of which waited for: 0 -> 0; matrix products, arithmetic and copies ran while one was open for 0% -> 0% of each run, Pallas kernels for 56% -> 55%
where the time goes in v12:
time: 36.5 us; the launch traced here: 36.1 us
  Pallas kernels  23.8 us (65%)
  starting transfers between devices  11.1 us (30%)
  between operations  1.07 us (3%)
    pallas_call x2, Pallas kernels, tendencies(): pl.pallas_call(functools.partial(tend_kernel, inner, count, kept), out_sh...  15.9 us
    ppermute x8, starting transfers between devices, ring(): lax.ppermute(value, 'lon', [(i, (i + step) % lon_count) for i in range(lo...  8.13 us
    pallas_call x2, Pallas kernels, finish(): pl.pallas_call(functools.partial(finish_kernel, inner, count), out_shape=...  5.71 us
    ppermute x1, starting transfers between devices, shards(): strip_a = lax.ppermute(to_a, 'lat', [(i, i ^ 1) for i in range(lat_count)])  2.33 us
    pallas_call x1, Pallas kernels, shards(): pl.pallas_call(pack_kernel, out_shape=[like(strip, columns)] * 2 + [like(...  2.18 us
  transfers between devices with their start and end apart: 10, of which 0 were waited for; matrix products, arithmetic and copies ran while one was open for 0% of the time, Pallas kernels for 55%

profile of v12, /device:TPU:0, one launch (start us, length us, event | category | flops | bytes accessed | tf_op | source)
XLA Modules:
  0.0 36.1 jit_solution(17919337462195425458)
XLA Ops:
  0.6 0.0 copy-start.10
  0.6 0.0 copy-start.11
  0.7 0.0 copy-start.3
  0.7 0.0 copy-start.2
  0.7 0.0 copy-start.1
  0.7 0.0 copy-start
  0.7 0.0 copy-start.6
  0.7 2.2 %pack_edges.1 = (f32[200,896]{1,0:T(8,128)S(1)}, f32[200,896]{1,0:T(8,128)S(1)}, f32[48,128]{1,0:T(8,128)S(1)}, f32[48,128]{1,0:T(8,128)S(1)}, f32[3,16,8,256]{3,2,1,0:T(8,128)S(1)}) custom-call(f32[16,16,896]{2,1,0:T(8,128)} %refs_0_.9, f32[16,16,896]{2,1,0:T(8,128)} %refs_1_.9, f32[16,16,896]{2,1,0:T(8,128)} %refs_2_.9, f32[16,16,896]{2,1,0:T(8,128)} %refs_3_.9, ...), custom_call_target="tpu_custom_call" | custom-call | tf_op jit(solution)/shard_map/pack_edges/pallas_call | solution.py:566
  2.9 0.5 %collective-permute-start = (f32[48,128]{1,0:T(8,128)S(1)}, f32[48,128]{1,0:T(8,128)S(1)}, u32[]{:S(2)}, u32[]{:S(2)}) collective-permute-start(f32[48,128]{1,0:T(8,128)S(1)} %get-tuple-element.30), channel_id=1, source_target_pairs={{0,1},{1,2},{2,3},{3,0},{4,5},{5,6},{6,7},{7,4},{8,9},{9,10},{10,1... | collective-permute-start | bytes 73736 | tf_op jit(solution)/shard_map/ppermute | solution.py:583
  3.4 2.0 %collective-permute-start.1 = (f32[48,128]{1,0:T(8,128)S(1)}, f32[48,128]{1,0:T(8,128)S(1)}, u32[]{:S(2)}, u32[]{:S(2)}) collective-permute-start(f32[48,128]{1,0:T(8,128)S(1)} %get-tuple-element.31), channel_id=1, source_target_pairs={{0,3},{1,0},{2,1},{3,2},{4,7},{5,4},{6,5},{7,6},{8,11},{9,8},{10,9... | collective-permute-start | bytes 73736 | tf_op jit(solution)/shard_map/ppermute | solution.py:583
  5.4 2.3 %collective-permute-start.2 = (f32[200,896]{1,0:T(8,128)S(1)}, f32[200,896]{1,0:T(8,128)S(1)}, u32[]{:S(2)}, u32[]{:S(2)}) collective-permute-start(f32[200,896]{1,0:T(8,128)S(1)} %get-tuple-element.33), channel_id=1, source_target_pairs={{0,4},{4,0},{8,12},{12,8},{1,5},{5,1},{9,13},{13,9},{2,6},{6,2},{1... | collective-permute-start | bytes 2150408 | tf_op jit(solution)/shard_map/ppermute | solution.py:588
  7.7 0.7 %collective-permute-start.3 = (f32[200,896]{1,0:T(8,128)S(1)}, f32[200,896]{1,0:T(8,128)S(1)}, u32[]{:S(2)}, u32[]{:S(2)}) collective-permute-start(f32[200,896]{1,0:T(8,128)S(1)} %get-tuple-element.34), channel_id=1, source_target_pairs={{4,8},{8,4},{5,9},{9,5},{6,10},{10,6},{7,11},{11,7},{20,24},{24,20... | collective-permute-start | bytes 2150408 | tf_op jit(solution)/shard_map/ppermute | solution.py:589
  8.4 0.0 collective-permute-done.refs_5_
  8.4 0.0 collective-permute-done.1.refs_6_
  8.4 0.0 copy-done.10
  8.5 0.0 copy-done.11
  8.5 0.0 copy-done.3
  8.5 0.0 copy-done.2
  8.5 0.0 copy-done.1
  8.5 0.0 copy-done
  8.5 0.0 copy-done.6
  8.5 0.0 copy-start.7
  8.5 0.0 copy-start.8
  8.5 0.0 copy-start.9
  8.6 12.3 %tend_inner.1 = (f32[16,16,896]{2,1,0:T(8,128)}, f32[16,16,896]{2,1,0:T(8,128)}, f32[16,16,896]{2,1,0:T(8,128)}, f32[16,16,896]{2,1,0:T(8,128)}, f32[4,208,256]{...) custom-call(f32[64]{0:T(128)S(1)} %copy-done.11, ...), custom_call_target="tpu_custom_call" | custom-call | flops 14909440000 | bytes 4194304 | tf_op jit(solution)/shard_map/tend_inner/pallas_call | solution.py:604
  20.8 1.6 %collective-permute-start.9 = (f32[104,128]{1,0:T(8,128)S(1)}, f32[104,128]{1,0:T(8,128)S(1)}, u32[]{:S(2)}, u32[]{:S(2)}) collective-permute-start(f32[104,128]{1,0:T(8,128)S(1)} %get-tuple-element.46), channel_id=1, source_target_pairs={{0,2},{1,3},{2,0},{3,1},{4,6},{5,7},{6,4},{7,5},{8,10},{9,11},{10,... | collective-permute-start | bytes 159752 | tf_op jit(solution)/shard_map/ppermute | solution.py:583
  22.4 0.0 collective-permute-start.7
  22.4 1.7 %collective-permute-start.8 = (f32[208,128]{1,0:T(8,128)S(1)}, f32[208,128]{1,0:T(8,128)S(1)}, u32[]{:S(2)}, u32[]{:S(2)}) collective-permute-start(f32[208,128]{1,0:T(8,128)S(1)} %get-tuple-element.45), channel_id=1, source_target_pairs={{0,3},{1,0},{2,1},{3,2},{4,7},{5,4},{6,5},{7,6},{8,11},{9,8},{10,9... | collective-permute-start | bytes 319496 | tf_op jit(solution)/shard_map/ppermute | solution.py:583
  24.1 0.0 collective-permute-done.2.refs_8_
  24.1 0.0 collective-permute-done.3.refs_9_
  24.1 0.0 copy-done.7
  24.1 0.0 copy-done.8
  24.1 0.0 copy-done.9
  24.1 0.0 copy-start.4
  24.2 0.0 copy-start.5
  24.2 3.7 %tend_edge.1 = (f32[16,16,896]{2,1,0:T(8,128)}, f32[16,16,896]{2,1,0:T(8,128)}, f32[16,16,896]{2,1,0:T(8,128)}, f32[16,16,896]{2,1,0:T(8,128)}, f32[4,48,256]{2,...) custom-call(f32[64]{0:T(128)S(1)} %copy-done.11, ...), custom_call_target="tpu_custom_call", output_to_operand_aliasing={{0}: (16, {}), {1}: (17, {}), {2}: (18, {}), {3}: (19, {})} | custom-call | flops 6881280000 | bytes 4194304 | tf_op jit(solution)/shard_map/tend_edge/pallas_call | solution.py:604
  27.9 0.1 collective-permute-start.4
  27.9 1.7 %collective-permute-start.5 = (f32[48,128]{1,0:T(8,128)S(1)}, f32[48,128]{1,0:T(8,128)S(1)}, u32[]{:S(2)}, u32[]{:S(2)}) collective-permute-start(f32[48,128]{1,0:T(8,128)S(1)} %get-tuple-element.41), channel_id=1, source_target_pairs={{0,3},{1,0},{2,1},{3,2},{4,7},{5,4},{6,5},{7,6},{8,11},{9,8},{10,9... | collective-permute-start | bytes 73736 | tf_op jit(solution)/shard_map/ppermute | solution.py:583
  29.7 0.0 collective-permute-done.9.refs_6_
  29.7 0.5 %collective-permute-start.6 = (f32[24,128]{1,0:T(8,128)S(1)}, f32[24,128]{1,0:T(8,128)S(1)}, u32[]{:S(2)}, u32[]{:S(2)}) collective-permute-start(f32[24,128]{1,0:T(8,128)S(1)} %get-tuple-element.42), channel_id=1, source_target_pairs={{0,2},{1,3},{2,0},{3,1},{4,6},{5,7},{6,4},{7,5},{8,10},{9,11},{10,... | collective-permute-start | bytes 36872 | tf_op jit(solution)/shard_map/ppermute | solution.py:583
  30.2 0.0 collective-permute-done.7.refs_4_
  30.2 0.0 collective-permute-done.8.refs_5_
  30.2 0.0 copy-done.4
  30.2 0.0 copy-done.5
  30.2 3.8 %finish_inner.1 = (f32[16,16,896]{2,1,0:T(8,128)}, f32[16,16,896]{2,1,0:T(8,128)}, f32[16,16,896]{2,1,0:T(8,128)}, f32[16,16,896]{2,1,0:T(8,128)}) custom-call(f32[16,16,896]{2,1,0:T(8,128)S(1)} %copy-done, f32[16,16,896]{2,1,0:T(8,128)S(1)} %copy-done.1, ...), custom_call_target="tpu_custom_call", output_to_operand_aliasing={{0}: (11, {}), {1}: (12, {}), {2}: (13, {}), {3}: (14, {})} | custom-call | tf_op jit(solution)/shard_map/finish_inner/pallas_call | solution.py:641
  34.0 0.0 collective-permute-done.6.refs_6_
  34.0 0.0 collective-permute-done.4.refs_4_
  34.1 0.0 collective-permute-done.5.refs_5_
  34.1 1.9 %finish_edge.1 = (f32[16,16,896]{2,1,0:T(8,128)}, f32[16,16,896]{2,1,0:T(8,128)}, f32[16,16,896]{2,1,0:T(8,128)}, f32[16,16,896]{2,1,0:T(8,128)}) custom-call(f32[16,16,896]{2,1,0:T(8,128)S(1)} %copy-done, f32[16,16,896]{2,1,0:T(8,128)S(1)} %copy-done.1, ...), custom_call_target="tpu_custom_call", output_to_operand_aliasing={{0}: (11, {}), {1}: (12, {}), {2}: (13, {}), {3}: (14, {})} | custom-call | tf_op jit(solution)/shard_map/finish_edge/pallas_call | solution.py:641
Async XLA Ops:
  0.6 7.8 %copy-start.10 = (f32[64]{0:T(128)S(1)}, f32[64]{0:T(128)}, u32[]{:S(2)}) copy-start(f32[64]{0:T(128)} %constant.23.clone.spin) | copy-start | bytes 772
  0.6 7.8 %copy-start.11 = (f32[64]{0:T(128)S(1)}, f32[64]{0:T(128)}, u32[]{:S(2)}) copy-start(f32[64]{0:T(128)} %constant.22.clone.metric) | copy-start | bytes 772
  0.7 7.8 %copy-start.3 = (f32[16,16,896]{2,1,0:T(8,128)S(1)}, f32[16,16,896]{2,1,0:T(8,128)}, u32[]{:S(2)}) copy-start(f32[16,16,896]{2,1,0:T(8,128)} %refs_3_.9) | copy-start | bytes 2752516
  0.7 7.8 %copy-start.2 = (f32[16,16,896]{2,1,0:T(8,128)S(1)}, f32[16,16,896]{2,1,0:T(8,128)}, u32[]{:S(2)}) copy-start(f32[16,16,896]{2,1,0:T(8,128)} %refs_2_.9) | copy-start | bytes 2752516
  0.7 7.8 %copy-start.1 = (f32[16,16,896]{2,1,0:T(8,128)S(1)}, f32[16,16,896]{2,1,0:T(8,128)}, u32[]{:S(2)}) copy-start(f32[16,16,896]{2,1,0:T(8,128)} %refs_1_.9) | copy-start | bytes 2752516
  0.7 7.8 %copy-start = (f32[16,16,896]{2,1,0:T(8,128)S(1)}, f32[16,16,896]{2,1,0:T(8,128)}, u32[]{:S(2)}) copy-start(f32[16,16,896]{2,1,0:T(8,128)} %refs_0_.9) | copy-start | bytes 2752516
  0.7 7.8 %copy-start.6 = (f32[16,896]{1,0:T(8,128)S(1)}, f32[16,896]{1,0:T(8,128)}, u32[]{:S(2)}) copy-start(f32[16,896]{1,0:T(8,128)} %refs_4_.5) | copy-start | bytes 172036
  2.9 5.5 %collective-permute-start = (f32[48,128]{1,0:T(8,128)S(1)}, f32[48,128]{1,0:T(8,128)S(1)}, u32[]{:S(2)}, u32[]{:S(2)}) collective-permute-start(f32[48,128]{1,0:T(8,128)S(1)} %get-tuple-element.30), channel_id=1, source_target_pairs={{0,1},{1,2},{2,3},{3,0},{4,5},{5,6},{6,7},{7,4},{8,9},{9,10},{10,1... | collective-permute-start | bytes 73736 | tf_op jit(solution)/shard_map/ppermute | solution.py:583
  3.4 5.0 %collective-permute-start.1 = (f32[48,128]{1,0:T(8,128)S(1)}, f32[48,128]{1,0:T(8,128)S(1)}, u32[]{:S(2)}, u32[]{:S(2)}) collective-permute-start(f32[48,128]{1,0:T(8,128)S(1)} %get-tuple-element.31), channel_id=1, source_target_pairs={{0,3},{1,0},{2,1},{3,2},{4,7},{5,4},{6,5},{7,6},{8,11},{9,8},{10,9... | collective-permute-start | bytes 73736 | tf_op jit(solution)/shard_map/ppermute | solution.py:583
  5.4 18.7 %collective-permute-start.2 = (f32[200,896]{1,0:T(8,128)S(1)}, f32[200,896]{1,0:T(8,128)S(1)}, u32[]{:S(2)}, u32[]{:S(2)}) collective-permute-start(f32[200,896]{1,0:T(8,128)S(1)} %get-tuple-element.33), channel_id=1, source_target_pairs={{0,4},{4,0},{8,12},{12,8},{1,5},{5,1},{9,13},{13,9},{2,6},{6,2},{1... | collective-permute-start | bytes 2150408 | tf_op jit(solution)/shard_map/ppermute | solution.py:588
  7.7 16.4 %collective-permute-start.3 = (f32[200,896]{1,0:T(8,128)S(1)}, f32[200,896]{1,0:T(8,128)S(1)}, u32[]{:S(2)}, u32[]{:S(2)}) collective-permute-start(f32[200,896]{1,0:T(8,128)S(1)} %get-tuple-element.34), channel_id=1, source_target_pairs={{4,8},{8,4},{5,9},{9,5},{6,10},{10,6},{7,11},{11,7},{20,24},{24,20... | collective-permute-start | bytes 2150408 | tf_op jit(solution)/shard_map/ppermute | solution.py:589
  8.5 15.6 %copy-start.7 = (bf16[2688,256]{1,0:T(8,128)(2,1)S(1)}, bf16[2688,256]{1,0:T(8,128)(2,1)}, u32[]{:S(2)}) copy-start(bf16[2688,256]{1,0:T(8,128)(2,1)} %constant.18.clone.refs_9_.refs_12_) | copy-start | bytes 4128772
  8.5 15.6 %copy-start.8 = (bf16[768,512]{1,0:T(8,128)(2,1)S(1)}, bf16[768,512]{1,0:T(8,128)(2,1)}, u32[]{:S(2)}) copy-start(bf16[768,512]{1,0:T(8,128)(2,1)} %constant.19.clone.refs_10_.refs_13_) | copy-start | bytes 2359300
  8.5 15.6 %copy-start.9 = (bf16[512,256]{1,0:T(8,128)(2,1)S(1)}, bf16[512,256]{1,0:T(8,128)(2,1)}, u32[]{:S(2)}) copy-start(bf16[512,256]{1,0:T(8,128)(2,1)} %constant.17.clone.refs_8_.refs_11_) | copy-start | bytes 786436
  20.8 8.9 %collective-permute-start.9 = (f32[104,128]{1,0:T(8,128)S(1)}, f32[104,128]{1,0:T(8,128)S(1)}, u32[]{:S(2)}, u32[]{:S(2)}) collective-permute-start(f32[104,128]{1,0:T(8,128)S(1)} %get-tuple-element.46), channel_id=1, source_target_pairs={{0,2},{1,3},{2,0},{3,1},{4,6},{5,7},{6,4},{7,5},{8,10},{9,11},{10,... | collective-permute-start | bytes 159752 | tf_op jit(solution)/shard_map/ppermute | solution.py:583
  22.4 7.9 %collective-permute-start.7 = (f32[208,128]{1,0:T(8,128)S(1)}, f32[208,128]{1,0:T(8,128)S(1)}, u32[]{:S(2)}, u32[]{:S(2)}) collective-permute-start(f32[208,128]{1,0:T(8,128)S(1)} %get-tuple-element.44), channel_id=1, source_target_pairs={{0,1},{1,2},{2,3},{3,0},{4,5},{5,6},{6,7},{7,4},{8,9},{9,10},{10,1... | collective-permute-start | bytes 319496 | tf_op jit(solution)/shard_map/ppermute | solution.py:583
  22.4 7.9 %collective-permute-start.8 = (f32[208,128]{1,0:T(8,128)S(1)}, f32[208,128]{1,0:T(8,128)S(1)}, u32[]{:S(2)}, u32[]{:S(2)}) collective-permute-start(f32[208,128]{1,0:T(8,128)S(1)} %get-tuple-element.45), channel_id=1, source_target_pairs={{0,3},{1,0},{2,1},{3,2},{4,7},{5,4},{6,5},{7,6},{8,11},{9,8},{10,9... | collective-permute-start | bytes 319496 | tf_op jit(solution)/shard_map/ppermute | solution.py:583
  24.1 6.1 %copy-start.4 = (bf16[768,896]{1,0:T(8,128)(2,1)S(1)}, bf16[768,896]{1,0:T(8,128)(2,1)}, u32[]{:S(2)}) copy-start(bf16[768,896]{1,0:T(8,128)(2,1)} %constant.21.clone.refs_10_) | copy-start | bytes 4128772
  24.2 6.1 %copy-start.5 = (bf16[128,256]{1,0:T(8,128)(2,1)S(1)}, bf16[128,256]{1,0:T(8,128)(2,1)}, u32[]{:S(2)}) copy-start(bf16[128,256]{1,0:T(8,128)(2,1)} %constant.20.clone.refs_9_) | copy-start | bytes 196612
  27.9 6.2 %collective-permute-start.4 = (f32[48,128]{1,0:T(8,128)S(1)}, f32[48,128]{1,0:T(8,128)S(1)}, u32[]{:S(2)}, u32[]{:S(2)}) collective-permute-start(f32[48,128]{1,0:T(8,128)S(1)} %get-tuple-element.40), channel_id=1, source_target_pairs={{0,1},{1,2},{2,3},{3,0},{4,5},{5,6},{6,7},{7,4},{8,9},{9,10},{10,1... | collective-permute-start | bytes 73736 | tf_op jit(solution)/shard_map/ppermute | solution.py:583
  27.9 6.1 %collective-permute-start.5 = (f32[48,128]{1,0:T(8,128)S(1)}, f32[48,128]{1,0:T(8,128)S(1)}, u32[]{:S(2)}, u32[]{:S(2)}) collective-permute-start(f32[48,128]{1,0:T(8,128)S(1)} %get-tuple-element.41), channel_id=1, source_target_pairs={{0,3},{1,0},{2,1},{3,2},{4,7},{5,4},{6,5},{7,6},{8,11},{9,8},{10,9... | collective-permute-start | bytes 73736 | tf_op jit(solution)/shard_map/ppermute | solution.py:583
  29.7 4.4 %collective-permute-start.6 = (f32[24,128]{1,0:T(8,128)S(1)}, f32[24,128]{1,0:T(8,128)S(1)}, u32[]{:S(2)}, u32[]{:S(2)}) collective-permute-start(f32[24,128]{1,0:T(8,128)S(1)} %get-tuple-element.42), channel_id=1, source_target_pairs={{0,2},{1,3},{2,0},{3,1},{4,6},{5,7},{6,4},{7,5},{8,10},{9,11},{10,... | collective-permute-start | bytes 36872 | tf_op jit(solution)/shard_map/ppermute | solution.py:583

commit v13 on v12

--- a/solution.py
+++ b/solution.py
@@ -135,12 +135,12 @@
     return jnp.where(north, rows - 1 - entry % 3, entry % 3)
 
 
-def entry_row(inner, entry, rows):
-    if not inner:
-        return edge_row(entry, rows)
+def entry_row(sides, entry, rows):
+    if sides:
+        return edge_row(entry + 3 * sides[0], rows)
     if isinstance(entry, int):
-        return entry + 3 if entry < rows - 6 else edge_row(entry - (rows - 6) + 3, rows)
-    return jnp.where(entry < rows - 6, entry + 3, edge_row(entry - (rows - 6) + 3, rows))
+        return entry + 3 if entry < rows - 6 else edge_row((entry - (rows - 6) + 3) % 6, rows)
+    return jnp.where(entry < rows - 6, entry + 3, edge_row((entry - (rows - 6) + 3) % 6, rows))
 
 
 def by_parity(even, odd):
@@ -245,14 +245,17 @@
     return over_levels(stencil(middle, plus, minus)[0] / (60.0 * middle))
 
 
-def spread_waves(waves, part, inner, kept, levels):
+def spread_waves(waves, part, sides, kept, levels):
     rows = waves.shape[1]
-    numbers = [entry_row(inner, entry, rows) for entry in range(kept)]
+    numbers = [entry_row(sides, entry, rows) for entry in range(kept)]
     return jnp.concatenate([waves[part, n] for n in numbers for _ in range(levels // 8)], axis=0)
 
 
-def tend_kernel(inner, count, kept, metric, spin, *refs):
-    edge_rows = not inner
+PAIRS = ((3, 0), (1, 2))
+
+
+def tend_kernel(sides, count, kept, metric, spin, *refs):
+    inner = not sides
     refs = list(refs)
 
     def some(n):
@@ -262,42 +265,47 @@
 
     fields = some(4)
     mass, west, east, waves = some(4)
-    strips = some(2) if edge_rows else None
-    mass_x = some(1)[0] if edge_rows else None
+    strips = dict(zip(sides, some(len(sides))))
+    mass_x, edge_cross = (None, None) if inner else some(2)
     tables_in = some(3)
-    if edge_rows:
+    if not inner:
+        some(2 if kept else 0)
         some(4)
     outs = some(4)
-    local, to_east, to_west, to_far = some(4)
-    mass_x = some(1)[0] if inner else mass_x
-    high, low, new, kept_parts, mass_y, sems = some(6)
-    crosses = some(mass.shape[1] // LANES)
+    if kept:
+        local, to_east, to_west, to_far = some(4)
+    mass_x, edge_cross = some(2) if inner else (mass_x, edge_cross)
+    new, mass_y, push, sems = some(4)
+    kept_parts = some(2) if kept else None
+    if inner:
+        high, low, cross_all = some(3)
+        crosses = some(mass.shape[1] // LANES)
     tables = refs if inner else tables_in
     band, spread, own = tables
     rows, columns = mass.shape
     levels = fields[0].shape[1]
-    items = count * levels
     kept_items = kept * levels
     tiles = columns // LANES
 
     fetched = start_all(zip(tables_in, tables), sems, 24) if inner else []
-    if edge_rows:
-        tail = 12 * levels
-        lines = [strip[tail : tail + 3] for strip in strips]
-        upper = by_parity(lines[0], lines[1])
-        lower = by_parity(lines[1], lines[0])
-        lower = jnp.concatenate([lower[2:3], lower[1:2], lower[0:1]], axis=0)
-        mass_y[0:3] = mass_slope_y(jnp.concatenate([lower, mass[0:6]], axis=0))
-        mass_y[rows - 3 :] = mass_slope_y(jnp.concatenate([mass[rows - 6 :], upper], axis=0))
-    else:
+    if inner:
         blank = jnp.zeros((3, columns), F32)
         mass_x[...] = mass_slope_x(mass, west, east, levels)
         mass_y[...] = mass_slope_y(jnp.concatenate([blank, mass[...], blank], axis=0))
 
+    def edge_mass():
+        for n, side in enumerate(sides):
+            lines = [strips[side][12 * levels + m : 12 * levels + m + 1] for m in (2, 1, 0)]
+            north = edge_row(3 * side, rows) != 0
+            for m in range(6):
+                lines.append(jnp.where(north, mass[rows - 1 - m : rows - m], mass[m : m + 1]))
+            slope = mass_slope_y(jnp.concatenate(lines, axis=0))
+            mass_y[3 * n : 3 * n + 3] = slope * jnp.where(north, -1.0, 1.0)
+
     lane = lax.broadcasted_iota(jnp.int32, (levels, LANES), 1)
 
     def cut(i, carry):
-        row = entry_row(inner, i, rows)
+        row = entry_row(sides, i, rows)
         halo = pl.ds(pl.multiple_of((row % 2) * levels, levels), levels)
         for f in range(4):
             lead = 16 * (row // 2) + 3 * f
@@ -314,20 +322,36 @@
                 before = tile
         return carry
 
-    def slopes_x(t, size):
-        span = slice(t * LANES, (t + 2) * LANES)
-        parts = [table[:, 0:size, :, span].reshape(4 * size * levels, 2 * LANES) for table in (high, low)]
-        product = dot(jnp.concatenate(parts, axis=1), band[...])
-        crosses[t][:, 0:size] = product.reshape(4, size, levels, 2 * LANES)
+    def columns_of(t, width=1):
+        if isinstance(t, int):
+            return slice(t * LANES, (t + width) * LANES)
+        return pl.ds(pl.multiple_of(t * LANES, LANES), width * LANES)
+
+    def slopes_x(t):
+        span = columns_of(t, 2)
+        parts = [table[:, :, :, span].reshape(4 * rows * levels, 2 * LANES) for table in (high, low)]
+        product = dot(jnp.concatenate(parts, axis=1), band[...]).reshape(4, rows, levels, 2 * LANES)
+        if isinstance(t, int):
+            crosses[t][...] = product[:, : rows - 6]
+        else:
+            cross_all[t] = product[:, : rows - 6]
+        edge_cross[t] = product[:, rows - 6 :]
+
+    def cross_of(t, f, entry):
+        if inner and entry < rows - 6:
+            return (crosses[t], (f, entry)) if isinstance(t, int) else (cross_all, (t, f, entry))
+        if inner:
+            return edge_cross, (t, f, entry - (rows - 6))
+        return edge_cross, (t, f, (entry + 3 * sides[0] + 3) % 6)
 
     start_row = lax.axis_index("lat") * rows
 
     def whole(lines):
         return jnp.concatenate([lines] * (levels // 8), axis=0)
 
-    def tendency(t, first, numbers, row_of, emit, inward=1.0):
+    def tendency(pair, t, first, numbers, lines, row_of, emit, inward=1.0):
         size = len(numbers)
-        span = slice(t * LANES, (t + 1) * LANES)
+        span = columns_of(t)
         metrics = [metric[start_row + n] for n in numbers]
         spins = [spin[start_row + n] for n in numbers]
         centers = [[row_of(f, j, span) for j in range(size)] for f in range(3)]
@@ -338,13 +362,14 @@
             fast_size.append(jnp.abs(fast[j]))
             up.append(centers[1][j] * per_row)
             up_size.append(jnp.abs(up[j]))
-        push_x, push_y = [None] * size, [None] * size
-        for f in (3, 0, 1, 2):
+        push_x = [None] * size
+        for f in PAIRS[pair]:
             column = [row_of(f, j, span) for j in range(-3, size + 3)]
             for j in range(size):
                 q = column[j + 3]
-                slope_x = crosses[t][f, first + j, :, :LANES]
-                smooth_x = crosses[t][f, first + j, :, LANES:]
+                table, place = cross_of(t, f, first + j)
+                slope_x = table[(*place, slice(None), slice(0, LANES))]
+                smooth_x = table[(*place, slice(None), slice(LANES, 2 * LANES))]
                 slope_y, smooth_y = stencil(q, column[j + 4 : j + 7], column[j + 2 :: -1][:3])
                 change = (fast_size[j] * smooth_x - fast[j] * slope_x) + (
                     up_size[j] * smooth_y - up[j] * slope_y
@@ -352,14 +377,14 @@
                 if f == 3:
                     theta = centers[2][j]
                     over_x = whole(mass_x[numbers[j], :, span])
-                    over_y = whole(mass_y[numbers[j], :, span])
+                    over_y = whole(mass_y[lines[j], :, span])
                     push_x[j] = metrics[j] * ((1.0 / 60.0) * slope_x + theta * over_x)
-                    push_y[j] = per_row * slope_y + theta * over_y
+                    push[first + j, :, span] = per_row * slope_y + theta * over_y
                 elif f == 0:
                     change = change + (spins[j] * centers[1][j] - push_x[j])
                 elif f == 1:
-                    change = change - (spins[j] * centers[0][j] + push_y[j])
-                emit(f, first + j, span, q, change)
+                    change = change - (spins[j] * centers[0][j] + push[first + j, :, span])
+                emit(f, first + j, t, q, change)
 
     def edge_group(side, first):
         edge = edge_row(3 * side, rows)
@@ -373,88 +398,128 @@
             start = levels * (3 * f - j - 1)
             return strips[side][start : start + levels, span]
 
-        return first, [edge + step * j for j in range(3)], row_of, step.astype(F32)
+        numbers = [edge + step * j for j in range(3)]
+        lines = numbers if inner else [first + j for j in range(3)]
+        return first, numbers, lines, row_of, step.astype(F32)
 
     def inner_group(first, size):
         def row_of(f, j, span):
             return fields[f][3 + first + j, :, span]
 
-        return first, [3 + first + j for j in range(size)], row_of, 1.0
-
-    def run(groups, size, emit):
-        lax.fori_loop(0, size, cut, 0)
-        wait_all(fetched[:1])
-        slopes_x(0, size)
-        for t in range(tiles):
-            if t + 1 < tiles:
-                slopes_x(t + 1, size)
-            for first, numbers, row_of, inward in groups:
-                tendency(t, first, numbers, row_of, emit, inward)
+        numbers = [3 + first + j for j in range(size)]
+        return first, numbers, numbers, row_of, 1.0
+
+    def run(groups, emit, then=None):
+        if inner:
+            lax.fori_loop(0, rows, cut, 0)
+            wait_all(fetched[:1])
+            slopes_x(0)
+        else:
+            edge_mass()
+        for pair in range(2):
+            for t in range(tiles):
+                if inner and pair == 0 and t + 1 < tiles:
+                    slopes_x(t + 1)
+                for first, numbers, lines, row_of, inward in groups:
+                    tendency(pair, t, first, numbers, lines, row_of, emit, inward)
+            if then:
+                then(pair)
+
+    def run_rolled(groups, emit):
+        if inner:
+            lax.fori_loop(0, rows, cut, 0)
+            wait_all(fetched[:1])
+        else:
+            edge_mass()
+
+        def step(t, carry):
+            if inner:
+                slopes_x(t)
+            for pair in range(2):
+                for first, numbers, lines, row_of, inward in groups:
+                    tendency(pair, t, first, numbers, lines, row_of, emit, inward)
+            return carry
+
+        lax.fori_loop(0, tiles, step, 0)
 
     half = (rows - 6) // 2
     inner_groups = [inner_group(0, half), inner_group(half, rows - 6 - half)]
 
     def write_out(f):
-        if edge_rows:
-            return [(new.at[f, n], outs[f].at[edge_row(n, rows)]) for n in range(6)]
+        if not inner:
+            return [(new.at[f, n], outs[f].at[entry_row(sides, n, rows)]) for n in range(count)]
         return [(new.at[f, 0 : rows - 6], outs[f].at[3 : rows - 3])]
 
     @pl.when(jnp.logical_not(is_polar()))
     def _():
-        def emit(f, i, span, q, change):
-            new[f, i, :, span] = q + STEP * change
+        def emit(f, i, t, q, change):
+            new[f, i, :, columns_of(t)] = q + STEP * change
 
         if inner:
-            run(inner_groups, rows - 6, emit)
+            run_rolled(inner_groups, emit)
         else:
-            run([edge_group(0, 0), edge_group(1, 3)], 6, emit)
+            run_rolled([edge_group(side, 3 * n) for n, side in enumerate(sides)], emit)
         pairs = [pair for f in range(4) for pair in write_out(f)]
         wait_all(start_all(pairs, sems))
         wait_all(fetched[1:])
 
+    if not kept:
+        return
+
     @pl.when(is_polar())
     def _():
-        def emit(f, i, span, q, change):
+        def emit(f, i, t, q, change):
+            pair = 0 if f in PAIRS[0] else 1
+            n = PAIRS[pair].index(f)
             top = change.astype(BF16)
-            first = span.start
-            kept_parts[f, i, :, first : first + LANES] = top
-            kept_parts[f, i, :, 2 * columns + first : 2 * columns + first + LANES] = top
+            first = t * LANES
+            kept_parts[pair][n, i, :, first : first + LANES] = top
+            kept_parts[pair][n, i, :, 2 * columns + first : 2 * columns + first + LANES] = top
             rest = (change - top.astype(F32)).astype(BF16)
-            kept_parts[f, i, :, columns + first : columns + first + LANES] = rest
+            kept_parts[pair][n, i, :, columns + first : columns + first + LANES] = rest
+
+        nodal = [None] * 4
+        c_all, s_all, d_all = [
+            spread_waves(waves, part, sides, kept, levels) for part in range(3)
+        ]
+
+        def to_nodes(pair):
+            if pair == 0:
+                wait_all(fetched[1:])
+            if not inner and pair == 0:
+                return
+            ready = [pair] if inner else [0, 1]
+            parts = [kept_parts[n][...].reshape(2 * kept_items, 3 * columns) for n in ready]
+            both = dot(jnp.concatenate(parts, axis=0), spread[...])
+            for n, f in enumerate([f for n in ready for f in PAIRS[n]]):
+                nodal[f] = both[n * kept_items : (n + 1) * kept_items]
 
         if inner:
-            run(inner_groups + [edge_group(1, rows - 6)] * (kept > rows - 6), kept, emit)
+            groups = inner_groups + [edge_group(1, rows - 6)] * (kept > rows - 6)
         else:
-            run([edge_group(side, 3 * side) for side in range(kept // 3)], kept, emit)
-        wait_all(fetched[1:])
-        c_all, s_all, d_all = [
-            spread_waves(waves, part, inner, kept, levels) for part in range(3)
-        ]
-        nodal = dot(kept_parts[...].reshape(4 * kept_items, 3 * columns), spread[...])
-        turned = []
-        for f in range(4):
-            part = nodal[f * kept_items : (f + 1) * kept_items]
-            turned += [c_all * part, s_all * part]
-        turned = split(jnp.concatenate(turned, axis=0))
-        moved = dot(turned, own[...])
-        sent = moved[:, NODES : NODES + LANES]
-        moved = moved[:, :NODES]
-        for f in range(4):
-            at = 2 * f * kept_items
-            local[f] = (
-                s_all * moved[at : at + kept_items]
-                - c_all * moved[at + kept_items : at + 2 * kept_items]
-                + d_all * nodal[f * kept_items : (f + 1) * kept_items]
-            )
+            groups = [edge_group(side, 3 * n) for n, side in enumerate(sides)]
+        run(groups, emit, to_nodes)
+        sent = [None] * 8
+        for ready in PAIRS if inner else (PAIRS[0] + PAIRS[1],):
+            turned = []
+            for f in ready:
+                turned += [c_all * nodal[f], s_all * nodal[f]]
+            moved = dot(split(jnp.concatenate(turned, axis=0)), own[...])
+            for n, f in enumerate(ready):
+                of_cos = moved[2 * n * kept_items : (2 * n + 1) * kept_items]
+                of_sin = moved[(2 * n + 1) * kept_items : (2 * n + 2) * kept_items]
+                local[f] = s_all * of_cos[:, :NODES] - c_all * of_sin[:, :NODES] + d_all * nodal[f]
+                sent[2 * f] = of_cos[:, NODES : NODES + LANES]
+                sent[2 * f + 1] = of_sin[:, NODES : NODES + LANES]
         wide = lax.broadcasted_iota(jnp.int32, (kept_items, LANES), 1)
         for out, first, size in ((to_east, 0, NEAR), (to_west, NEAR, NEAR), (to_far, 2 * NEAR, FAR)):
             total = jnp.zeros((kept_items, LANES), F32)
-            for g in range(8):
-                part = sent[g * kept_items : (g + 1) * kept_items]
+            for g in range(7, -1, -1):
+                part = sent[g]
                 turn = (size * g - first) % LANES
                 if turn:
                     part = pltpu.roll(part, turn, 1)
-                total = jnp.where((wide >= size * g) & (wide < size * (g + 1)), part, total)
+                total = jnp.where(wide < size * (g + 1), part, total)
             if size == NEAR:
                 out[...] = total
             else:
@@ -463,7 +528,8 @@
                 out[...] = total[:, 0].reshape(kept_items // 2, LANES) + upper
 
 
-def finish_kernel(inner, count, *refs):
+def finish_kernel(sides, count, *refs):
+    inner = not sides
     fields = refs[:4]
     from_west, from_east, from_far, local, waves, take, gather = refs[4:11]
     outs = refs[15:19]
@@ -496,7 +562,7 @@
             top = part.astype(BF16).astype(F32)
             come.append((top + turn(part - top, MESSAGE) + turn(top, 2 * MESSAGE)).astype(BF16))
         moved = dot(jnp.concatenate(come, axis=0), take[...])
-        c_all, s_all = [spread_waves(waves, part, inner, count, levels) for part in range(2)]
+        c_all, s_all = [spread_waves(waves, part, sides, count, levels) for part in range(2)]
         writes = []
         for half in range(2):
             value = []
@@ -510,12 +576,12 @@
             pairs = []
             for f in (2 * half, 2 * half + 1):
                 for n in range(count):
-                    new[f, n] = fields[f][entry_row(inner, n, rows)] + change[f % 2, n]
+                    new[f, n] = fields[f][entry_row(sides, n, rows)] + change[f % 2, n]
                 off_edge = rows - 6 if inner else 0
                 if inner:
                     pairs.append((new.at[f, 0:off_edge], outs[f].at[3 : rows - 3]))
                 for n in range(off_edge, count):
-                    pairs.append((new.at[f, n], outs[f].at[entry_row(inner, n, rows)]))
+                    pairs.append((new.at[f, n], outs[f].at[entry_row(sides, n, rows)]))
             writes += start_all(pairs, sems, 12 * half)
         wait_all(writes)
 
@@ -590,56 +656,59 @@
 
     at_poles = lat_count == 4
     inner_count = rows - 3 if at_poles else rows - 6
-    edge_kept = 3 if at_poles else 6
-
-    def tendencies(inner, old):
-        count, kept = (inner_count, inner_count) if inner else (6, edge_kept)
+
+    def tendencies(sides, kept, old=(), shared=()):
+        inner = not sides
+        count = kept if inner else 3 * len(sides)
         kept_items = kept * levels
+        halos = [] if inner else [*[(strip_a, strip_b)[side] for side in sides], *shared]
         weights = [tables[k] for k in ("band", "spread", "own")]
         if inner:
             weights = [in_hbm(w) for w in weights]
-        halos = [] if inner else [strip_a, strip_b, *old[4:]]
-        old = old[:4]
         args = [metric, spin, *fields, mass, west, east, waves, *halos, *weights]
+        ahead = [tables["take"], tables["gather"]] if kept and not inner else []
+        sent = [like(4, kept_items, NODES)] + [like(kept_items, LANES)] * 2 + [like(kept_items // 2, LANES)]
+        tiles = columns // LANES
+        results = sent * (kept > 0)
+        if inner:
+            results += [like(rows, 8, columns), like(tiles, 4, 6, levels, 2 * LANES)]
+        part = pltpu.VMEM((2, kept, levels, 3 * columns), BF16)
         return pl.pallas_call(
-            functools.partial(tend_kernel, inner, count, kept),
-            out_shape=[like(rows, levels, columns)] * 4
-            + [like(4, kept_items, NODES)]
-            + [like(kept_items, LANES)] * 2
-            + [like(kept_items // 2, LANES)]
-            + [like(rows, 8, columns)] * inner,
+            functools.partial(tend_kernel, sides, count, kept),
+            out_shape=[like(rows, levels, columns)] * 4 + results,
             in_specs=[smem()] * 2
             + [vmem()] * (len(args) - 5)
             + [anywhere() if inner else vmem()] * 3
+            + [vmem()] * len(ahead)
             + [anywhere()] * len(old),
-            out_specs=[anywhere()] * 4 + [vmem()] * (4 + inner),
+            out_specs=[anywhere()] * 4 + [vmem()] * len(results),
             scratch_shapes=[
-                pltpu.VMEM((4, count, levels, columns + LANES), BF16),
-                pltpu.VMEM((4, count, levels, columns + LANES), BF16),
                 pltpu.VMEM((4, count, levels, columns), F32),
-                pltpu.VMEM((4, kept, levels, 3 * columns), BF16),
-                pltpu.VMEM((rows, 8, columns), F32),
+                pltpu.VMEM((rows if inner else count, 8, columns), F32),
+                pltpu.VMEM((count, levels, columns), F32),
                 pltpu.SemaphoreType.DMA((28,)),
-                *[pltpu.VMEM((4, count, levels, 2 * LANES), F32)] * (columns // LANES),
+                *[part] * (2 if kept else 0),
+                *[pltpu.VMEM((4, rows, levels, columns + LANES), BF16)] * (2 if inner else 0),
+                *[pltpu.VMEM((tiles, 4, rows - 6, levels, 2 * LANES), F32)] * inner,
+                *[pltpu.VMEM((4, rows - 6, levels, 2 * LANES), F32)] * (tiles if inner else 0),
                 *[pltpu.VMEM(w.shape, w.dtype) for w in weights if inner],
             ],
-            input_output_aliases={len(args) + f: f for f in range(4)} if old else {},
+            input_output_aliases={len(args) + len(ahead) + f: f for f in range(4)} if old else {},
             compiler_params=params(40),
             cost_estimate=pl.CostEstimate(
                 flops=count * levels * 4 * columns * 20000, bytes_accessed=2**22, transcendentals=0
             ),
             name="tend_inner" if inner else "tend_edge",
-        )(*args, *old)
+        )(*args, *ahead, *old)
 
     def exchange(east_part, west_part, far_part):
         return ring(east_part, 1), ring(west_part, -1), ring(far_part, 2)
 
-    def finish(inner, received, local, old):
-        count = inner_count if inner else edge_kept
+    def finish(sides, count, received, local, old):
         weights = [tables[k] for k in ("take", "gather")]
         args = [*fields, *received, local, waves, *weights]
         return pl.pallas_call(
-            functools.partial(finish_kernel, inner, count),
+            functools.partial(finish_kernel, sides, count),
             out_shape=[like(rows, levels, columns)] * 4,
             in_specs=[vmem()] * len(args) + [anywhere()] * 4,
             out_specs=[anywhere()] * 4,
@@ -649,16 +718,20 @@
             ],
             input_output_aliases={len(args) + f: f for f in range(4)},
             compiler_params=params(24),
-            name="finish_inner" if inner else "finish_edge",
+            name="finish_edge" if sides else "finish_inner",
         )(*args, *old)
 
-    *outs, local_inner, a, b, c, mass_x = tendencies(True, [])
+    *outs, local_inner, a, b, c, mass_x, edge_cross = tendencies((), inner_count)
+    shared = (mass_x, edge_cross)
     received_inner = exchange(a, b, c)
-    outs = [*outs, mass_x]
-    *outs, local_edge, a, b, c = tendencies(False, outs)
+    sides = (0,) if at_poles else (0, 1)
+    kept = 3 * len(sides)
+    *outs, local_edge, a, b, c = tendencies(sides, kept, outs, shared)
     received_edge = exchange(a, b, c)
-    outs = finish(True, received_inner, local_inner, outs)
-    outs = finish(False, received_edge, local_edge, outs)
+    if at_poles:
+        outs = tendencies((1,), 0, outs, shared)
+    outs = finish((), inner_count, received_inner, local_inner, outs)
+    outs = finish(sides, kept, received_edge, local_edge, outs)
     return tuple(outs)
 
 

time: 36.5 us -> 36.4 us (level)
  waiting for transfers between devices: 0.03 us -> 0.97 us
  Pallas kernels: 23.8 us -> 23 us
    ppermute x1, waiting for transfers between devices: 0.01 us -> 0.95 us  [shards(): strip_a = lax.ppermute(to_a, 'lat', [(i, i ^ 1) for i in range(lat_count)])]
    pallas_call x4 -> x5, Pallas kernels: 21.7 us -> 20.8 us  [the longest x3 14.9 us: tendencies(): pl.pallas_call(functools.partial(tend_kernel, sides, count, kept), out_sh...]
  transfers between devices with their start and end apart: 10 -> 10, of which waited for: 0 -> 1; matrix products, arithmetic and copies ran while one was open for 0% -> 0% of each run, Pallas kernels for 55% -> 52%
where the time goes in v13:
time: 36.4 us; the launch traced here: 36.2 us
  Pallas kernels  23 us (63%)
  starting transfers between devices  11.1 us (30%)
  between operations  1.07 us (3%)
  waiting for transfers between devices  0.97 us (3%)
    pallas_call x3, Pallas kernels, tendencies(): pl.pallas_call(functools.partial(tend_kernel, sides, count, kept), out_sh...  14.9 us
    ppermute x8, starting transfers between devices, ring(): lax.ppermute(value, 'lon', [(i, (i + step) % lon_count) for i in range(lo...  8.07 us
    pallas_call x2, Pallas kernels, finish(): pl.pallas_call(functools.partial(finish_kernel, sides, count), out_shape=...  5.88 us
    ppermute x1, starting transfers between devices, shards(): strip_a = lax.ppermute(to_a, 'lat', [(i, i ^ 1) for i in range(lat_count)])  2.33 us
    pallas_call x1, Pallas kernels, shards(): pl.pallas_call(pack_kernel, out_shape=[like(strip, columns)] * 2 + [like(...  2.18 us
    ppermute x1, waiting for transfers between devices, shards(): strip_a = lax.ppermute(to_a, 'lat', [(i, i ^ 1) for i in range(lat_count)])  0.95 us
  transfers between devices with their start and end apart: 10, of which 1 were waited for; matrix products, arithmetic and copies ran while one was open for 0% of the time, Pallas kernels for 52%

profile of v13, /device:TPU:0, one launch (start us, length us, event | category | flops | bytes accessed | tf_op | source)
XLA Modules:
  0.0 36.2 jit_solution(9418844351025619917)
XLA Ops:
  0.6 0.0 copy-start.10
  0.6 0.0 copy-start.11
  0.7 0.0 copy-start.3
  0.7 0.0 copy-start.2
  0.7 0.0 copy-start.1
  0.7 0.0 copy-start
  0.7 0.0 copy-start.9
  0.7 2.2 %pack_edges.1 = (f32[200,896]{1,0:T(8,128)S(1)}, f32[200,896]{1,0:T(8,128)S(1)}, f32[48,128]{1,0:T(8,128)S(1)}, f32[48,128]{1,0:T(8,128)S(1)}, f32[3,16,8,256]{3,2,1,0:T(8,128)S(1)}) custom-call(f32[16,16,896]{2,1,0:T(8,128)} %refs_0_.11, f32[16,16,896]{2,1,0:T(8,128)} %refs_1_.11, f32[16,16,896]{2,1,0:T(8,128)} %refs_2_.11, f32[16,16,896]{2,1,0:T(8,128)} %refs_3_.11, ...), custom_call_target="tpu_custom_call" | custom-call | tf_op jit(solution)/shard_map/pack_edges/pallas_call | solution.py:632
  2.9 0.5 %collective-permute-start = (f32[48,128]{1,0:T(8,128)S(1)}, f32[48,128]{1,0:T(8,128)S(1)}, u32[]{:S(2)}, u32[]{:S(2)}) collective-permute-start(f32[48,128]{1,0:T(8,128)S(1)} %get-tuple-element.35), channel_id=1, source_target_pairs={{0,1},{1,2},{2,3},{3,0},{4,5},{5,6},{6,7},{7,4},{8,9},{9,10},{10,1... | collective-permute-start | bytes 73736 | tf_op jit(solution)/shard_map/ppermute | solution.py:649
  3.4 2.0 %collective-permute-start.1 = (f32[48,128]{1,0:T(8,128)S(1)}, f32[48,128]{1,0:T(8,128)S(1)}, u32[]{:S(2)}, u32[]{:S(2)}) collective-permute-start(f32[48,128]{1,0:T(8,128)S(1)} %get-tuple-element.36), channel_id=1, source_target_pairs={{0,3},{1,0},{2,1},{3,2},{4,7},{5,4},{6,5},{7,6},{8,11},{9,8},{10,9... | collective-permute-start | bytes 73736 | tf_op jit(solution)/shard_map/ppermute | solution.py:649
  5.4 2.3 %collective-permute-start.2 = (f32[200,896]{1,0:T(8,128)S(1)}, f32[200,896]{1,0:T(8,128)S(1)}, u32[]{:S(2)}, u32[]{:S(2)}) collective-permute-start(f32[200,896]{1,0:T(8,128)S(1)} %get-tuple-element.38), channel_id=1, source_target_pairs={{0,4},{4,0},{8,12},{12,8},{1,5},{5,1},{9,13},{13,9},{2,6},{6,2},{1... | collective-permute-start | bytes 2150408 | tf_op jit(solution)/shard_map/ppermute | solution.py:654
  7.7 0.7 %collective-permute-start.9 = (f32[200,896]{1,0:T(8,128)S(1)}, f32[200,896]{1,0:T(8,128)S(1)}, u32[]{:S(2)}, u32[]{:S(2)}) collective-permute-start(f32[200,896]{1,0:T(8,128)S(1)} %get-tuple-element.53), channel_id=1, source_target_pairs={{4,8},{8,4},{5,9},{9,5},{6,10},{10,6},{7,11},{11,7},{20,24},{24,20... | collective-permute-start | bytes 2150408 | tf_op jit(solution)/shard_map/ppermute | solution.py:655
  8.4 0.0 collective-permute-done.refs_5_
  8.4 0.0 collective-permute-done.1.refs_6_
  8.4 0.0 copy-done.10
  8.5 0.0 copy-done.11
  8.5 0.0 copy-done.3
  8.5 0.0 copy-done.2
  8.5 0.0 copy-done.1
  8.5 0.0 copy-done
  8.5 0.0 copy-done.9
  8.5 0.0 copy-start.4
  8.5 0.0 copy-start.5
  8.5 0.0 copy-start.6
  8.6 0.0 copy-start.7
  8.6 0.0 copy-start.8
  8.6 11.1 %tend_inner.1 = (f32[16,16,896]{2,1,0:T(8,128)}, f32[16,16,896]{2,1,0:T(8,128)}, f32[16,16,896]{2,1,0:T(8,128)}, f32[16,16,896]{2,1,0:T(8,128)}, f32[4,208,256]{...) custom-call(f32[64]{0:T(128)S(1)} %copy-done.11, ...), custom_call_target="tpu_custom_call" | custom-call | flops 14909440000 | bytes 4194304 | tf_op jit(solution)/shard_map/tend_inner/pallas_call | solution.py:676
  19.7 1.6 %collective-permute-start.8 = (f32[104,128]{1,0:T(8,128)S(1)}, f32[104,128]{1,0:T(8,128)S(1)}, u32[]{:S(2)}, u32[]{:S(2)}) collective-permute-start(f32[104,128]{1,0:T(8,128)S(1)} %get-tuple-element.51), channel_id=1, source_target_pairs={{0,2},{1,3},{2,0},{3,1},{4,6},{5,7},{6,4},{7,5},{8,10},{9,11},{10,... | collective-permute-start | bytes 159752 | tf_op jit(solution)/shard_map/ppermute | solution.py:649
  21.3 0.0 collective-permute-start.6
  21.3 1.7 %collective-permute-start.7 = (f32[208,128]{1,0:T(8,128)S(1)}, f32[208,128]{1,0:T(8,128)S(1)}, u32[]{:S(2)}, u32[]{:S(2)}) collective-permute-start(f32[208,128]{1,0:T(8,128)S(1)} %get-tuple-element.50), channel_id=1, source_target_pairs={{0,3},{1,0},{2,1},{3,2},{4,7},{5,4},{6,5},{7,6},{8,11},{9,8},{10,9... | collective-permute-start | bytes 319496 | tf_op jit(solution)/shard_map/ppermute | solution.py:649
  23.0 0.9 %collective-permute-done.2.refs_8_ = f32[200,896]{1,0:T(8,128)S(1)} collective-permute-done((f32[200,896]{1,0:T(8,128)S(1)}, f32[200,896]{1,0:T(8,128)S(1)}, u32[]{:S(2)}, u32[]{:S(2)}) %collective-permute-start.2) | collective-permute-done | bytes 716832 | tf_op jit(solution)/shard_map/ppermute | solution.py:654
  24.0 0.0 copy-done.4
  24.0 0.0 copy-done.5
  24.0 0.0 copy-done.6
  24.0 0.0 copy-done.7
  24.0 0.0 copy-done.8
  24.0 3.0 %tend_edge.2 = (f32[16,16,896]{2,1,0:T(8,128)}, f32[16,16,896]{2,1,0:T(8,128)}, f32[16,16,896]{2,1,0:T(8,128)}, f32[16,16,896]{2,1,0:T(8,128)}, f32[4,48,256]{2,...) custom-call(f32[64]{0:T(128)S(1)} %copy-done.11, ...), custom_call_target="tpu_custom_call", output_to_operand_aliasing={{0}: (18, {}), {1}: (19, {}), {2}: (20, {}), {3}: (21, {})} | custom-call | flops 3440640000 | bytes 4194304 | tf_op jit(solution)/shard_map/tend_edge/pallas_call | solution.py:676
  27.0 0.5 %collective-permute-start.5 = (f32[24,128]{1,0:T(8,128)S(1)}, f32[24,128]{1,0:T(8,128)S(1)}, u32[]{:S(2)}, u32[]{:S(2)}) collective-permute-start(f32[24,128]{1,0:T(8,128)S(1)} %get-tuple-element.47), channel_id=1, source_target_pairs={{0,2},{1,3},{2,0},{3,1},{4,6},{5,7},{6,4},{7,5},{8,10},{9,11},{10,... | collective-permute-start | bytes 36872 | tf_op jit(solution)/shard_map/ppermute | solution.py:649
  27.5 0.0 collective-permute-done.8.refs_6_
  27.5 0.0 collective-permute-start.3
  27.5 0.0 collective-permute-done.9.refs_8_
  27.6 1.7 %collective-permute-start.4 = (f32[48,128]{1,0:T(8,128)S(1)}, f32[48,128]{1,0:T(8,128)S(1)}, u32[]{:S(2)}, u32[]{:S(2)}) collective-permute-start(f32[48,128]{1,0:T(8,128)S(1)} %get-tuple-element.46), channel_id=1, source_target_pairs={{0,3},{1,0},{2,1},{3,2},{4,7},{5,4},{6,5},{7,6},{8,11},{9,8},{10,9... | collective-permute-start | bytes 73736 | tf_op jit(solution)/shard_map/ppermute | solution.py:649
  29.3 0.8 %tend_edge.3 = (f32[16,16,896]{2,1,0:T(8,128)}, f32[16,16,896]{2,1,0:T(8,128)}, f32[16,16,896]{2,1,0:T(8,128)}, f32[16,16,896]{2,1,0:T(8,128)}) custom-call(f32[64]{0:T(128)S(1)} %copy-done.11, f32[64]{0:T(128)S(1)} %copy-done.10, f32[16,16,896]{2,1,0:T(8,128)S(1)} %copy-done, ...), custom_call_target="tpu_custom_call", output_to_operand_aliasing={{0}: (16, {}), {1}: (17, {}), {2}: (18, {}), {3}: (19, {})} | custom-call | flops 3440640000 | bytes 4194304 | tf_op jit(solution)/shard_map/tend_edge/pallas_call | solution.py:676
  30.1 0.0 collective-permute-done.6.refs_4_
  30.1 0.0 collective-permute-done.7.refs_5_
  30.1 4.0 %finish_inner.1 = (f32[16,16,896]{2,1,0:T(8,128)}, f32[16,16,896]{2,1,0:T(8,128)}, f32[16,16,896]{2,1,0:T(8,128)}, f32[16,16,896]{2,1,0:T(8,128)}) custom-call(f32[16,16,896]{2,1,0:T(8,128)S(1)} %copy-done, f32[16,16,896]{2,1,0:T(8,128)S(1)} %copy-done.1, ...), custom_call_target="tpu_custom_call", output_to_operand_aliasing={{0}: (11, {}), {1}: (12, {}), {2}: (13, {}), {3}: (14, {})} | custom-call | tf_op jit(solution)/shard_map/finish_inner/pallas_call | solution.py:710
  34.1 0.0 collective-permute-done.5.refs_6_
  34.1 0.0 collective-permute-done.3.refs_4_
  34.1 0.0 collective-permute-done.4.refs_5_
  34.1 1.9 %finish_edge.1 = (f32[16,16,896]{2,1,0:T(8,128)}, f32[16,16,896]{2,1,0:T(8,128)}, f32[16,16,896]{2,1,0:T(8,128)}, f32[16,16,896]{2,1,0:T(8,128)}) custom-call(f32[16,16,896]{2,1,0:T(8,128)S(1)} %copy-done, f32[16,16,896]{2,1,0:T(8,128)S(1)} %copy-done.1, ...), custom_call_target="tpu_custom_call", output_to_operand_aliasing={{0}: (11, {}), {1}: (12, {}), {2}: (13, {}), {3}: (14, {})} | custom-call | tf_op jit(solution)/shard_map/finish_edge/pallas_call | solution.py:710
Async XLA Ops:
  0.6 7.8 %copy-start.10 = (f32[64]{0:T(128)S(1)}, f32[64]{0:T(128)}, u32[]{:S(2)}) copy-start(f32[64]{0:T(128)} %constant.23.clone.spin) | copy-start | bytes 772
  0.6 7.8 %copy-start.11 = (f32[64]{0:T(128)S(1)}, f32[64]{0:T(128)}, u32[]{:S(2)}) copy-start(f32[64]{0:T(128)} %constant.22.clone.metric) | copy-start | bytes 772
  0.7 7.8 %copy-start.3 = (f32[16,16,896]{2,1,0:T(8,128)S(1)}, f32[16,16,896]{2,1,0:T(8,128)}, u32[]{:S(2)}) copy-start(f32[16,16,896]{2,1,0:T(8,128)} %refs_3_.11) | copy-start | bytes 2752516
  0.7 7.8 %copy-start.2 = (f32[16,16,896]{2,1,0:T(8,128)S(1)}, f32[16,16,896]{2,1,0:T(8,128)}, u32[]{:S(2)}) copy-start(f32[16,16,896]{2,1,0:T(8,128)} %refs_2_.11) | copy-start | bytes 2752516
  0.7 7.8 %copy-start.1 = (f32[16,16,896]{2,1,0:T(8,128)S(1)}, f32[16,16,896]{2,1,0:T(8,128)}, u32[]{:S(2)}) copy-start(f32[16,16,896]{2,1,0:T(8,128)} %refs_1_.11) | copy-start | bytes 2752516
  0.7 7.8 %copy-start = (f32[16,16,896]{2,1,0:T(8,128)S(1)}, f32[16,16,896]{2,1,0:T(8,128)}, u32[]{:S(2)}) copy-start(f32[16,16,896]{2,1,0:T(8,128)} %refs_0_.11) | copy-start | bytes 2752516
  0.7 7.8 %copy-start.9 = (f32[16,896]{1,0:T(8,128)S(1)}, f32[16,896]{1,0:T(8,128)}, u32[]{:S(2)}) copy-start(f32[16,896]{1,0:T(8,128)} %refs_4_.7) | copy-start | bytes 172036
  2.9 5.5 %collective-permute-start = (f32[48,128]{1,0:T(8,128)S(1)}, f32[48,128]{1,0:T(8,128)S(1)}, u32[]{:S(2)}, u32[]{:S(2)}) collective-permute-start(f32[48,128]{1,0:T(8,128)S(1)} %get-tuple-element.35), channel_id=1, source_target_pairs={{0,1},{1,2},{2,3},{3,0},{4,5},{5,6},{6,7},{7,4},{8,9},{9,10},{10,1... | collective-permute-start | bytes 73736 | tf_op jit(solution)/shard_map/ppermute | solution.py:649
  3.4 5.0 %collective-permute-start.1 = (f32[48,128]{1,0:T(8,128)S(1)}, f32[48,128]{1,0:T(8,128)S(1)}, u32[]{:S(2)}, u32[]{:S(2)}) collective-permute-start(f32[48,128]{1,0:T(8,128)S(1)} %get-tuple-element.36), channel_id=1, source_target_pairs={{0,3},{1,0},{2,1},{3,2},{4,7},{5,4},{6,5},{7,6},{8,11},{9,8},{10,9... | collective-permute-start | bytes 73736 | tf_op jit(solution)/shard_map/ppermute | solution.py:649
  5.4 18.6 %collective-permute-start.2 = (f32[200,896]{1,0:T(8,128)S(1)}, f32[200,896]{1,0:T(8,128)S(1)}, u32[]{:S(2)}, u32[]{:S(2)}) collective-permute-start(f32[200,896]{1,0:T(8,128)S(1)} %get-tuple-element.38), channel_id=1, source_target_pairs={{0,4},{4,0},{8,12},{12,8},{1,5},{5,1},{9,13},{13,9},{2,6},{6,2},{1... | collective-permute-start | bytes 2150408 | tf_op jit(solution)/shard_map/ppermute | solution.py:654
  7.7 19.8 %collective-permute-start.9 = (f32[200,896]{1,0:T(8,128)S(1)}, f32[200,896]{1,0:T(8,128)S(1)}, u32[]{:S(2)}, u32[]{:S(2)}) collective-permute-start(f32[200,896]{1,0:T(8,128)S(1)} %get-tuple-element.53), channel_id=1, source_target_pairs={{4,8},{8,4},{5,9},{9,5},{6,10},{10,6},{7,11},{11,7},{20,24},{24,20... | collective-permute-start | bytes 2150408 | tf_op jit(solution)/shard_map/ppermute | solution.py:655
  8.5 15.4 %copy-start.4 = (bf16[768,896]{1,0:T(8,128)(2,1)S(1)}, bf16[768,896]{1,0:T(8,128)(2,1)}, u32[]{:S(2)}) copy-start(bf16[768,896]{1,0:T(8,128)(2,1)} %constant.21.clone.refs_15_.refs_10_) | copy-start | bytes 4128772
  8.5 15.4 %copy-start.5 = (bf16[2688,256]{1,0:T(8,128)(2,1)S(1)}, bf16[2688,256]{1,0:T(8,128)(2,1)}, u32[]{:S(2)}) copy-start(bf16[2688,256]{1,0:T(8,128)(2,1)} %constant.18.clone.refs_9_.refs_12_) | copy-start | bytes 4128772
  8.5 15.4 %copy-start.6 = (bf16[768,512]{1,0:T(8,128)(2,1)S(1)}, bf16[768,512]{1,0:T(8,128)(2,1)}, u32[]{:S(2)}) copy-start(bf16[768,512]{1,0:T(8,128)(2,1)} %constant.19.clone.refs_10_.refs_13_) | copy-start | bytes 2359300
  8.6 15.4 %copy-start.7 = (bf16[512,256]{1,0:T(8,128)(2,1)S(1)}, bf16[512,256]{1,0:T(8,128)(2,1)}, u32[]{:S(2)}) copy-start(bf16[512,256]{1,0:T(8,128)(2,1)} %constant.17.clone.refs_8_.refs_11_) | copy-start | bytes 786436
  8.6 15.4 %copy-start.8 = (bf16[128,256]{1,0:T(8,128)(2,1)S(1)}, bf16[128,256]{1,0:T(8,128)(2,1)}, u32[]{:S(2)}) copy-start(bf16[128,256]{1,0:T(8,128)(2,1)} %constant.20.clone.refs_14_.refs_9_) | copy-start | bytes 196612
  19.7 7.8 %collective-permute-start.8 = (f32[104,128]{1,0:T(8,128)S(1)}, f32[104,128]{1,0:T(8,128)S(1)}, u32[]{:S(2)}, u32[]{:S(2)}) collective-permute-start(f32[104,128]{1,0:T(8,128)S(1)} %get-tuple-element.51), channel_id=1, source_target_pairs={{0,2},{1,3},{2,0},{3,1},{4,6},{5,7},{6,4},{7,5},{8,10},{9,11},{10,... | collective-permute-start | bytes 159752 | tf_op jit(solution)/shard_map/ppermute | solution.py:649
  21.3 8.8 %collective-permute-start.6 = (f32[208,128]{1,0:T(8,128)S(1)}, f32[208,128]{1,0:T(8,128)S(1)}, u32[]{:S(2)}, u32[]{:S(2)}) collective-permute-start(f32[208,128]{1,0:T(8,128)S(1)} %get-tuple-element.49), channel_id=1, source_target_pairs={{0,1},{1,2},{2,3},{3,0},{4,5},{5,6},{6,7},{7,4},{8,9},{9,10},{10,1... | collective-permute-start | bytes 319496 | tf_op jit(solution)/shard_map/ppermute | solution.py:649
  21.3 8.9 %collective-permute-start.7 = (f32[208,128]{1,0:T(8,128)S(1)}, f32[208,128]{1,0:T(8,128)S(1)}, u32[]{:S(2)}, u32[]{:S(2)}) collective-permute-start(f32[208,128]{1,0:T(8,128)S(1)} %get-tuple-element.50), channel_id=1, source_target_pairs={{0,3},{1,0},{2,1},{3,2},{4,7},{5,4},{6,5},{7,6},{8,11},{9,8},{10,9... | collective-permute-start | bytes 319496 | tf_op jit(solution)/shard_map/ppermute | solution.py:649
  27.0 7.1 %collective-permute-start.5 = (f32[24,128]{1,0:T(8,128)S(1)}, f32[24,128]{1,0:T(8,128)S(1)}, u32[]{:S(2)}, u32[]{:S(2)}) collective-permute-start(f32[24,128]{1,0:T(8,128)S(1)} %get-tuple-element.47), channel_id=1, source_target_pairs={{0,2},{1,3},{2,0},{3,1},{4,6},{5,7},{6,4},{7,5},{8,10},{9,11},{10,... | collective-permute-start | bytes 36872 | tf_op jit(solution)/shard_map/ppermute | solution.py:649
  27.5 6.6 %collective-permute-start.3 = (f32[48,128]{1,0:T(8,128)S(1)}, f32[48,128]{1,0:T(8,128)S(1)}, u32[]{:S(2)}, u32[]{:S(2)}) collective-permute-start(f32[48,128]{1,0:T(8,128)S(1)} %get-tuple-element.45), channel_id=1, source_target_pairs={{0,1},{1,2},{2,3},{3,0},{4,5},{5,6},{6,7},{7,4},{8,9},{9,10},{10,1... | collective-permute-start | bytes 73736 | tf_op jit(solution)/shard_map/ppermute | solution.py:649
  27.6 6.6 %collective-permute-start.4 = (f32[48,128]{1,0:T(8,128)S(1)}, f32[48,128]{1,0:T(8,128)S(1)}, u32[]{:S(2)}, u32[]{:S(2)}) collective-permute-start(f32[48,128]{1,0:T(8,128)S(1)} %get-tuple-element.46), channel_id=1, source_target_pairs={{0,3},{1,0},{2,1},{3,2},{4,7},{5,4},{6,5},{7,6},{8,11},{9,8},{10,9... | collective-permute-start | bytes 73736 | tf_op jit(solution)/shard_map/ppermute | solution.py:649

commit v14 on v13

--- a/solution.py
+++ b/solution.py
@@ -147,27 +147,54 @@
     return jnp.where(lax.axis_index("lat") % 2 == 0, even, odd)
 
 
+def strip_copies(fields, strip, side):
+    rows, levels = fields[0].shape[:2]
+    pairs = []
+    for m in range(3):
+        row = edge_row(3 * side + m, rows)
+        for f, q in enumerate(fields):
+            pairs.append((q.at[row], strip.at[pl.ds(levels * (3 * f + m), levels)]))
+    return pairs
+
+
+def mass_tail(mass, strip, side, levels):
+    rows, columns = mass.shape
+    tail = 12 * levels
+    north = jnp.concatenate([mass[rows - 1 - m : rows - m] for m in range(3)], axis=0)
+    strip[tail : tail + 3] = jnp.where(edge_row(3 * side, rows) != 0, north, mass[0:3])
+    strip[tail + 3 : tail + 8] = jnp.zeros((5, columns), F32)
+
+
+def pack_b_kernel(*refs):
+    fields = refs[:4]
+    mass, _, strip, own_mass, sems = refs[4:]
+    owner = lax.axis_index("lat")
+
+    @pl.when((owner > 0) & (owner < lax.axis_size("lat") - 1))
+    def _():
+        copies = start_all([(mass, own_mass)], sems)
+        copies += start_all(strip_copies(fields, strip, 1), sems, 1)
+        wait_all(copies[:1])
+        mass_tail(own_mass, strip, 1, fields[0].shape[1])
+        wait_all(copies[1:])
+
+
 def pack_kernel(*refs):
     fields = refs[:4]
-    mass, cutoffs_in, nodes_in, strip_a, strip_b, west, east, waves = refs[4:12]
-    edge, own_mass, cutoffs, nodes, sems = refs[12:]
+    mass, cutoffs_in, metric_in, spin_in, nodes_in, strip, west, east, waves, factors = refs[4:14]
+    edge, own_mass, cutoffs, metric, spin, nodes, sems = refs[14:]
     rows, columns = mass.shape
     levels = edge.shape[3]
-    tail = 12 * levels
-    first = start_all([(cutoffs_in, cutoffs), (nodes_in, nodes)], sems, 33)
+    first = start_all(
+        [(cutoffs_in, cutoffs), (nodes_in, nodes), (metric_in, metric), (spin_in, spin)], sems, 33
+    )
     small = start_all(
         [(mass, own_mass)]
         + [(q.at[:, :, 0:LANES], edge.at[0, f]) for f, q in enumerate(fields)]
         + [(q.at[:, :, columns - LANES : columns], edge.at[1, f]) for f, q in enumerate(fields)],
         sems,
     )
-    pairs = []
-    for entry in range(6):
-        strip = strip_a if entry < 3 else strip_b
-        row = edge_row(entry, rows)
-        for f, q in enumerate(fields):
-            pairs.append((q.at[row], strip.at[pl.ds(levels * (3 * f + entry % 3), levels)]))
-    large = start_all(pairs, sems, 9)
+    large = start_all(strip_copies(fields, strip, 0), sems, 9)
 
     wait_all(first)
     lat_count = lax.axis_size("lat")
@@ -185,13 +212,13 @@
     angle = (turns - 2.0 * circle * jnp.floor(turns * (0.5 / circle))) * (math.pi / circle)
     for part, table in enumerate((jnp.cos(angle), jnp.sin(angle), twice * (1.0 / circle))):
         waves[part] = jnp.broadcast_to(table[:, None, :], (rows, 8, NODES))
+    for r in range(rows):
+        row = owner * rows + r
+        factors[0, r] = jnp.full((8, LANES), metric[row] * (1.0 / 60.0))
+        factors[1, r] = jnp.full((8, LANES), spin[row])
 
     wait_all(small)
-    north = jnp.concatenate([own_mass[rows - 1 - m : rows - m] for m in range(3)], axis=0)
-    south = own_mass[0:3]
-    for strip, lines in ((strip_a, by_parity(north, south)), (strip_b, by_parity(south, north))):
-        strip[tail : tail + 3] = lines
-        strip[tail + 3 : tail + 8] = jnp.zeros((5, columns), F32)
+    mass_tail(own_mass, strip, 0, levels)
     lane = lax.broadcasted_iota(jnp.int32, (levels, LANES), 1)
     west[2 * levels :] = own_mass[:, 0:LANES]
     east[2 * levels :] = pltpu.roll(own_mass[:, columns - LANES : columns], 3, 1)
@@ -234,7 +261,7 @@
         return pltpu.roll(wide, (-k) % whole, 1)[:, LANES : LANES + columns]
 
     slope = stencil(middle, [at(1), at(2), at(3)], [at(-1), at(-2), at(-3)])[0]
-    return over_levels(slope / (60.0 * middle))
+    return over_levels(slope / middle)
 
 
 def mass_slope_y(tall):
@@ -242,7 +269,7 @@
     plus = [tall[3 + k : 3 + k + size] for k in (1, 2, 3)]
     minus = [tall[3 - k : 3 - k + size] for k in (1, 2, 3)]
     middle = tall[3 : 3 + size]
-    return over_levels(stencil(middle, plus, minus)[0] / (60.0 * middle))
+    return over_levels(stencil(middle, plus, minus)[0] / middle)
 
 
 def spread_waves(waves, part, sides, kept, levels):
@@ -254,7 +281,7 @@
 PAIRS = ((3, 0), (1, 2))
 
 
-def tend_kernel(sides, count, kept, metric, spin, *refs):
+def tend_kernel(sides, count, kept, *refs):
     inner = not sides
     refs = list(refs)
 
@@ -264,7 +291,7 @@
         return taken
 
     fields = some(4)
-    mass, west, east, waves = some(4)
+    mass, west, east, waves, factors = some(5)
     strips = dict(zip(sides, some(len(sides))))
     mass_x, edge_cross = (None, None) if inner else some(2)
     tables_in = some(3)
@@ -299,8 +326,7 @@
             north = edge_row(3 * side, rows) != 0
             for m in range(6):
                 lines.append(jnp.where(north, mass[rows - 1 - m : rows - m], mass[m : m + 1]))
-            slope = mass_slope_y(jnp.concatenate(lines, axis=0))
-            mass_y[3 * n : 3 * n + 3] = slope * jnp.where(north, -1.0, 1.0)
+            mass_y[3 * n : 3 * n + 3] = mass_slope_y(jnp.concatenate(lines, axis=0))
 
     lane = lax.broadcasted_iota(jnp.int32, (levels, LANES), 1)
 
@@ -344,21 +370,18 @@
             return edge_cross, (t, f, entry - (rows - 6))
         return edge_cross, (t, f, (entry + 3 * sides[0] + 3) % 6)
 
-    start_row = lax.axis_index("lat") * rows
-
     def whole(lines):
         return jnp.concatenate([lines] * (levels // 8), axis=0)
 
     def tendency(pair, t, first, numbers, lines, row_of, emit, inward=1.0):
         size = len(numbers)
         span = columns_of(t)
-        metrics = [metric[start_row + n] for n in numbers]
-        spins = [spin[start_row + n] for n in numbers]
+        along = [whole(factors[0, n]) for n in numbers]
         centers = [[row_of(f, j, span) for j in range(size)] for f in range(3)]
         per_row = inward * (1.0 / 60.0)
         fast, fast_size, up, up_size = [], [], [], []
         for j in range(size):
-            fast.append(centers[0][j] * (metrics[j] * (1.0 / 60.0)))
+            fast.append(centers[0][j] * along[j])
             fast_size.append(jnp.abs(fast[j]))
             up.append(centers[1][j] * per_row)
             up_size.append(jnp.abs(up[j]))
@@ -378,12 +401,14 @@
                     theta = centers[2][j]
                     over_x = whole(mass_x[numbers[j], :, span])
                     over_y = whole(mass_y[lines[j], :, span])
-                    push_x[j] = metrics[j] * ((1.0 / 60.0) * slope_x + theta * over_x)
-                    push[first + j, :, span] = per_row * slope_y + theta * over_y
+                    if inner and not isinstance(inward, float):
+                        over_y = over_y * inward
+                    push_x[j] = along[j] * (slope_x + theta * over_x)
+                    push[first + j, :, span] = per_row * (slope_y + theta * over_y)
                 elif f == 0:
-                    change = change + (spins[j] * centers[1][j] - push_x[j])
+                    change = change + (whole(factors[1, numbers[j]]) * centers[1][j] - push_x[j])
                 elif f == 1:
-                    change = change - (spins[j] * centers[0][j] + push[first + j, :, span])
+                    change = change - (whole(factors[1, numbers[j]]) * centers[0][j] + push[first + j, :, span])
                 emit(f, first + j, t, q, change)
 
     def edge_group(side, first):
@@ -564,34 +589,31 @@
         moved = dot(jnp.concatenate(come, axis=0), take[...])
         c_all, s_all = [spread_waves(waves, part, sides, count, levels) for part in range(2)]
         writes = []
-        for half in range(2):
+        chunks = [(f,) for f in range(4)] if inner else [(0, 1, 2, 3)]
+        for chunk in chunks:
             value = []
-            for f in (2 * half, 2 * half + 1):
+            for f in chunk:
                 at = 2 * f * items
                 value.append(
                     local[f] + (s_all * moved[at : at + items] - c_all * moved[at + items : at + 2 * items])
                 )
             change = dot(split(jnp.concatenate(value, axis=0)), gather[...])
-            change = change.reshape(2, count, levels, columns)
+            change = change.reshape(len(chunk), count, levels, columns)
             pairs = []
-            for f in (2 * half, 2 * half + 1):
+            for k, f in enumerate(chunk):
                 for n in range(count):
-                    new[f, n] = fields[f][entry_row(sides, n, rows)] + change[f % 2, n]
+                    new[f, n] = fields[f][entry_row(sides, n, rows)] + change[k, n]
                 off_edge = rows - 6 if inner else 0
                 if inner:
                     pairs.append((new.at[f, 0:off_edge], outs[f].at[3 : rows - 3]))
                 for n in range(off_edge, count):
                     pairs.append((new.at[f, n], outs[f].at[entry_row(sides, n, rows)]))
-            writes += start_all(pairs, sems, 12 * half)
+            writes += start_all(pairs, sems, len(writes))
         wait_all(writes)
 
 
 def vmem():
     return pl.BlockSpec(memory_space=pltpu.VMEM)
-
-
-def smem():
-    return pl.BlockSpec(memory_space=pltpu.SMEM)
 
 
 def anywhere():
@@ -629,21 +651,37 @@
     strip = 12 * levels + 8
     edge_lines = 2 * levels + rows
     far_fields = [in_hbm(q) for q in (*fields, mass)]
-    to_a, to_b, to_west, to_east, waves = pl.pallas_call(
+    to_a, to_west, to_east, waves, factors = pl.pallas_call(
         pack_kernel,
-        out_shape=[like(strip, columns)] * 2 + [like(edge_lines, LANES)] * 2 + [like(3, rows, 8, NODES)],
-        in_specs=[anywhere()] * 7,
+        out_shape=[
+            like(strip, columns),
+            *[like(edge_lines, LANES)] * 2,
+            like(3, rows, 8, NODES),
+            like(2, rows, 8, LANES),
+        ],
+        in_specs=[anywhere()] * 9,
         out_specs=[vmem()] * 5,
         scratch_shapes=[
             pltpu.VMEM((2, 4, rows, levels, LANES), F32),
             pltpu.VMEM((rows, columns), F32),
             pltpu.SMEM(cutoffs.shape, jnp.int32),
+            pltpu.SMEM(metric.shape, F32),
+            pltpu.SMEM(spin.shape, F32),
             pltpu.VMEM((1, NODES), F32),
-            pltpu.SemaphoreType.DMA((35,)),
+            pltpu.SemaphoreType.DMA((37,)),
         ],
         compiler_params=params(8),
         name="pack_edges",
-    )(*far_fields, in_hbm(cutoffs), in_hbm(tables["nodes"]))
+    )(*far_fields, in_hbm(cutoffs), in_hbm(metric), in_hbm(spin), in_hbm(tables["nodes"]))
+    to_b = pl.pallas_call(
+        pack_b_kernel,
+        out_shape=like(strip, columns),
+        in_specs=[anywhere()] * 6,
+        out_specs=vmem(),
+        scratch_shapes=[pltpu.VMEM((rows, columns), F32), pltpu.SemaphoreType.DMA((13,))],
+        compiler_params=params(8),
+        name="pack_b",
+    )(*far_fields, to_west)
 
     def ring(value, step):
         return lax.ppermute(value, "lon", [(i, (i + step) % lon_count) for i in range(lon_count)])
@@ -665,7 +703,7 @@
         weights = [tables[k] for k in ("band", "spread", "own")]
         if inner:
             weights = [in_hbm(w) for w in weights]
-        args = [metric, spin, *fields, mass, west, east, waves, *halos, *weights]
+        args = [*fields, mass, west, east, waves, factors, *halos, *weights]
         ahead = [tables["take"], tables["gather"]] if kept and not inner else []
         sent = [like(4, kept_items, NODES)] + [like(kept_items, LANES)] * 2 + [like(kept_items // 2, LANES)]
         tiles = columns // LANES
@@ -676,8 +714,7 @@
         return pl.pallas_call(
             functools.partial(tend_kernel, sides, count, kept),
             out_shape=[like(rows, levels, columns)] * 4 + results,
-            in_specs=[smem()] * 2
-            + [vmem()] * (len(args) - 5)
+            in_specs=[vmem()] * (len(args) - 3)
             + [anywhere() if inner else vmem()] * 3
             + [vmem()] * len(ahead)
             + [anywhere()] * len(old),

time: 36.4 us -> 35.9 us (0.986)
  waiting for transfers between devices: 0.97 us -> 3.14 us
  Pallas kernels: 23 us -> 21.1 us
  starting transfers between devices: 11.1 us -> 10.4 us
    pallas_call x3, Pallas kernels: 14.9 us -> 13.1 us  [tendencies(): pl.pallas_call(functools.partial(tend_kernel, sides, count, kept), out_sh...]
    ppermute x1, waiting for transfers between devices: 0.95 us -> 2.4 us  [shards(): strip_a = lax.ppermute(to_a, 'lat', [(i, i ^ 1) for i in range(lat_count)])]
    ppermute x8, waiting for transfers between devices: 0.02 us -> 0.74 us  [ring(): lax.ppermute(value, 'lon', [(i, (i + step) % lon_count) for i in range(lo...]
    ppermute x1, starting transfers between devices: 2.33 us -> 1.64 us  [shards(): strip_a = lax.ppermute(to_a, 'lat', [(i, i ^ 1) for i in range(lat_count)])]
    pallas_call x1 -> x2, Pallas kernels: 2.18 us -> 2.15 us  [the longest x1 2.04 us: shards(): pl.pallas_call(pack_kernel, out_shape=[like(strip, columns), *[like(edge_...]
  transfers between devices with their start and end apart: 10 -> 10, of which waited for: 1 -> 2; matrix products, arithmetic and copies ran while one was open for 0% -> 0% of each run, Pallas kernels for 52% -> 48%
where the time goes in v14:
time: 35.9 us; the launch traced here: 35.7 us
  Pallas kernels  21.1 us (59%)
  starting transfers between devices  10.4 us (29%)
  waiting for transfers between devices  3.14 us (9%)
  between operations  1.02 us (3%)
    pallas_call x3, Pallas kernels, tendencies(): pl.pallas_call(functools.partial(tend_kernel, sides, count, kept), out_sh...  13.1 us
    ppermute x8, starting transfers between devices, ring(): lax.ppermute(value, 'lon', [(i, (i + step) % lon_count) for i in range(lo...  8.03 us
    pallas_call x2, Pallas kernels, finish(): pl.pallas_call(functools.partial(finish_kernel, sides, count), out_shape=...  5.83 us
    ppermute x1, waiting for transfers between devices, shards(): strip_a = lax.ppermute(to_a, 'lat', [(i, i ^ 1) for i in range(lat_count)])  2.4 us
    pallas_call x1, Pallas kernels, shards(): pl.pallas_call(pack_kernel, out_shape=[like(strip, columns), *[like(edge_...  2.04 us
    ppermute x1, starting transfers between devices, shards(): strip_a = lax.ppermute(to_a, 'lat', [(i, i ^ 1) for i in range(lat_count)])  1.64 us
    ppermute x8, waiting for transfers between devices, ring(): lax.ppermute(value, 'lon', [(i, (i + step) % lon_count) for i in range(lo...  0.74 us
  transfers between devices with their start and end apart: 10, of which 2 were waited for; matrix products, arithmetic and copies ran while one was open for 0% of the time, Pallas kernels for 48%

profile of v14, /device:TPU:0, one launch (start us, length us, event | category | flops | bytes accessed | tf_op | source)
XLA Modules:
  0.0 35.7 jit_solution(13807962411340567829)
XLA Ops:
  0.6 2.0 %pack_edges.1 = (f32[200,896]{1,0:T(8,128)S(1)}, f32[48,128]{1,0:T(8,128)S(1)}, f32[48,128]{1,0:T(8,128)S(1)}, f32[3,16,8,256]{3,2,1,0:T(8,128)S(1)}, f32[2,16,8,128]{3,2,1,0:T(8,128)S(1)}) custom-call(f32[16,16,896]{2,1,0:T(8,128)} %refs_0_.13, f32[16,16,896]{2,1,0:T(8,128)} %refs_1_.13, f32[16,16,896]{2,1,0:T(8,128)} %refs_2_.13, f32[16,16,896]{2,1,0:T(8,128)} %refs_3_.13, ...), custom_call_target="tpu_custom_call" | custom-call | tf_op jit(solution)/shard_map/pack_edges/pallas_call | solution.py:654
  2.7 2.4 %collective-permute-start.1 = (f32[48,128]{1,0:T(8,128)S(1)}, f32[48,128]{1,0:T(8,128)S(1)}, u32[]{:S(2)}, u32[]{:S(2)}) collective-permute-start(f32[48,128]{1,0:T(8,128)S(1)} %get-tuple-element.36.refs_5_), channel_id=1, source_target_pairs={{0,3},{1,0},{2,1},{3,2},{4,7},{5,4},{6,5},{7,6},{8,11},{9,8},{10,9... | collective-permute-start | bytes 73736 | tf_op jit(solution)/shard_map/ppermute | solution.py:687
  5.1 0.0 collective-permute-start
  5.1 0.0 copy-start
  5.1 0.0 copy-start.1
  5.1 0.0 copy-start.2
  5.1 0.0 copy-start.3
  5.1 0.0 copy-start.8
  5.1 1.6 %collective-permute-start.2 = (f32[200,896]{1,0:T(8,128)S(1)}, f32[200,896]{1,0:T(8,128)S(1)}, u32[]{:S(2)}, u32[]{:S(2)}) collective-permute-start(f32[200,896]{1,0:T(8,128)S(1)} %get-tuple-element.39), channel_id=1, source_target_pairs={{0,4},{4,0},{8,12},{12,8},{1,5},{5,1},{9,13},{13,9},{2,6},{6,2},{1... | collective-permute-start | bytes 2150408 | tf_op jit(solution)/shard_map/ppermute | solution.py:692
  6.8 0.1 pack_b.1
  6.9 0.7 %collective-permute-start.9 = (f32[200,896]{1,0:T(8,128)S(1)}, f32[200,896]{1,0:T(8,128)S(1)}, u32[]{:S(2)}, u32[]{:S(2)}) collective-permute-start(f32[200,896]{1,0:T(8,128)S(1)} %pack_b.1), channel_id=1, source_target_pairs={{4,8},{8,4},{5,9},{9,5},{6,10},{10,6},{7,11},{11,7},{20,24},{24,20... | collective-permute-start | bytes 2150408 | tf_op jit(solution)/shard_map/ppermute | solution.py:693
  7.6 0.0 collective-permute-done.1.refs_6_
  7.6 0.7 %collective-permute-done.refs_5_ = f32[48,128]{1,0:T(8,128)S(1)} collective-permute-done((f32[48,128]{1,0:T(8,128)S(1)}, f32[48,128]{1,0:T(8,128)S(1)}, u32[]{:S(2)}, u32[]{:S(2)}) %collective-permute-start) | collective-permute-done | bytes 24608 | tf_op jit(solution)/shard_map/ppermute | solution.py:687
  8.4 0.0 copy-done
  8.4 0.0 copy-done.1
  8.4 0.0 copy-done.2
  8.4 0.0 copy-done.3
  8.4 0.0 copy-done.8
  8.4 0.0 copy-start.4
  8.4 0.0 copy-start.5
  8.4 0.0 copy-start.6
  8.4 0.0 copy-start.7
  8.4 0.0 copy-start.9
  8.5 10.4 %tend_inner.1 = (f32[16,16,896]{2,1,0:T(8,128)}, f32[16,16,896]{2,1,0:T(8,128)}, f32[16,16,896]{2,1,0:T(8,128)}, f32[16,16,896]{2,1,0:T(8,128)}, f32[4,208,256]{...) custom-call(f32[16,16,896]{2,1,0:T(8,128)S(1)} %copy-done, ...), custom_call_target="tpu_custom_call" | custom-call | flops 14909440000 | bytes 4194304 | tf_op jit(solution)/shard_map/tend_inner/pallas_call | solution.py:714
  18.9 0.1 collective-permute-start.6
  18.9 1.7 %collective-permute-start.7 = (f32[208,128]{1,0:T(8,128)S(1)}, f32[208,128]{1,0:T(8,128)S(1)}, u32[]{:S(2)}, u32[]{:S(2)}) collective-permute-start(f32[208,128]{1,0:T(8,128)S(1)} %get-tuple-element.51), channel_id=1, source_target_pairs={{0,3},{1,0},{2,1},{3,2},{4,7},{5,4},{6,5},{7,6},{8,11},{9,8},{10,9... | collective-permute-start | bytes 319496 | tf_op jit(solution)/shard_map/ppermute | solution.py:687
  20.7 0.8 %collective-permute-start.8 = (f32[104,128]{1,0:T(8,128)S(1)}, f32[104,128]{1,0:T(8,128)S(1)}, u32[]{:S(2)}, u32[]{:S(2)}) collective-permute-start(f32[104,128]{1,0:T(8,128)S(1)} %get-tuple-element.52), channel_id=1, source_target_pairs={{0,2},{1,3},{2,0},{3,1},{4,6},{5,7},{6,4},{7,5},{8,10},{9,11},{10,... | collective-permute-start | bytes 159752 | tf_op jit(solution)/shard_map/ppermute | solution.py:687
  21.5 2.4 %collective-permute-done.2.refs_9_ = f32[200,896]{1,0:T(8,128)S(1)} collective-permute-done((f32[200,896]{1,0:T(8,128)S(1)}, f32[200,896]{1,0:T(8,128)S(1)}, u32[]{:S(2)}, u32[]{:S(2)}) %collective-permute-start.2) | collective-permute-done | bytes 716832 | tf_op jit(solution)/shard_map/ppermute | solution.py:692
  23.9 0.0 copy-done.4
  23.9 0.0 copy-done.5
  23.9 0.0 copy-done.6
  23.9 0.0 copy-done.7
  23.9 0.0 copy-done.9
  23.9 2.5 %tend_edge.2 = (f32[16,16,896]{2,1,0:T(8,128)}, f32[16,16,896]{2,1,0:T(8,128)}, f32[16,16,896]{2,1,0:T(8,128)}, f32[16,16,896]{2,1,0:T(8,128)}, f32[4,48,256]{2,...) custom-call(f32[16,16,896]{2,1,0:T(8,128)S(1)} %copy-done, ...), custom_call_target="tpu_custom_call", output_to_operand_aliasing={{0}: (17, {}), {1}: (18, {}), {2}: (19, {}), {3}: (20, {})} | custom-call | flops 3440640000 | bytes 4194304 | tf_op jit(solution)/shard_map/tend_edge/pallas_call | solution.py:714
  26.4 0.1 collective-permute-start.3
  26.4 0.0 collective-permute-done.8.refs_6_
  26.5 1.7 %collective-permute-start.4 = (f32[48,128]{1,0:T(8,128)S(1)}, f32[48,128]{1,0:T(8,128)S(1)}, u32[]{:S(2)}, u32[]{:S(2)}) collective-permute-start(f32[48,128]{1,0:T(8,128)S(1)} %get-tuple-element.47), channel_id=1, source_target_pairs={{0,3},{1,0},{2,1},{3,2},{4,7},{5,4},{6,5},{7,6},{8,11},{9,8},{10,9... | collective-permute-start | bytes 73736 | tf_op jit(solution)/shard_map/ppermute | solution.py:687
  28.2 0.0 collective-permute-done.9.refs_9_
  28.2 1.2 %collective-permute-start.5 = (f32[24,128]{1,0:T(8,128)S(1)}, f32[24,128]{1,0:T(8,128)S(1)}, u32[]{:S(2)}, u32[]{:S(2)}) collective-permute-start(f32[24,128]{1,0:T(8,128)S(1)} %get-tuple-element.48), channel_id=1, source_target_pairs={{0,2},{1,3},{2,0},{3,1},{4,6},{5,7},{6,4},{7,5},{8,10},{9,11},{10,... | collective-permute-start | bytes 36872 | tf_op jit(solution)/shard_map/ppermute | solution.py:687
  29.4 0.3 tend_edge.3
  29.6 0.0 collective-permute-done.6.refs_4_
  29.7 0.0 collective-permute-done.7.refs_5_
  29.7 3.8 %finish_inner.1 = (f32[16,16,896]{2,1,0:T(8,128)}, f32[16,16,896]{2,1,0:T(8,128)}, f32[16,16,896]{2,1,0:T(8,128)}, f32[16,16,896]{2,1,0:T(8,128)}) custom-call(f32[16,16,896]{2,1,0:T(8,128)S(1)} %copy-done, f32[16,16,896]{2,1,0:T(8,128)S(1)} %copy-done.1, ...), custom_call_target="tpu_custom_call", output_to_operand_aliasing={{0}: (11, {}), {1}: (12, {}), {2}: (13, {}), {3}: (14, {})} | custom-call | tf_op jit(solution)/shard_map/finish_inner/pallas_call | solution.py:747
  33.5 0.0 collective-permute-done.5.refs_6_
  33.5 0.0 collective-permute-done.3.refs_4_
  33.5 0.0 collective-permute-done.4.refs_5_
  33.5 2.0 %finish_edge.1 = (f32[16,16,896]{2,1,0:T(8,128)}, f32[16,16,896]{2,1,0:T(8,128)}, f32[16,16,896]{2,1,0:T(8,128)}, f32[16,16,896]{2,1,0:T(8,128)}) custom-call(f32[16,16,896]{2,1,0:T(8,128)S(1)} %copy-done, f32[16,16,896]{2,1,0:T(8,128)S(1)} %copy-done.1, ...), custom_call_target="tpu_custom_call", output_to_operand_aliasing={{0}: (11, {}), {1}: (12, {}), {2}: (13, {}), {3}: (14, {})} | custom-call | tf_op jit(solution)/shard_map/finish_edge/pallas_call | solution.py:747
Async XLA Ops:
  2.7 5.0 %collective-permute-start.1 = (f32[48,128]{1,0:T(8,128)S(1)}, f32[48,128]{1,0:T(8,128)S(1)}, u32[]{:S(2)}, u32[]{:S(2)}) collective-permute-start(f32[48,128]{1,0:T(8,128)S(1)} %get-tuple-element.36.refs_5_), channel_id=1, source_target_pairs={{0,3},{1,0},{2,1},{3,2},{4,7},{5,4},{6,5},{7,6},{8,11},{9,8},{10,9... | collective-permute-start | bytes 73736 | tf_op jit(solution)/shard_map/ppermute | solution.py:687
  5.1 3.3 %collective-permute-start = (f32[48,128]{1,0:T(8,128)S(1)}, f32[48,128]{1,0:T(8,128)S(1)}, u32[]{:S(2)}, u32[]{:S(2)}) collective-permute-start(f32[48,128]{1,0:T(8,128)S(1)} %get-tuple-element.35), channel_id=1, source_target_pairs={{0,1},{1,2},{2,3},{3,0},{4,5},{5,6},{6,7},{7,4},{8,9},{9,10},{10,1... | collective-permute-start | bytes 73736 | tf_op jit(solution)/shard_map/ppermute | solution.py:687
  5.1 3.3 %copy-start = (f32[16,16,896]{2,1,0:T(8,128)S(1)}, f32[16,16,896]{2,1,0:T(8,128)}, u32[]{:S(2)}) copy-start(f32[16,16,896]{2,1,0:T(8,128)} %refs_0_.13) | copy-start | bytes 2752516
  5.1 3.3 %copy-start.1 = (f32[16,16,896]{2,1,0:T(8,128)S(1)}, f32[16,16,896]{2,1,0:T(8,128)}, u32[]{:S(2)}) copy-start(f32[16,16,896]{2,1,0:T(8,128)} %refs_1_.13) | copy-start | bytes 2752516
  5.1 3.3 %copy-start.2 = (f32[16,16,896]{2,1,0:T(8,128)S(1)}, f32[16,16,896]{2,1,0:T(8,128)}, u32[]{:S(2)}) copy-start(f32[16,16,896]{2,1,0:T(8,128)} %refs_2_.13) | copy-start | bytes 2752516
  5.1 3.3 %copy-start.3 = (f32[16,16,896]{2,1,0:T(8,128)S(1)}, f32[16,16,896]{2,1,0:T(8,128)}, u32[]{:S(2)}) copy-start(f32[16,16,896]{2,1,0:T(8,128)} %refs_3_.13) | copy-start | bytes 2752516
  5.1 3.2 %copy-start.8 = (f32[16,896]{1,0:T(8,128)S(1)}, f32[16,896]{1,0:T(8,128)}, u32[]{:S(2)}) copy-start(f32[16,896]{1,0:T(8,128)} %refs_4_.9) | copy-start | bytes 172036
  5.1 18.7 %collective-permute-start.2 = (f32[200,896]{1,0:T(8,128)S(1)}, f32[200,896]{1,0:T(8,128)S(1)}, u32[]{:S(2)}, u32[]{:S(2)}) collective-permute-start(f32[200,896]{1,0:T(8,128)S(1)} %get-tuple-element.39), channel_id=1, source_target_pairs={{0,4},{4,0},{8,12},{12,8},{1,5},{5,1},{9,13},{13,9},{2,6},{6,2},{1... | collective-permute-start | bytes 2150408 | tf_op jit(solution)/shard_map/ppermute | solution.py:692
  6.9 21.3 %collective-permute-start.9 = (f32[200,896]{1,0:T(8,128)S(1)}, f32[200,896]{1,0:T(8,128)S(1)}, u32[]{:S(2)}, u32[]{:S(2)}) collective-permute-start(f32[200,896]{1,0:T(8,128)S(1)} %pack_b.1), channel_id=1, source_target_pairs={{4,8},{8,4},{5,9},{9,5},{6,10},{10,6},{7,11},{11,7},{20,24},{24,20... | collective-permute-start | bytes 2150408 | tf_op jit(solution)/shard_map/ppermute | solution.py:693
  8.4 15.5 %copy-start.4 = (bf16[768,896]{1,0:T(8,128)(2,1)S(1)}, bf16[768,896]{1,0:T(8,128)(2,1)}, u32[]{:S(2)}) copy-start(bf16[768,896]{1,0:T(8,128)(2,1)} %constant.21.clone.refs_16_.refs_10_) | copy-start | bytes 4128772
  8.4 15.5 %copy-start.5 = (bf16[2688,256]{1,0:T(8,128)(2,1)S(1)}, bf16[2688,256]{1,0:T(8,128)(2,1)}, u32[]{:S(2)}) copy-start(bf16[2688,256]{1,0:T(8,128)(2,1)} %constant.18.clone.refs_10_.refs_13_) | copy-start | bytes 4128772
  8.4 15.5 %copy-start.6 = (bf16[768,512]{1,0:T(8,128)(2,1)S(1)}, bf16[768,512]{1,0:T(8,128)(2,1)}, u32[]{:S(2)}) copy-start(bf16[768,512]{1,0:T(8,128)(2,1)} %constant.19.clone.refs_11_.refs_14_) | copy-start | bytes 2359300
  8.4 15.5 %copy-start.7 = (bf16[512,256]{1,0:T(8,128)(2,1)S(1)}, bf16[512,256]{1,0:T(8,128)(2,1)}, u32[]{:S(2)}) copy-start(bf16[512,256]{1,0:T(8,128)(2,1)} %constant.17.clone.refs_9_.refs_12_) | copy-start | bytes 786436
  8.4 15.5 %copy-start.9 = (bf16[128,256]{1,0:T(8,128)(2,1)S(1)}, bf16[128,256]{1,0:T(8,128)(2,1)}, u32[]{:S(2)}) copy-start(bf16[128,256]{1,0:T(8,128)(2,1)} %constant.20.clone.refs_15_.refs_9_) | copy-start | bytes 196612
  18.9 10.8 %collective-permute-start.6 = (f32[208,128]{1,0:T(8,128)S(1)}, f32[208,128]{1,0:T(8,128)S(1)}, u32[]{:S(2)}, u32[]{:S(2)}) collective-permute-start(f32[208,128]{1,0:T(8,128)S(1)} %get-tuple-element.50), channel_id=1, source_target_pairs={{0,1},{1,2},{2,3},{3,0},{4,5},{5,6},{6,7},{7,4},{8,9},{9,10},{10,1... | collective-permute-start | bytes 319496 | tf_op jit(solution)/shard_map/ppermute | solution.py:687
  18.9 10.7 %collective-permute-start.7 = (f32[208,128]{1,0:T(8,128)S(1)}, f32[208,128]{1,0:T(8,128)S(1)}, u32[]{:S(2)}, u32[]{:S(2)}) collective-permute-start(f32[208,128]{1,0:T(8,128)S(1)} %get-tuple-element.51), channel_id=1, source_target_pairs={{0,3},{1,0},{2,1},{3,2},{4,7},{5,4},{6,5},{7,6},{8,11},{9,8},{10,9... | collective-permute-start | bytes 319496 | tf_op jit(solution)/shard_map/ppermute | solution.py:687
  20.7 5.8 %collective-permute-start.8 = (f32[104,128]{1,0:T(8,128)S(1)}, f32[104,128]{1,0:T(8,128)S(1)}, u32[]{:S(2)}, u32[]{:S(2)}) collective-permute-start(f32[104,128]{1,0:T(8,128)S(1)} %get-tuple-element.52), channel_id=1, source_target_pairs={{0,2},{1,3},{2,0},{3,1},{4,6},{5,7},{6,4},{7,5},{8,10},{9,11},{10,... | collective-permute-start | bytes 159752 | tf_op jit(solution)/shard_map/ppermute | solution.py:687
  26.4 7.1 %collective-permute-start.3 = (f32[48,128]{1,0:T(8,128)S(1)}, f32[48,128]{1,0:T(8,128)S(1)}, u32[]{:S(2)}, u32[]{:S(2)}) collective-permute-start(f32[48,128]{1,0:T(8,128)S(1)} %get-tuple-element.46), channel_id=1, source_target_pairs={{0,1},{1,2},{2,3},{3,0},{4,5},{5,6},{6,7},{7,4},{8,9},{9,10},{10,1... | collective-permute-start | bytes 73736 | tf_op jit(solution)/shard_map/ppermute | solution.py:687
  26.5 7.1 %collective-permute-start.4 = (f32[48,128]{1,0:T(8,128)S(1)}, f32[48,128]{1,0:T(8,128)S(1)}, u32[]{:S(2)}, u32[]{:S(2)}) collective-permute-start(f32[48,128]{1,0:T(8,128)S(1)} %get-tuple-element.47), channel_id=1, source_target_pairs={{0,3},{1,0},{2,1},{3,2},{4,7},{5,4},{6,5},{7,6},{8,11},{9,8},{10,9... | collective-permute-start | bytes 73736 | tf_op jit(solution)/shard_map/ppermute | solution.py:687
  28.2 5.3 %collective-permute-start.5 = (f32[24,128]{1,0:T(8,128)S(1)}, f32[24,128]{1,0:T(8,128)S(1)}, u32[]{:S(2)}, u32[]{:S(2)}) collective-permute-start(f32[24,128]{1,0:T(8,128)S(1)} %get-tuple-element.48), channel_id=1, source_target_pairs={{0,2},{1,3},{2,0},{3,1},{4,6},{5,7},{6,4},{7,5},{8,10},{9,11},{10,... | collective-permute-start | bytes 36872 | tf_op jit(solution)/shard_map/ppermute | solution.py:687

commit v15 on v14

--- a/solution.py
+++ b/solution.py
@@ -347,6 +347,28 @@
                 low[f, i, :, t * LANES : (t + 1) * LANES] = (whole - top.astype(F32)).astype(BF16)
                 before = tile
         return carry
+
+    def cut_tile(t):
+        for i in range(rows):
+            row = entry_row(sides, i, rows)
+            first = (row % 2) * levels
+            if not isinstance(row, int):
+                first = pl.multiple_of(first, levels)
+            halo = pl.ds(first, levels)
+
+            def shifted(f, n):
+                lead = 16 * (row // 2) + 3 * f
+                if n < 0:
+                    return pltpu.roll(west[halo, :], (LANES - lead) % LANES, 1)
+                if n == tiles:
+                    return pltpu.roll(east[halo, :], (LANES + 3 - lead) % LANES, 1)
+                return pltpu.roll(fields[f][row, :, n * LANES : (n + 1) * LANES], 3, 1)
+
+            for f in range(4):
+                whole = jnp.where(lane < 3, shifted(f, t - 1), shifted(f, t))
+                top = whole.astype(BF16)
+                high[f, i, :, t * LANES : (t + 1) * LANES] = top
+                low[f, i, :, t * LANES : (t + 1) * LANES] = (whole - top.astype(F32)).astype(BF16)
 
     def columns_of(t, width=1):
         if isinstance(t, int):
@@ -436,15 +458,19 @@
 
     def run(groups, emit, then=None):
         if inner:
-            lax.fori_loop(0, rows, cut, 0)
+            cut_tile(0)
+            cut_tile(1)
             wait_all(fetched[:1])
             slopes_x(0)
+            cut_tile(2)
         else:
             edge_mass()
         for pair in range(2):
             for t in range(tiles):
                 if inner and pair == 0 and t + 1 < tiles:
                     slopes_x(t + 1)
+                    if t + 3 <= tiles:
+                        cut_tile(t + 3)
                 for first, numbers, lines, row_of, inward in groups:
                     tendency(pair, t, first, numbers, lines, row_of, emit, inward)
             if then:
@@ -589,7 +615,7 @@
         moved = dot(jnp.concatenate(come, axis=0), take[...])
         c_all, s_all = [spread_waves(waves, part, sides, count, levels) for part in range(2)]
         writes = []
-        chunks = [(f,) for f in range(4)] if inner else [(0, 1, 2, 3)]
+        chunks = [(f,) for f in range(4)] if inner else [(0, 1), (2, 3)]
         for chunk in chunks:
             value = []
             for f in chunk:
@@ -733,7 +759,7 @@
             input_output_aliases={len(args) + len(ahead) + f: f for f in range(4)} if old else {},
             compiler_params=params(40),
             cost_estimate=pl.CostEstimate(
-                flops=count * levels * 4 * columns * 20000, bytes_accessed=2**22, transcendentals=0
+                flops=count * levels * 4 * columns * 4000, bytes_accessed=2**22, transcendentals=0
             ),
             name="tend_inner" if inner else "tend_edge",
         )(*args, *ahead, *old)

time: 35.9 us -> 34.2 us (0.953)
  Pallas kernels: 21.1 us -> 19.4 us
  starting transfers between devices: 10.4 us -> 9.05 us
  waiting for transfers between devices: 3.14 us -> 4.46 us
    ppermute x8, waiting for transfers between devices: 0.74 us -> 4.46 us  [ring(): lax.ppermute(value, 'lon', [(i, (i + step) % lon_count) for i in range(lo...]
    ppermute x8, starting transfers between devices: 8.03 us -> 5.12 us  [ring(): lax.ppermute(value, 'lon', [(i, (i + step) % lon_count) for i in range(lo...]
    ppermute x1, waiting for transfers between devices: 2.4 us -> 0.01 us  [shards(): strip_a = lax.ppermute(to_a, 'lat', [(i, i ^ 1) for i in range(lat_count)])]
    ppermute x1, starting transfers between devices: 1.64 us -> 3.09 us  [shards(): strip_a = lax.ppermute(to_a, 'lat', [(i, i ^ 1) for i in range(lat_count)])]
    pallas_call x3, Pallas kernels: 13.1 us -> 11.7 us  [tendencies(): pl.pallas_call(functools.partial(tend_kernel, sides, count, kept), out_sh...]
  transfers between devices with their start and end apart: 10 -> 10, of which waited for: 2 -> 3; matrix products, arithmetic and copies ran while one was open for 0% -> 0% of each run, Pallas kernels for 48% -> 45%
where the time goes in v15:
time: 34.2 us; the launch traced here: 34 us
  Pallas kernels  19.4 us (57%)
  starting transfers between devices  9.05 us (26%)
  waiting for transfers between devices  4.46 us (13%)
  between operations  1.01 us (3%)
    pallas_call x3, Pallas kernels, tendencies(): pl.pallas_call(functools.partial(tend_kernel, sides, count, kept), out_sh...  11.7 us
    pallas_call x2, Pallas kernels, finish(): pl.pallas_call(functools.partial(finish_kernel, sides, count), out_shape=...  5.57 us
    ppermute x8, starting transfers between devices, ring(): lax.ppermute(value, 'lon', [(i, (i + step) % lon_count) for i in range(lo...  5.12 us
    ppermute x8, waiting for transfers between devices, ring(): lax.ppermute(value, 'lon', [(i, (i + step) % lon_count) for i in range(lo...  4.46 us
    ppermute x1, starting transfers between devices, shards(): strip_a = lax.ppermute(to_a, 'lat', [(i, i ^ 1) for i in range(lat_count)])  3.09 us
    pallas_call x1, Pallas kernels, shards(): pl.pallas_call(pack_kernel, out_shape=[like(strip, columns), *[like(edge_...  2.04 us
    ppermute x1, starting transfers between devices, shards(): strip_b = lax.ppermute(to_b, 'lat', odd_up + [(j, i) for i, j in odd_up])  0.84 us
  transfers between devices with their start and end apart: 10, of which 3 were waited for; matrix products, arithmetic and copies ran while one was open for 0% of the time, Pallas kernels for 45%

profile of v15, /device:TPU:0, one launch (start us, length us, event | category | flops | bytes accessed | tf_op | source)
XLA Modules:
  0.0 34.0 jit_solution(1525339291850979928)
XLA Ops:
  0.6 2.0 %pack_edges.1 = (f32[200,896]{1,0:T(8,128)S(1)}, f32[48,128]{1,0:T(8,128)S(1)}, f32[48,128]{1,0:T(8,128)S(1)}, f32[3,16,8,256]{3,2,1,0:T(8,128)S(1)}, f32[2,16,8,128]{3,2,1,0:T(8,128)S(1)}) custom-call(f32[16,16,896]{2,1,0:T(8,128)} %refs_0_.13, f32[16,16,896]{2,1,0:T(8,128)} %refs_1_.13, f32[16,16,896]{2,1,0:T(8,128)} %refs_2_.13, f32[16,16,896]{2,1,0:T(8,128)} %refs_3_.13, ...), custom_call_target="tpu_custom_call" | custom-call | tf_op jit(solution)/shard_map/pack_edges/pallas_call | solution.py:680
  2.7 3.1 %collective-permute-start.2 = (f32[200,896]{1,0:T(8,128)S(1)}, f32[200,896]{1,0:T(8,128)S(1)}, u32[]{:S(2)}, u32[]{:S(2)}) collective-permute-start(f32[200,896]{1,0:T(8,128)S(1)} %get-tuple-element.39), channel_id=1, source_target_pairs={{0,4},{4,0},{8,12},{12,8},{1,5},{5,1},{9,13},{13,9},{2,6},{6,2},{1... | collective-permute-start | bytes 2150408 | tf_op jit(solution)/shard_map/ppermute | solution.py:718
  5.8 0.0 copy-start
  5.8 0.0 copy-start.1
  5.8 0.0 copy-start.2
  5.8 0.0 copy-start.3
  5.8 0.0 copy-start.8
  5.8 0.1 pack_b.1
  5.9 0.8 %collective-permute-start.9 = (f32[200,896]{1,0:T(8,128)S(1)}, f32[200,896]{1,0:T(8,128)S(1)}, u32[]{:S(2)}, u32[]{:S(2)}) collective-permute-start(f32[200,896]{1,0:T(8,128)S(1)} %pack_b.1), channel_id=1, source_target_pairs={{4,8},{8,4},{5,9},{9,5},{6,10},{10,6},{7,11},{11,7},{20,24},{24,20... | collective-permute-start | bytes 2150408 | tf_op jit(solution)/shard_map/ppermute | solution.py:719
  6.8 0.7 %collective-permute-start.1 = (f32[48,128]{1,0:T(8,128)S(1)}, f32[48,128]{1,0:T(8,128)S(1)}, u32[]{:S(2)}, u32[]{:S(2)}) collective-permute-start(f32[48,128]{1,0:T(8,128)S(1)} %get-tuple-element.36.refs_5_), channel_id=1, source_target_pairs={{0,3},{1,0},{2,1},{3,2},{4,7},{5,4},{6,5},{7,6},{8,11},{9,8},{10,9... | collective-permute-start | bytes 73736 | tf_op jit(solution)/shard_map/ppermute | solution.py:713
  7.5 0.0 collective-permute-start
  7.5 1.5 %collective-permute-done.1.refs_6_ = f32[48,128]{1,0:T(8,128)S(1)} collective-permute-done((f32[48,128]{1,0:T(8,128)S(1)}, f32[48,128]{1,0:T(8,128)S(1)}, u32[]{:S(2)}, u32[]{:S(2)}) %collective-permute-start.1) | collective-permute-done | bytes 24608 | tf_op jit(solution)/shard_map/ppermute | solution.py:713
  9.0 1.7 %collective-permute-done.refs_5_ = f32[48,128]{1,0:T(8,128)S(1)} collective-permute-done((f32[48,128]{1,0:T(8,128)S(1)}, f32[48,128]{1,0:T(8,128)S(1)}, u32[]{:S(2)}, u32[]{:S(2)}) %collective-permute-start) | collective-permute-done | bytes 24608 | tf_op jit(solution)/shard_map/ppermute | solution.py:713
  10.7 0.0 copy-done
  10.7 0.0 copy-done.1
  10.7 0.0 copy-done.2
  10.7 0.0 copy-done.3
  10.7 0.0 copy-done.8
  10.8 0.0 copy-start.4
  10.8 0.0 copy-start.5
  10.8 0.0 copy-start.6
  10.8 0.0 copy-start.7
  10.8 0.0 copy-start.9
  10.8 9.0 %tend_inner.1 = (f32[16,16,896]{2,1,0:T(8,128)}, f32[16,16,896]{2,1,0:T(8,128)}, f32[16,16,896]{2,1,0:T(8,128)}, f32[16,16,896]{2,1,0:T(8,128)}, f32[4,208,256]{...) custom-call(f32[16,16,896]{2,1,0:T(8,128)S(1)} %copy-done, ...), custom_call_target="tpu_custom_call" | custom-call | flops 2981888000 | bytes 4194304 | tf_op jit(solution)/shard_map/tend_inner/pallas_call | solution.py:740
  19.8 0.1 collective-permute-start.6
  19.9 1.7 %collective-permute-start.7 = (f32[208,128]{1,0:T(8,128)S(1)}, f32[208,128]{1,0:T(8,128)S(1)}, u32[]{:S(2)}, u32[]{:S(2)}) collective-permute-start(f32[208,128]{1,0:T(8,128)S(1)} %get-tuple-element.51), channel_id=1, source_target_pairs={{0,3},{1,0},{2,1},{3,2},{4,7},{5,4},{6,5},{7,6},{8,11},{9,8},{10,9... | collective-permute-start | bytes 319496 | tf_op jit(solution)/shard_map/ppermute | solution.py:713
  21.6 0.9 %collective-permute-start.8 = (f32[104,128]{1,0:T(8,128)S(1)}, f32[104,128]{1,0:T(8,128)S(1)}, u32[]{:S(2)}, u32[]{:S(2)}) collective-permute-start(f32[104,128]{1,0:T(8,128)S(1)} %get-tuple-element.52), channel_id=1, source_target_pairs={{0,2},{1,3},{2,0},{3,1},{4,6},{5,7},{6,4},{7,5},{8,10},{9,11},{10,... | collective-permute-start | bytes 159752 | tf_op jit(solution)/shard_map/ppermute | solution.py:713
  22.5 0.0 collective-permute-done.2.refs_9_
  22.5 0.0 copy-done.4
  22.5 0.0 copy-done.5
  22.5 0.0 copy-done.6
  22.5 0.0 copy-done.7
  22.5 0.0 copy-done.9
  22.5 2.5 %tend_edge.2 = (f32[16,16,896]{2,1,0:T(8,128)}, f32[16,16,896]{2,1,0:T(8,128)}, f32[16,16,896]{2,1,0:T(8,128)}, f32[16,16,896]{2,1,0:T(8,128)}, f32[4,48,256]{2,...) custom-call(f32[16,16,896]{2,1,0:T(8,128)S(1)} %copy-done, ...), custom_call_target="tpu_custom_call", output_to_operand_aliasing={{0}: (17, {}), {1}: (18, {}), {2}: (19, {}), {3}: (20, {})} | custom-call | flops 688128000 | bytes 4194304 | tf_op jit(solution)/shard_map/tend_edge/pallas_call | solution.py:740
  25.0 0.1 collective-permute-start.3
  25.1 1.2 %collective-permute-done.8.refs_6_ = f32[104,128]{1,0:T(8,128)S(1)} collective-permute-done((f32[104,128]{1,0:T(8,128)S(1)}, f32[104,128]{1,0:T(8,128)S(1)}, u32[]{:S(2)}, u32[]{:S(2)}) %collective-permute-start.8) | collective-permute-done | bytes 53280 | tf_op jit(solution)/shard_map/ppermute | solution.py:713
  26.3 0.5 %collective-permute-start.4 = (f32[48,128]{1,0:T(8,128)S(1)}, f32[48,128]{1,0:T(8,128)S(1)}, u32[]{:S(2)}, u32[]{:S(2)}) collective-permute-start(f32[48,128]{1,0:T(8,128)S(1)} %get-tuple-element.47), channel_id=1, source_target_pairs={{0,3},{1,0},{2,1},{3,2},{4,7},{5,4},{6,5},{7,6},{8,11},{9,8},{10,9... | collective-permute-start | bytes 73736 | tf_op jit(solution)/shard_map/ppermute | solution.py:713
  26.8 0.0 collective-permute-done.9.refs_9_
  26.8 1.1 %collective-permute-start.5 = (f32[24,128]{1,0:T(8,128)S(1)}, f32[24,128]{1,0:T(8,128)S(1)}, u32[]{:S(2)}, u32[]{:S(2)}) collective-permute-start(f32[24,128]{1,0:T(8,128)S(1)} %get-tuple-element.48), channel_id=1, source_target_pairs={{0,2},{1,3},{2,0},{3,1},{4,6},{5,7},{6,4},{7,5},{8,10},{9,11},{10,... | collective-permute-start | bytes 36872 | tf_op jit(solution)/shard_map/ppermute | solution.py:713
  27.9 0.3 tend_edge.3
  28.2 0.0 collective-permute-done.6.refs_4_
  28.2 0.0 collective-permute-done.7.refs_5_
  28.2 3.6 %finish_inner.1 = (f32[16,16,896]{2,1,0:T(8,128)}, f32[16,16,896]{2,1,0:T(8,128)}, f32[16,16,896]{2,1,0:T(8,128)}, f32[16,16,896]{2,1,0:T(8,128)}) custom-call(f32[16,16,896]{2,1,0:T(8,128)S(1)} %copy-done, f32[16,16,896]{2,1,0:T(8,128)S(1)} %copy-done.1, ...), custom_call_target="tpu_custom_call", output_to_operand_aliasing={{0}: (11, {}), {1}: (12, {}), {2}: (13, {}), {3}: (14, {})} | custom-call | tf_op jit(solution)/shard_map/finish_inner/pallas_call | solution.py:773
  31.9 0.0 collective-permute-done.5.refs_6_
  31.9 0.0 collective-permute-done.3.refs_4_
  31.9 0.0 collective-permute-done.4.refs_5_
  31.9 1.9 %finish_edge.1 = (f32[16,16,896]{2,1,0:T(8,128)}, f32[16,16,896]{2,1,0:T(8,128)}, f32[16,16,896]{2,1,0:T(8,128)}, f32[16,16,896]{2,1,0:T(8,128)}) custom-call(f32[16,16,896]{2,1,0:T(8,128)S(1)} %copy-done, f32[16,16,896]{2,1,0:T(8,128)S(1)} %copy-done.1, ...), custom_call_target="tpu_custom_call", output_to_operand_aliasing={{0}: (11, {}), {1}: (12, {}), {2}: (13, {}), {3}: (14, {})} | custom-call | tf_op jit(solution)/shard_map/finish_edge/pallas_call | solution.py:773
Async XLA Ops:
  2.7 19.8 %collective-permute-start.2 = (f32[200,896]{1,0:T(8,128)S(1)}, f32[200,896]{1,0:T(8,128)S(1)}, u32[]{:S(2)}, u32[]{:S(2)}) collective-permute-start(f32[200,896]{1,0:T(8,128)S(1)} %get-tuple-element.39), channel_id=1, source_target_pairs={{0,4},{4,0},{8,12},{12,8},{1,5},{5,1},{9,13},{13,9},{2,6},{6,2},{1... | collective-permute-start | bytes 2150408 | tf_op jit(solution)/shard_map/ppermute | solution.py:718
  5.8 5.0 %copy-start = (f32[16,16,896]{2,1,0:T(8,128)S(1)}, f32[16,16,896]{2,1,0:T(8,128)}, u32[]{:S(2)}) copy-start(f32[16,16,896]{2,1,0:T(8,128)} %refs_0_.13) | copy-start | bytes 2752516
  5.8 5.0 %copy-start.1 = (f32[16,16,896]{2,1,0:T(8,128)S(1)}, f32[16,16,896]{2,1,0:T(8,128)}, u32[]{:S(2)}) copy-start(f32[16,16,896]{2,1,0:T(8,128)} %refs_1_.13) | copy-start | bytes 2752516
  5.8 5.0 %copy-start.2 = (f32[16,16,896]{2,1,0:T(8,128)S(1)}, f32[16,16,896]{2,1,0:T(8,128)}, u32[]{:S(2)}) copy-start(f32[16,16,896]{2,1,0:T(8,128)} %refs_2_.13) | copy-start | bytes 2752516
  5.8 5.0 %copy-start.3 = (f32[16,16,896]{2,1,0:T(8,128)S(1)}, f32[16,16,896]{2,1,0:T(8,128)}, u32[]{:S(2)}) copy-start(f32[16,16,896]{2,1,0:T(8,128)} %refs_3_.13) | copy-start | bytes 2752516
  5.8 5.0 %copy-start.8 = (f32[16,896]{1,0:T(8,128)S(1)}, f32[16,896]{1,0:T(8,128)}, u32[]{:S(2)}) copy-start(f32[16,896]{1,0:T(8,128)} %refs_4_.9) | copy-start | bytes 172036
  5.9 20.9 %collective-permute-start.9 = (f32[200,896]{1,0:T(8,128)S(1)}, f32[200,896]{1,0:T(8,128)S(1)}, u32[]{:S(2)}, u32[]{:S(2)}) collective-permute-start(f32[200,896]{1,0:T(8,128)S(1)} %pack_b.1), channel_id=1, source_target_pairs={{4,8},{8,4},{5,9},{9,5},{6,10},{10,6},{7,11},{11,7},{20,24},{24,20... | collective-permute-start | bytes 2150408 | tf_op jit(solution)/shard_map/ppermute | solution.py:719
  6.8 2.2 %collective-permute-start.1 = (f32[48,128]{1,0:T(8,128)S(1)}, f32[48,128]{1,0:T(8,128)S(1)}, u32[]{:S(2)}, u32[]{:S(2)}) collective-permute-start(f32[48,128]{1,0:T(8,128)S(1)} %get-tuple-element.36.refs_5_), channel_id=1, source_target_pairs={{0,3},{1,0},{2,1},{3,2},{4,7},{5,4},{6,5},{7,6},{8,11},{9,8},{10,9... | collective-permute-start | bytes 73736 | tf_op jit(solution)/shard_map/ppermute | solution.py:713
  7.5 3.3 %collective-permute-start = (f32[48,128]{1,0:T(8,128)S(1)}, f32[48,128]{1,0:T(8,128)S(1)}, u32[]{:S(2)}, u32[]{:S(2)}) collective-permute-start(f32[48,128]{1,0:T(8,128)S(1)} %get-tuple-element.35), channel_id=1, source_target_pairs={{0,1},{1,2},{2,3},{3,0},{4,5},{5,6},{6,7},{7,4},{8,9},{9,10},{10,1... | collective-permute-start | bytes 73736 | tf_op jit(solution)/shard_map/ppermute | solution.py:713
  10.8 11.7 %copy-start.4 = (bf16[768,896]{1,0:T(8,128)(2,1)S(1)}, bf16[768,896]{1,0:T(8,128)(2,1)}, u32[]{:S(2)}) copy-start(bf16[768,896]{1,0:T(8,128)(2,1)} %constant.21.clone.refs_16_.refs_10_) | copy-start | bytes 4128772
  10.8 11.7 %copy-start.5 = (bf16[2688,256]{1,0:T(8,128)(2,1)S(1)}, bf16[2688,256]{1,0:T(8,128)(2,1)}, u32[]{:S(2)}) copy-start(bf16[2688,256]{1,0:T(8,128)(2,1)} %constant.18.clone.refs_10_.refs_13_) | copy-start | bytes 4128772
  10.8 11.7 %copy-start.6 = (bf16[768,512]{1,0:T(8,128)(2,1)S(1)}, bf16[768,512]{1,0:T(8,128)(2,1)}, u32[]{:S(2)}) copy-start(bf16[768,512]{1,0:T(8,128)(2,1)} %constant.19.clone.refs_11_.refs_14_) | copy-start | bytes 2359300
  10.8 11.7 %copy-start.7 = (bf16[512,256]{1,0:T(8,128)(2,1)S(1)}, bf16[512,256]{1,0:T(8,128)(2,1)}, u32[]{:S(2)}) copy-start(bf16[512,256]{1,0:T(8,128)(2,1)} %constant.17.clone.refs_9_.refs_12_) | copy-start | bytes 786436
  10.8 11.7 %copy-start.9 = (bf16[128,256]{1,0:T(8,128)(2,1)S(1)}, bf16[128,256]{1,0:T(8,128)(2,1)}, u32[]{:S(2)}) copy-start(bf16[128,256]{1,0:T(8,128)(2,1)} %constant.20.clone.refs_15_.refs_9_) | copy-start | bytes 196612
  19.8 8.4 %collective-permute-start.6 = (f32[208,128]{1,0:T(8,128)S(1)}, f32[208,128]{1,0:T(8,128)S(1)}, u32[]{:S(2)}, u32[]{:S(2)}) collective-permute-start(f32[208,128]{1,0:T(8,128)S(1)} %get-tuple-element.50), channel_id=1, source_target_pairs={{0,1},{1,2},{2,3},{3,0},{4,5},{5,6},{6,7},{7,4},{8,9},{9,10},{10,1... | collective-permute-start | bytes 319496 | tf_op jit(solution)/shard_map/ppermute | solution.py:713
  19.9 8.3 %collective-permute-start.7 = (f32[208,128]{1,0:T(8,128)S(1)}, f32[208,128]{1,0:T(8,128)S(1)}, u32[]{:S(2)}, u32[]{:S(2)}) collective-permute-start(f32[208,128]{1,0:T(8,128)S(1)} %get-tuple-element.51), channel_id=1, source_target_pairs={{0,3},{1,0},{2,1},{3,2},{4,7},{5,4},{6,5},{7,6},{8,11},{9,8},{10,9... | collective-permute-start | bytes 319496 | tf_op jit(solution)/shard_map/ppermute | solution.py:713
  21.6 4.7 %collective-permute-start.8 = (f32[104,128]{1,0:T(8,128)S(1)}, f32[104,128]{1,0:T(8,128)S(1)}, u32[]{:S(2)}, u32[]{:S(2)}) collective-permute-start(f32[104,128]{1,0:T(8,128)S(1)} %get-tuple-element.52), channel_id=1, source_target_pairs={{0,2},{1,3},{2,0},{3,1},{4,6},{5,7},{6,4},{7,5},{8,10},{9,11},{10,... | collective-permute-start | bytes 159752 | tf_op jit(solution)/shard_map/ppermute | solution.py:713
  25.0 6.9 %collective-permute-start.3 = (f32[48,128]{1,0:T(8,128)S(1)}, f32[48,128]{1,0:T(8,128)S(1)}, u32[]{:S(2)}, u32[]{:S(2)}) collective-permute-start(f32[48,128]{1,0:T(8,128)S(1)} %get-tuple-element.46), channel_id=1, source_target_pairs={{0,1},{1,2},{2,3},{3,0},{4,5},{5,6},{6,7},{7,4},{8,9},{9,10},{10,1... | collective-permute-start | bytes 73736 | tf_op jit(solution)/shard_map/ppermute | solution.py:713
  26.3 5.6 %collective-permute-start.4 = (f32[48,128]{1,0:T(8,128)S(1)}, f32[48,128]{1,0:T(8,128)S(1)}, u32[]{:S(2)}, u32[]{:S(2)}) collective-permute-start(f32[48,128]{1,0:T(8,128)S(1)} %get-tuple-element.47), channel_id=1, source_target_pairs={{0,3},{1,0},{2,1},{3,2},{4,7},{5,4},{6,5},{7,6},{8,11},{9,8},{10,9... | collective-permute-start | bytes 73736 | tf_op jit(solution)/shard_map/ppermute | solution.py:713
  26.8 5.1 %collective-permute-start.5 = (f32[24,128]{1,0:T(8,128)S(1)}, f32[24,128]{1,0:T(8,128)S(1)}, u32[]{:S(2)}, u32[]{:S(2)}) collective-permute-start(f32[24,128]{1,0:T(8,128)S(1)} %get-tuple-element.48), channel_id=1, source_target_pairs={{0,2},{1,3},{2,0},{3,1},{4,6},{5,7},{6,4},{7,5},{8,10},{9,11},{10,... | collective-permute-start | bytes 36872 | tf_op jit(solution)/shard_map/ppermute | solution.py:713

commit v16 on v15

--- a/solution.py
+++ b/solution.py
@@ -605,24 +605,24 @@
             by = by % LANES
             return pltpu.roll(value, by, 1) if by else value
 
-        come = []
-        for g in range(8):
+        def come(g):
             part = jnp.where(wide < NEAR, turn(near_west, -NEAR * g), turn(near_east, NEAR - NEAR * g))
             part = jnp.where(wide < 2 * NEAR, part, turn(far, 2 * NEAR - FAR * g))
             part = jnp.where(wide < MESSAGE, part, 0.0)
             top = part.astype(BF16).astype(F32)
-            come.append((top + turn(part - top, MESSAGE) + turn(top, 2 * MESSAGE)).astype(BF16))
-        moved = dot(jnp.concatenate(come, axis=0), take[...])
+            return (top + turn(part - top, MESSAGE) + turn(top, 2 * MESSAGE)).astype(BF16)
+
         c_all, s_all = [spread_waves(waves, part, sides, count, levels) for part in range(2)]
         writes = []
         chunks = [(f,) for f in range(4)] if inner else [(0, 1), (2, 3)]
         for chunk in chunks:
+            groups = [come(2 * f + part) for f in chunk for part in range(2)]
+            moved = dot(jnp.concatenate(groups, axis=0), take[...])
             value = []
-            for f in chunk:
-                at = 2 * f * items
-                value.append(
-                    local[f] + (s_all * moved[at : at + items] - c_all * moved[at + items : at + 2 * items])
-                )
+            for k, f in enumerate(chunk):
+                of_cos = moved[2 * k * items : (2 * k + 1) * items]
+                of_sin = moved[(2 * k + 1) * items : (2 * k + 2) * items]
+                value.append(local[f] + (s_all * of_cos - c_all * of_sin))
             change = dot(split(jnp.concatenate(value, axis=0)), gather[...])
             change = change.reshape(len(chunk), count, levels, columns)
             pairs = []

time: 34.2 us -> 34.3 us (level)
  no operation moved by 1% of the time
where the time goes in v16:
time: 34.3 us; the launch traced here: 34.1 us
  Pallas kernels  19.5 us (57%)
  starting transfers between devices  9.05 us (26%)
  waiting for transfers between devices  4.46 us (13%)
  between operations  1.01 us (3%)
    pallas_call x3, Pallas kernels, tendencies(): pl.pallas_call(functools.partial(tend_kernel, sides, count, kept), out_sh...  11.7 us
    pallas_call x2, Pallas kernels, finish(): pl.pallas_call(functools.partial(finish_kernel, sides, count), out_shape=...  5.7 us
    ppermute x8, starting transfers between devices, ring(): lax.ppermute(value, 'lon', [(i, (i + step) % lon_count) for i in range(lo...  5.12 us
    ppermute x8, waiting for transfers between devices, ring(): lax.ppermute(value, 'lon', [(i, (i + step) % lon_count) for i in range(lo...  4.46 us
    ppermute x1, starting transfers between devices, shards(): strip_a = lax.ppermute(to_a, 'lat', [(i, i ^ 1) for i in range(lat_count)])  3.09 us
    pallas_call x1, Pallas kernels, shards(): pl.pallas_call(pack_kernel, out_shape=[like(strip, columns), *[like(edge_...  2.04 us
    ppermute x1, starting transfers between devices, shards(): strip_b = lax.ppermute(to_b, 'lat', odd_up + [(j, i) for i, j in odd_up])  0.84 us
  transfers between devices with their start and end apart: 10, of which 3 were waited for; matrix products, arithmetic and copies ran while one was open for 0% of the time, Pallas kernels for 45%

profile of v16, /device:TPU:0, one launch (start us, length us, event | category | flops | bytes accessed | tf_op | source)
XLA Modules:
  0.0 34.1 jit_solution(6470526734936939434)
XLA Ops:
  0.6 2.0 %pack_edges.1 = (f32[200,896]{1,0:T(8,128)S(1)}, f32[48,128]{1,0:T(8,128)S(1)}, f32[48,128]{1,0:T(8,128)S(1)}, f32[3,16,8,256]{3,2,1,0:T(8,128)S(1)}, f32[2,16,8,128]{3,2,1,0:T(8,128)S(1)}) custom-call(f32[16,16,896]{2,1,0:T(8,128)} %refs_0_.13, f32[16,16,896]{2,1,0:T(8,128)} %refs_1_.13, f32[16,16,896]{2,1,0:T(8,128)} %refs_2_.13, f32[16,16,896]{2,1,0:T(8,128)} %refs_3_.13, ...), custom_call_target="tpu_custom_call" | custom-call | tf_op jit(solution)/shard_map/pack_edges/pallas_call | solution.py:680
  2.7 3.1 %collective-permute-start.2 = (f32[200,896]{1,0:T(8,128)S(1)}, f32[200,896]{1,0:T(8,128)S(1)}, u32[]{:S(2)}, u32[]{:S(2)}) collective-permute-start(f32[200,896]{1,0:T(8,128)S(1)} %get-tuple-element.39), channel_id=1, source_target_pairs={{0,4},{4,0},{8,12},{12,8},{1,5},{5,1},{9,13},{13,9},{2,6},{6,2},{1... | collective-permute-start | bytes 2150408 | tf_op jit(solution)/shard_map/ppermute | solution.py:718
  5.8 0.0 copy-start
  5.8 0.0 copy-start.1
  5.8 0.0 copy-start.2
  5.8 0.0 copy-start.3
  5.8 0.0 copy-start.8
  5.8 0.1 pack_b.1
  5.9 0.8 %collective-permute-start.9 = (f32[200,896]{1,0:T(8,128)S(1)}, f32[200,896]{1,0:T(8,128)S(1)}, u32[]{:S(2)}, u32[]{:S(2)}) collective-permute-start(f32[200,896]{1,0:T(8,128)S(1)} %pack_b.1), channel_id=1, source_target_pairs={{4,8},{8,4},{5,9},{9,5},{6,10},{10,6},{7,11},{11,7},{20,24},{24,20... | collective-permute-start | bytes 2150408 | tf_op jit(solution)/shard_map/ppermute | solution.py:719
  6.8 0.7 %collective-permute-start.1 = (f32[48,128]{1,0:T(8,128)S(1)}, f32[48,128]{1,0:T(8,128)S(1)}, u32[]{:S(2)}, u32[]{:S(2)}) collective-permute-start(f32[48,128]{1,0:T(8,128)S(1)} %get-tuple-element.36.refs_5_), channel_id=1, source_target_pairs={{0,3},{1,0},{2,1},{3,2},{4,7},{5,4},{6,5},{7,6},{8,11},{9,8},{10,9... | collective-permute-start | bytes 73736 | tf_op jit(solution)/shard_map/ppermute | solution.py:713
  7.5 0.0 collective-permute-start
  7.5 1.5 %collective-permute-done.1.refs_6_ = f32[48,128]{1,0:T(8,128)S(1)} collective-permute-done((f32[48,128]{1,0:T(8,128)S(1)}, f32[48,128]{1,0:T(8,128)S(1)}, u32[]{:S(2)}, u32[]{:S(2)}) %collective-permute-start.1) | collective-permute-done | bytes 24608 | tf_op jit(solution)/shard_map/ppermute | solution.py:713
  9.0 1.7 %collective-permute-done.refs_5_ = f32[48,128]{1,0:T(8,128)S(1)} collective-permute-done((f32[48,128]{1,0:T(8,128)S(1)}, f32[48,128]{1,0:T(8,128)S(1)}, u32[]{:S(2)}, u32[]{:S(2)}) %collective-permute-start) | collective-permute-done | bytes 24608 | tf_op jit(solution)/shard_map/ppermute | solution.py:713
  10.7 0.0 copy-done
  10.7 0.0 copy-done.1
  10.7 0.0 copy-done.2
  10.7 0.0 copy-done.3
  10.7 0.0 copy-done.8
  10.8 0.0 copy-start.4
  10.8 0.0 copy-start.5
  10.8 0.0 copy-start.6
  10.8 0.0 copy-start.7
  10.8 0.0 copy-start.9
  10.8 9.0 %tend_inner.1 = (f32[16,16,896]{2,1,0:T(8,128)}, f32[16,16,896]{2,1,0:T(8,128)}, f32[16,16,896]{2,1,0:T(8,128)}, f32[16,16,896]{2,1,0:T(8,128)}, f32[4,208,256]{...) custom-call(f32[16,16,896]{2,1,0:T(8,128)S(1)} %copy-done, ...), custom_call_target="tpu_custom_call" | custom-call | flops 2981888000 | bytes 4194304 | tf_op jit(solution)/shard_map/tend_inner/pallas_call | solution.py:740
  19.8 0.1 collective-permute-start.6
  19.9 1.7 %collective-permute-start.7 = (f32[208,128]{1,0:T(8,128)S(1)}, f32[208,128]{1,0:T(8,128)S(1)}, u32[]{:S(2)}, u32[]{:S(2)}) collective-permute-start(f32[208,128]{1,0:T(8,128)S(1)} %get-tuple-element.51), channel_id=1, source_target_pairs={{0,3},{1,0},{2,1},{3,2},{4,7},{5,4},{6,5},{7,6},{8,11},{9,8},{10,9... | collective-permute-start | bytes 319496 | tf_op jit(solution)/shard_map/ppermute | solution.py:713
  21.6 0.9 %collective-permute-start.8 = (f32[104,128]{1,0:T(8,128)S(1)}, f32[104,128]{1,0:T(8,128)S(1)}, u32[]{:S(2)}, u32[]{:S(2)}) collective-permute-start(f32[104,128]{1,0:T(8,128)S(1)} %get-tuple-element.52), channel_id=1, source_target_pairs={{0,2},{1,3},{2,0},{3,1},{4,6},{5,7},{6,4},{7,5},{8,10},{9,11},{10,... | collective-permute-start | bytes 159752 | tf_op jit(solution)/shard_map/ppermute | solution.py:713
  22.5 0.0 collective-permute-done.2.refs_9_
  22.5 0.0 copy-done.4
  22.5 0.0 copy-done.5
  22.5 0.0 copy-done.6
  22.5 0.0 copy-done.7
  22.5 0.0 copy-done.9
  22.5 2.5 %tend_edge.2 = (f32[16,16,896]{2,1,0:T(8,128)}, f32[16,16,896]{2,1,0:T(8,128)}, f32[16,16,896]{2,1,0:T(8,128)}, f32[16,16,896]{2,1,0:T(8,128)}, f32[4,48,256]{2,...) custom-call(f32[16,16,896]{2,1,0:T(8,128)S(1)} %copy-done, ...), custom_call_target="tpu_custom_call", output_to_operand_aliasing={{0}: (17, {}), {1}: (18, {}), {2}: (19, {}), {3}: (20, {})} | custom-call | flops 688128000 | bytes 4194304 | tf_op jit(solution)/shard_map/tend_edge/pallas_call | solution.py:740
  25.0 0.1 collective-permute-start.3
  25.1 1.2 %collective-permute-done.8.refs_6_ = f32[104,128]{1,0:T(8,128)S(1)} collective-permute-done((f32[104,128]{1,0:T(8,128)S(1)}, f32[104,128]{1,0:T(8,128)S(1)}, u32[]{:S(2)}, u32[]{:S(2)}) %collective-permute-start.8) | collective-permute-done | bytes 53280 | tf_op jit(solution)/shard_map/ppermute | solution.py:713
  26.3 0.5 %collective-permute-start.4 = (f32[48,128]{1,0:T(8,128)S(1)}, f32[48,128]{1,0:T(8,128)S(1)}, u32[]{:S(2)}, u32[]{:S(2)}) collective-permute-start(f32[48,128]{1,0:T(8,128)S(1)} %get-tuple-element.47), channel_id=1, source_target_pairs={{0,3},{1,0},{2,1},{3,2},{4,7},{5,4},{6,5},{7,6},{8,11},{9,8},{10,9... | collective-permute-start | bytes 73736 | tf_op jit(solution)/shard_map/ppermute | solution.py:713
  26.8 0.0 collective-permute-done.9.refs_9_
  26.8 1.1 %collective-permute-start.5 = (f32[24,128]{1,0:T(8,128)S(1)}, f32[24,128]{1,0:T(8,128)S(1)}, u32[]{:S(2)}, u32[]{:S(2)}) collective-permute-start(f32[24,128]{1,0:T(8,128)S(1)} %get-tuple-element.48), channel_id=1, source_target_pairs={{0,2},{1,3},{2,0},{3,1},{4,6},{5,7},{6,4},{7,5},{8,10},{9,11},{10,... | collective-permute-start | bytes 36872 | tf_op jit(solution)/shard_map/ppermute | solution.py:713
  27.9 0.3 tend_edge.3
  28.2 0.0 collective-permute-done.6.refs_4_
  28.2 0.0 collective-permute-done.7.refs_5_
  28.2 3.6 %finish_inner.1 = (f32[16,16,896]{2,1,0:T(8,128)}, f32[16,16,896]{2,1,0:T(8,128)}, f32[16,16,896]{2,1,0:T(8,128)}, f32[16,16,896]{2,1,0:T(8,128)}) custom-call(f32[16,16,896]{2,1,0:T(8,128)S(1)} %copy-done, f32[16,16,896]{2,1,0:T(8,128)S(1)} %copy-done.1, ...), custom_call_target="tpu_custom_call", output_to_operand_aliasing={{0}: (11, {}), {1}: (12, {}), {2}: (13, {}), {3}: (14, {})} | custom-call | tf_op jit(solution)/shard_map/finish_inner/pallas_call | solution.py:773
  31.8 0.0 collective-permute-done.5.refs_6_
  31.9 0.0 collective-permute-done.3.refs_4_
  31.9 0.0 collective-permute-done.4.refs_5_
  31.9 2.1 %finish_edge.1 = (f32[16,16,896]{2,1,0:T(8,128)}, f32[16,16,896]{2,1,0:T(8,128)}, f32[16,16,896]{2,1,0:T(8,128)}, f32[16,16,896]{2,1,0:T(8,128)}) custom-call(f32[16,16,896]{2,1,0:T(8,128)S(1)} %copy-done, f32[16,16,896]{2,1,0:T(8,128)S(1)} %copy-done.1, ...), custom_call_target="tpu_custom_call", output_to_operand_aliasing={{0}: (11, {}), {1}: (12, {}), {2}: (13, {}), {3}: (14, {})} | custom-call | tf_op jit(solution)/shard_map/finish_edge/pallas_call | solution.py:773
Async XLA Ops:
  2.7 19.8 %collective-permute-start.2 = (f32[200,896]{1,0:T(8,128)S(1)}, f32[200,896]{1,0:T(8,128)S(1)}, u32[]{:S(2)}, u32[]{:S(2)}) collective-permute-start(f32[200,896]{1,0:T(8,128)S(1)} %get-tuple-element.39), channel_id=1, source_target_pairs={{0,4},{4,0},{8,12},{12,8},{1,5},{5,1},{9,13},{13,9},{2,6},{6,2},{1... | collective-permute-start | bytes 2150408 | tf_op jit(solution)/shard_map/ppermute | solution.py:718
  5.8 5.0 %copy-start = (f32[16,16,896]{2,1,0:T(8,128)S(1)}, f32[16,16,896]{2,1,0:T(8,128)}, u32[]{:S(2)}) copy-start(f32[16,16,896]{2,1,0:T(8,128)} %refs_0_.13) | copy-start | bytes 2752516
  5.8 5.0 %copy-start.1 = (f32[16,16,896]{2,1,0:T(8,128)S(1)}, f32[16,16,896]{2,1,0:T(8,128)}, u32[]{:S(2)}) copy-start(f32[16,16,896]{2,1,0:T(8,128)} %refs_1_.13) | copy-start | bytes 2752516
  5.8 5.0 %copy-start.2 = (f32[16,16,896]{2,1,0:T(8,128)S(1)}, f32[16,16,896]{2,1,0:T(8,128)}, u32[]{:S(2)}) copy-start(f32[16,16,896]{2,1,0:T(8,128)} %refs_2_.13) | copy-start | bytes 2752516
  5.8 5.0 %copy-start.3 = (f32[16,16,896]{2,1,0:T(8,128)S(1)}, f32[16,16,896]{2,1,0:T(8,128)}, u32[]{:S(2)}) copy-start(f32[16,16,896]{2,1,0:T(8,128)} %refs_3_.13) | copy-start | bytes 2752516
  5.8 5.0 %copy-start.8 = (f32[16,896]{1,0:T(8,128)S(1)}, f32[16,896]{1,0:T(8,128)}, u32[]{:S(2)}) copy-start(f32[16,896]{1,0:T(8,128)} %refs_4_.9) | copy-start | bytes 172036
  5.9 20.9 %collective-permute-start.9 = (f32[200,896]{1,0:T(8,128)S(1)}, f32[200,896]{1,0:T(8,128)S(1)}, u32[]{:S(2)}, u32[]{:S(2)}) collective-permute-start(f32[200,896]{1,0:T(8,128)S(1)} %pack_b.1), channel_id=1, source_target_pairs={{4,8},{8,4},{5,9},{9,5},{6,10},{10,6},{7,11},{11,7},{20,24},{24,20... | collective-permute-start | bytes 2150408 | tf_op jit(solution)/shard_map/ppermute | solution.py:719
  6.8 2.2 %collective-permute-start.1 = (f32[48,128]{1,0:T(8,128)S(1)}, f32[48,128]{1,0:T(8,128)S(1)}, u32[]{:S(2)}, u32[]{:S(2)}) collective-permute-start(f32[48,128]{1,0:T(8,128)S(1)} %get-tuple-element.36.refs_5_), channel_id=1, source_target_pairs={{0,3},{1,0},{2,1},{3,2},{4,7},{5,4},{6,5},{7,6},{8,11},{9,8},{10,9... | collective-permute-start | bytes 73736 | tf_op jit(solution)/shard_map/ppermute | solution.py:713
  7.5 3.3 %collective-permute-start = (f32[48,128]{1,0:T(8,128)S(1)}, f32[48,128]{1,0:T(8,128)S(1)}, u32[]{:S(2)}, u32[]{:S(2)}) collective-permute-start(f32[48,128]{1,0:T(8,128)S(1)} %get-tuple-element.35), channel_id=1, source_target_pairs={{0,1},{1,2},{2,3},{3,0},{4,5},{5,6},{6,7},{7,4},{8,9},{9,10},{10,1... | collective-permute-start | bytes 73736 | tf_op jit(solution)/shard_map/ppermute | solution.py:713
  10.8 11.7 %copy-start.4 = (bf16[768,896]{1,0:T(8,128)(2,1)S(1)}, bf16[768,896]{1,0:T(8,128)(2,1)}, u32[]{:S(2)}) copy-start(bf16[768,896]{1,0:T(8,128)(2,1)} %constant.21.clone.refs_16_.refs_10_) | copy-start | bytes 4128772
  10.8 11.7 %copy-start.5 = (bf16[2688,256]{1,0:T(8,128)(2,1)S(1)}, bf16[2688,256]{1,0:T(8,128)(2,1)}, u32[]{:S(2)}) copy-start(bf16[2688,256]{1,0:T(8,128)(2,1)} %constant.18.clone.refs_10_.refs_13_) | copy-start | bytes 4128772
  10.8 11.7 %copy-start.6 = (bf16[768,512]{1,0:T(8,128)(2,1)S(1)}, bf16[768,512]{1,0:T(8,128)(2,1)}, u32[]{:S(2)}) copy-start(bf16[768,512]{1,0:T(8,128)(2,1)} %constant.19.clone.refs_11_.refs_14_) | copy-start | bytes 2359300
  10.8 11.7 %copy-start.7 = (bf16[512,256]{1,0:T(8,128)(2,1)S(1)}, bf16[512,256]{1,0:T(8,128)(2,1)}, u32[]{:S(2)}) copy-start(bf16[512,256]{1,0:T(8,128)(2,1)} %constant.17.clone.refs_9_.refs_12_) | copy-start | bytes 786436
  10.8 11.7 %copy-start.9 = (bf16[128,256]{1,0:T(8,128)(2,1)S(1)}, bf16[128,256]{1,0:T(8,128)(2,1)}, u32[]{:S(2)}) copy-start(bf16[128,256]{1,0:T(8,128)(2,1)} %constant.20.clone.refs_15_.refs_9_) | copy-start | bytes 196612
  19.8 8.4 %collective-permute-start.6 = (f32[208,128]{1,0:T(8,128)S(1)}, f32[208,128]{1,0:T(8,128)S(1)}, u32[]{:S(2)}, u32[]{:S(2)}) collective-permute-start(f32[208,128]{1,0:T(8,128)S(1)} %get-tuple-element.50), channel_id=1, source_target_pairs={{0,1},{1,2},{2,3},{3,0},{4,5},{5,6},{6,7},{7,4},{8,9},{9,10},{10,1... | collective-permute-start | bytes 319496 | tf_op jit(solution)/shard_map/ppermute | solution.py:713
  19.9 8.3 %collective-permute-start.7 = (f32[208,128]{1,0:T(8,128)S(1)}, f32[208,128]{1,0:T(8,128)S(1)}, u32[]{:S(2)}, u32[]{:S(2)}) collective-permute-start(f32[208,128]{1,0:T(8,128)S(1)} %get-tuple-element.51), channel_id=1, source_target_pairs={{0,3},{1,0},{2,1},{3,2},{4,7},{5,4},{6,5},{7,6},{8,11},{9,8},{10,9... | collective-permute-start | bytes 319496 | tf_op jit(solution)/shard_map/ppermute | solution.py:713
  21.6 4.7 %collective-permute-start.8 = (f32[104,128]{1,0:T(8,128)S(1)}, f32[104,128]{1,0:T(8,128)S(1)}, u32[]{:S(2)}, u32[]{:S(2)}) collective-permute-start(f32[104,128]{1,0:T(8,128)S(1)} %get-tuple-element.52), channel_id=1, source_target_pairs={{0,2},{1,3},{2,0},{3,1},{4,6},{5,7},{6,4},{7,5},{8,10},{9,11},{10,... | collective-permute-start | bytes 159752 | tf_op jit(solution)/shard_map/ppermute | solution.py:713
  25.0 6.9 %collective-permute-start.3 = (f32[48,128]{1,0:T(8,128)S(1)}, f32[48,128]{1,0:T(8,128)S(1)}, u32[]{:S(2)}, u32[]{:S(2)}) collective-permute-start(f32[48,128]{1,0:T(8,128)S(1)} %get-tuple-element.46), channel_id=1, source_target_pairs={{0,1},{1,2},{2,3},{3,0},{4,5},{5,6},{6,7},{7,4},{8,9},{9,10},{10,1... | collective-permute-start | bytes 73736 | tf_op jit(solution)/shard_map/ppermute | solution.py:713
  26.3 5.6 %collective-permute-start.4 = (f32[48,128]{1,0:T(8,128)S(1)}, f32[48,128]{1,0:T(8,128)S(1)}, u32[]{:S(2)}, u32[]{:S(2)}) collective-permute-start(f32[48,128]{1,0:T(8,128)S(1)} %get-tuple-element.47), channel_id=1, source_target_pairs={{0,3},{1,0},{2,1},{3,2},{4,7},{5,4},{6,5},{7,6},{8,11},{9,8},{10,9... | collective-permute-start | bytes 73736 | tf_op jit(solution)/shard_map/ppermute | solution.py:713
  26.8 5.0 %collective-permute-start.5 = (f32[24,128]{1,0:T(8,128)S(1)}, f32[24,128]{1,0:T(8,128)S(1)}, u32[]{:S(2)}, u32[]{:S(2)}) collective-permute-start(f32[24,128]{1,0:T(8,128)S(1)} %get-tuple-element.48), channel_id=1, source_target_pairs={{0,2},{1,3},{2,0},{3,1},{4,6},{5,7},{6,4},{7,5},{8,10},{9,11},{10,... | collective-permute-start | bytes 36872 | tf_op jit(solution)/shard_map/ppermute | solution.py:713
